TPU v7x, 512 devices: a whole 4x8x8 slice. The times are simulated.
512 devices in a mesh: blk: 32 (over z_hi, x, core), rows: 16 (over z_lo, y).
Axes of the slice: x: 4, y: 8, z: 8 (z_hi: 4, z_lo: 2; z = z_hi * 2 + z_lo), core: 2. Of those that a mesh axis runs over, the one named last changes fastest.
Arguments:
- hidden_in: bfloat16 [128, 8192], P('rows', 'blk'), may hold values from -6 to 6
- norm_gain: bfloat16 [8192], P('blk'), may hold values from 0.25 to 1.75
- w_query: bfloat16 [8192, 8192], P('blk', 'rows'), may hold values from -0.0625 to 0.0625
- w_keyval: bfloat16 [8192, 2048], P('blk', 'rows'), may hold values from -0.25 to 0.25
- w_out: bfloat16 [8192, 8192], P('rows', 'blk'), may hold values from -0.0625 to 0.0625
- prefix_keys: bfloat16 [65536, 1024], P(('blk', 'rows')), may hold values from -60 to 60
- prefix_values: bfloat16 [65536, 1024], P(('blk', 'rows')), may hold values from -6 to 6
- own_keys: bfloat16 [128, 256, 1024], P('rows', 'blk'), may hold values from -12 to 12
- own_values: bfloat16 [128, 256, 1024], P('rows', 'blk'), may hold values from -6 to 6
- positions: int32 [128], replicated, may hold values from 65536 to 131071
- lengths: int32 [128], P('rows'), may hold values from 1 to 256, as said below
Outputs:
- hidden_out: bfloat16 [128, 8192], P('rows', 'blk')
Inputs may be any that keep to these rules, and one draw needn't show every extreme that they name: `lengths`: own cache slots at or beyond a row's length are ignored; some row has exactly 256 live slots.
All inputs are finite; a program needn't handle non-finite values.
Results may differ from a plain program's by a relative error of at most 0.02.
Values may be sent and summed in bfloat16 or wider, within the bound.
No kernel may reach another device: no remote copies, remote signals or barrier semaphores. Data moves between devices by JAX's collectives and lax.ppermute only.
A program may use at most 64 MiB of HBM per device.

v0:
```python
import jax
import jax.numpy as jnp
import numpy as np
from jax import lax
from jax.sharding import PartitionSpec as P

HD = 128


def freq_table(width):
    return (1.0 / 500000.0 ** (np.arange(0, width, 2) / width)).astype(np.float32)


def rotate_pairs(values, positions):
    width = values.shape[-1]
    half_w = width // 2
    angles = (
        positions.astype(jnp.float32)[:, None, None]
        * jnp.asarray(freq_table(width), jnp.float32)[None, None, :]
    )
    cosine = jnp.cos(angles)
    sine = jnp.sin(angles)
    first = values[..., :half_w]
    second = values[..., half_w:]
    return jnp.concatenate(
        [first * cosine - second * sine, second * cosine + first * sine], axis=-1
    )


def on_device(
    hidden_in,
    norm_gain,
    w_query,
    w_keyval,
    w_out,
    prefix_keys,
    prefix_values,
    own_keys,
    own_values,
    positions,
    lengths,
):
    blk_count = lax.axis_size("blk")
    rows_dev = hidden_in.shape[0]
    inputs = hidden_in.astype(jnp.float32)
    square = lax.psum(jnp.sum(inputs * inputs, axis=1), "blk")
    mean_sq = square / (hidden_in.shape[1] * blk_count)
    normed = (
        inputs * lax.rsqrt(mean_sq + 1e-05)[:, None] * norm_gain.astype(jnp.float32)[None, :]
    ).astype(jnp.bfloat16)
    every_row = lax.all_gather(normed, "rows", axis=0, tiled=True)
    query_part = jnp.dot(every_row, w_query, preferred_element_type=jnp.float32)
    keyval_part = jnp.dot(every_row, w_keyval, preferred_element_type=jnp.float32)
    query_sum, keyval_sum = lax.psum((query_part, keyval_part), "blk")
    query_raw, keyval_raw = (
        lax.all_gather(query_sum.astype(jnp.bfloat16), "rows", axis=1, tiled=True),
        lax.all_gather(keyval_sum.astype(jnp.bfloat16), "rows", axis=1, tiled=True),
    )
    total_rows = query_raw.shape[0]
    heads = query_raw.shape[1] // HD
    kv_heads = keyval_raw.shape[1] // (2 * HD)
    group = heads // kv_heads
    query = rotate_pairs(
        query_raw.astype(jnp.float32).reshape(total_rows, heads, HD), positions
    ).astype(jnp.bfloat16)
    new_key = rotate_pairs(
        keyval_raw[:, : kv_heads * HD].astype(jnp.float32).reshape(total_rows, kv_heads, HD),
        positions,
    ).astype(jnp.bfloat16)
    new_value = keyval_raw[:, kv_heads * HD :].reshape(total_rows, kv_heads, HD)
    grouped = query.reshape(total_rows, kv_heads, group, HD)
    scale = HD ** (-0.5)
    cache_keys = prefix_keys.reshape(-1, kv_heads, HD)
    cache_values = prefix_values.reshape(-1, kv_heads, HD)
    scores = (
        jnp.einsum("rkgd,tkd->rkgt", grouped, cache_keys, preferred_element_type=jnp.float32)
        * scale
    )
    peak = jnp.max(scores, axis=-1)
    row_start = lax.axis_index("rows") * rows_dev
    blk_index = lax.axis_index("blk")
    own_query = lax.dynamic_slice_in_dim(grouped, row_start, rows_dev, 0)
    slots = own_keys.shape[1]
    own_k = own_keys.reshape(rows_dev, slots, kv_heads, HD)
    own_v = own_values.reshape(rows_dev, slots, kv_heads, HD)
    own_scores = (
        jnp.einsum("rkgd,rtkd->rkgt", own_query, own_k, preferred_element_type=jnp.float32) * scale
    )
    slot_ids = blk_index * slots + jnp.arange(slots, dtype=jnp.int32)
    valid = slot_ids[None, :] < lengths[:, None]
    own_scores = jnp.where(valid[:, None, None, :], own_scores, -jnp.inf)
    own_new_key = lax.dynamic_slice_in_dim(new_key, row_start, rows_dev, 0)
    own_new_value = lax.dynamic_slice_in_dim(new_value, row_start, rows_dev, 0)
    new_scores = (
        jnp.einsum("rkgd,rkd->rkg", own_query, own_new_key, preferred_element_type=jnp.float32)
        * scale
    )
    new_scores = jnp.where(blk_index == 0, new_scores, -jnp.inf)
    own_peak = jnp.maximum(jnp.max(own_scores, axis=-1), new_scores)
    peak_rows = jnp.maximum(lax.dynamic_slice_in_dim(peak, row_start, rows_dev, 0), own_peak)
    local_peak = lax.dynamic_update_slice_in_dim(peak, peak_rows, row_start, 0)
    top = lax.pmax(local_peak.astype(jnp.bfloat16), ("blk", "rows")).astype(local_peak.dtype)
    top_own = lax.dynamic_slice_in_dim(top, row_start, rows_dev, 0)
    weights = jnp.exp(scores - peak[..., None])
    shrink = jnp.exp(peak - top)
    accum = (
        jnp.einsum(
            "rkgt,tkd->rkgd",
            weights.astype(jnp.bfloat16),
            cache_values,
            preferred_element_type=jnp.float32,
        )
        * shrink[..., None]
    )
    mass = jnp.sum(weights, axis=-1) * shrink
    own_w = jnp.exp(own_scores - top_own[..., None])
    new_w = jnp.exp(new_scores - top_own)
    new_half = lax.optimization_barrier(new_w.astype(jnp.bfloat16)).astype(jnp.float32)
    own_accum = jnp.einsum(
        "rkgt,rtkd->rkgd", own_w.astype(jnp.bfloat16), own_v, preferred_element_type=jnp.float32
    )
    own_accum = own_accum + new_half[..., None] * own_new_value.astype(jnp.float32)[:, :, None, :]
    own_mass = jnp.sum(own_w, axis=-1) + new_w
    accum = lax.dynamic_update_slice_in_dim(
        accum, lax.dynamic_slice_in_dim(accum, row_start, rows_dev, 0) + own_accum, row_start, 0
    )
    mass = lax.dynamic_update_slice_in_dim(
        mass, lax.dynamic_slice_in_dim(mass, row_start, rows_dev, 0) + own_mass, row_start, 0
    )
    head_accum = accum.reshape(total_rows, heads, HD)
    head_mass = mass.reshape(total_rows, heads)
    part_accum, part_mass = (
        lax.psum_scatter(
            head_accum.astype(jnp.bfloat16), "rows", scatter_dimension=1, tiled=True
        ).astype(jnp.float32),
        lax.psum_scatter(
            head_mass.astype(jnp.bfloat16), "rows", scatter_dimension=1, tiled=True
        ).astype(jnp.float32),
    )
    summed_accum, summed_mass = (
        lax.psum(part_accum.astype(jnp.bfloat16), "blk").astype(jnp.float32),
        lax.psum(part_mass.astype(jnp.bfloat16), "blk").astype(jnp.float32),
    )
    attended = (summed_accum / summed_mass[..., None]).astype(jnp.bfloat16).reshape(total_rows, -1)
    mixed = lax.psum_scatter(
        jnp.dot(attended, w_out, preferred_element_type=jnp.float32).astype(jnp.bfloat16),
        "rows",
        scatter_dimension=0,
        tiled=True,
    ).astype(jnp.float32)
    return (inputs + mixed).astype(jnp.bfloat16)


def solution(mesh):
    return jax.shard_map(
        on_device,
        mesh=mesh,
        in_specs=(
            P("rows", "blk"),
            P("blk"),
            P("blk", "rows"),
            P("blk", "rows"),
            P("rows", "blk"),
            P(("blk", "rows"), None),
            P(("blk", "rows"), None),
            P("rows", "blk", None),
            P("rows", "blk", None),
            P(),
            P("rows"),
        ),
        out_specs=P("rows", "blk"),
        check_vma=False,
    )
```

profile of v0, /device:TPU:1, one launch (start us, length us, event | category | flops | bytes accessed | tf_op | source)
XLA Modules:
  0.0 858.9 jit_solution(5085030833321258879)
XLA Ops:
  6.5 0.8 fusion.31
  7.4 76.1 %psum.35 = f32[8]{0:T(128)S(1)} all-reduce(f32[8]{0:T(128)S(1)} %fusion.31), channel_id=1, replica_groups=mesh['blk'=32,'rows'=16] {'blk'}, use_global_device_ids=true, to_apply=%region_1.0 | all-reduce | flops 8 | bytes 64 | tf_op jit(solution)/shard_map/psum | solution.py:46
  83.5 0.7 convert_element_type.80
  84.2 0.8 fusion.33
  84.9 27.2 %all_gather.9 = bf16[128,256]{1,0:T(8,128)(2,1)S(1)} all-gather(bf16[8,256]{1,0:T(8,128)(2,1)S(1)} %fusion.33), channel_id=1, replica_groups=mesh['blk'=32,'rows'=16] {'rows'}, dimensions={0}, use_global_device_ids=true | all-gather | bytes 69632 | tf_op jit(solution)/shard_map/all_gather | solution.py:51
  112.1 1.0 fusion.40
  113.3 148.4 %all-reduce.6 = (bf16[128,512]{1,0:T(8,128)(2,1)}, bf16[128,128]{1,0:T(8,128)(2,1)S(1)}) all-reduce(f32[128,512]{1,0:T(8,128)S(1)} %fusion.39, f32[128,128]{1,0:T(8,128)S(1)} %fusion.40), channel_id=1, replica_groups=mesh['blk'=32,'rows'=16] {'blk'}, use_global_device_ids=true, to_apply=%region_2.0 | all-reduce | flops 81920 | bytes 491520 | tf_op jit(solution)/shard_map/psum | solution.py:54
  261.8 0.7 convert_element_type.83
  262.4 1.0 copy.88
  263.4 1.0 copy.89
  264.4 28.8 %all_gather.11 = bf16[128,2048]{1,0:T(8,128)(2,1)S(1)} all-gather(bf16[128,128]{1,0:T(8,128)(2,1)S(1)} %get-tuple-element.6), channel_id=1, replica_groups=mesh['blk'=32,'rows'=16] {'rows'}, dimensions={1}, use_global_device_ids=true | all-gather | bytes 557056 | tf_op jit(solution)/shard_map/all_gather | solution.py:57
  294.2 27.3 %all-gather.2.cloned.1.call-done = bf16[128,8192]{1,0:T(8,128)(2,1)} async-done(((bf16[128,512]{1,0:T(8,128)(2,1)}), bf16[128,8192]{1,0:T(8,128)(2,1)}) %all-gather.2.cloned.1.call-update) | async-done | bytes 2097168 | tf_op jit(solution)/shard_map/all_gather | solution.py:56
  321.6 2.0 convert_bitcast_fusion
  323.6 0.7 copy.87
  324.3 1.5 subtract_convert_fusion
  325.9 1.4 copy.63
  327.2 1.4 copy.64
  328.7 3.5 bitcast_reduce_fusion
  332.5 3.1 fusion.1
  336.2 108.5 %pmax.7 = bf16[128,8,8]{0,2,1:T(8,128)(2,1)S(1)} all-reduce(bf16[128,8,8]{0,2,1:T(8,128)(2,1)S(1)} %convert_element_type.86), channel_id=1, replica_groups=mesh['blk'=32,'rows'=16] {'blk','rows'}, use_global_device_ids=true, to_apply=%region_6.7 | all-reduce | flops 8192 | bytes 32768 | tf_op jit(solution)/shard_map/pmax | solution.py:102
  444.9 3.7 bitcast_multiply_fusion
  449.1 0.4 convert_element_type.92
  449.6 2.9 copy.74
  452.6 1.3 dynamic-slice
  455.0 56.6 %reduce-scatter.3.cloned.1.call-done = bf16[128,4,128]{0,2,1:T(8,128)(2,1)} async-done(((bf16[128,64,128]{0,2,1:T(8,128)(2,1)}), bf16[128,4,128]{0,2,1:T(8,128)(2,1)}) %reduce-scatter.3.cloned.1.call-update) | async-done | bytes 131088 | tf_op jit(solution)/shard_map/reduce_scatter | solution.py:133
  511.7 49.6 %all-reduce = bf16[128,64]{0,1:T(8,128)(2,1)S(1)} all-reduce(bf16[128,64]{0,1:T(8,128)(2,1)S(1)} %convert_bitcast_fusion.2), channel_id=3, replica_groups=mesh['blk'=32,'rows'=16] {'rows'}, use_global_device_ids=true, to_apply=%region_11.12.clone | all-reduce | flops 8192 | bytes 32768
  561.3 92.2 %psum.39 = bf16[128,4]{0,1:T(4,128)(2,1)S(1)} all-reduce(bf16[128,4]{0,1:T(4,128)(2,1)S(1)} %constant_dynamic-slice_fusion.2), channel_id=1, replica_groups=mesh['blk'=32,'rows'=16] {'blk'}, use_global_device_ids=true, to_apply=%region_12.13 | all-reduce | flops 512 | bytes 2048 | tf_op jit(solution)/shard_map/psum | solution.py:142
  653.5 135.6 %all-reduce.5.cloned.1.call-done = bf16[128,4,128]{0,2,1:T(8,128)(2,1)} async-done(((bf16[128,4,128]{0,2,1:T(8,128)(2,1)}), bf16[128,4,128]{0,2,1:T(8,128)(2,1)}) %all-reduce.5.cloned.1.call-update) | async-done | bytes 131088 | tf_op jit(solution)/shard_map/psum | solution.py:141
  789.1 0.9 divide_convert_fusion
  790.1 0.8 convolution_convert_fusion
  790.9 60.2 %reduce-scatter.5.cloned.1.call-done = bf16[8,256]{1,0:T(8,128)(2,1)} async-done(((bf16[128,256]{1,0:T(8,128)(2,1)}), bf16[8,256]{1,0:T(8,128)(2,1)}) %reduce-scatter.5.cloned.1.call-update) | async-done | bytes 4112 | tf_op jit(solution)/shard_map/reduce_scatter | solution.py:145
  851.1 1.3 fusion.34
  (57 shorter events, 3.7 us)
Async XLA Ops:
  6.5 106.6 %copy-start = (bf16[256,512]{1,0:T(8,128)(2,1)S(1)}, bf16[256,512]{1,0:T(8,128)(2,1)}, u32[]{:S(2)}) copy-start(bf16[256,512]{1,0:T(8,128)(2,1)} %param.15) | copy-start | bytes 786436
  6.5 286.9 %copy-start.5 = (f32[64]{0:T(128)S(1)}, f32[64]{0:T(128)}, u32[]{:S(2)}) copy-start(f32[64]{0:T(128)} %constant.30.clone) | copy-start | bytes 772
  6.5 287.6 %copy-start.6 = (s32[8]{0:T(128)S(1)}, s32[8]{0:T(128)}, u32[]{:S(2)}) copy-start(s32[8]{0:T(128)} %param.23) | copy-start | bytes 100
  6.5 315.0 %all-gather.2.cloned.1.call-start = ((), (), s32[]{:S(2)}) async-start(), calls=%async_computation.2 | async-start | bytes 2228224 | tf_op jit(solution)/shard_map/all_gather | solution.py:56
  261.7 249.9 %reduce-scatter.3.cloned.1.call-start = ((), (), s32[]{:S(2)}) async-start(), calls=%async_computation.3 | async-start | bytes 2228224 | tf_op jit(solution)/shard_map/reduce_scatter | solution.py:133
  332.2 3.4 copy-start.2
  444.9 3.7 copy-start.3
  449.5 340.5 %copy-start.1 = (bf16[512,256]{1,0:T(8,128)(2,1)S(1)}, bf16[512,256]{1,0:T(8,128)(2,1)}, u32[]{:S(2)}) copy-start(bf16[512,256]{1,0:T(8,128)(2,1)} %param.17) | copy-start | bytes 786436
  449.5 401.6 %copy-start.4 = (bf16[8,256]{1,0:T(8,128)(2,1)S(1)}, bf16[8,256]{1,0:T(8,128)(2,1)}, u32[]{:S(2)}) copy-start(bf16[8,256]{1,0:T(8,128)(2,1)} %param.13) | copy-start | bytes 12292
  452.5 336.6 %all-reduce.5.cloned.1.call-start = ((), (), s32[]{:S(2)}) async-start(), calls=%async_computation.4 | async-start | bytes 262144 | tf_op jit(solution)/shard_map/psum | solution.py:141
  511.6 339.5 %reduce-scatter.5.cloned.1.call-start = ((), (), s32[]{:S(2)}) async-start(), calls=%async_computation.5 | async-start | bytes 69632 | tf_op jit(solution)/shard_map/reduce_scatter | solution.py:145
Sparse Core Ops, SparseCore 0:
  261.8 59.6 all-gather.1
  452.6 58.9 reduce-scatter.2
  514.5 274.5 all-reduce.4
  792.0 59.0 reduce-scatter.4
where the time goes:
time: 871 us; the launch traced here: 859 us
  blocking collectives  531 us (61%)
  waiting for transfers between devices  280 us (32%)
  between operations  14.1 us (2%)
  other arithmetic  13.7 us (2%)
  local copies, waits for them, and re-layouts  10.6 us (1%)
  matrix products  9.89 us (1%)
    psum x1, blocking collectives, on_device(): query_sum, keyval_sum = lax.psum((query_part, keyval_part), 'blk')  148 us
    psum x1, waiting for transfers between devices, on_device(): lax.psum(part_accum.astype(jnp.bfloat16), 'blk').astype(jnp.float32)  136 us
    pmax x1, blocking collectives, on_device(): lax.pmax(local_peak.astype(jnp.bfloat16), ('blk', 'rows'))  108 us
    psum x1, blocking collectives, on_device(): lax.psum(part_mass.astype(jnp.bfloat16), 'blk').astype(jnp.float32)  92.2 us
    psum x1, blocking collectives, on_device(): square = lax.psum(jnp.sum(inputs * inputs, axis=1), 'blk')  76.1 us
    reduce_scatter x1, waiting for transfers between devices, on_device(): lax.psum_scatter(jnp.dot(attended, w_out, preferred_element_type=jnp.floa...  60.2 us
    reduce_scatter x1, waiting for transfers between devices, on_device(): lax.psum_scatter(head_accum.astype(jnp.bfloat16), 'rows', scatter_dimensi...  56.6 us
    unnamed x1, blocking collectives  49.6 us
  transfers between devices with their start and end apart: 4, of which 4 were waited for; matrix products, arithmetic and copies ran while one was open for 1% of the time, Pallas kernels for 0%

commit v1 on v0

v1 whole, which is shorter than its diff:
```python
import jax
import jax.numpy as jnp
import numpy as np
from jax import lax
from jax.experimental import pallas as pl
from jax.experimental.pallas import tpu as pltpu
from jax.sharding import PartitionSpec as P

HD = 128
F32 = jnp.float32
BF = jnp.bfloat16
VM = pl.BlockSpec(memory_space=pltpu.VMEM)
SM = pl.BlockSpec(memory_space=pltpu.SMEM)
NT = (((1,), (1,)), ((), ()))
K0, V0, OK0, OV0, X0, L0, END = 0, 64, 128, 160, 192, 208, 224


def params():
    return pltpu.CompilerParams(vmem_limit_bytes=48 * 1024 * 1024)


def iota(shape, dim):
    return lax.broadcasted_iota(jnp.int32, shape, dim)


def pack_body(who, lens, keys, values, own_k, own_v, hidden, out):
    b, r = who[0], who[1]
    x = hidden[...].astype(F32)
    x_tile = jnp.concatenate([x[:, :HD], x[:, HD:]], axis=0).astype(BF)
    lane = iota((16, HD), 1) - 32 * lax.rem(r, 4)
    inside = (lane >= 0) & (lane < 32)
    slot = 8 * b + lax.rem(lane + HD, 8)
    which = lax.div(lane + HD, 8) - 16
    for p in range(2):
        live = jnp.zeros((16, HD), jnp.int32)
        for k in range(4):
            live = jnp.where(which == k, lens[4 * p + k], live)
        flags = jnp.where(inside & (slot < live), 1.0, 0.0).astype(BF)
        for h in range(8):
            col = slice(h * HD, (h + 1) * HD)
            d = 2 * h + p
            out[d, K0:V0, :] = keys[64 * p : 64 * p + 64, col]
            out[d, V0:OK0, :] = values[64 * p : 64 * p + 64, col]
            out[d, OK0:OV0, :] = own_k[32 * p : 32 * p + 32, col]
            out[d, OV0:X0, :] = own_v[32 * p : 32 * p + 32, col]
            out[d, X0:L0, :] = x_tile
            out[d, L0:END, :] = flags


def project_body(x_ref, gain, wq, wkv, out):
    xr = x_ref[...].astype(F32)
    x = jnp.concatenate(
        [xr[:, :8, :].reshape(128, HD), xr[:, 8:, :].reshape(128, HD)], axis=1
    )
    square = lax.dot_general(
        jnp.ones((8, 2 * HD), F32), x * x, NT,
        precision=lax.Precision.HIGHEST, preferred_element_type=F32,
    )
    high = square.astype(BF).astype(F32)
    sq_tile = jnp.where(iota((8, HD), 0) == 0, high, 0.0)
    sq_tile = jnp.where(iota((8, HD), 0) == 1, square - high, sq_tile)
    xg = (x * gain[...].astype(F32)).astype(BF)
    q = jnp.dot(xg, wq[...], preferred_element_type=F32)
    kv = jnp.dot(xg, wkv[...], preferred_element_type=F32)
    for g in range(8):
        for h in range(4):
            b = 4 * g + h
            out[b, 0:16, :] = q[16 * g : 16 * g + 16, HD * h : HD * h + HD].astype(BF)
            first = 8 * (b // 2)
            out[b, 16:32, :] = jnp.concatenate([kv[first : first + 8, :], sq_tile], axis=0).astype(BF)


def rotate(u, cosine, sine):
    return u * cosine + pltpu.roll(u, HD // 2, 1) * sine


def query_body(who, parts, cosine, sine, q_out, kv_out):
    b, r = who[0], who[1]
    total = jnp.sum(parts[...].astype(F32), axis=0)
    square = total[24:25, :] + total[25:26, :]
    inv = lax.rsqrt(square / 8192.0 + 1e-05)
    lane16, sub16 = iota((16, HD), 1), iota((16, HD), 0)
    col = jnp.sum(jnp.where(lane16 == 16 * lax.div(b, 4) + sub16, inv, 0.0), axis=1, keepdims=True)
    lane8, sub8 = iota((8, HD), 1), iota((8, HD), 0)
    col8 = jnp.sum(jnp.where(lane8 == 8 * lax.div(b, 2) + sub8, inv, 0.0), axis=1, keepdims=True)
    cos, sin = cosine[...], sine[...]
    raw = (total[0:16, :] * col).astype(BF).astype(F32)
    query = rotate(raw, cos, sin).astype(BF)
    for i in range(q_out.shape[0]):
        q_out[i, :, :] = query
    upper = lax.rem(lax.div(b, 2), 2) == 1
    cos8 = jnp.where(upper, cos[8:16, :], cos[0:8, :])
    sin8 = jnp.where(upper, sin[8:16, :], sin[0:8, :])
    raw8 = (total[16:24, :] * col8).astype(BF).astype(F32)
    new = jnp.where(r < 8, rotate(raw8, cos8, sin8), raw8)
    kv_out[...] = jnp.concatenate([new, jnp.zeros((8, HD), F32)], axis=0).astype(BF)


def attend_body(who, mine, other, q_ref, new_a, new_b, out):
    b, r = who[0], who[1]
    scale = HD ** (-0.5)
    even = lax.rem(r, 2) == 0
    fa, fb = new_a[...].astype(F32), new_b[...].astype(F32)
    new_k = jnp.where(even, fa, fb).astype(BF)
    new_v = jnp.where(even, fb, fa).astype(BF)
    sources = (mine, other)
    halves = (lax.rem(r, 2), 1 - lax.rem(r, 2))
    keys = [s[:, K0:V0, :].reshape(1024, HD) for s in sources]
    values = [s[:, V0:OK0, :].reshape(1024, HD) for s in sources]
    row_q = iota((128, HD), 0)
    row_q = 16 * (row_q // 64) + row_q % 16
    lane = iota((128, HD), 1)
    row_new = 8 * lax.div(b, 2) + iota((128, 16), 1)
    mine_new = (iota((128, 16), 1) // 4) == lax.rem(b, 2)
    lane_s = iota((128, HD), 1)
    for t in range(4):
        q = q_ref[8 * t : 8 * t + 8].reshape(128, HD)
        scores, vals = [], []
        for k, v in zip(keys, values):
            scores.append(lax.dot_general(q, k, NT, preferred_element_type=F32) * scale)
            vals.append(v)
        for s, half in zip(sources, halves):
            own_k = s[4 * t : 4 * t + 4, OK0:OV0, :].reshape(128, HD)
            own_v = s[4 * t : 4 * t + 4, OV0:X0, :].reshape(128, HD)
            live = jnp.sum(s[4 * t : 4 * t + 4, L0:END, :].astype(F32), axis=0)[0:1, :]
            row_k = 8 * (lane // 32) + 4 * half + (lane % 32) // 8
            good = (row_k == row_q) & (live > 0.5)
            sc = lax.dot_general(q, own_k, NT, preferred_element_type=F32) * scale
            scores.append(jnp.where(good, sc, -jnp.inf))
            vals.append(own_v)
        sc = lax.dot_general(q, new_k, NT, preferred_element_type=F32) * scale
        good = mine_new & (row_new == row_q[:, :16] + 32 * t)
        scores.append(jnp.where(good, sc, -jnp.inf))
        vals.append(new_v)
        peak = jnp.max(scores[0], axis=1, keepdims=True)
        for sc in scores[1:]:
            peak = jnp.maximum(peak, jnp.max(sc, axis=1, keepdims=True))
        high = peak.astype(BF).astype(F32)
        low = (peak - high).astype(BF).astype(F32)
        shift = high + low
        mass = jnp.zeros((128, 1), F32)
        acc = jnp.zeros((128, HD), F32)
        for sc, v in zip(scores, vals):
            w = jnp.exp(sc - shift)
            mass = mass + jnp.sum(w, axis=1, keepdims=True)
            acc = acc + jnp.dot(w.astype(BF), v, preferred_element_type=F32)
        mass_high = mass.astype(BF).astype(F32)
        stats = jnp.where(
            lane_s == 0, high,
            jnp.where(lane_s == 1, low, jnp.where(lane_s == 2, mass_high, jnp.where(lane_s == 3, mass - mass_high, 0.0))),
        )
        out[8 * t : 8 * t + 8, 0:16, :] = acc.astype(BF).reshape(8, 16, HD)
        out[8 * t : 8 * t + 8, 16:32, :] = stats.astype(BF).reshape(8, 16, HD)


def combine_body(parts, out):
    acc = parts[:, 0:16, :].astype(F32)
    stats = parts[:, 16:32, :].astype(F32)
    peak = stats[:, :, 0:1] + stats[:, :, 1:2]
    mass = stats[:, :, 2:3] + stats[:, :, 3:4]
    top = jnp.max(peak, axis=0, keepdims=True)
    shrink = jnp.exp(peak - top)
    whole = jnp.sum(mass * shrink, axis=0)
    summed = jnp.sum(acc * shrink, axis=0)
    attended = (summed / whole).astype(BF)
    for i in range(out.shape[0]):
        out[i, :, :] = attended


def output_body(att, w, out):
    groups = att[...].reshape(8, 4, 16, HD)
    total = jnp.zeros(out.shape, F32)
    for h in range(4):
        total = total + jnp.dot(
            groups[:, h].reshape(128, HD), w[HD * h : HD * h + HD, :], preferred_element_type=F32
        )
    out[...] = total.astype(BF)


def rotary_tables(positions):
    freq = (1.0 / 500000.0 ** (np.arange(0, HD, 2) / HD)).astype(np.float32)
    angles = positions.astype(F32)[:, None] * jnp.asarray(np.concatenate([freq, freq]), F32)[None, :]
    sign = np.concatenate([-np.ones(HD // 2), np.ones(HD // 2)]).astype(np.float32)
    return jnp.cos(angles), jnp.sin(angles) * jnp.asarray(sign)[None, :]


def on_device(
    hidden_in,
    norm_gain,
    w_query,
    w_keyval,
    w_out,
    prefix_keys,
    prefix_values,
    own_keys,
    own_values,
    positions,
    lengths,
):
    b, r = lax.axis_index("blk"), lax.axis_index("rows")
    who = jnp.stack([b, r]).astype(jnp.int32)
    sds = jax.ShapeDtypeStruct
    packed = pl.pallas_call(
        pack_body,
        out_shape=sds((16, END, HD), BF),
        in_specs=[SM, SM] + [VM] * 5,
        out_specs=VM,
        compiler_params=params(),
        name="pack",
    )(who, lengths, prefix_keys, prefix_values, own_keys.reshape(64, 1024), own_values.reshape(64, 1024), hidden_in)
    mine = lax.all_to_all(packed, "rows", 0, 0, tiled=True)
    other = lax.ppermute(mine, "rows", [(i, i ^ 1) for i in range(16)])
    parts = pl.pallas_call(
        project_body,
        grid=(1,),
        out_shape=sds((32, 32, HD), BF),
        in_specs=[
            pl.BlockSpec((16, L0 - X0, HD), lambda i: (0, X0 // 16, 0)),
            pl.BlockSpec((1, 256), lambda i: (0, 0)),
            pl.BlockSpec((256, 512), lambda i: (0, 0)),
            pl.BlockSpec((256, HD), lambda i: (0, 0)),
        ],
        out_specs=pl.BlockSpec((32, 32, HD), lambda i: (0, 0, 0)),
        compiler_params=params(),
        name="project",
    )(mine, norm_gain.reshape(1, 256), w_query, w_keyval)
    parts = lax.all_to_all(parts, "blk", 0, 0, tiled=True)
    cosine, sine = rotary_tables(lax.dynamic_slice_in_dim(positions, 16 * (b // 4), 16, 0))
    query, new = pl.pallas_call(
        query_body,
        out_shape=(sds((32, 16, HD), BF), sds((16, HD), BF)),
        in_specs=[SM, VM, VM, VM],
        out_specs=(VM, VM),
        compiler_params=params(),
        name="query",
    )(who, parts, cosine, sine)
    new_a = lax.ppermute(new, "rows", [(s, 2 * (s % 8) + s // 8) for s in range(16)])
    new_b = lax.ppermute(new, "rows", [(s, 2 * (s % 8) + 1 - s // 8) for s in range(16)])
    query = lax.all_to_all(query, "blk", 0, 0, tiled=True)
    partial = pl.pallas_call(
        attend_body,
        out_shape=sds((32, 32, HD), BF),
        in_specs=[SM] + [VM] * 5,
        out_specs=VM,
        compiler_params=params(),
        name="attend",
    )(who, mine, other, query, new_a, new_b)
    partial = lax.all_to_all(partial, "blk", 0, 0, tiled=True)
    attended = pl.pallas_call(
        combine_body,
        out_shape=sds((32, 16, HD), BF),
        in_specs=[VM],
        out_specs=VM,
        compiler_params=params(),
        name="combine",
    )(partial)
    attended = lax.all_to_all(attended, "blk", 0, 0, tiled=True)
    mixed = pl.pallas_call(
        output_body,
        out_shape=sds((128, 256), BF),
        in_specs=[VM, VM],
        out_specs=VM,
        compiler_params=params(),
        name="output",
    )(attended, w_out)
    mixed = lax.all_to_all(mixed.reshape(16, 8, 256), "rows", 0, 0, tiled=True)
    return (hidden_in.astype(F32) + jnp.sum(mixed.astype(F32), axis=0)).astype(BF)


def solution(mesh):
    return jax.shard_map(
        on_device,
        mesh=mesh,
        in_specs=(
            P("rows", "blk"),
            P("blk"),
            P("blk", "rows"),
            P("blk", "rows"),
            P("rows", "blk"),
            P(("blk", "rows"), None),
            P(("blk", "rows"), None),
            P("rows", "blk", None),
            P("rows", "blk", None),
            P(),
            P("rows"),
        ),
        out_specs=P("rows", "blk"),
        check_vma=False,
    )
```

time: 871 us -> 141 us (0.16); the launches traced: 859 us -> 140 us
  blocking collectives: 531 us -> 81.8 us
  waiting for transfers between devices: 280 us -> 20.4 us
  starting transfers between devices: 0.12 us -> 24.7 us
  between operations: 14.1 us -> 0.17 us
  other arithmetic: 13.7 us -> 0.88 us
  matrix products: 9.89 us -> 0 us
    psum x3 -> x0, blocking collectives: 317 us -> none  [the longest x1 148 us: on_device(): query_sum, keyval_sum = lax.psum((query_part, keyval_part), 'blk')]
    psum x1 -> x0, waiting for transfers between devices: 136 us -> none  [on_device(): lax.psum(part_accum.astype(jnp.bfloat16), 'blk').astype(jnp.float32)]
    reduce_scatter x2 -> x0, waiting for transfers between devices: 117 us -> none  [the longest x1 60.2 us: on_device(): lax.psum_scatter(jnp.dot(attended, w_out, preferred_element_type=jnp.floa...]
    pmax x1 -> x0, blocking collectives: 108 us -> none  [on_device(): lax.pmax(local_peak.astype(jnp.bfloat16), ('blk', 'rows'))]
    all_to_all x0 -> x4, blocking collectives: none -> 81.8 us  [the longest x1 31.7 us: on_device(): mine = lax.all_to_all(packed, 'rows', 0, 0, tiled=True)]
    all_gather x2 -> x0, blocking collectives: 56 us -> none  [the longest x1 28.8 us: on_device(): lax.all_gather(keyval_sum.astype(jnp.bfloat16), 'rows', axis=1, tiled=True)]
    unnamed x1 -> x0, blocking collectives: 49.6 us -> none
    all_gather x1 -> x0, waiting for transfers between devices: 27.3 us -> none  [on_device(): lax.all_gather(query_sum.astype(jnp.bfloat16), 'rows', axis=1, tiled=True)]
  transfers between devices with their start and end apart: 4 -> 5, of which waited for: 4 -> 3; matrix products, arithmetic and copies ran while one was open for 1% -> 0% of each run, Pallas kernels for 0% -> 2%
where the time goes in v1:
time: 141 us; the launch traced here: 140 us
  blocking collectives  81.8 us (58%)
  starting transfers between devices  24.7 us (18%)
  waiting for transfers between devices  20.4 us (14%)
  Pallas kernels  6.9 us (5%)
  local copies, waits for them, and re-layouts  5.63 us (4%)
    all_to_all x1, blocking collectives, on_device(): mine = lax.all_to_all(packed, 'rows', 0, 0, tiled=True)  31.7 us
    all_to_all x1, blocking collectives, on_device(): mixed = lax.all_to_all(mixed.reshape(16, 8, 256), 'rows', 0, 0, tiled=True)  19.9 us
    all_to_all x1, blocking collectives, on_device(): partial = lax.all_to_all(partial, 'blk', 0, 0, tiled=True)  16.5 us
    all_to_all x1, starting transfers between devices, on_device(): parts = lax.all_to_all(parts, 'blk', 0, 0, tiled=True)  14.6 us
    all_to_all x1, blocking collectives, on_device(): attended = lax.all_to_all(attended, 'blk', 0, 0, tiled=True)  13.7 us
    all_to_all x1, waiting for transfers between devices, on_device(): parts = lax.all_to_all(parts, 'blk', 0, 0, tiled=True)  12.3 us
    all_to_all x1, waiting for transfers between devices, on_device(): query = lax.all_to_all(query, 'blk', 0, 0, tiled=True)  5.96 us
    unnamed x26, local copies, waits for them, and re-layouts  5.63 us
  transfers between devices with their start and end apart: 5, of which 3 were waited for; matrix products, arithmetic and copies ran while one was open for 0% of the time, Pallas kernels for 2%

profile of v1, /device:TPU:1, one launch (start us, length us, event | category | flops | bytes accessed | tf_op | source)
XLA Modules:
  0.0 140.4 jit_solution(1286174471048952983)
XLA Ops:
  0.0 0.1 pad_add_fusion.who
  0.1 0.6 copy-done.7
  0.7 0.0 copy-done.8
  0.7 0.9 copy-done.2
  1.7 0.9 copy-done.3
  2.6 0.9 copy-done.4
  3.5 0.9 copy-done.5
  4.4 0.7 pack.1
  5.1 0.0 copy-start.11
  5.2 31.7 %all_to_all.30.x_ref.mine = bf16[16,224,128]{2,1,0:T(8,128)(2,1)S(1)} all-to-all(bf16[16,224,128]{2,1,0:T(8,128)(2,1)S(1)} %pack.1), channel_id=1, replica_groups=mesh['blk'=32,'rows'=16] {'rows'}, dimensions={0} | all-to-all | bytes 1835008 | tf_op jit(solution)/shard_map/all_to_all | solution.py:211
  36.9 3.9 %collective-permute-start = (bf16[16,224,128]{2,1,0:T(8,128)(2,1)S(1)}, bf16[16,224,128]{2,1,0:T(8,128)(2,1)S(1)}, u32[]{:S(2)}, u32[]{:S(2)}) collective-permute-start(bf16[16,224,128]{2,1,0:T(8,128)(2,1)S(1)} %all_to_all.30.x_ref.mine), channel_id=1, source_target_pairs={{0,1},{1,0},{2,3},{3,2},{4,5},{5,4},{6,7},{7,6},{8,9},{9,8},{10,11... | collective-permute-start | bytes 2752520 | tf_op jit(solution)/shard_map/ppermute | solution.py:212
  40.8 1.0 project.1
  41.8 14.6 %all-to-all-start.1 = ((bf16[32,32,128]{2,1,0:T(8,128)(2,1)}), bf16[32,32,128]{2,1,0:T(8,128)(2,1)S(1)}, u32[]{:S(2)}, u32[]{:S(2)}) async-start(bf16[32,32,128]{2,1,0:T(8,128)(2,1)} %project.1), calls=%async_computation.1 | async-start | bytes 524288 | tf_op jit(solution)/shard_map/all_to_all | solution.py:227
  56.4 0.6 copy-done.12
  57.1 0.1 dynamic-slice_convert_fusion
  57.2 0.6 copy-done.9
  57.7 0.0 copy-done.10
  57.8 0.1 fusion
  57.9 12.3 %all-to-all-done.1.parts = bf16[32,32,128]{2,1,0:T(8,128)(2,1)S(1)} async-done(((bf16[32,32,128]{2,1,0:T(8,128)(2,1)}), bf16[32,32,128]{2,1,0:T(8,128)(2,1)S(1)}, u32[]{:S(2)}, u32[]{:S(2)}) %all-to-all-start.1) | async-done | bytes 262176 | tf_op jit(solution)/shard_map/all_to_all | solution.py:227
  70.2 1.4 query.1
  71.6 3.6 %all-to-all-start.2 = ((bf16[32,16,128]{2,1,0:T(8,128)(2,1)}), bf16[32,16,128]{2,1,0:T(8,128)(2,1)S(1)}, u32[]{:S(2)}, u32[]{:S(2)}) async-start(bf16[32,16,128]{2,1,0:T(8,128)(2,1)} %get-tuple-element.7), calls=%async_computation.2 | async-start | bytes 262144 | tf_op jit(solution)/shard_map/all_to_all | solution.py:239
  75.2 1.9 %collective-permute-start.2 = (bf16[16,128]{1,0:T(8,128)(2,1)S(1)}, bf16[16,128]{1,0:T(8,128)(2,1)S(1)}, u32[]{:S(2)}, u32[]{:S(2)}) collective-permute-start(bf16[16,128]{1,0:T(8,128)(2,1)S(1)} %get-tuple-element.8), channel_id=1, source_target_pairs={{0,1},{1,3},{2,5},{3,7},{4,9},{5,11},{6,13},{7,15},{8,0},{9,2},{10... | collective-permute-start | bytes 12296 | tf_op jit(solution)/shard_map/ppermute | solution.py:238
  77.2 0.7 collective-permute-start.1
  77.8 2.1 %collective-permute-done.2.new_b = bf16[16,128]{1,0:T(8,128)(2,1)S(1)} collective-permute-done((bf16[16,128]{1,0:T(8,128)(2,1)S(1)}, bf16[16,128]{1,0:T(8,128)(2,1)S(1)}, u32[]{:S(2)}, u32[]{:S(2)}) %collective-permute-start.2) | collective-permute-done | bytes 4128 | tf_op jit(solution)/shard_map/ppermute | solution.py:238
  79.9 6.0 %all-to-all-done.2.q_ref = bf16[32,16,128]{2,1,0:T(8,128)(2,1)S(1)} async-done(((bf16[32,16,128]{2,1,0:T(8,128)(2,1)}), bf16[32,16,128]{2,1,0:T(8,128)(2,1)S(1)}, u32[]{:S(2)}, u32[]{:S(2)}) %all-to-all-start.2) | async-done | bytes 131104 | tf_op jit(solution)/shard_map/all_to_all | solution.py:239
  85.9 3.3 %attend.1 = bf16[32,32,128]{2,1,0:T(8,128)(2,1)S(1)} custom-call(s32[2]{0:T(128)S(1)} %pad_add_fusion.who, bf16[16,224,128]{2,1,0:T(8,128)(2,1)S(1)} %all_to_all.30.x_ref.mine, bf16[16,224,128]{2,1,0:T(8,128)(2,1)S(1)} %collective-permute-done.other, bf16[32,16,128]{2,1,0:T(8,128)(2,1)S(1)} %all-to-all-done.2.q_ref, ...), custom_call_target="tpu_custom_call" | custom-call | tf_op jit(solution)/shard_map/attend/pallas_call | solution.py:240
  89.2 16.5 %all_to_all.31.parts = bf16[32,32,128]{2,1,0:T(8,128)(2,1)S(1)} all-to-all(bf16[32,32,128]{2,1,0:T(8,128)(2,1)S(1)} %attend.1), channel_id=1, replica_groups=mesh['blk'=32,'rows'=16] {'blk'}, dimensions={0} | all-to-all | bytes 524288 | tf_op jit(solution)/shard_map/all_to_all | solution.py:248
  105.6 0.3 combine.1
  106.0 13.7 %all_to_all.32.att = bf16[32,16,128]{2,1,0:T(8,128)(2,1)S(1)} all-to-all(bf16[32,16,128]{2,1,0:T(8,128)(2,1)S(1)} %combine.1), channel_id=1, replica_groups=mesh['blk'=32,'rows'=16] {'blk'}, dimensions={0} | all-to-all | bytes 262144 | tf_op jit(solution)/shard_map/all_to_all | solution.py:257
  119.6 0.2 output.1
  119.8 19.9 %all_to_all.33 = bf16[16,8,256]{2,1,0:T(8,128)(2,1)S(1)} all-to-all(bf16[16,8,256]{2,1,0:T(8,128)(2,1)S(1)} %bitcast.5), channel_id=1, replica_groups=mesh['blk'=32,'rows'=16] {'rows'}, dimensions={0} | all-to-all | bytes 131072 | tf_op jit(solution)/shard_map/all_to_all | solution.py:266
  139.8 0.6 add_convert_fusion
  (20 shorter events, 0.1 us)
Async XLA Ops:
  0.0 0.7 copy-start.7
  0.1 0.7 copy-start.8
  0.7 0.9 copy-start.2
  1.7 0.9 copy-start.3
  2.6 0.9 copy-start.4
  3.5 0.9 copy-start.5
  5.1 35.6 %copy-start.11 = (bf16[256]{0:T(256)(128)(2,1)S(1)}, bf16[256]{0:T(256)(128)(2,1)}, u32[]{:S(2)}) copy-start(bf16[256]{0:T(256)(128)(2,1)} %param.14) | copy-start | bytes 1540
  5.2 35.7 %copy-start = (bf16[256,512]{1,0:T(8,128)(2,1)S(1)}, bf16[256,512]{1,0:T(8,128)(2,1)}, u32[]{:S(2)}) copy-start(bf16[256,512]{1,0:T(8,128)(2,1)} %wq.1) | copy-start | bytes 786436
  5.2 35.6 %copy-start.6 = (bf16[256,128]{1,0:T(8,128)(2,1)S(1)}, bf16[256,128]{1,0:T(8,128)(2,1)}, u32[]{:S(2)}) copy-start(bf16[256,128]{1,0:T(8,128)(2,1)} %wkv.1) | copy-start | bytes 196612
  36.9 49.0 %collective-permute-start = (bf16[16,224,128]{2,1,0:T(8,128)(2,1)S(1)}, bf16[16,224,128]{2,1,0:T(8,128)(2,1)S(1)}, u32[]{:S(2)}, u32[]{:S(2)}) collective-permute-start(bf16[16,224,128]{2,1,0:T(8,128)(2,1)S(1)} %all_to_all.30.x_ref.mine), channel_id=1, source_target_pairs={{0,1},{1,0},{2,3},{3,2},{4,5},{5,4},{6,7},{7,6},{8,9},{9,8},{10,11... | collective-permute-start | bytes 2752520 | tf_op jit(solution)/shard_map/ppermute | solution.py:212
  41.8 28.4 %all-to-all-start.1 = ((bf16[32,32,128]{2,1,0:T(8,128)(2,1)}), bf16[32,32,128]{2,1,0:T(8,128)(2,1)S(1)}, u32[]{:S(2)}, u32[]{:S(2)}) async-start(bf16[32,32,128]{2,1,0:T(8,128)(2,1)} %project.1), calls=%async_computation.1 | async-start | bytes 524288 | tf_op jit(solution)/shard_map/all_to_all | solution.py:227
  56.4 0.7 copy-start.12
  57.1 0.7 copy-start.9
  57.1 0.7 copy-start.10
  71.6 14.3 %all-to-all-start.2 = ((bf16[32,16,128]{2,1,0:T(8,128)(2,1)}), bf16[32,16,128]{2,1,0:T(8,128)(2,1)S(1)}, u32[]{:S(2)}, u32[]{:S(2)}) async-start(bf16[32,16,128]{2,1,0:T(8,128)(2,1)} %get-tuple-element.7), calls=%async_computation.2 | async-start | bytes 262144 | tf_op jit(solution)/shard_map/all_to_all | solution.py:239
  75.2 4.7 %collective-permute-start.2 = (bf16[16,128]{1,0:T(8,128)(2,1)S(1)}, bf16[16,128]{1,0:T(8,128)(2,1)S(1)}, u32[]{:S(2)}, u32[]{:S(2)}) collective-permute-start(bf16[16,128]{1,0:T(8,128)(2,1)S(1)} %get-tuple-element.8), channel_id=1, source_target_pairs={{0,1},{1,3},{2,5},{3,7},{4,9},{5,11},{6,13},{7,15},{8,0},{9,2},{10... | collective-permute-start | bytes 12296 | tf_op jit(solution)/shard_map/ppermute | solution.py:238
  77.2 2.8 %collective-permute-start.1 = (bf16[16,128]{1,0:T(8,128)(2,1)S(1)}, bf16[16,128]{1,0:T(8,128)(2,1)S(1)}, u32[]{:S(2)}, u32[]{:S(2)}) collective-permute-start(bf16[16,128]{1,0:T(8,128)(2,1)S(1)} %get-tuple-element.8), channel_id=1, source_target_pairs={{0,0},{1,2},{2,4},{3,6},{4,8},{5,10},{6,12},{7,14},{8,1},{9,3},{10... | collective-permute-start | bytes 12296 | tf_op jit(solution)/shard_map/ppermute | solution.py:237
  105.6 14.0 %copy-start.1 = (bf16[512,256]{1,0:T(8,128)(2,1)S(1)}, bf16[512,256]{1,0:T(8,128)(2,1)}, u32[]{:S(2)}) copy-start(bf16[512,256]{1,0:T(8,128)(2,1)} %w.1) | copy-start | bytes 786436

commit v2 on v1

--- a/solution.py
+++ b/solution.py
@@ -12,42 +12,52 @@
 VM = pl.BlockSpec(memory_space=pltpu.VMEM)
 SM = pl.BlockSpec(memory_space=pltpu.SMEM)
 NT = (((1,), (1,)), ((), ()))
-K0, V0, OK0, OV0, X0, L0, END = 0, 64, 128, 160, 192, 208, 224
-
-
-def params():
-    return pltpu.CompilerParams(vmem_limit_bytes=48 * 1024 * 1024)
+K0, V0, OK0, OV0, X0, END = 0, 64, 128, 160, 192, 208
+
+
+def params(mib=48):
+    return pltpu.CompilerParams(vmem_limit_bytes=mib * 1024 * 1024)
 
 
 def iota(shape, dim):
     return lax.broadcasted_iota(jnp.int32, shape, dim)
 
 
-def pack_body(who, lens, keys, values, own_k, own_v, hidden, out):
-    b, r = who[0], who[1]
+def pack_body(who, lens, hidden, keys_hbm, values_hbm, own_k_hbm, own_v_hbm, out, keys, values, own_k, own_v, sems):
+    copies = [
+        pltpu.make_async_copy(src, dst, sems.at[i])
+        for i, (src, dst) in enumerate(
+            ((keys_hbm, keys), (values_hbm, values), (own_k_hbm, own_k), (own_v_hbm, own_v))
+        )
+    ]
+    for copy in copies:
+        copy.start()
+    b = who[0]
     x = hidden[...].astype(F32)
     x_tile = jnp.concatenate([x[:, :HD], x[:, HD:]], axis=0).astype(BF)
-    lane = iota((16, HD), 1) - 32 * lax.rem(r, 4)
-    inside = (lane >= 0) & (lane < 32)
-    slot = 8 * b + lax.rem(lane + HD, 8)
-    which = lax.div(lane + HD, 8) - 16
+    sub = iota((32, HD), 0)
+    slot = 8 * b + sub % 8
+    dead = []
     for p in range(2):
-        live = jnp.zeros((16, HD), jnp.int32)
+        live = jnp.zeros((32, HD), jnp.int32)
         for k in range(4):
-            live = jnp.where(which == k, lens[4 * p + k], live)
-        flags = jnp.where(inside & (slot < live), 1.0, 0.0).astype(BF)
+            live = jnp.where(sub // 8 == k, lens[4 * p + k], live)
+        dead.append(slot >= live)
+    for copy in copies:
+        copy.wait()
+    for p in range(2):
         for h in range(8):
             col = slice(h * HD, (h + 1) * HD)
             d = 2 * h + p
             out[d, K0:V0, :] = keys[64 * p : 64 * p + 64, col]
             out[d, V0:OK0, :] = values[64 * p : 64 * p + 64, col]
-            out[d, OK0:OV0, :] = own_k[32 * p : 32 * p + 32, col]
+            own = own_k[32 * p : 32 * p + 32, col].astype(F32)
+            out[d, OK0:OV0, :] = jnp.where(dead[p], jnp.nan, own).astype(BF)
             out[d, OV0:X0, :] = own_v[32 * p : 32 * p + 32, col]
-            out[d, X0:L0, :] = x_tile
-            out[d, L0:END, :] = flags
-
-
-def project_body(x_ref, gain, wq, wkv, out):
+            out[d, X0:END, :] = x_tile
+
+
+def project_body(who, x_ref, gain, wq, wa, wb, out):
     xr = x_ref[...].astype(F32)
     x = jnp.concatenate(
         [xr[:, :8, :].reshape(128, HD), xr[:, 8:, :].reshape(128, HD)], axis=1
@@ -61,13 +71,17 @@
     sq_tile = jnp.where(iota((8, HD), 0) == 1, square - high, sq_tile)
     xg = (x * gain[...].astype(F32)).astype(BF)
     q = jnp.dot(xg, wq[...], preferred_element_type=F32)
-    kv = jnp.dot(xg, wkv[...], preferred_element_type=F32)
-    for g in range(8):
-        for h in range(4):
-            b = 4 * g + h
-            out[b, 0:16, :] = q[16 * g : 16 * g + 16, HD * h : HD * h + HD].astype(BF)
-            first = 8 * (b // 2)
-            out[b, 16:32, :] = jnp.concatenate([kv[first : first + 8, :], sq_tile], axis=0).astype(BF)
+    even = lax.rem(who[1], 2) == 0
+    first = jnp.dot(xg, wa[...], preferred_element_type=F32)
+    second = jnp.dot(xg, wb[...], preferred_element_type=F32)
+    key = jnp.where(even, first, second)
+    value = jnp.where(even, second, first)
+    for b in range(32):
+        g, h = b // 4, b % 4
+        out[b, 0:16, :] = q[16 * g : 16 * g + 16, HD * h : HD * h + HD].astype(BF)
+        out[b, 16:32, :] = jnp.concatenate(
+            [key[4 * b : 4 * b + 4, :], value[4 * b : 4 * b + 4, :], sq_tile], axis=0
+        ).astype(BF)
 
 
 def rotate(u, cosine, sine):
@@ -75,34 +89,26 @@
 
 
 def query_body(who, parts, cosine, sine, q_out, kv_out):
-    b, r = who[0], who[1]
+    b = who[0]
     total = jnp.sum(parts[...].astype(F32), axis=0)
     square = total[24:25, :] + total[25:26, :]
     inv = lax.rsqrt(square / 8192.0 + 1e-05)
-    lane16, sub16 = iota((16, HD), 1), iota((16, HD), 0)
-    col = jnp.sum(jnp.where(lane16 == 16 * lax.div(b, 4) + sub16, inv, 0.0), axis=1, keepdims=True)
-    lane8, sub8 = iota((8, HD), 1), iota((8, HD), 0)
-    col8 = jnp.sum(jnp.where(lane8 == 8 * lax.div(b, 2) + sub8, inv, 0.0), axis=1, keepdims=True)
-    cos, sin = cosine[...], sine[...]
-    raw = (total[0:16, :] * col).astype(BF).astype(F32)
-    query = rotate(raw, cos, sin).astype(BF)
+    lane, sub = iota((24, HD), 1), iota((24, HD), 0)
+    row = jnp.where(sub < 16, 16 * lax.div(b, 4) + sub, 4 * b + sub % 4)
+    col = jnp.sum(jnp.where(lane == row, inv, 0.0), axis=1, keepdims=True)
+    raw = (total[0:24, :] * col).astype(BF).astype(F32)
+    turned = rotate(raw, cosine[...], sine[...])
+    query = turned[0:16, :].astype(BF)
     for i in range(q_out.shape[0]):
         q_out[i, :, :] = query
-    upper = lax.rem(lax.div(b, 2), 2) == 1
-    cos8 = jnp.where(upper, cos[8:16, :], cos[0:8, :])
-    sin8 = jnp.where(upper, sin[8:16, :], sin[0:8, :])
-    raw8 = (total[16:24, :] * col8).astype(BF).astype(F32)
-    new = jnp.where(r < 8, rotate(raw8, cos8, sin8), raw8)
-    kv_out[...] = jnp.concatenate([new, jnp.zeros((8, HD), F32)], axis=0).astype(BF)
-
-
-def attend_body(who, mine, other, q_ref, new_a, new_b, out):
+    kv_out[...] = jnp.concatenate([turned[16:24, :], jnp.zeros((8, HD), F32)], axis=0).astype(BF)
+
+
+def attend_body(who, mine, other, q_ref, new_ref, out):
     b, r = who[0], who[1]
     scale = HD ** (-0.5)
-    even = lax.rem(r, 2) == 0
-    fa, fb = new_a[...].astype(F32), new_b[...].astype(F32)
-    new_k = jnp.where(even, fa, fb).astype(BF)
-    new_v = jnp.where(even, fb, fa).astype(BF)
+    new_k = new_ref[...]
+    new_v = pltpu.roll(new_k.astype(F32), 12, 0).astype(BF)
     sources = (mine, other)
     halves = (lax.rem(r, 2), 1 - lax.rem(r, 2))
     keys = [s[:, K0:V0, :].reshape(1024, HD) for s in sources]
@@ -110,8 +116,7 @@
     row_q = iota((128, HD), 0)
     row_q = 16 * (row_q // 64) + row_q % 16
     lane = iota((128, HD), 1)
-    row_new = 8 * lax.div(b, 2) + iota((128, 16), 1)
-    mine_new = (iota((128, 16), 1) // 4) == lax.rem(b, 2)
+    new_id = iota((128, 16), 1)
     lane_s = iota((128, HD), 1)
     for t in range(4):
         q = q_ref[8 * t : 8 * t + 8].reshape(128, HD)
@@ -122,14 +127,13 @@
         for s, half in zip(sources, halves):
             own_k = s[4 * t : 4 * t + 4, OK0:OV0, :].reshape(128, HD)
             own_v = s[4 * t : 4 * t + 4, OV0:X0, :].reshape(128, HD)
-            live = jnp.sum(s[4 * t : 4 * t + 4, L0:END, :].astype(F32), axis=0)[0:1, :]
             row_k = 8 * (lane // 32) + 4 * half + (lane % 32) // 8
-            good = (row_k == row_q) & (live > 0.5)
             sc = lax.dot_general(q, own_k, NT, preferred_element_type=F32) * scale
+            good = (row_k == row_q) & (sc == sc)
             scores.append(jnp.where(good, sc, -jnp.inf))
             vals.append(own_v)
         sc = lax.dot_general(q, new_k, NT, preferred_element_type=F32) * scale
-        good = mine_new & (row_new == row_q[:, :16] + 32 * t)
+        good = (new_id < 4) & (4 * b + new_id == row_q[:, :16] + 32 * t)
         scores.append(jnp.where(good, sc, -jnp.inf))
         vals.append(new_v)
         peak = jnp.max(scores[0], axis=1, keepdims=True)
@@ -200,51 +204,69 @@
     b, r = lax.axis_index("blk"), lax.axis_index("rows")
     who = jnp.stack([b, r]).astype(jnp.int32)
     sds = jax.ShapeDtypeStruct
+    first_w = lax.ppermute(w_keyval, "rows", [(s, 2 * (s % 8) + s // 8) for s in range(16)])
+    second_w = lax.ppermute(w_keyval, "rows", [(s, 2 * (s % 8) + 1 - s // 8) for s in range(16)])
     packed = pl.pallas_call(
         pack_body,
         out_shape=sds((16, END, HD), BF),
-        in_specs=[SM, SM] + [VM] * 5,
+        in_specs=[SM, SM, VM] + [pl.BlockSpec(memory_space=pltpu.HBM)] * 4,
         out_specs=VM,
-        compiler_params=params(),
+        scratch_shapes=[
+            pltpu.VMEM((128, 1024), BF),
+            pltpu.VMEM((128, 1024), BF),
+            pltpu.VMEM((64, 1024), BF),
+            pltpu.VMEM((64, 1024), BF),
+            pltpu.SemaphoreType.DMA((4,)),
+        ],
         name="pack",
-    )(who, lengths, prefix_keys, prefix_values, own_keys.reshape(64, 1024), own_values.reshape(64, 1024), hidden_in)
+    )(who, lengths, hidden_in, prefix_keys, prefix_values, own_keys.reshape(64, 1024), own_values.reshape(64, 1024))
     mine = lax.all_to_all(packed, "rows", 0, 0, tiled=True)
-    other = lax.ppermute(mine, "rows", [(i, i ^ 1) for i in range(16)])
     parts = pl.pallas_call(
         project_body,
         grid=(1,),
         out_shape=sds((32, 32, HD), BF),
         in_specs=[
-            pl.BlockSpec((16, L0 - X0, HD), lambda i: (0, X0 // 16, 0)),
+            SM,
+            pl.BlockSpec((16, END - X0, HD), lambda i: (0, X0 // 16, 0)),
             pl.BlockSpec((1, 256), lambda i: (0, 0)),
             pl.BlockSpec((256, 512), lambda i: (0, 0)),
             pl.BlockSpec((256, HD), lambda i: (0, 0)),
+            pl.BlockSpec((256, HD), lambda i: (0, 0)),
         ],
         out_specs=pl.BlockSpec((32, 32, HD), lambda i: (0, 0, 0)),
         compiler_params=params(),
         name="project",
-    )(mine, norm_gain.reshape(1, 256), w_query, w_keyval)
+    )(who, mine, norm_gain.reshape(1, 256), w_query, first_w, second_w)
+    positions, parts = lax.optimization_barrier((positions, parts))
     parts = lax.all_to_all(parts, "blk", 0, 0, tiled=True)
-    cosine, sine = rotary_tables(lax.dynamic_slice_in_dim(positions, 16 * (b // 4), 16, 0))
+    places = jnp.concatenate(
+        [
+            lax.dynamic_slice_in_dim(positions, 16 * (b // 4), 16, 0),
+            lax.dynamic_slice_in_dim(positions, 4 * b, 4, 0),
+            jnp.zeros(4, positions.dtype),
+        ]
+    )
+    cosine, sine = rotary_tables(places)
+    mine, cosine = lax.optimization_barrier((mine, cosine))
+    other = lax.ppermute(mine, "rows", [(i, i ^ 1) for i in range(16)])
     query, new = pl.pallas_call(
         query_body,
         out_shape=(sds((32, 16, HD), BF), sds((16, HD), BF)),
         in_specs=[SM, VM, VM, VM],
         out_specs=(VM, VM),
         compiler_params=params(),
+        cost_estimate=pl.CostEstimate(flops=2 * 10**9, bytes_accessed=1 << 20, transcendentals=0),
         name="query",
     )(who, parts, cosine, sine)
-    new_a = lax.ppermute(new, "rows", [(s, 2 * (s % 8) + s // 8) for s in range(16)])
-    new_b = lax.ppermute(new, "rows", [(s, 2 * (s % 8) + 1 - s // 8) for s in range(16)])
     query = lax.all_to_all(query, "blk", 0, 0, tiled=True)
     partial = pl.pallas_call(
         attend_body,
         out_shape=sds((32, 32, HD), BF),
-        in_specs=[SM] + [VM] * 5,
+        in_specs=[SM] + [VM] * 4,
         out_specs=VM,
         compiler_params=params(),
         name="attend",
-    )(who, mine, other, query, new_a, new_b)
+    )(who, mine, other, query, new)
     partial = lax.all_to_all(partial, "blk", 0, 0, tiled=True)
     attended = pl.pallas_call(
         combine_body,

time: 141 us -> 132 us (0.936)
  blocking collectives: 81.8 us -> 62.7 us
  starting transfers between devices: 24.7 us -> 32.4 us
  local copies, waits for them, and re-layouts: 5.63 us -> 2.07 us
  waiting for transfers between devices: 20.4 us -> 23.9 us
  Pallas kernels: 6.9 us -> 8.99 us
    all_to_all x1, blocking collectives: 31.7 us -> 13.7 us  [on_device(): query = lax.all_to_all(query, 'blk', 0, 0, tiled=True)]
    ppermute x2, waiting for transfers between devices: 2.08 us -> 12.2 us  [the longest x1 12.2 us: on_device(): lax.ppermute(w_keyval, 'rows', [(s, 2 * (s % 8) + 1 - s // 8) for s in ra...]
    all_to_all x1, starting transfers between devices: 3.63 us -> 9.71 us  [on_device(): mine = lax.all_to_all(packed, 'rows', 0, 0, tiled=True)]
    all_to_all x1, waiting for transfers between devices: 12.3 us -> 7.57 us  [on_device(): parts = lax.all_to_all(parts, 'blk', 0, 0, tiled=True)]
    all_to_all x1, blocking collectives: 19.9 us -> 15.8 us  [on_device(): mixed = lax.all_to_all(mixed.reshape(16, 8, 256), 'rows', 0, 0, tiled=True)]
    unnamed x26 -> x18, local copies, waits for them, and re-layouts: 5.63 us -> 1.92 us
    all_to_all x1, blocking collectives: 16.5 us -> 19.6 us  [on_device(): partial = lax.all_to_all(partial, 'blk', 0, 0, tiled=True)]
    pallas_call x1, Pallas kernels: 0.69 us -> 2.87 us  [on_device(): pl.pallas_call(pack_body, out_shape=sds((16, END, HD), BF), in_specs=[SM,...]
  transfers between devices with their start and end apart: 5 -> 5, of which waited for: 3 -> 3; matrix products, arithmetic and copies ran while one was open for 0% -> 0% of each run, Pallas kernels for 2% -> 1%
where the time goes in v2:
time: 132 us
  blocking collectives  62.7 us (48%)
  starting transfers between devices  32.4 us (25%)
  waiting for transfers between devices  23.9 us (18%)
  Pallas kernels  8.99 us (7%)
  local copies, waits for them, and re-layouts  2.07 us (2%)
  other arithmetic  1.38 us (1%)
    all_to_all x1, blocking collectives, on_device(): partial = lax.all_to_all(partial, 'blk', 0, 0, tiled=True)  19.6 us
    all_to_all x1, blocking collectives, on_device(): mixed = lax.all_to_all(mixed.reshape(16, 8, 256), 'rows', 0, 0, tiled=True)  15.8 us
    all_to_all x1, starting transfers between devices, on_device(): parts = lax.all_to_all(parts, 'blk', 0, 0, tiled=True)  14.7 us
    all_to_all x1, blocking collectives, on_device(): query = lax.all_to_all(query, 'blk', 0, 0, tiled=True)  13.7 us
    all_to_all x1, blocking collectives, on_device(): attended = lax.all_to_all(attended, 'blk', 0, 0, tiled=True)  13.6 us
    ppermute x1, waiting for transfers between devices, on_device(): lax.ppermute(w_keyval, 'rows', [(s, 2 * (s % 8) + 1 - s // 8) for s in ra...  12.2 us
    all_to_all x1, starting transfers between devices, on_device(): mine = lax.all_to_all(packed, 'rows', 0, 0, tiled=True)  9.71 us
    all_to_all x1, waiting for transfers between devices, on_device(): parts = lax.all_to_all(parts, 'blk', 0, 0, tiled=True)  7.57 us
  transfers between devices with their start and end apart: 5, of which 3 were waited for; matrix products, arithmetic and copies ran while one was open for 0% of the time, Pallas kernels for 1%

profile of v2, /device:TPU:1, one launch (start us, length us, event | category | flops | bytes accessed | tf_op | source)
XLA Modules:
  0.0 131.6 jit_solution(14579655764412712450)
XLA Ops:
  0.0 0.6 pad_add_fusion.who
  0.6 2.9 %pack.1 = bf16[16,208,128]{2,1,0:T(8,128)(2,1)} custom-call(s32[2]{0:T(128)} %pad_add_fusion.who, s32[8]{0:T(128)} %lens.1, bf16[8,256]{1,0:T(8,128)(2,1)} %hidden.1, bf16[128,1024]{1,0:T(8,128)(2,1)} %keys_hbm.1, bf16[128,1024]{1,0:T(8,128)(2,1)} %values_hbm.1, bf16[64,1024]{1,0:T(8,128)(2,1)} %bitcast.6, bf16[64,1024]{1,0:T(8,128)(2,1)} %bitcast.7), custom_call_target="tpu_custom_call" | custom-call | tf_op jit(solution)/shard_map/pack/pallas_call | solution.py:209
  3.4 0.0 copy-start.6
  3.5 9.7 %all-to-all-start = ((bf16[16,208,128]{2,1,0:T(8,128)(2,1)}), bf16[16,208,128]{2,1,0:T(8,128)(2,1)S(1)}, u32[]{:S(2)}, u32[]{:S(2)}) async-start(bf16[16,208,128]{2,1,0:T(8,128)(2,1)} %pack.1), calls=%async_computation | async-start | bytes 1703936 | tf_op jit(solution)/shard_map/all_to_all | solution.py:223
  13.2 3.3 %collective-permute-start.1 = (bf16[256,128]{1,0:T(8,128)(2,1)S(1)}, bf16[256,128]{1,0:T(8,128)(2,1)S(1)}, u32[]{:S(2)}, u32[]{:S(2)}) collective-permute-start(bf16[256,128]{1,0:T(8,128)(2,1)S(1)} %copy-done.6), channel_id=1, source_target_pairs={{0,1},{1,3},{2,5},{3,7},{4,9},{5,11},{6,13},{7,15},{8,0},{9,2},{10... | collective-permute-start | bytes 196616 | tf_op jit(solution)/shard_map/ppermute | solution.py:208
  16.5 0.7 collective-permute-start
  17.1 0.0 copy-start.7
  17.2 0.6 copy-done.7
  17.8 12.2 %collective-permute-done.1.wb = bf16[256,128]{1,0:T(8,128)(2,1)S(1)} collective-permute-done((bf16[256,128]{1,0:T(8,128)(2,1)S(1)}, bf16[256,128]{1,0:T(8,128)(2,1)S(1)}, u32[]{:S(2)}, u32[]{:S(2)}) %collective-permute-start.1) | collective-permute-done | bytes 65568 | tf_op jit(solution)/shard_map/ppermute | solution.py:208
  30.0 4.1 %all-to-all-done.x_ref.mine = bf16[16,208,128]{2,1,0:T(8,128)(2,1)S(1)} async-done(((bf16[16,208,128]{2,1,0:T(8,128)(2,1)}), bf16[16,208,128]{2,1,0:T(8,128)(2,1)S(1)}, u32[]{:S(2)}, u32[]{:S(2)}) %all-to-all-start) | async-done | bytes 852000 | tf_op jit(solution)/shard_map/all_to_all | solution.py:223
  34.2 1.6 %project.1 = bf16[32,32,128]{2,1,0:T(8,128)(2,1)} custom-call(s32[2]{0:T(128)S(1)} %copy-done.2, bf16[16,208,128]{2,1,0:T(8,128)(2,1)S(1)} %all-to-all-done.x_ref.mine, bf16[1,256]{1,0:T(2,128)(2,1)S(1)} %reshape.35.gain, bf16[256,512]{1,0:T(8,128)(2,1)S(1)} %copy-done, bf16[256,128]{1,0:T(8,128)(2,1)S(1)} %collective-permute-done.wa, ...), custom_call_target="tpu_custom_call" | custom-call | tf_op jit(solution)/shard_map/project/pallas_call | solution.py:224
  35.7 0.1 dynamic_slice.7
  35.8 0.1 dynamic_slice.6
  35.9 14.7 %all-to-all-start.1 = ((bf16[32,32,128]{2,1,0:T(8,128)(2,1)}), bf16[32,32,128]{2,1,0:T(8,128)(2,1)S(1)}, u32[]{:S(2)}, u32[]{:S(2)}) async-start(bf16[32,32,128]{2,1,0:T(8,128)(2,1)} %project.1), calls=%async_computation.1 | async-start | bytes 524288 | tf_op jit(solution)/shard_map/all_to_all | solution.py:241
  50.6 0.0 copy-start.4
  50.6 0.0 copy-start.5
  50.6 0.1 add_convert_fusion.1
  50.7 0.6 copy-done.4
  51.3 0.0 copy-done.5
  51.3 0.1 fusion
  51.4 4.0 %collective-permute-start.2 = (bf16[16,208,128]{2,1,0:T(8,128)(2,1)S(1)}, bf16[16,208,128]{2,1,0:T(8,128)(2,1)S(1)}, u32[]{:S(2)}, u32[]{:S(2)}) collective-permute-start(bf16[16,208,128]{2,1,0:T(8,128)(2,1)S(1)} %all-to-all-done.x_ref.mine), channel_id=1, source_target_pairs={{0,1},{1,0},{2,3},{3,2},{4,5},{5,4},{6,7},{7,6},{8,9},{9,8},{10,11... | collective-permute-start | bytes 2555912 | tf_op jit(solution)/shard_map/ppermute | solution.py:251
  55.5 7.6 %all-to-all-done.1.parts = bf16[32,32,128]{2,1,0:T(8,128)(2,1)S(1)} async-done(((bf16[32,32,128]{2,1,0:T(8,128)(2,1)}), bf16[32,32,128]{2,1,0:T(8,128)(2,1)S(1)}, u32[]{:S(2)}, u32[]{:S(2)}) %all-to-all-start.1) | async-done | bytes 262176 | tf_op jit(solution)/shard_map/all_to_all | solution.py:241
  63.0 0.7 query.1
  63.8 13.7 %all_to_all.30.q_ref = bf16[32,16,128]{2,1,0:T(8,128)(2,1)S(1)} all-to-all(bf16[32,16,128]{2,1,0:T(8,128)(2,1)S(1)} %get-tuple-element.15), channel_id=1, replica_groups=mesh['blk'=32,'rows'=16] {'blk'}, dimensions={0} | all-to-all | bytes 262144 | tf_op jit(solution)/shard_map/all_to_all | solution.py:261
  77.4 3.3 %attend.1 = bf16[32,32,128]{2,1,0:T(8,128)(2,1)S(1)} custom-call(s32[2]{0:T(128)S(1)} %copy-done.2, bf16[16,208,128]{2,1,0:T(8,128)(2,1)S(1)} %all-to-all-done.x_ref.mine, bf16[16,208,128]{2,1,0:T(8,128)(2,1)S(1)} %collective-permute-done.2.other, bf16[32,16,128]{2,1,0:T(8,128)(2,1)S(1)} %all_to_all.30.q_ref, bf16[16,128]{1,0:T(8,128)(2,1)S(1)} %get-tuple-element.16.new_ref), custom_call_target="tpu_custom_call" | custom-call | tf_op jit(solution)/shard_map/attend/pallas_call | solution.py:262
  80.7 19.6 %all_to_all.31.parts = bf16[32,32,128]{2,1,0:T(8,128)(2,1)S(1)} all-to-all(bf16[32,32,128]{2,1,0:T(8,128)(2,1)S(1)} %attend.1), channel_id=1, replica_groups=mesh['blk'=32,'rows'=16] {'blk'}, dimensions={0} | all-to-all | bytes 524288 | tf_op jit(solution)/shard_map/all_to_all | solution.py:270
  100.3 0.3 combine.1
  100.6 13.6 %all_to_all.32.att = bf16[32,16,128]{2,1,0:T(8,128)(2,1)S(1)} all-to-all(bf16[32,16,128]{2,1,0:T(8,128)(2,1)S(1)} %combine.1), channel_id=1, replica_groups=mesh['blk'=32,'rows'=16] {'blk'}, dimensions={0} | all-to-all | bytes 262144 | tf_op jit(solution)/shard_map/all_to_all | solution.py:279
  114.3 0.2 output.1
  114.5 15.8 %all_to_all.33 = bf16[16,8,256]{2,1,0:T(8,128)(2,1)S(1)} all-to-all(bf16[16,8,256]{2,1,0:T(8,128)(2,1)S(1)} %bitcast.5), channel_id=1, replica_groups=mesh['blk'=32,'rows'=16] {'rows'}, dimensions={0} | all-to-all | bytes 131072 | tf_op jit(solution)/shard_map/all_to_all | solution.py:288
  130.3 0.7 copy-done.3
  131.0 0.6 add_convert_fusion
  (15 shorter events, 0.1 us)
Async XLA Ops:
  3.4 9.7 %copy-start.6 = (bf16[256,128]{1,0:T(8,128)(2,1)S(1)}, bf16[256,128]{1,0:T(8,128)(2,1)}, u32[]{:S(2)}) copy-start(bf16[256,128]{1,0:T(8,128)(2,1)} %param.16) | copy-start | bytes 196612
  3.4 30.7 %copy-start = (bf16[256,512]{1,0:T(8,128)(2,1)S(1)}, bf16[256,512]{1,0:T(8,128)(2,1)}, u32[]{:S(2)}) copy-start(bf16[256,512]{1,0:T(8,128)(2,1)} %wq.1) | copy-start | bytes 786436
  3.5 30.7 %all-to-all-start = ((bf16[16,208,128]{2,1,0:T(8,128)(2,1)}), bf16[16,208,128]{2,1,0:T(8,128)(2,1)S(1)}, u32[]{:S(2)}, u32[]{:S(2)}) async-start(bf16[16,208,128]{2,1,0:T(8,128)(2,1)} %pack.1), calls=%async_computation | async-start | bytes 1703936 | tf_op jit(solution)/shard_map/all_to_all | solution.py:223
  13.2 16.8 %collective-permute-start.1 = (bf16[256,128]{1,0:T(8,128)(2,1)S(1)}, bf16[256,128]{1,0:T(8,128)(2,1)S(1)}, u32[]{:S(2)}, u32[]{:S(2)}) collective-permute-start(bf16[256,128]{1,0:T(8,128)(2,1)S(1)} %copy-done.6), channel_id=1, source_target_pairs={{0,1},{1,3},{2,5},{3,7},{4,9},{5,11},{6,13},{7,15},{8,0},{9,2},{10... | collective-permute-start | bytes 196616 | tf_op jit(solution)/shard_map/ppermute | solution.py:208
  16.5 13.6 %collective-permute-start = (bf16[256,128]{1,0:T(8,128)(2,1)S(1)}, bf16[256,128]{1,0:T(8,128)(2,1)S(1)}, u32[]{:S(2)}, u32[]{:S(2)}) collective-permute-start(bf16[256,128]{1,0:T(8,128)(2,1)S(1)} %copy-done.6), channel_id=1, source_target_pairs={{0,0},{1,2},{2,4},{3,6},{4,8},{5,10},{6,12},{7,14},{8,1},{9,3},{10... | collective-permute-start | bytes 196616 | tf_op jit(solution)/shard_map/ppermute | solution.py:207
  17.1 0.7 copy-start.7
  17.8 16.4 %copy-start.2 = (s32[2]{0:T(128)S(1)}, s32[2]{0:T(128)}, u32[]{:S(2)}) copy-start(s32[2]{0:T(128)} %pad_add_fusion.who) | copy-start | bytes 28
  17.8 17.9 %copy-start.8 = (s32[128]{0:T(128)S(1)}, s32[128]{0:T(128)}, u32[]{:S(2)}) copy-start(s32[128]{0:T(128)} %param.22) | copy-start | bytes 1540
  35.9 27.2 %all-to-all-start.1 = ((bf16[32,32,128]{2,1,0:T(8,128)(2,1)}), bf16[32,32,128]{2,1,0:T(8,128)(2,1)S(1)}, u32[]{:S(2)}, u32[]{:S(2)}) async-start(bf16[32,32,128]{2,1,0:T(8,128)(2,1)} %project.1), calls=%async_computation.1 | async-start | bytes 524288 | tf_op jit(solution)/shard_map/all_to_all | solution.py:241
  50.6 0.7 copy-start.4
  50.6 0.7 copy-start.5
  51.4 26.0 %collective-permute-start.2 = (bf16[16,208,128]{2,1,0:T(8,128)(2,1)S(1)}, bf16[16,208,128]{2,1,0:T(8,128)(2,1)S(1)}, u32[]{:S(2)}, u32[]{:S(2)}) collective-permute-start(bf16[16,208,128]{2,1,0:T(8,128)(2,1)S(1)} %all-to-all-done.x_ref.mine), channel_id=1, source_target_pairs={{0,1},{1,0},{2,3},{3,2},{4,5},{5,4},{6,7},{7,6},{8,9},{9,8},{10,11... | collective-permute-start | bytes 2555912 | tf_op jit(solution)/shard_map/ppermute | solution.py:251
  100.3 14.0 %copy-start.1 = (bf16[512,256]{1,0:T(8,128)(2,1)S(1)}, bf16[512,256]{1,0:T(8,128)(2,1)}, u32[]{:S(2)}) copy-start(bf16[512,256]{1,0:T(8,128)(2,1)} %w.1) | copy-start | bytes 786436
  130.3 0.7 copy-start.3

commit v3 on v2

--- a/solution.py
+++ b/solution.py
@@ -57,7 +57,11 @@
             out[d, X0:END, :] = x_tile
 
 
-def project_body(who, x_ref, gain, wq, wa, wb, out):
+def half_swap(x):
+    return pltpu.roll(x, 4, 1)
+
+
+def project_body(x_ref, gain, wq, wkv, out):
     xr = x_ref[...].astype(F32)
     x = jnp.concatenate(
         [xr[:, :8, :].reshape(128, HD), xr[:, 8:, :].reshape(128, HD)], axis=1
@@ -67,56 +71,57 @@
         precision=lax.Precision.HIGHEST, preferred_element_type=F32,
     )
     high = square.astype(BF).astype(F32)
-    sq_tile = jnp.where(iota((8, HD), 0) == 0, high, 0.0)
-    sq_tile = jnp.where(iota((8, HD), 0) == 1, square - high, sq_tile)
+    sub = iota((16, 8, HD), 1)
+    squares = jnp.where(sub == 4, high[None], jnp.where(sub == 5, (square - high)[None], 0.0))
     xg = (x * gain[...].astype(F32)).astype(BF)
     q = jnp.dot(xg, wq[...], preferred_element_type=F32)
-    even = lax.rem(who[1], 2) == 0
-    first = jnp.dot(xg, wa[...], preferred_element_type=F32)
-    second = jnp.dot(xg, wb[...], preferred_element_type=F32)
-    key = jnp.where(even, first, second)
-    value = jnp.where(even, second, first)
-    for b in range(32):
-        g, h = b // 4, b % 4
-        out[b, 0:16, :] = q[16 * g : 16 * g + 16, HD * h : HD * h + HD].astype(BF)
-        out[b, 16:32, :] = jnp.concatenate(
-            [key[4 * b : 4 * b + 4, :], value[4 * b : 4 * b + 4, :], sq_tile], axis=0
-        ).astype(BF)
+    kv = jnp.dot(xg, wkv[...], preferred_element_type=F32).reshape(16, 8, HD)
+    heads = [q[:, HD * h : HD * h + HD].reshape(16, 8, HD) for h in range(4)]
+    low = sub < 4
+    for p in range(2):
+        tiles = []
+        for u in range(2):
+            first, second = heads[2 * u], heads[2 * u + 1]
+            if p == 0:
+                tiles.append(jnp.where(low, first, half_swap(second)))
+            else:
+                tiles.append(jnp.where(low, half_swap(first), second))
+        tiles.append(jnp.where(low, kv if p == 0 else half_swap(kv), squares))
+        tiles.append(jnp.zeros((16, 8, HD), F32))
+        chunks = jnp.concatenate(tiles, axis=1).astype(BF)
+        for j in range(16):
+            out[2 * j + p, :, :] = chunks[j]
 
 
 def rotate(u, cosine, sine):
     return u * cosine + pltpu.roll(u, HD // 2, 1) * sine
 
 
-def query_body(who, parts, cosine, sine, q_out, kv_out):
-    b = who[0]
+def query_body(who, parts, cosine, sine, q_out, q_own, kv_out):
     total = jnp.sum(parts[...].astype(F32), axis=0)
-    square = total[24:25, :] + total[25:26, :]
+    square = total[20:21, :] + total[21:22, :]
     inv = lax.rsqrt(square / 8192.0 + 1e-05)
     lane, sub = iota((24, HD), 1), iota((24, HD), 0)
-    row = jnp.where(sub < 16, 16 * lax.div(b, 4) + sub, 4 * b + sub % 4)
-    col = jnp.sum(jnp.where(lane == row, inv, 0.0), axis=1, keepdims=True)
+    col = jnp.sum(jnp.where(lane == 4 * who[0] + sub % 4, inv, 0.0), axis=1, keepdims=True)
     raw = (total[0:24, :] * col).astype(BF).astype(F32)
     turned = rotate(raw, cosine[...], sine[...])
     query = turned[0:16, :].astype(BF)
+    q_own[...] = query
     for i in range(q_out.shape[0]):
         q_out[i, :, :] = query
     kv_out[...] = jnp.concatenate([turned[16:24, :], jnp.zeros((8, HD), F32)], axis=0).astype(BF)
 
 
-def attend_body(who, mine, other, q_ref, new_ref, out):
-    b, r = who[0], who[1]
+def attend_body(who, mine, other, q_ref, out):
+    r = who[1]
     scale = HD ** (-0.5)
-    new_k = new_ref[...]
-    new_v = pltpu.roll(new_k.astype(F32), 12, 0).astype(BF)
     sources = (mine, other)
     halves = (lax.rem(r, 2), 1 - lax.rem(r, 2))
     keys = [s[:, K0:V0, :].reshape(1024, HD) for s in sources]
     values = [s[:, V0:OK0, :].reshape(1024, HD) for s in sources]
     row_q = iota((128, HD), 0)
-    row_q = 16 * (row_q // 64) + row_q % 16
+    row_q = 4 * (row_q // 16) + row_q % 4
     lane = iota((128, HD), 1)
-    new_id = iota((128, 16), 1)
     lane_s = iota((128, HD), 1)
     for t in range(4):
         q = q_ref[8 * t : 8 * t + 8].reshape(128, HD)
@@ -132,10 +137,6 @@
             good = (row_k == row_q) & (sc == sc)
             scores.append(jnp.where(good, sc, -jnp.inf))
             vals.append(own_v)
-        sc = lax.dot_general(q, new_k, NT, preferred_element_type=F32) * scale
-        good = (new_id < 4) & (4 * b + new_id == row_q[:, :16] + 32 * t)
-        scores.append(jnp.where(good, sc, -jnp.inf))
-        vals.append(new_v)
         peak = jnp.max(scores[0], axis=1, keepdims=True)
         for sc in scores[1:]:
             peak = jnp.maximum(peak, jnp.max(sc, axis=1, keepdims=True))
@@ -157,26 +158,38 @@
         out[8 * t : 8 * t + 8, 16:32, :] = stats.astype(BF).reshape(8, 16, HD)
 
 
-def combine_body(parts, out):
+def combine_body(who, parts, q_own, new_a, new_b, out):
+    even = lax.rem(who[1], 2) == 0
+    first, second = new_a[...].astype(F32), new_b[...].astype(F32)
+    new_k = jnp.concatenate([jnp.where(even, first, second)[0:4, :]] * 4, axis=0)
+    new_v = jnp.concatenate([jnp.where(even, second, first)[0:4, :]] * 4, axis=0)
+    new = jnp.sum(q_own[...].astype(F32) * new_k, axis=1, keepdims=True) * HD ** (-0.5)
     acc = parts[:, 0:16, :].astype(F32)
     stats = parts[:, 16:32, :].astype(F32)
     peak = stats[:, :, 0:1] + stats[:, :, 1:2]
     mass = stats[:, :, 2:3] + stats[:, :, 3:4]
-    top = jnp.max(peak, axis=0, keepdims=True)
-    shrink = jnp.exp(peak - top)
-    whole = jnp.sum(mass * shrink, axis=0)
-    summed = jnp.sum(acc * shrink, axis=0)
+    top = jnp.maximum(jnp.max(peak, axis=0), new)
+    shrink = jnp.exp(peak - top[None])
+    new_w = jnp.exp(new - top)
+    whole = jnp.sum(mass * shrink, axis=0) + new_w
+    summed = jnp.sum(acc * shrink, axis=0) + new_w * new_v
     attended = (summed / whole).astype(BF)
     for i in range(out.shape[0]):
         out[i, :, :] = attended
 
 
 def output_body(att, w, out):
-    groups = att[...].reshape(8, 4, 16, HD)
+    tiles = att[...].astype(F32).reshape(16, 2, 2, 8, HD)
+    low = iota((16, 8, HD), 1) < 4
     total = jnp.zeros(out.shape, F32)
     for h in range(4):
+        first, second = tiles[:, 0, h // 2], tiles[:, 1, h // 2]
+        if h % 2 == 0:
+            rows = jnp.where(low, first, half_swap(second))
+        else:
+            rows = jnp.where(low, half_swap(first), second)
         total = total + jnp.dot(
-            groups[:, h].reshape(128, HD), w[HD * h : HD * h + HD, :], preferred_element_type=F32
+            rows.reshape(128, HD).astype(BF), w[HD * h : HD * h + HD, :], preferred_element_type=F32
         )
     out[...] = total.astype(BF)
 
@@ -204,8 +217,6 @@
     b, r = lax.axis_index("blk"), lax.axis_index("rows")
     who = jnp.stack([b, r]).astype(jnp.int32)
     sds = jax.ShapeDtypeStruct
-    first_w = lax.ppermute(w_keyval, "rows", [(s, 2 * (s % 8) + s // 8) for s in range(16)])
-    second_w = lax.ppermute(w_keyval, "rows", [(s, 2 * (s % 8) + 1 - s // 8) for s in range(16)])
     packed = pl.pallas_call(
         pack_body,
         out_shape=sds((16, END, HD), BF),
@@ -226,56 +237,52 @@
         grid=(1,),
         out_shape=sds((32, 32, HD), BF),
         in_specs=[
-            SM,
             pl.BlockSpec((16, END - X0, HD), lambda i: (0, X0 // 16, 0)),
             pl.BlockSpec((1, 256), lambda i: (0, 0)),
             pl.BlockSpec((256, 512), lambda i: (0, 0)),
             pl.BlockSpec((256, HD), lambda i: (0, 0)),
-            pl.BlockSpec((256, HD), lambda i: (0, 0)),
         ],
         out_specs=pl.BlockSpec((32, 32, HD), lambda i: (0, 0, 0)),
         compiler_params=params(),
         name="project",
-    )(who, mine, norm_gain.reshape(1, 256), w_query, first_w, second_w)
+    )(mine, norm_gain.reshape(1, 256), w_query, w_keyval)
     positions, parts = lax.optimization_barrier((positions, parts))
     parts = lax.all_to_all(parts, "blk", 0, 0, tiled=True)
-    places = jnp.concatenate(
-        [
-            lax.dynamic_slice_in_dim(positions, 16 * (b // 4), 16, 0),
-            lax.dynamic_slice_in_dim(positions, 4 * b, 4, 0),
-            jnp.zeros(4, positions.dtype),
-        ]
-    )
+    places = lax.dynamic_slice_in_dim(positions, 4 * b, 4, 0)
+    still = jnp.zeros_like(places)
+    places = jnp.concatenate([places] * 4 + [jnp.where(r < 8, places, still), still])
     cosine, sine = rotary_tables(places)
     mine, cosine = lax.optimization_barrier((mine, cosine))
     other = lax.ppermute(mine, "rows", [(i, i ^ 1) for i in range(16)])
-    query, new = pl.pallas_call(
+    query, q_own, new = pl.pallas_call(
         query_body,
-        out_shape=(sds((32, 16, HD), BF), sds((16, HD), BF)),
+        out_shape=(sds((32, 16, HD), BF), sds((16, HD), BF), sds((16, HD), BF)),
         in_specs=[SM, VM, VM, VM],
-        out_specs=(VM, VM),
+        out_specs=(VM, VM, VM),
         compiler_params=params(),
         cost_estimate=pl.CostEstimate(flops=2 * 10**9, bytes_accessed=1 << 20, transcendentals=0),
         name="query",
     )(who, parts, cosine, sine)
+    new_a = lax.ppermute(new, "rows", [(s, 2 * (s % 8) + s // 8) for s in range(16)])
+    new_b = lax.ppermute(new, "rows", [(s, 2 * (s % 8) + 1 - s // 8) for s in range(16)])
     query = lax.all_to_all(query, "blk", 0, 0, tiled=True)
     partial = pl.pallas_call(
         attend_body,
         out_shape=sds((32, 32, HD), BF),
-        in_specs=[SM] + [VM] * 4,
+        in_specs=[SM] + [VM] * 3,
         out_specs=VM,
         compiler_params=params(),
         name="attend",
-    )(who, mine, other, query, new)
+    )(who, mine, other, query)
     partial = lax.all_to_all(partial, "blk", 0, 0, tiled=True)
     attended = pl.pallas_call(
         combine_body,
         out_shape=sds((32, 16, HD), BF),
-        in_specs=[VM],
+        in_specs=[SM] + [VM] * 4,
         out_specs=VM,
         compiler_params=params(),
         name="combine",
-    )(partial)
+    )(who, partial, q_own, new_a, new_b)
     attended = lax.all_to_all(attended, "blk", 0, 0, tiled=True)
     mixed = pl.pallas_call(
         output_body,

time: 132 us -> 135 us (1.023)
  blocking collectives: 62.7 us -> 46.9 us
  waiting for transfers between devices: 23.9 us -> 38.4 us
  starting transfers between devices: 32.4 us -> 36.8 us
    all_to_all x1 -> x0, blocking collectives: 19.6 us -> none  [on_device(): partial = lax.all_to_all(partial, 'blk', 0, 0, tiled=True)]
    all_to_all x1, waiting for transfers between devices: 4.14 us -> 20.3 us  [on_device(): mine = lax.all_to_all(packed, 'rows', 0, 0, tiled=True)]
    ppermute x2, waiting for transfers between devices: 12.2 us -> 2.54 us  [the longest x1 2.54 us: on_device(): lax.ppermute(new, 'rows', [(s, 2 * (s % 8) + 1 - s // 8) for s in range(1...]
    all_to_all x0 -> x1, waiting for transfers between devices: none -> 5.83 us  [on_device(): partial = lax.all_to_all(partial, 'blk', 0, 0, tiled=True)]
    all_to_all x0 -> x1, starting transfers between devices: none -> 4.09 us  [on_device(): partial = lax.all_to_all(partial, 'blk', 0, 0, tiled=True)]
    all_to_all x1, waiting for transfers between devices: 7.57 us -> 9.72 us  [on_device(): parts = lax.all_to_all(parts, 'blk', 0, 0, tiled=True)]
    all_to_all x1, blocking collectives: 13.6 us -> 15.2 us  [on_device(): attended = lax.all_to_all(attended, 'blk', 0, 0, tiled=True)]
  transfers between devices with their start and end apart: 5 -> 6, of which waited for: 3 -> 4; matrix products, arithmetic and copies ran while one was open for 0% -> 0% of each run, Pallas kernels for 1% -> 1%
where the time goes in v3:
time: 135 us
  blocking collectives  46.9 us (35%)
  waiting for transfers between devices  38.4 us (28%)
  starting transfers between devices  36.8 us (27%)
  Pallas kernels  9.67 us (7%)
  other arithmetic  1.43 us (1%)
  local copies, waits for them, and re-layouts  1.43 us (1%)
    all_to_all x1, waiting for transfers between devices, on_device(): mine = lax.all_to_all(packed, 'rows', 0, 0, tiled=True)  20.3 us
    all_to_all x1, blocking collectives, on_device(): mixed = lax.all_to_all(mixed.reshape(16, 8, 256), 'rows', 0, 0, tiled=True)  16.8 us
    all_to_all x1, blocking collectives, on_device(): attended = lax.all_to_all(attended, 'blk', 0, 0, tiled=True)  15.2 us
    all_to_all x1, blocking collectives, on_device(): query = lax.all_to_all(query, 'blk', 0, 0, tiled=True)  14.9 us
    all_to_all x1, starting transfers between devices, on_device(): parts = lax.all_to_all(parts, 'blk', 0, 0, tiled=True)  14.6 us
    all_to_all x1, waiting for transfers between devices, on_device(): parts = lax.all_to_all(parts, 'blk', 0, 0, tiled=True)  9.72 us
    all_to_all x1, starting transfers between devices, on_device(): mine = lax.all_to_all(packed, 'rows', 0, 0, tiled=True)  9.71 us
    all_to_all x1, waiting for transfers between devices, on_device(): partial = lax.all_to_all(partial, 'blk', 0, 0, tiled=True)  5.83 us
  transfers between devices with their start and end apart: 6, of which 4 were waited for; matrix products, arithmetic and copies ran while one was open for 0% of the time, Pallas kernels for 1%

profile of v3, /device:TPU:1, one launch (start us, length us, event | category | flops | bytes accessed | tf_op | source)
XLA Modules:
  0.0 134.8 jit_solution(17022171262054047406)
XLA Ops:
  0.0 0.6 pad_add_fusion.who
  0.6 2.9 %pack.1 = bf16[16,208,128]{2,1,0:T(8,128)(2,1)} custom-call(s32[2]{0:T(128)} %pad_add_fusion.who, s32[8]{0:T(128)} %lens.1, bf16[8,256]{1,0:T(8,128)(2,1)} %hidden.1, bf16[128,1024]{1,0:T(8,128)(2,1)} %keys_hbm.1, bf16[128,1024]{1,0:T(8,128)(2,1)} %values_hbm.1, bf16[64,1024]{1,0:T(8,128)(2,1)} %bitcast.6, bf16[64,1024]{1,0:T(8,128)(2,1)} %bitcast.7), custom_call_target="tpu_custom_call" | custom-call | tf_op jit(solution)/shard_map/pack/pallas_call | solution.py:220
  3.5 0.0 copy-start
  3.5 0.0 copy-start.2
  3.5 9.7 %all-to-all-start = ((bf16[16,208,128]{2,1,0:T(8,128)(2,1)}), bf16[16,208,128]{2,1,0:T(8,128)(2,1)S(1)}, u32[]{:S(2)}, u32[]{:S(2)}) async-start(bf16[16,208,128]{2,1,0:T(8,128)(2,1)} %pack.1), calls=%async_computation | async-start | bytes 1703936 | tf_op jit(solution)/shard_map/all_to_all | solution.py:234
  13.2 0.0 copy-start.8
  13.2 0.6 copy-done.8
  13.9 20.3 %all-to-all-done.x_ref.mine = bf16[16,208,128]{2,1,0:T(8,128)(2,1)S(1)} async-done(((bf16[16,208,128]{2,1,0:T(8,128)(2,1)}), bf16[16,208,128]{2,1,0:T(8,128)(2,1)S(1)}, u32[]{:S(2)}, u32[]{:S(2)}) %all-to-all-start) | async-done | bytes 852000 | tf_op jit(solution)/shard_map/all_to_all | solution.py:234
  34.2 0.0 copy-done
  34.2 1.0 project.1
  35.3 0.1 broadcast_select_fusion
  35.3 0.1 concatenate.7
  35.4 14.6 %all-to-all-start.1 = ((bf16[32,32,128]{2,1,0:T(8,128)(2,1)}), bf16[32,32,128]{2,1,0:T(8,128)(2,1)S(1)}, u32[]{:S(2)}, u32[]{:S(2)}) async-start(bf16[32,32,128]{2,1,0:T(8,128)(2,1)} %project.1), calls=%async_computation.1 | async-start | bytes 524288 | tf_op jit(solution)/shard_map/all_to_all | solution.py:250
  50.1 0.1 fusion
  50.2 3.2 %collective-permute-start = (bf16[16,208,128]{2,1,0:T(8,128)(2,1)S(1)}, bf16[16,208,128]{2,1,0:T(8,128)(2,1)S(1)}, u32[]{:S(2)}, u32[]{:S(2)}) collective-permute-start(bf16[16,208,128]{2,1,0:T(8,128)(2,1)S(1)} %all-to-all-done.x_ref.mine), channel_id=1, source_target_pairs={{0,1},{1,0},{2,3},{3,2},{4,5},{5,4},{6,7},{7,6},{8,9},{9,8},{10,11... | collective-permute-start | bytes 2555912 | tf_op jit(solution)/shard_map/ppermute | solution.py:256
  53.5 9.7 %all-to-all-done.1.parts = bf16[32,32,128]{2,1,0:T(8,128)(2,1)S(1)} async-done(((bf16[32,32,128]{2,1,0:T(8,128)(2,1)}), bf16[32,32,128]{2,1,0:T(8,128)(2,1)S(1)}, u32[]{:S(2)}, u32[]{:S(2)}) %all-to-all-start.1) | async-done | bytes 262176 | tf_op jit(solution)/shard_map/all_to_all | solution.py:250
  63.2 0.7 query.1
  63.9 14.9 %all_to_all.30.q_ref = bf16[32,16,128]{2,1,0:T(8,128)(2,1)S(1)} all-to-all(bf16[32,16,128]{2,1,0:T(8,128)(2,1)S(1)} %get-tuple-element.16), channel_id=1, replica_groups=mesh['blk'=32,'rows'=16] {'blk'}, dimensions={0} | all-to-all | bytes 262144 | tf_op jit(solution)/shard_map/all_to_all | solution.py:268
  78.8 0.0 collective-permute-done.other
  78.8 3.9 %attend.1 = bf16[32,32,128]{2,1,0:T(8,128)(2,1)} custom-call(s32[2]{0:T(128)S(1)} %copy-done.3, bf16[16,208,128]{2,1,0:T(8,128)(2,1)S(1)} %all-to-all-done.x_ref.mine, bf16[16,208,128]{2,1,0:T(8,128)(2,1)S(1)} %collective-permute-done.other, bf16[32,16,128]{2,1,0:T(8,128)(2,1)S(1)} %all_to_all.30.q_ref), custom_call_target="tpu_custom_call" | custom-call | tf_op jit(solution)/shard_map/attend/pallas_call | solution.py:269
  82.7 4.1 %all-to-all-start.3 = ((bf16[32,32,128]{2,1,0:T(8,128)(2,1)}), bf16[32,32,128]{2,1,0:T(8,128)(2,1)S(1)}, u32[]{:S(2)}, u32[]{:S(2)}) async-start(bf16[32,32,128]{2,1,0:T(8,128)(2,1)} %attend.1), calls=%async_computation.3 | async-start | bytes 524288 | tf_op jit(solution)/shard_map/all_to_all | solution.py:277
  86.8 0.7 collective-permute-start.1
  87.5 4.5 %collective-permute-start.2 = (bf16[16,128]{1,0:T(8,128)(2,1)S(1)}, bf16[16,128]{1,0:T(8,128)(2,1)S(1)}, u32[]{:S(2)}, u32[]{:S(2)}) collective-permute-start(bf16[16,128]{1,0:T(8,128)(2,1)S(1)} %get-tuple-element.18), channel_id=1, source_target_pairs={{0,1},{1,3},{2,5},{3,7},{4,9},{5,11},{6,13},{7,15},{8,0},{9,2},{10... | collective-permute-start | bytes 12296 | tf_op jit(solution)/shard_map/ppermute | solution.py:267
  92.0 0.0 collective-permute-done.1.new_a
  92.0 2.5 %collective-permute-done.2.new_b = bf16[16,128]{1,0:T(8,128)(2,1)S(1)} collective-permute-done((bf16[16,128]{1,0:T(8,128)(2,1)S(1)}, bf16[16,128]{1,0:T(8,128)(2,1)S(1)}, u32[]{:S(2)}, u32[]{:S(2)}) %collective-permute-start.2) | collective-permute-done | bytes 4128 | tf_op jit(solution)/shard_map/ppermute | solution.py:267
  94.5 5.8 %all-to-all-done.3.parts = bf16[32,32,128]{2,1,0:T(8,128)(2,1)S(1)} async-done(((bf16[32,32,128]{2,1,0:T(8,128)(2,1)}), bf16[32,32,128]{2,1,0:T(8,128)(2,1)S(1)}, u32[]{:S(2)}, u32[]{:S(2)}) %all-to-all-start.3) | async-done | bytes 262176 | tf_op jit(solution)/shard_map/all_to_all | solution.py:277
  100.4 0.9 combine.1
  101.3 15.2 %all_to_all.31.att = bf16[32,16,128]{2,1,0:T(8,128)(2,1)S(1)} all-to-all(bf16[32,16,128]{2,1,0:T(8,128)(2,1)S(1)} %combine.1), channel_id=1, replica_groups=mesh['blk'=32,'rows'=16] {'blk'}, dimensions={0} | all-to-all | bytes 262144 | tf_op jit(solution)/shard_map/all_to_all | solution.py:286
  116.4 0.2 output.1
  116.6 16.8 %all_to_all.32 = bf16[16,8,256]{2,1,0:T(8,128)(2,1)S(1)} all-to-all(bf16[16,8,256]{2,1,0:T(8,128)(2,1)S(1)} %bitcast.5), channel_id=1, replica_groups=mesh['blk'=32,'rows'=16] {'rows'}, dimensions={0} | all-to-all | bytes 131072 | tf_op jit(solution)/shard_map/all_to_all | solution.py:295
  133.5 0.7 copy-done.4
  134.2 0.6 add_convert_fusion
  (16 shorter events, 0.1 us)
Async XLA Ops:
  3.5 30.7 %copy-start = (bf16[256,512]{1,0:T(8,128)(2,1)S(1)}, bf16[256,512]{1,0:T(8,128)(2,1)}, u32[]{:S(2)}) copy-start(bf16[256,512]{1,0:T(8,128)(2,1)} %wq.1) | copy-start | bytes 786436
  3.5 30.7 %copy-start.2 = (bf16[256,128]{1,0:T(8,128)(2,1)S(1)}, bf16[256,128]{1,0:T(8,128)(2,1)}, u32[]{:S(2)}) copy-start(bf16[256,128]{1,0:T(8,128)(2,1)} %wkv.1) | copy-start | bytes 196612
  3.5 30.7 %all-to-all-start = ((bf16[16,208,128]{2,1,0:T(8,128)(2,1)}), bf16[16,208,128]{2,1,0:T(8,128)(2,1)S(1)}, u32[]{:S(2)}, u32[]{:S(2)}) async-start(bf16[16,208,128]{2,1,0:T(8,128)(2,1)} %pack.1), calls=%async_computation | async-start | bytes 1703936 | tf_op jit(solution)/shard_map/all_to_all | solution.py:234
  13.2 0.7 copy-start.8
  13.9 21.4 %copy-start.5 = (s32[128]{0:T(128)S(1)}, s32[128]{0:T(128)}, u32[]{:S(2)}) copy-start(s32[128]{0:T(128)} %param.22) | copy-start | bytes 1540
  35.4 14.6 %copy-start.6 = (f32[128]{0:T(128)S(1)}, f32[128]{0:T(128)}, u32[]{:S(2)}) copy-start(f32[128]{0:T(128)} %constant.24.clone) | copy-start | bytes 1540
  35.4 14.6 %copy-start.7 = (f32[128]{0:T(128)S(1)}, f32[128]{0:T(128)}, u32[]{:S(2)}) copy-start(f32[128]{0:T(128)} %constant.25.clone) | copy-start | bytes 1540
  35.4 27.7 %all-to-all-start.1 = ((bf16[32,32,128]{2,1,0:T(8,128)(2,1)}), bf16[32,32,128]{2,1,0:T(8,128)(2,1)S(1)}, u32[]{:S(2)}, u32[]{:S(2)}) async-start(bf16[32,32,128]{2,1,0:T(8,128)(2,1)} %project.1), calls=%async_computation.1 | async-start | bytes 524288 | tf_op jit(solution)/shard_map/all_to_all | solution.py:250
  50.2 13.0 %copy-start.3 = (s32[2]{0:T(128)S(1)}, s32[2]{0:T(128)}, u32[]{:S(2)}) copy-start(s32[2]{0:T(128)} %pad_add_fusion.who) | copy-start | bytes 28
  50.2 28.6 %collective-permute-start = (bf16[16,208,128]{2,1,0:T(8,128)(2,1)S(1)}, bf16[16,208,128]{2,1,0:T(8,128)(2,1)S(1)}, u32[]{:S(2)}, u32[]{:S(2)}) collective-permute-start(bf16[16,208,128]{2,1,0:T(8,128)(2,1)S(1)} %all-to-all-done.x_ref.mine), channel_id=1, source_target_pairs={{0,1},{1,0},{2,3},{3,2},{4,5},{5,4},{6,7},{7,6},{8,9},{9,8},{10,11... | collective-permute-start | bytes 2555912 | tf_op jit(solution)/shard_map/ppermute | solution.py:256
  82.7 17.6 %all-to-all-start.3 = ((bf16[32,32,128]{2,1,0:T(8,128)(2,1)}), bf16[32,32,128]{2,1,0:T(8,128)(2,1)S(1)}, u32[]{:S(2)}, u32[]{:S(2)}) async-start(bf16[32,32,128]{2,1,0:T(8,128)(2,1)} %attend.1), calls=%async_computation.3 | async-start | bytes 524288 | tf_op jit(solution)/shard_map/all_to_all | solution.py:277
  86.8 5.2 %collective-permute-start.1 = (bf16[16,128]{1,0:T(8,128)(2,1)S(1)}, bf16[16,128]{1,0:T(8,128)(2,1)S(1)}, u32[]{:S(2)}, u32[]{:S(2)}) collective-permute-start(bf16[16,128]{1,0:T(8,128)(2,1)S(1)} %get-tuple-element.18), channel_id=1, source_target_pairs={{0,0},{1,2},{2,4},{3,6},{4,8},{5,10},{6,12},{7,14},{8,1},{9,3},{10... | collective-permute-start | bytes 12296 | tf_op jit(solution)/shard_map/ppermute | solution.py:266
  87.5 7.0 %collective-permute-start.2 = (bf16[16,128]{1,0:T(8,128)(2,1)S(1)}, bf16[16,128]{1,0:T(8,128)(2,1)S(1)}, u32[]{:S(2)}, u32[]{:S(2)}) collective-permute-start(bf16[16,128]{1,0:T(8,128)(2,1)S(1)} %get-tuple-element.18), channel_id=1, source_target_pairs={{0,1},{1,3},{2,5},{3,7},{4,9},{5,11},{6,13},{7,15},{8,0},{9,2},{10... | collective-permute-start | bytes 12296 | tf_op jit(solution)/shard_map/ppermute | solution.py:267
  100.4 16.1 %copy-start.1 = (bf16[512,256]{1,0:T(8,128)(2,1)S(1)}, bf16[512,256]{1,0:T(8,128)(2,1)}, u32[]{:S(2)}) copy-start(bf16[512,256]{1,0:T(8,128)(2,1)} %w.1) | copy-start | bytes 786436
  133.5 0.7 copy-start.4

commit v4 on v3

--- a/solution.py
+++ b/solution.py
@@ -264,8 +264,8 @@
         name="query",
     )(who, parts, cosine, sine)
     new_a = lax.ppermute(new, "rows", [(s, 2 * (s % 8) + s // 8) for s in range(16)])
-    new_b = lax.ppermute(new, "rows", [(s, 2 * (s % 8) + 1 - s // 8) for s in range(16)])
     query = lax.all_to_all(query, "blk", 0, 0, tiled=True)
+    query, new_a = lax.optimization_barrier((query, new_a))
     partial = pl.pallas_call(
         attend_body,
         out_shape=sds((32, 32, HD), BF),
@@ -274,6 +274,8 @@
         compiler_params=params(),
         name="attend",
     )(who, mine, other, query)
+    partial, new = lax.optimization_barrier((partial, new))
+    new_b = lax.ppermute(new, "rows", [(s, 2 * (s % 8) + 1 - s // 8) for s in range(16)])
     partial = lax.all_to_all(partial, "blk", 0, 0, tiled=True)
     attended = pl.pallas_call(
         combine_body,

time: 135 us -> 135 us (level)
  blocking collectives: 46.9 us -> 32.3 us
  waiting for transfers between devices: 38.4 us -> 48.2 us
  starting transfers between devices: 36.8 us -> 40.7 us
    all_to_all x1 -> x0, blocking collectives: 14.9 us -> none  [on_device(): query = lax.all_to_all(query, 'blk', 0, 0, tiled=True)]
    all_to_all x0 -> x1, waiting for transfers between devices: none -> 9.96 us  [on_device(): query = lax.all_to_all(query, 'blk', 0, 0, tiled=True)]
    all_to_all x0 -> x1, starting transfers between devices: none -> 4.43 us  [on_device(): query = lax.all_to_all(query, 'blk', 0, 0, tiled=True)]
    all_to_all x1, blocking collectives: 15.2 us -> 18.9 us  [on_device(): attended = lax.all_to_all(attended, 'blk', 0, 0, tiled=True)]
    all_to_all x1, blocking collectives: 16.8 us -> 13.5 us  [on_device(): mixed = lax.all_to_all(mixed.reshape(16, 8, 256), 'rows', 0, 0, tiled=True)]
    all_to_all x1, waiting for transfers between devices: 5.83 us -> 2.78 us  [on_device(): partial = lax.all_to_all(partial, 'blk', 0, 0, tiled=True)]
    ppermute x1, waiting for transfers between devices: 2.54 us -> 5.45 us  [on_device(): lax.ppermute(new, 'rows', [(s, 2 * (s % 8) + 1 - s // 8) for s in range(1...]
  transfers between devices with their start and end apart: 6 -> 7, of which waited for: 4 -> 5; matrix products, arithmetic and copies ran while one was open for 0% -> 0% of each run, Pallas kernels for 1% -> 1%
where the time goes in v4:
time: 135 us
  waiting for transfers between devices  48.2 us (36%)
  starting transfers between devices  40.7 us (30%)
  blocking collectives  32.3 us (24%)
  Pallas kernels  10.3 us (8%)
  other arithmetic  1.43 us (1%)
  local copies, waits for them, and re-layouts  1.43 us (1%)
    all_to_all x1, waiting for transfers between devices, on_device(): mine = lax.all_to_all(packed, 'rows', 0, 0, tiled=True)  20.3 us
    all_to_all x1, blocking collectives, on_device(): attended = lax.all_to_all(attended, 'blk', 0, 0, tiled=True)  18.9 us
    all_to_all x1, starting transfers between devices, on_device(): parts = lax.all_to_all(parts, 'blk', 0, 0, tiled=True)  14.6 us
    all_to_all x1, blocking collectives, on_device(): mixed = lax.all_to_all(mixed.reshape(16, 8, 256), 'rows', 0, 0, tiled=True)  13.5 us
    all_to_all x1, waiting for transfers between devices, on_device(): query = lax.all_to_all(query, 'blk', 0, 0, tiled=True)  9.96 us
    all_to_all x1, waiting for transfers between devices, on_device(): parts = lax.all_to_all(parts, 'blk', 0, 0, tiled=True)  9.72 us
    all_to_all x1, starting transfers between devices, on_device(): mine = lax.all_to_all(packed, 'rows', 0, 0, tiled=True)  9.71 us
    ppermute x1, waiting for transfers between devices, on_device(): lax.ppermute(new, 'rows', [(s, 2 * (s % 8) + 1 - s // 8) for s in range(1...  5.45 us
  transfers between devices with their start and end apart: 7, of which 5 were waited for; matrix products, arithmetic and copies ran while one was open for 0% of the time, Pallas kernels for 1%

profile of v4, /device:TPU:1, one launch (start us, length us, event | category | flops | bytes accessed | tf_op | source)
XLA Modules:
  0.0 134.7 jit_solution(1967769417389742282)
XLA Ops:
  0.0 0.6 pad_add_fusion.who
  0.6 2.9 %pack.1 = bf16[16,208,128]{2,1,0:T(8,128)(2,1)} custom-call(s32[2]{0:T(128)} %pad_add_fusion.who, s32[8]{0:T(128)} %lens.1, bf16[8,256]{1,0:T(8,128)(2,1)} %hidden.1, bf16[128,1024]{1,0:T(8,128)(2,1)} %keys_hbm.1, bf16[128,1024]{1,0:T(8,128)(2,1)} %values_hbm.1, bf16[64,1024]{1,0:T(8,128)(2,1)} %bitcast.6, bf16[64,1024]{1,0:T(8,128)(2,1)} %bitcast.7), custom_call_target="tpu_custom_call" | custom-call | tf_op jit(solution)/shard_map/pack/pallas_call | solution.py:220
  3.5 0.0 copy-start
  3.5 0.0 copy-start.2
  3.5 9.7 %all-to-all-start = ((bf16[16,208,128]{2,1,0:T(8,128)(2,1)}), bf16[16,208,128]{2,1,0:T(8,128)(2,1)S(1)}, u32[]{:S(2)}, u32[]{:S(2)}) async-start(bf16[16,208,128]{2,1,0:T(8,128)(2,1)} %pack.1), calls=%async_computation | async-start | bytes 1703936 | tf_op jit(solution)/shard_map/all_to_all | solution.py:234
  13.2 0.0 copy-start.8
  13.2 0.6 copy-done.8
  13.9 20.3 %all-to-all-done.x_ref.mine = bf16[16,208,128]{2,1,0:T(8,128)(2,1)S(1)} async-done(((bf16[16,208,128]{2,1,0:T(8,128)(2,1)}), bf16[16,208,128]{2,1,0:T(8,128)(2,1)S(1)}, u32[]{:S(2)}, u32[]{:S(2)}) %all-to-all-start) | async-done | bytes 852000 | tf_op jit(solution)/shard_map/all_to_all | solution.py:234
  34.2 1.0 project.1
  35.2 0.1 broadcast_select_fusion
  35.3 0.1 concatenate.7
  35.4 14.6 %all-to-all-start.1 = ((bf16[32,32,128]{2,1,0:T(8,128)(2,1)}), bf16[32,32,128]{2,1,0:T(8,128)(2,1)S(1)}, u32[]{:S(2)}, u32[]{:S(2)}) async-start(bf16[32,32,128]{2,1,0:T(8,128)(2,1)} %project.1), calls=%async_computation.1 | async-start | bytes 524288 | tf_op jit(solution)/shard_map/all_to_all | solution.py:250
  50.1 0.1 fusion
  50.2 3.2 %collective-permute-start = (bf16[16,208,128]{2,1,0:T(8,128)(2,1)S(1)}, bf16[16,208,128]{2,1,0:T(8,128)(2,1)S(1)}, u32[]{:S(2)}, u32[]{:S(2)}) collective-permute-start(bf16[16,208,128]{2,1,0:T(8,128)(2,1)S(1)} %all-to-all-done.x_ref.mine), channel_id=1, source_target_pairs={{0,1},{1,0},{2,3},{3,2},{4,5},{5,4},{6,7},{7,6},{8,9},{9,8},{10,11... | collective-permute-start | bytes 2555912 | tf_op jit(solution)/shard_map/ppermute | solution.py:256
  53.4 9.7 %all-to-all-done.1.parts = bf16[32,32,128]{2,1,0:T(8,128)(2,1)S(1)} async-done(((bf16[32,32,128]{2,1,0:T(8,128)(2,1)}), bf16[32,32,128]{2,1,0:T(8,128)(2,1)S(1)}, u32[]{:S(2)}, u32[]{:S(2)}) %all-to-all-start.1) | async-done | bytes 262176 | tf_op jit(solution)/shard_map/all_to_all | solution.py:250
  63.2 1.4 %query.1 = (bf16[32,16,128]{2,1,0:T(8,128)(2,1)}, bf16[16,128]{1,0:T(8,128)(2,1)S(1)}, bf16[16,128]{1,0:T(8,128)(2,1)S(1)}) custom-call(s32[2]{0:T(128)S(1)} %copy-done.3, bf16[32,32,128]{2,1,0:T(8,128)(2,1)S(1)} %all-to-all-done.1.parts, f32[24,128]{1,0:T(8,128)S(1)} %get-tuple-element.19.cosine, f32[24,128]{1,0:T(8,128)S(1)} %get-tuple-element.29.sine), custom_call_target="tpu_custom_call" | custom-call | flops 2000000000 | bytes 1048576 | tf_op jit(solution)/shard_map/query/pallas_call | solution.py:257
  64.6 4.4 %all-to-all-start.2 = ((bf16[32,16,128]{2,1,0:T(8,128)(2,1)}), bf16[32,16,128]{2,1,0:T(8,128)(2,1)S(1)}, u32[]{:S(2)}, u32[]{:S(2)}) async-start(bf16[32,16,128]{2,1,0:T(8,128)(2,1)} %get-tuple-element.20), calls=%async_computation.2 | async-start | bytes 262144 | tf_op jit(solution)/shard_map/all_to_all | solution.py:267
  69.0 0.7 collective-permute-start.1
  69.7 0.0 collective-permute-done.1.new_a
  69.7 10.0 %all-to-all-done.2.q_ref = bf16[32,16,128]{2,1,0:T(8,128)(2,1)S(1)} async-done(((bf16[32,16,128]{2,1,0:T(8,128)(2,1)}), bf16[32,16,128]{2,1,0:T(8,128)(2,1)S(1)}, u32[]{:S(2)}, u32[]{:S(2)}) %all-to-all-start.2) | async-done | bytes 131104 | tf_op jit(solution)/shard_map/all_to_all | solution.py:267
  79.6 0.0 collective-permute-done.other
  79.6 3.9 %attend.1 = bf16[32,32,128]{2,1,0:T(8,128)(2,1)} custom-call(s32[2]{0:T(128)S(1)} %copy-done.3, bf16[16,208,128]{2,1,0:T(8,128)(2,1)S(1)} %all-to-all-done.x_ref.mine, bf16[16,208,128]{2,1,0:T(8,128)(2,1)S(1)} %collective-permute-done.other, bf16[32,16,128]{2,1,0:T(8,128)(2,1)S(1)} %all-to-all-done.2.q_ref), custom_call_target="tpu_custom_call" | custom-call | tf_op jit(solution)/shard_map/attend/pallas_call | solution.py:269
  83.6 3.7 %all-to-all-start.3 = ((bf16[32,32,128]{2,1,0:T(8,128)(2,1)}), bf16[32,32,128]{2,1,0:T(8,128)(2,1)S(1)}, u32[]{:S(2)}, u32[]{:S(2)}) async-start(bf16[32,32,128]{2,1,0:T(8,128)(2,1)} %attend.1), calls=%async_computation.3 | async-start | bytes 524288 | tf_op jit(solution)/shard_map/all_to_all | solution.py:279
  87.3 4.4 %collective-permute-start.2 = (bf16[16,128]{1,0:T(8,128)(2,1)S(1)}, bf16[16,128]{1,0:T(8,128)(2,1)S(1)}, u32[]{:S(2)}, u32[]{:S(2)}) collective-permute-start(bf16[16,128]{1,0:T(8,128)(2,1)S(1)} %get-tuple-element.26), channel_id=1, source_target_pairs={{0,1},{1,3},{2,5},{3,7},{4,9},{5,11},{6,13},{7,15},{8,0},{9,2},{10... | collective-permute-start | bytes 12296 | tf_op jit(solution)/shard_map/ppermute | solution.py:278
  91.7 5.4 %collective-permute-done.2.new_b = bf16[16,128]{1,0:T(8,128)(2,1)S(1)} collective-permute-done((bf16[16,128]{1,0:T(8,128)(2,1)S(1)}, bf16[16,128]{1,0:T(8,128)(2,1)S(1)}, u32[]{:S(2)}, u32[]{:S(2)}) %collective-permute-start.2) | collective-permute-done | bytes 4128 | tf_op jit(solution)/shard_map/ppermute | solution.py:278
  97.1 2.8 %all-to-all-done.3.parts = bf16[32,32,128]{2,1,0:T(8,128)(2,1)S(1)} async-done(((bf16[32,32,128]{2,1,0:T(8,128)(2,1)}), bf16[32,32,128]{2,1,0:T(8,128)(2,1)S(1)}, u32[]{:S(2)}, u32[]{:S(2)}) %all-to-all-start.3) | async-done | bytes 262176 | tf_op jit(solution)/shard_map/all_to_all | solution.py:279
  99.9 0.9 combine.1
  100.8 18.9 %all_to_all.30.att = bf16[32,16,128]{2,1,0:T(8,128)(2,1)S(1)} all-to-all(bf16[32,16,128]{2,1,0:T(8,128)(2,1)S(1)} %combine.1), channel_id=1, replica_groups=mesh['blk'=32,'rows'=16] {'blk'}, dimensions={0} | all-to-all | bytes 262144 | tf_op jit(solution)/shard_map/all_to_all | solution.py:288
  119.7 0.2 output.1
  119.9 13.5 %all_to_all.31 = bf16[16,8,256]{2,1,0:T(8,128)(2,1)S(1)} all-to-all(bf16[16,8,256]{2,1,0:T(8,128)(2,1)S(1)} %bitcast.5), channel_id=1, replica_groups=mesh['blk'=32,'rows'=16] {'rows'}, dimensions={0} | all-to-all | bytes 131072 | tf_op jit(solution)/shard_map/all_to_all | solution.py:297
  133.4 0.7 copy-done.4
  134.1 0.6 add_convert_fusion
  (17 shorter events, 0.1 us)
Async XLA Ops:
  3.5 30.7 %copy-start = (bf16[256,512]{1,0:T(8,128)(2,1)S(1)}, bf16[256,512]{1,0:T(8,128)(2,1)}, u32[]{:S(2)}) copy-start(bf16[256,512]{1,0:T(8,128)(2,1)} %wq.1) | copy-start | bytes 786436
  3.5 30.7 %copy-start.2 = (bf16[256,128]{1,0:T(8,128)(2,1)S(1)}, bf16[256,128]{1,0:T(8,128)(2,1)}, u32[]{:S(2)}) copy-start(bf16[256,128]{1,0:T(8,128)(2,1)} %wkv.1) | copy-start | bytes 196612
  3.5 30.7 %all-to-all-start = ((bf16[16,208,128]{2,1,0:T(8,128)(2,1)}), bf16[16,208,128]{2,1,0:T(8,128)(2,1)S(1)}, u32[]{:S(2)}, u32[]{:S(2)}) async-start(bf16[16,208,128]{2,1,0:T(8,128)(2,1)} %pack.1), calls=%async_computation | async-start | bytes 1703936 | tf_op jit(solution)/shard_map/all_to_all | solution.py:234
  13.2 0.7 copy-start.8
  13.9 21.4 %copy-start.5 = (s32[128]{0:T(128)S(1)}, s32[128]{0:T(128)}, u32[]{:S(2)}) copy-start(s32[128]{0:T(128)} %param.22) | copy-start | bytes 1540
  35.4 14.6 %copy-start.6 = (f32[128]{0:T(128)S(1)}, f32[128]{0:T(128)}, u32[]{:S(2)}) copy-start(f32[128]{0:T(128)} %constant.25.clone) | copy-start | bytes 1540
  35.4 14.6 %copy-start.7 = (f32[128]{0:T(128)S(1)}, f32[128]{0:T(128)}, u32[]{:S(2)}) copy-start(f32[128]{0:T(128)} %constant.24.clone) | copy-start | bytes 1540
  35.4 27.7 %all-to-all-start.1 = ((bf16[32,32,128]{2,1,0:T(8,128)(2,1)}), bf16[32,32,128]{2,1,0:T(8,128)(2,1)S(1)}, u32[]{:S(2)}, u32[]{:S(2)}) async-start(bf16[32,32,128]{2,1,0:T(8,128)(2,1)} %project.1), calls=%async_computation.1 | async-start | bytes 524288 | tf_op jit(solution)/shard_map/all_to_all | solution.py:250
  50.2 13.0 %copy-start.3 = (s32[2]{0:T(128)S(1)}, s32[2]{0:T(128)}, u32[]{:S(2)}) copy-start(s32[2]{0:T(128)} %pad_add_fusion.who) | copy-start | bytes 28
  50.2 29.4 %collective-permute-start = (bf16[16,208,128]{2,1,0:T(8,128)(2,1)S(1)}, bf16[16,208,128]{2,1,0:T(8,128)(2,1)S(1)}, u32[]{:S(2)}, u32[]{:S(2)}) collective-permute-start(bf16[16,208,128]{2,1,0:T(8,128)(2,1)S(1)} %all-to-all-done.x_ref.mine), channel_id=1, source_target_pairs={{0,1},{1,0},{2,3},{3,2},{4,5},{5,4},{6,7},{7,6},{8,9},{9,8},{10,11... | collective-permute-start | bytes 2555912 | tf_op jit(solution)/shard_map/ppermute | solution.py:256
  64.6 15.1 %all-to-all-start.2 = ((bf16[32,16,128]{2,1,0:T(8,128)(2,1)}), bf16[32,16,128]{2,1,0:T(8,128)(2,1)S(1)}, u32[]{:S(2)}, u32[]{:S(2)}) async-start(bf16[32,16,128]{2,1,0:T(8,128)(2,1)} %get-tuple-element.20), calls=%async_computation.2 | async-start | bytes 262144 | tf_op jit(solution)/shard_map/all_to_all | solution.py:267
  69.0 0.7 collective-permute-start.1
  83.6 16.3 %all-to-all-start.3 = ((bf16[32,32,128]{2,1,0:T(8,128)(2,1)}), bf16[32,32,128]{2,1,0:T(8,128)(2,1)S(1)}, u32[]{:S(2)}, u32[]{:S(2)}) async-start(bf16[32,32,128]{2,1,0:T(8,128)(2,1)} %attend.1), calls=%async_computation.3 | async-start | bytes 524288 | tf_op jit(solution)/shard_map/all_to_all | solution.py:279
  87.3 9.9 %collective-permute-start.2 = (bf16[16,128]{1,0:T(8,128)(2,1)S(1)}, bf16[16,128]{1,0:T(8,128)(2,1)S(1)}, u32[]{:S(2)}, u32[]{:S(2)}) collective-permute-start(bf16[16,128]{1,0:T(8,128)(2,1)S(1)} %get-tuple-element.26), channel_id=1, source_target_pairs={{0,1},{1,3},{2,5},{3,7},{4,9},{5,11},{6,13},{7,15},{8,0},{9,2},{10... | collective-permute-start | bytes 12296 | tf_op jit(solution)/shard_map/ppermute | solution.py:278
  99.9 19.8 %copy-start.1 = (bf16[512,256]{1,0:T(8,128)(2,1)S(1)}, bf16[512,256]{1,0:T(8,128)(2,1)}, u32[]{:S(2)}) copy-start(bf16[512,256]{1,0:T(8,128)(2,1)} %w.1) | copy-start | bytes 786436
  133.4 0.7 copy-start.4

commit v5 on v3

--- a/solution.py
+++ b/solution.py
@@ -61,34 +61,66 @@
     return pltpu.roll(x, 4, 1)
 
 
-def project_body(x_ref, gain, wq, wkv, out):
+def half_swap(x):
+    return pltpu.roll(x, 4, 1)
+
+
+def gathered_rows(x_ref):
     xr = x_ref[...].astype(F32)
-    x = jnp.concatenate(
+    return jnp.concatenate(
         [xr[:, :8, :].reshape(128, HD), xr[:, 8:, :].reshape(128, HD)], axis=1
     )
+
+
+def by_rows_of_four(blocks, p):
+    blocks = [block.reshape(16, 8, HD) for block in blocks]
+    low = iota((16, 8, HD), 1) < 4
+    tiles = []
+    for u in range(2):
+        first, second = blocks[2 * u], blocks[2 * u + 1]
+        if p == 0:
+            tiles.append(jnp.where(low, first, half_swap(second)))
+        else:
+            tiles.append(jnp.where(low, half_swap(first), second))
+    return tiles
+
+
+def project_body(x_ref, gain, wq, out):
+    x = gathered_rows(x_ref)
     square = lax.dot_general(
         jnp.ones((8, 2 * HD), F32), x * x, NT,
         precision=lax.Precision.HIGHEST, preferred_element_type=F32,
     )
     high = square.astype(BF).astype(F32)
-    sub = iota((16, 8, HD), 1)
-    squares = jnp.where(sub == 4, high[None], jnp.where(sub == 5, (square - high)[None], 0.0))
+    sub = iota((8, HD), 0)
+    squares = jnp.where(sub == 0, high, jnp.where(sub == 1, square - high, 0.0))
+    squares = jnp.concatenate([squares, jnp.zeros((8, HD), F32)], axis=0).astype(BF)
     xg = (x * gain[...].astype(F32)).astype(BF)
     q = jnp.dot(xg, wq[...], preferred_element_type=F32)
-    kv = jnp.dot(xg, wkv[...], preferred_element_type=F32).reshape(16, 8, HD)
-    heads = [q[:, HD * h : HD * h + HD].reshape(16, 8, HD) for h in range(4)]
-    low = sub < 4
+    heads = [q[:, HD * h : HD * h + HD] for h in range(4)]
     for p in range(2):
-        tiles = []
-        for u in range(2):
-            first, second = heads[2 * u], heads[2 * u + 1]
-            if p == 0:
-                tiles.append(jnp.where(low, first, half_swap(second)))
-            else:
-                tiles.append(jnp.where(low, half_swap(first), second))
-        tiles.append(jnp.where(low, kv if p == 0 else half_swap(kv), squares))
-        tiles.append(jnp.zeros((16, 8, HD), F32))
-        chunks = jnp.concatenate(tiles, axis=1).astype(BF)
+        chunks = jnp.concatenate(by_rows_of_four(heads, p), axis=1).astype(BF)
+        for j in range(16):
+            out[2 * j + p, 0:16, :] = chunks[j]
+            out[2 * j + p, 16:32, :] = squares
+
+
+def keyval_body(who, x_ref, gain, wa, wb, out):
+    xg = (gathered_rows(x_ref) * gain[...].astype(F32)).astype(BF)
+    even = lax.rem(who[1], 2) == 0
+    first = jnp.dot(xg, wa[...], preferred_element_type=F32)
+    second = jnp.dot(xg, wb[...], preferred_element_type=F32)
+    key = jnp.where(even, first, second)
+    value = jnp.where(even, second, first)
+    lane = iota((128, HD), 1)
+    blocks = []
+    for j in range(4):
+        moved_k = pltpu.roll(key, (32 - 32 * j) % HD, 1)
+        moved_v = pltpu.roll(value, (64 - 32 * j) % HD, 1)
+        block = jnp.where(lane < 64, moved_k, moved_v)
+        blocks.append(jnp.where((lane >= 32) & (lane < 96), block, 0.0))
+    for p in range(2):
+        chunks = jnp.concatenate(by_rows_of_four(blocks, p), axis=1).astype(BF)
         for j in range(16):
             out[2 * j + p, :, :] = chunks[j]
 
@@ -97,22 +129,21 @@
     return u * cosine + pltpu.roll(u, HD // 2, 1) * sine
 
 
-def query_body(who, parts, cosine, sine, q_out, q_own, kv_out):
+def query_body(who, parts, cosine, sine, q_out, q_own, scale_out):
     total = jnp.sum(parts[...].astype(F32), axis=0)
-    square = total[20:21, :] + total[21:22, :]
+    square = total[16:17, :] + total[17:18, :]
     inv = lax.rsqrt(square / 8192.0 + 1e-05)
-    lane, sub = iota((24, HD), 1), iota((24, HD), 0)
+    lane, sub = iota((16, HD), 1), iota((16, HD), 0)
     col = jnp.sum(jnp.where(lane == 4 * who[0] + sub % 4, inv, 0.0), axis=1, keepdims=True)
-    raw = (total[0:24, :] * col).astype(BF).astype(F32)
-    turned = rotate(raw, cosine[...], sine[...])
-    query = turned[0:16, :].astype(BF)
+    scale_out[...] = jnp.broadcast_to(col, (16, HD))
+    raw = (total[0:16, :] * col).astype(BF).astype(F32)
+    query = rotate(raw, cosine[...], sine[...]).astype(BF)
     q_own[...] = query
     for i in range(q_out.shape[0]):
         q_out[i, :, :] = query
-    kv_out[...] = jnp.concatenate([turned[16:24, :], jnp.zeros((8, HD), F32)], axis=0).astype(BF)
-
-
-def attend_body(who, mine, other, q_ref, out):
+
+
+def attend_body(who, mine, other, q_ref, kv_part, out):
     r = who[1]
     scale = HD ** (-0.5)
     sources = (mine, other)
@@ -155,17 +186,31 @@
             jnp.where(lane_s == 1, low, jnp.where(lane_s == 2, mass_high, jnp.where(lane_s == 3, mass - mass_high, 0.0))),
         )
         out[8 * t : 8 * t + 8, 0:16, :] = acc.astype(BF).reshape(8, 16, HD)
+        rest = kv_part[8 * t : 8 * t + 8].reshape(128, HD).astype(F32)
+        stats = jnp.where(lane_s < 32, stats, rest)
         out[8 * t : 8 * t + 8, 16:32, :] = stats.astype(BF).reshape(8, 16, HD)
 
 
-def combine_body(who, parts, q_own, new_a, new_b, out):
-    even = lax.rem(who[1], 2) == 0
-    first, second = new_a[...].astype(F32), new_b[...].astype(F32)
-    new_k = jnp.concatenate([jnp.where(even, first, second)[0:4, :]] * 4, axis=0)
-    new_v = jnp.concatenate([jnp.where(even, second, first)[0:4, :]] * 4, axis=0)
+def to_every_head(total, start):
+    lane, sub = iota((16, HD), 1), iota((16, HD), 0)
+    whole = jnp.zeros((16, HD), F32)
+    for j in range(4):
+        block = jnp.where(sub // 4 == j, total, 0.0)
+        block = block + pltpu.roll(block, 8, 0)
+        block = block + pltpu.roll(block, 4, 0)
+        block = pltpu.roll(block, (32 * j - start) % HD, 1)
+        whole = jnp.where(lane // 32 == j, block, whole)
+    return whole
+
+
+def combine_body(parts, q_own, scale, cosine, sine, out):
+    stats = parts[:, 16:32, :].astype(F32)
+    total = jnp.sum(stats, axis=0)
+    new_k = (to_every_head(total, 32) * scale[...]).astype(BF).astype(F32)
+    new_k = rotate(new_k, cosine[...], sine[...]).astype(BF).astype(F32)
+    new_v = (to_every_head(total, 64) * scale[...]).astype(BF).astype(F32)
     new = jnp.sum(q_own[...].astype(F32) * new_k, axis=1, keepdims=True) * HD ** (-0.5)
     acc = parts[:, 0:16, :].astype(F32)
-    stats = parts[:, 16:32, :].astype(F32)
     peak = stats[:, :, 0:1] + stats[:, :, 1:2]
     mass = stats[:, :, 2:3] + stats[:, :, 3:4]
     top = jnp.maximum(jnp.max(peak, axis=0), new)
@@ -217,6 +262,8 @@
     b, r = lax.axis_index("blk"), lax.axis_index("rows")
     who = jnp.stack([b, r]).astype(jnp.int32)
     sds = jax.ShapeDtypeStruct
+    first_w = lax.ppermute(w_keyval, "rows", [(s, 2 * (s % 8) + s // 8) for s in range(16)])
+    second_w = lax.ppermute(w_keyval, "rows", [(s, 2 * (s % 8) + 1 - s // 8) for s in range(16)])
     packed = pl.pallas_call(
         pack_body,
         out_shape=sds((16, END, HD), BF),
@@ -232,57 +279,59 @@
         name="pack",
     )(who, lengths, hidden_in, prefix_keys, prefix_values, own_keys.reshape(64, 1024), own_values.reshape(64, 1024))
     mine = lax.all_to_all(packed, "rows", 0, 0, tiled=True)
+    gain = norm_gain.reshape(1, 256)
+    x_spec = pl.BlockSpec((16, END - X0, HD), lambda i: (0, X0 // 16, 0))
+    gain_spec = pl.BlockSpec((1, 256), lambda i: (0, 0))
     parts = pl.pallas_call(
         project_body,
         grid=(1,),
         out_shape=sds((32, 32, HD), BF),
-        in_specs=[
-            pl.BlockSpec((16, END - X0, HD), lambda i: (0, X0 // 16, 0)),
-            pl.BlockSpec((1, 256), lambda i: (0, 0)),
-            pl.BlockSpec((256, 512), lambda i: (0, 0)),
-            pl.BlockSpec((256, HD), lambda i: (0, 0)),
-        ],
+        in_specs=[x_spec, gain_spec, pl.BlockSpec((256, 512), lambda i: (0, 0))],
         out_specs=pl.BlockSpec((32, 32, HD), lambda i: (0, 0, 0)),
         compiler_params=params(),
         name="project",
-    )(mine, norm_gain.reshape(1, 256), w_query, w_keyval)
+    )(mine, gain, w_query)
     positions, parts = lax.optimization_barrier((positions, parts))
     parts = lax.all_to_all(parts, "blk", 0, 0, tiled=True)
-    places = lax.dynamic_slice_in_dim(positions, 4 * b, 4, 0)
-    still = jnp.zeros_like(places)
-    places = jnp.concatenate([places] * 4 + [jnp.where(r < 8, places, still), still])
-    cosine, sine = rotary_tables(places)
-    mine, cosine = lax.optimization_barrier((mine, cosine))
+    cosine, sine = rotary_tables(jnp.concatenate([lax.dynamic_slice_in_dim(positions, 4 * b, 4, 0)] * 4))
+    mine, cosine, first_w, second_w = lax.optimization_barrier((mine, cosine, first_w, second_w))
     other = lax.ppermute(mine, "rows", [(i, i ^ 1) for i in range(16)])
-    query, q_own, new = pl.pallas_call(
+    kv_part = pl.pallas_call(
+        keyval_body,
+        grid=(1,),
+        out_shape=sds((32, 16, HD), BF),
+        in_specs=[SM, x_spec, gain_spec] + [pl.BlockSpec((256, HD), lambda i: (0, 0))] * 2,
+        out_specs=pl.BlockSpec((32, 16, HD), lambda i: (0, 0, 0)),
+        compiler_params=params(),
+        name="keyval",
+    )(who, mine, gain, first_w, second_w)
+    query, q_own, row_scale = pl.pallas_call(
         query_body,
-        out_shape=(sds((32, 16, HD), BF), sds((16, HD), BF), sds((16, HD), BF)),
+        out_shape=(sds((32, 16, HD), BF), sds((16, HD), BF), sds((16, HD), F32)),
         in_specs=[SM, VM, VM, VM],
         out_specs=(VM, VM, VM),
         compiler_params=params(),
         cost_estimate=pl.CostEstimate(flops=2 * 10**9, bytes_accessed=1 << 20, transcendentals=0),
         name="query",
     )(who, parts, cosine, sine)
-    new_a = lax.ppermute(new, "rows", [(s, 2 * (s % 8) + s // 8) for s in range(16)])
-    new_b = lax.ppermute(new, "rows", [(s, 2 * (s % 8) + 1 - s // 8) for s in range(16)])
     query = lax.all_to_all(query, "blk", 0, 0, tiled=True)
     partial = pl.pallas_call(
         attend_body,
         out_shape=sds((32, 32, HD), BF),
-        in_specs=[SM] + [VM] * 3,
+        in_specs=[SM] + [VM] * 4,
         out_specs=VM,
         compiler_params=params(),
         name="attend",
-    )(who, mine, other, query)
+    )(who, mine, other, query, kv_part)
     partial = lax.all_to_all(partial, "blk", 0, 0, tiled=True)
     attended = pl.pallas_call(
         combine_body,
         out_shape=sds((32, 16, HD), BF),
-        in_specs=[SM] + [VM] * 4,
+        in_specs=[VM] * 5,
         out_specs=VM,
         compiler_params=params(),
         name="combine",
-    )(who, partial, q_own, new_a, new_b)
+    )(partial, q_own, row_scale, cosine, sine)
     attended = lax.all_to_all(attended, "blk", 0, 0, tiled=True)
     mixed = pl.pallas_call(
         output_body,

time: 135 us -> 130 us (0.963)
  waiting for transfers between devices: 38.4 us -> 35.1 us
  blocking collectives: 46.9 us -> 44.2 us
    all_to_all x1, blocking collectives: 16.8 us -> 12.6 us  [on_device(): mixed = lax.all_to_all(mixed.reshape(16, 8, 256), 'rows', 0, 0, tiled=True)]
    all_to_all x1, waiting for transfers between devices: 5.83 us -> 9.83 us  [on_device(): query = lax.all_to_all(query, 'blk', 0, 0, tiled=True)]
    all_to_all x1, waiting for transfers between devices: 20.3 us -> 16.4 us  [on_device(): mine = lax.all_to_all(packed, 'rows', 0, 0, tiled=True)]
    ppermute x2, waiting for transfers between devices: 2.54 us -> 0.01 us  [the longest x1 0.01 us: on_device(): lax.ppermute(w_keyval, 'rows', [(s, 2 * (s % 8) + 1 - s // 8) for s in ra...]
    all_to_all x1, blocking collectives: 14.9 us -> 17.3 us  [on_device(): partial = lax.all_to_all(partial, 'blk', 0, 0, tiled=True)]
  transfers between devices with their start and end apart: 6 -> 6, of which waited for: 4 -> 3; matrix products, arithmetic and copies ran while one was open for 0% -> 0% of each run, Pallas kernels for 1% -> 2%
where the time goes in v5:
time: 130 us; the launch traced here: 129 us
  blocking collectives  44.2 us (34%)
  starting transfers between devices  36.8 us (28%)
  waiting for transfers between devices  35.1 us (27%)
  Pallas kernels  9.98 us (8%)
  other arithmetic  1.46 us (1%)
  local copies, waits for them, and re-layouts  1.42 us (1%)
    all_to_all x1, blocking collectives, on_device(): partial = lax.all_to_all(partial, 'blk', 0, 0, tiled=True)  17.3 us
    all_to_all x1, waiting for transfers between devices, on_device(): mine = lax.all_to_all(packed, 'rows', 0, 0, tiled=True)  16.4 us
    all_to_all x1, starting transfers between devices, on_device(): parts = lax.all_to_all(parts, 'blk', 0, 0, tiled=True)  14.8 us
    all_to_all x1, blocking collectives, on_device(): attended = lax.all_to_all(attended, 'blk', 0, 0, tiled=True)  14.3 us
    all_to_all x1, blocking collectives, on_device(): mixed = lax.all_to_all(mixed.reshape(16, 8, 256), 'rows', 0, 0, tiled=True)  12.6 us
    all_to_all x1, waiting for transfers between devices, on_device(): query = lax.all_to_all(query, 'blk', 0, 0, tiled=True)  9.83 us
    all_to_all x1, starting transfers between devices, on_device(): mine = lax.all_to_all(packed, 'rows', 0, 0, tiled=True)  9.71 us
    all_to_all x1, waiting for transfers between devices, on_device(): parts = lax.all_to_all(parts, 'blk', 0, 0, tiled=True)  8.88 us
  transfers between devices with their start and end apart: 6, of which 3 were waited for; matrix products, arithmetic and copies ran while one was open for 0% of the time, Pallas kernels for 2%

profile of v5, /device:TPU:1, one launch (start us, length us, event | category | flops | bytes accessed | tf_op | source)
XLA Modules:
  0.0 129.1 jit_solution(8343068729212678760)
XLA Ops:
  0.0 0.6 pad_add_fusion.who
  0.6 2.9 %pack.1 = bf16[16,208,128]{2,1,0:T(8,128)(2,1)} custom-call(s32[2]{0:T(128)} %pad_add_fusion.who, s32[8]{0:T(128)} %lens.1, bf16[8,256]{1,0:T(8,128)(2,1)} %hidden.1, bf16[128,1024]{1,0:T(8,128)(2,1)} %keys_hbm.1, bf16[128,1024]{1,0:T(8,128)(2,1)} %values_hbm.1, bf16[64,1024]{1,0:T(8,128)(2,1)} %bitcast.6, bf16[64,1024]{1,0:T(8,128)(2,1)} %bitcast.7), custom_call_target="tpu_custom_call" | custom-call | tf_op jit(solution)/shard_map/pack/pallas_call | solution.py:267
  3.5 0.0 copy-start.6
  3.5 0.0 copy-start.1
  3.5 9.7 %all-to-all-start = ((bf16[16,208,128]{2,1,0:T(8,128)(2,1)}), bf16[16,208,128]{2,1,0:T(8,128)(2,1)S(1)}, u32[]{:S(2)}, u32[]{:S(2)}) async-start(bf16[16,208,128]{2,1,0:T(8,128)(2,1)} %pack.1), calls=%async_computation | async-start | bytes 1703936 | tf_op jit(solution)/shard_map/all_to_all | solution.py:281
  13.3 3.3 %collective-permute-start.1 = (bf16[256,128]{1,0:T(8,128)(2,1)S(1)}, bf16[256,128]{1,0:T(8,128)(2,1)S(1)}, u32[]{:S(2)}, u32[]{:S(2)}) collective-permute-start(bf16[256,128]{1,0:T(8,128)(2,1)S(1)} %copy-done.6), channel_id=1, source_target_pairs={{0,1},{1,3},{2,5},{3,7},{4,9},{5,11},{6,13},{7,15},{8,0},{9,2},{10... | collective-permute-start | bytes 196616 | tf_op jit(solution)/shard_map/ppermute | solution.py:266
  16.5 0.7 collective-permute-start
  17.2 0.0 copy-start.7
  17.2 0.6 copy-done.7
  17.9 16.4 %all-to-all-done.x_ref.mine = bf16[16,208,128]{2,1,0:T(8,128)(2,1)S(1)} async-done(((bf16[16,208,128]{2,1,0:T(8,128)(2,1)}), bf16[16,208,128]{2,1,0:T(8,128)(2,1)S(1)}, u32[]{:S(2)}, u32[]{:S(2)}) %all-to-all-start) | async-done | bytes 852000 | tf_op jit(solution)/shard_map/all_to_all | solution.py:281
  34.2 1.0 project.1
  35.2 0.1 dynamic_slice.3
  35.3 0.1 add_convert_fusion.1
  35.4 14.8 %all-to-all-start.1 = ((bf16[32,32,128]{2,1,0:T(8,128)(2,1)}), bf16[32,32,128]{2,1,0:T(8,128)(2,1)S(1)}, u32[]{:S(2)}, u32[]{:S(2)}) async-start(bf16[32,32,128]{2,1,0:T(8,128)(2,1)} %project.1), calls=%async_computation.1 | async-start | bytes 524288 | tf_op jit(solution)/shard_map/all_to_all | solution.py:295
  50.3 0.1 fusion
  50.4 0.0 collective-permute-done.1.wb
  50.4 0.0 collective-permute-done.wa
  50.4 4.0 %collective-permute-start.2 = (bf16[16,208,128]{2,1,0:T(8,128)(2,1)S(1)}, bf16[16,208,128]{2,1,0:T(8,128)(2,1)S(1)}, u32[]{:S(2)}, u32[]{:S(2)}) collective-permute-start(bf16[16,208,128]{2,1,0:T(8,128)(2,1)S(1)} %all-to-all-done.x_ref.mine), channel_id=1, source_target_pairs={{0,1},{1,0},{2,3},{3,2},{4,5},{5,4},{6,7},{7,6},{8,9},{9,8},{10,11... | collective-permute-start | bytes 2555912 | tf_op jit(solution)/shard_map/ppermute | solution.py:298
  54.5 8.9 %all-to-all-done.1.parts = bf16[32,32,128]{2,1,0:T(8,128)(2,1)S(1)} async-done(((bf16[32,32,128]{2,1,0:T(8,128)(2,1)}), bf16[32,32,128]{2,1,0:T(8,128)(2,1)S(1)}, u32[]{:S(2)}, u32[]{:S(2)}) %all-to-all-start.1) | async-done | bytes 262176 | tf_op jit(solution)/shard_map/all_to_all | solution.py:295
  63.3 1.4 %query.1 = (bf16[32,16,128]{2,1,0:T(8,128)(2,1)}, bf16[16,128]{1,0:T(8,128)(2,1)S(1)}, f32[16,128]{1,0:T(8,128)S(1)}) custom-call(s32[2]{0:T(128)S(1)} %copy-done.2, bf16[32,32,128]{2,1,0:T(8,128)(2,1)S(1)} %all-to-all-done.1.parts, f32[16,128]{1,0:T(8,128)S(1)} %get-tuple-element.17.cosine, f32[16,128]{1,0:T(8,128)S(1)} %get-tuple-element.23.sine), custom_call_target="tpu_custom_call" | custom-call | flops 2000000000 | bytes 1048576 | tf_op jit(solution)/shard_map/query/pallas_call | solution.py:308
  64.7 4.3 %all-to-all-start.2 = ((bf16[32,16,128]{2,1,0:T(8,128)(2,1)}), bf16[32,16,128]{2,1,0:T(8,128)(2,1)S(1)}, u32[]{:S(2)}, u32[]{:S(2)}) async-start(bf16[32,16,128]{2,1,0:T(8,128)(2,1)} %get-tuple-element.18), calls=%async_computation.2 | async-start | bytes 262144 | tf_op jit(solution)/shard_map/all_to_all | solution.py:317
  69.1 0.8 keyval.1.kv_part
  69.9 9.8 %all-to-all-done.2.q_ref = bf16[32,16,128]{2,1,0:T(8,128)(2,1)S(1)} async-done(((bf16[32,16,128]{2,1,0:T(8,128)(2,1)}), bf16[32,16,128]{2,1,0:T(8,128)(2,1)S(1)}, u32[]{:S(2)}, u32[]{:S(2)}) %all-to-all-start.2) | async-done | bytes 131104 | tf_op jit(solution)/shard_map/all_to_all | solution.py:317
  79.7 0.0 collective-permute-done.2.other
  79.7 3.2 %attend.1 = bf16[32,32,128]{2,1,0:T(8,128)(2,1)S(1)} custom-call(s32[2]{0:T(128)S(1)} %copy-done.2, bf16[16,208,128]{2,1,0:T(8,128)(2,1)S(1)} %all-to-all-done.x_ref.mine, bf16[16,208,128]{2,1,0:T(8,128)(2,1)S(1)} %collective-permute-done.2.other, bf16[32,16,128]{2,1,0:T(8,128)(2,1)S(1)} %all-to-all-done.2.q_ref, bf16[32,16,128]{2,1,0:T(8,128)(2,1)S(1)} %keyval.1.kv_part), custom_call_target="tpu_custom_call" | custom-call | tf_op jit(solution)/shard_map/attend/pallas_call | solution.py:318
  82.9 17.3 %all_to_all.30.parts = bf16[32,32,128]{2,1,0:T(8,128)(2,1)S(1)} all-to-all(bf16[32,32,128]{2,1,0:T(8,128)(2,1)S(1)} %attend.1), channel_id=1, replica_groups=mesh['blk'=32,'rows'=16] {'blk'}, dimensions={0} | all-to-all | bytes 524288 | tf_op jit(solution)/shard_map/all_to_all | solution.py:326
  100.2 0.5 combine.1
  100.7 14.3 %all_to_all.31.att = bf16[32,16,128]{2,1,0:T(8,128)(2,1)S(1)} all-to-all(bf16[32,16,128]{2,1,0:T(8,128)(2,1)S(1)} %combine.1), channel_id=1, replica_groups=mesh['blk'=32,'rows'=16] {'blk'}, dimensions={0} | all-to-all | bytes 262144 | tf_op jit(solution)/shard_map/all_to_all | solution.py:335
  115.1 0.2 output.1
  115.3 12.6 %all_to_all.32 = bf16[16,8,256]{2,1,0:T(8,128)(2,1)S(1)} all-to-all(bf16[16,8,256]{2,1,0:T(8,128)(2,1)S(1)} %bitcast.5), channel_id=1, replica_groups=mesh['blk'=32,'rows'=16] {'rows'}, dimensions={0} | all-to-all | bytes 131072 | tf_op jit(solution)/shard_map/all_to_all | solution.py:344
  127.9 0.7 copy-done.3
  128.5 0.6 add_convert_fusion
  (15 shorter events, 0.0 us)
Async XLA Ops:
  3.5 9.7 %copy-start.6 = (bf16[256,128]{1,0:T(8,128)(2,1)S(1)}, bf16[256,128]{1,0:T(8,128)(2,1)}, u32[]{:S(2)}) copy-start(bf16[256,128]{1,0:T(8,128)(2,1)} %param.16) | copy-start | bytes 196612
  3.5 30.7 %copy-start.1 = (bf16[256,512]{1,0:T(8,128)(2,1)S(1)}, bf16[256,512]{1,0:T(8,128)(2,1)}, u32[]{:S(2)}) copy-start(bf16[256,512]{1,0:T(8,128)(2,1)} %wq.1) | copy-start | bytes 786436
  3.5 30.7 %all-to-all-start = ((bf16[16,208,128]{2,1,0:T(8,128)(2,1)}), bf16[16,208,128]{2,1,0:T(8,128)(2,1)S(1)}, u32[]{:S(2)}, u32[]{:S(2)}) async-start(bf16[16,208,128]{2,1,0:T(8,128)(2,1)} %pack.1), calls=%async_computation | async-start | bytes 1703936 | tf_op jit(solution)/shard_map/all_to_all | solution.py:281
  13.3 37.1 %collective-permute-start.1 = (bf16[256,128]{1,0:T(8,128)(2,1)S(1)}, bf16[256,128]{1,0:T(8,128)(2,1)S(1)}, u32[]{:S(2)}, u32[]{:S(2)}) collective-permute-start(bf16[256,128]{1,0:T(8,128)(2,1)S(1)} %copy-done.6), channel_id=1, source_target_pairs={{0,1},{1,3},{2,5},{3,7},{4,9},{5,11},{6,13},{7,15},{8,0},{9,2},{10... | collective-permute-start | bytes 196616 | tf_op jit(solution)/shard_map/ppermute | solution.py:266
  16.5 33.9 %collective-permute-start = (bf16[256,128]{1,0:T(8,128)(2,1)S(1)}, bf16[256,128]{1,0:T(8,128)(2,1)S(1)}, u32[]{:S(2)}, u32[]{:S(2)}) collective-permute-start(bf16[256,128]{1,0:T(8,128)(2,1)S(1)} %copy-done.6), channel_id=1, source_target_pairs={{0,0},{1,2},{2,4},{3,6},{4,8},{5,10},{6,12},{7,14},{8,1},{9,3},{10... | collective-permute-start | bytes 196616 | tf_op jit(solution)/shard_map/ppermute | solution.py:265
  17.2 0.7 copy-start.7
  17.9 17.4 %copy-start.8 = (s32[128]{0:T(128)S(1)}, s32[128]{0:T(128)}, u32[]{:S(2)}) copy-start(s32[128]{0:T(128)} %param.22) | copy-start | bytes 1540
  35.4 14.8 %copy-start.4 = (f32[128]{0:T(128)S(1)}, f32[128]{0:T(128)}, u32[]{:S(2)}) copy-start(f32[128]{0:T(128)} %constant.22.clone) | copy-start | bytes 1540
  35.4 14.9 %copy-start.5 = (f32[128]{0:T(128)S(1)}, f32[128]{0:T(128)}, u32[]{:S(2)}) copy-start(f32[128]{0:T(128)} %constant.21.clone) | copy-start | bytes 1540
  35.4 27.9 %all-to-all-start.1 = ((bf16[32,32,128]{2,1,0:T(8,128)(2,1)}), bf16[32,32,128]{2,1,0:T(8,128)(2,1)S(1)}, u32[]{:S(2)}, u32[]{:S(2)}) async-start(bf16[32,32,128]{2,1,0:T(8,128)(2,1)} %project.1), calls=%async_computation.1 | async-start | bytes 524288 | tf_op jit(solution)/shard_map/all_to_all | solution.py:295
  50.4 12.9 %copy-start.2 = (s32[2]{0:T(128)S(1)}, s32[2]{0:T(128)}, u32[]{:S(2)}) copy-start(s32[2]{0:T(128)} %pad_add_fusion.who) | copy-start | bytes 28
  50.4 29.3 %collective-permute-start.2 = (bf16[16,208,128]{2,1,0:T(8,128)(2,1)S(1)}, bf16[16,208,128]{2,1,0:T(8,128)(2,1)S(1)}, u32[]{:S(2)}, u32[]{:S(2)}) collective-permute-start(bf16[16,208,128]{2,1,0:T(8,128)(2,1)S(1)} %all-to-all-done.x_ref.mine), channel_id=1, source_target_pairs={{0,1},{1,0},{2,3},{3,2},{4,5},{5,4},{6,7},{7,6},{8,9},{9,8},{10,11... | collective-permute-start | bytes 2555912 | tf_op jit(solution)/shard_map/ppermute | solution.py:298
  64.7 15.0 %all-to-all-start.2 = ((bf16[32,16,128]{2,1,0:T(8,128)(2,1)}), bf16[32,16,128]{2,1,0:T(8,128)(2,1)S(1)}, u32[]{:S(2)}, u32[]{:S(2)}) async-start(bf16[32,16,128]{2,1,0:T(8,128)(2,1)} %get-tuple-element.18), calls=%async_computation.2 | async-start | bytes 262144 | tf_op jit(solution)/shard_map/all_to_all | solution.py:317
  100.2 14.9 %copy-start = (bf16[512,256]{1,0:T(8,128)(2,1)S(1)}, bf16[512,256]{1,0:T(8,128)(2,1)}, u32[]{:S(2)}) copy-start(bf16[512,256]{1,0:T(8,128)(2,1)} %w.1) | copy-start | bytes 786436
  127.9 0.7 copy-start.3

commit v6 on v5

--- a/solution.py
+++ b/solution.py
@@ -7,6 +7,7 @@
 from jax.sharding import PartitionSpec as P
 
 HD = 128
+LOG2E = float(np.log2(np.e))
 F32 = jnp.float32
 BF = jnp.bfloat16
 VM = pl.BlockSpec(memory_space=pltpu.VMEM)
@@ -23,16 +24,20 @@
     return lax.broadcasted_iota(jnp.int32, shape, dim)
 
 
-def pack_body(who, lens, hidden, keys_hbm, values_hbm, own_k_hbm, own_v_hbm, out, keys, values, own_k, own_v, sems):
-    copies = [
+def pack_body(lens, hidden, keys_hbm, values_hbm, own_k_hbm, own_v_hbm, out, keys, values, own_k, own_v, packed, sems):
+    inward = [
         pltpu.make_async_copy(src, dst, sems.at[i])
         for i, (src, dst) in enumerate(
-            ((keys_hbm, keys), (values_hbm, values), (own_k_hbm, own_k), (own_v_hbm, own_v))
+            ((own_k_hbm, own_k), (keys_hbm, keys), (values_hbm, values), (own_v_hbm, own_v))
         )
     ]
-    for copy in copies:
+    for copy in inward:
         copy.start()
-    b = who[0]
+    outward = [
+        pltpu.make_async_copy(packed.at[:, first:last, :], out.at[:, first:last, :], sems.at[4 + i])
+        for i, (first, last) in enumerate(((OK0, OV0), (K0, V0), (V0, OK0), (OV0, END)))
+    ]
+    b = lax.axis_index("blk")
     x = hidden[...].astype(F32)
     x_tile = jnp.concatenate([x[:, :HD], x[:, HD:]], axis=0).astype(BF)
     sub = iota((32, HD), 0)
@@ -43,18 +48,25 @@
         for k in range(4):
             live = jnp.where(sub // 8 == k, lens[4 * p + k], live)
         dead.append(slot >= live)
-    for copy in copies:
+    for step in range(4):
+        inward[step].wait()
+        for p in range(2):
+            for h in range(8):
+                col = slice(h * HD, (h + 1) * HD)
+                d = 2 * h + p
+                if step == 0:
+                    own = own_k[32 * p : 32 * p + 32, col].astype(F32)
+                    packed[d, OK0:OV0, :] = jnp.where(dead[p], jnp.nan, own).astype(BF)
+                elif step == 1:
+                    packed[d, K0:V0, :] = keys[64 * p : 64 * p + 64, col]
+                elif step == 2:
+                    packed[d, V0:OK0, :] = values[64 * p : 64 * p + 64, col]
+                else:
+                    packed[d, OV0:X0, :] = own_v[32 * p : 32 * p + 32, col]
+                    packed[d, X0:END, :] = x_tile
+        outward[step].start()
+    for copy in outward:
         copy.wait()
-    for p in range(2):
-        for h in range(8):
-            col = slice(h * HD, (h + 1) * HD)
-            d = 2 * h + p
-            out[d, K0:V0, :] = keys[64 * p : 64 * p + 64, col]
-            out[d, V0:OK0, :] = values[64 * p : 64 * p + 64, col]
-            own = own_k[32 * p : 32 * p + 32, col].astype(F32)
-            out[d, OK0:OV0, :] = jnp.where(dead[p], jnp.nan, own).astype(BF)
-            out[d, OV0:X0, :] = own_v[32 * p : 32 * p + 32, col]
-            out[d, X0:END, :] = x_tile
 
 
 def half_swap(x):
@@ -94,15 +106,14 @@
     high = square.astype(BF).astype(F32)
     sub = iota((8, HD), 0)
     squares = jnp.where(sub == 0, high, jnp.where(sub == 1, square - high, 0.0))
-    squares = jnp.concatenate([squares, jnp.zeros((8, HD), F32)], axis=0).astype(BF)
+    squares = jnp.broadcast_to(squares[None], (16, 8, HD))
     xg = (x * gain[...].astype(F32)).astype(BF)
     q = jnp.dot(xg, wq[...], preferred_element_type=F32)
     heads = [q[:, HD * h : HD * h + HD] for h in range(4)]
     for p in range(2):
-        chunks = jnp.concatenate(by_rows_of_four(heads, p), axis=1).astype(BF)
+        chunks = jnp.concatenate(by_rows_of_four(heads, p) + [squares], axis=1).astype(BF)
         for j in range(16):
-            out[2 * j + p, 0:16, :] = chunks[j]
-            out[2 * j + p, 16:32, :] = squares
+            out[2 * j + p, :, :] = chunks[j]
 
 
 def keyval_body(who, x_ref, gain, wa, wb, out):
@@ -145,7 +156,7 @@
 
 def attend_body(who, mine, other, q_ref, kv_part, out):
     r = who[1]
-    scale = HD ** (-0.5)
+    scale = HD ** (-0.5) * LOG2E
     sources = (mine, other)
     halves = (lax.rem(r, 2), 1 - lax.rem(r, 2))
     keys = [s[:, K0:V0, :].reshape(1024, HD) for s in sources]
@@ -158,26 +169,27 @@
         q = q_ref[8 * t : 8 * t + 8].reshape(128, HD)
         scores, vals = [], []
         for k, v in zip(keys, values):
-            scores.append(lax.dot_general(q, k, NT, preferred_element_type=F32) * scale)
+            scores.append(lax.dot_general(q, k, NT, preferred_element_type=F32))
             vals.append(v)
         for s, half in zip(sources, halves):
             own_k = s[4 * t : 4 * t + 4, OK0:OV0, :].reshape(128, HD)
             own_v = s[4 * t : 4 * t + 4, OV0:X0, :].reshape(128, HD)
             row_k = 8 * (lane // 32) + 4 * half + (lane % 32) // 8
-            sc = lax.dot_general(q, own_k, NT, preferred_element_type=F32) * scale
+            sc = lax.dot_general(q, own_k, NT, preferred_element_type=F32)
             good = (row_k == row_q) & (sc == sc)
             scores.append(jnp.where(good, sc, -jnp.inf))
             vals.append(own_v)
         peak = jnp.max(scores[0], axis=1, keepdims=True)
         for sc in scores[1:]:
             peak = jnp.maximum(peak, jnp.max(sc, axis=1, keepdims=True))
+        peak = peak * scale
         high = peak.astype(BF).astype(F32)
         low = (peak - high).astype(BF).astype(F32)
         shift = high + low
         mass = jnp.zeros((128, 1), F32)
         acc = jnp.zeros((128, HD), F32)
         for sc, v in zip(scores, vals):
-            w = jnp.exp(sc - shift)
+            w = jnp.exp2(sc * scale - shift)
             mass = mass + jnp.sum(w, axis=1, keepdims=True)
             acc = acc + jnp.dot(w.astype(BF), v, preferred_element_type=F32)
         mass_high = mass.astype(BF).astype(F32)
@@ -209,13 +221,13 @@
     new_k = (to_every_head(total, 32) * scale[...]).astype(BF).astype(F32)
     new_k = rotate(new_k, cosine[...], sine[...]).astype(BF).astype(F32)
     new_v = (to_every_head(total, 64) * scale[...]).astype(BF).astype(F32)
-    new = jnp.sum(q_own[...].astype(F32) * new_k, axis=1, keepdims=True) * HD ** (-0.5)
+    new = jnp.sum(q_own[...].astype(F32) * new_k, axis=1, keepdims=True) * (HD ** (-0.5) * LOG2E)
     acc = parts[:, 0:16, :].astype(F32)
     peak = stats[:, :, 0:1] + stats[:, :, 1:2]
     mass = stats[:, :, 2:3] + stats[:, :, 3:4]
     top = jnp.maximum(jnp.max(peak, axis=0), new)
-    shrink = jnp.exp(peak - top[None])
-    new_w = jnp.exp(new - top)
+    shrink = jnp.exp2(peak - top[None])
+    new_w = jnp.exp2(new - top)
     whole = jnp.sum(mass * shrink, axis=0) + new_w
     summed = jnp.sum(acc * shrink, axis=0) + new_w * new_v
     attended = (summed / whole).astype(BF)
@@ -223,7 +235,8 @@
         out[i, :, :] = attended
 
 
-def output_body(att, w, out):
+def output_body(att, w, hidden, out, kept):
+    kept[...] = hidden[...].astype(F32)
     tiles = att[...].astype(F32).reshape(16, 2, 2, 8, HD)
     low = iota((16, 8, HD), 1) < 4
     total = jnp.zeros(out.shape, F32)
@@ -267,17 +280,18 @@
     packed = pl.pallas_call(
         pack_body,
         out_shape=sds((16, END, HD), BF),
-        in_specs=[SM, SM, VM] + [pl.BlockSpec(memory_space=pltpu.HBM)] * 4,
-        out_specs=VM,
+        in_specs=[SM, VM] + [pl.BlockSpec(memory_space=pltpu.HBM)] * 4,
+        out_specs=pl.BlockSpec(memory_space=pltpu.HBM),
         scratch_shapes=[
             pltpu.VMEM((128, 1024), BF),
             pltpu.VMEM((128, 1024), BF),
             pltpu.VMEM((64, 1024), BF),
             pltpu.VMEM((64, 1024), BF),
-            pltpu.SemaphoreType.DMA((4,)),
+            pltpu.VMEM((16, END, HD), BF),
+            pltpu.SemaphoreType.DMA((8,)),
         ],
         name="pack",
-    )(who, lengths, hidden_in, prefix_keys, prefix_values, own_keys.reshape(64, 1024), own_values.reshape(64, 1024))
+    )(lengths, hidden_in, prefix_keys, prefix_values, own_keys.reshape(64, 1024), own_values.reshape(64, 1024))
     mine = lax.all_to_all(packed, "rows", 0, 0, tiled=True)
     gain = norm_gain.reshape(1, 256)
     x_spec = pl.BlockSpec((16, END - X0, HD), lambda i: (0, X0 // 16, 0))
@@ -285,9 +299,9 @@
     parts = pl.pallas_call(
         project_body,
         grid=(1,),
-        out_shape=sds((32, 32, HD), BF),
+        out_shape=sds((32, 24, HD), BF),
         in_specs=[x_spec, gain_spec, pl.BlockSpec((256, 512), lambda i: (0, 0))],
-        out_specs=pl.BlockSpec((32, 32, HD), lambda i: (0, 0, 0)),
+        out_specs=pl.BlockSpec((32, 24, HD), lambda i: (0, 0, 0)),
         compiler_params=params(),
         name="project",
     )(mine, gain, w_query)
@@ -303,15 +317,17 @@
         in_specs=[SM, x_spec, gain_spec] + [pl.BlockSpec((256, HD), lambda i: (0, 0))] * 2,
         out_specs=pl.BlockSpec((32, 16, HD), lambda i: (0, 0, 0)),
         compiler_params=params(),
+        cost_estimate=pl.CostEstimate(flops=10**9, bytes_accessed=1 << 18, transcendentals=0),
         name="keyval",
     )(who, mine, gain, first_w, second_w)
+    cosine, kv_part = lax.optimization_barrier((cosine, kv_part))
     query, q_own, row_scale = pl.pallas_call(
         query_body,
         out_shape=(sds((32, 16, HD), BF), sds((16, HD), BF), sds((16, HD), F32)),
         in_specs=[SM, VM, VM, VM],
         out_specs=(VM, VM, VM),
         compiler_params=params(),
-        cost_estimate=pl.CostEstimate(flops=2 * 10**9, bytes_accessed=1 << 20, transcendentals=0),
+        cost_estimate=pl.CostEstimate(flops=2 * 10**10, bytes_accessed=1 << 20, transcendentals=0),
         name="query",
     )(who, parts, cosine, sine)
     query = lax.all_to_all(query, "blk", 0, 0, tiled=True)
@@ -333,16 +349,16 @@
         name="combine",
     )(partial, q_own, row_scale, cosine, sine)
     attended = lax.all_to_all(attended, "blk", 0, 0, tiled=True)
-    mixed = pl.pallas_call(
+    mixed, kept = pl.pallas_call(
         output_body,
-        out_shape=sds((128, 256), BF),
-        in_specs=[VM, VM],
-        out_specs=VM,
+        out_shape=(sds((128, 256), BF), sds((8, 256), F32)),
+        in_specs=[VM] * 3,
+        out_specs=(VM, VM),
         compiler_params=params(),
         name="output",
-    )(attended, w_out)
+    )(attended, w_out, hidden_in)
     mixed = lax.all_to_all(mixed.reshape(16, 8, 256), "rows", 0, 0, tiled=True)
-    return (hidden_in.astype(F32) + jnp.sum(mixed.astype(F32), axis=0)).astype(BF)
+    return (kept + jnp.sum(mixed.astype(F32), axis=0)).astype(BF)
 
 
 def solution(mesh):

time: 130 us -> 129 us (level)
  blocking collectives: 44.2 us -> 62.1 us
  waiting for transfers between devices: 35.1 us -> 22.1 us
  starting transfers between devices: 36.8 us -> 32.5 us
    all_to_all x0 -> x1, blocking collectives: none -> 15.2 us  [on_device(): query = lax.all_to_all(query, 'blk', 0, 0, tiled=True)]
    all_to_all x1 -> x0, waiting for transfers between devices: 9.83 us -> none  [on_device(): query = lax.all_to_all(query, 'blk', 0, 0, tiled=True)]
    all_to_all x1 -> x0, starting transfers between devices: 4.32 us -> none  [on_device(): query = lax.all_to_all(query, 'blk', 0, 0, tiled=True)]
    all_to_all x1, waiting for transfers between devices: 8.88 us -> 5.78 us  [on_device(): parts = lax.all_to_all(parts, 'blk', 0, 0, tiled=True)]
    all_to_all x1, blocking collectives: 17.3 us -> 20 us  [on_device(): partial = lax.all_to_all(partial, 'blk', 0, 0, tiled=True)]
  transfers between devices with their start and end apart: 6 -> 5, of which waited for: 3 -> 2; matrix products, arithmetic and copies ran while one was open for 0% -> 0% of each run, Pallas kernels for 2% -> 2%
where the time goes in v6:
time: 129 us; the launch traced here: 128 us
  blocking collectives  62.1 us (48%)
  starting transfers between devices  32.5 us (25%)
  waiting for transfers between devices  22.1 us (17%)
  Pallas kernels  9.05 us (7%)
  local copies, waits for them, and re-layouts  1.35 us (1%)
    all_to_all x1, blocking collectives, on_device(): partial = lax.all_to_all(partial, 'blk', 0, 0, tiled=True)  20 us
    all_to_all x1, waiting for transfers between devices, on_device(): mine = lax.all_to_all(packed, 'rows', 0, 0, tiled=True)  16.3 us
    all_to_all x1, blocking collectives, on_device(): query = lax.all_to_all(query, 'blk', 0, 0, tiled=True)  15.2 us
    all_to_all x1, starting transfers between devices, on_device(): parts = lax.all_to_all(parts, 'blk', 0, 0, tiled=True)  14.8 us
    all_to_all x1, blocking collectives, on_device(): attended = lax.all_to_all(attended, 'blk', 0, 0, tiled=True)  14.3 us
    all_to_all x1, blocking collectives, on_device(): mixed = lax.all_to_all(mixed.reshape(16, 8, 256), 'rows', 0, 0, tiled=True)  12.6 us
    all_to_all x1, starting transfers between devices, on_device(): mine = lax.all_to_all(packed, 'rows', 0, 0, tiled=True)  9.71 us
    all_to_all x1, waiting for transfers between devices, on_device(): parts = lax.all_to_all(parts, 'blk', 0, 0, tiled=True)  5.78 us
  transfers between devices with their start and end apart: 5, of which 2 were waited for; matrix products, arithmetic and copies ran while one was open for 0% of the time, Pallas kernels for 2%

profile of v6, /device:TPU:1, one launch (start us, length us, event | category | flops | bytes accessed | tf_op | source)
XLA Modules:
  0.0 128.1 jit_solution(3071657206332052117)
XLA Ops:
  0.0 2.7 %pack.1 = bf16[16,208,128]{2,1,0:T(8,128)(2,1)} custom-call(s32[8]{0:T(128)} %lens.1, bf16[8,256]{1,0:T(8,128)(2,1)} %hidden.3, bf16[128,1024]{1,0:T(8,128)(2,1)} %keys_hbm.1, bf16[128,1024]{1,0:T(8,128)(2,1)} %values_hbm.1, bf16[64,1024]{1,0:T(8,128)(2,1)} %bitcast.6, bf16[64,1024]{1,0:T(8,128)(2,1)} %bitcast.7), custom_call_target="tpu_custom_call" | custom-call | tf_op jit(solution)/shard_map/pack/pallas_call | solution.py:280
  2.7 0.0 copy-start.5
  2.7 0.0 copy-start.1
  2.7 9.7 %all-to-all-start = ((bf16[16,208,128]{2,1,0:T(8,128)(2,1)}), bf16[16,208,128]{2,1,0:T(8,128)(2,1)S(1)}, u32[]{:S(2)}, u32[]{:S(2)}) async-start(bf16[16,208,128]{2,1,0:T(8,128)(2,1)} %pack.1), calls=%async_computation | async-start | bytes 1703936 | tf_op jit(solution)/shard_map/all_to_all | solution.py:295
  12.4 3.3 %collective-permute-start.1 = (bf16[256,128]{1,0:T(8,128)(2,1)S(1)}, bf16[256,128]{1,0:T(8,128)(2,1)S(1)}, u32[]{:S(2)}, u32[]{:S(2)}) collective-permute-start(bf16[256,128]{1,0:T(8,128)(2,1)S(1)} %copy-done.5), channel_id=1, source_target_pairs={{0,1},{1,3},{2,5},{3,7},{4,9},{5,11},{6,13},{7,15},{8,0},{9,2},{10... | collective-permute-start | bytes 196616 | tf_op jit(solution)/shard_map/ppermute | solution.py:279
  15.7 0.7 collective-permute-start
  16.4 0.0 copy-start.6
  16.4 0.6 copy-done.6
  17.1 0.1 pad_add_fusion.who
  17.1 16.3 %all-to-all-done.x_ref.mine = bf16[16,208,128]{2,1,0:T(8,128)(2,1)S(1)} async-done(((bf16[16,208,128]{2,1,0:T(8,128)(2,1)}), bf16[16,208,128]{2,1,0:T(8,128)(2,1)S(1)}, u32[]{:S(2)}, u32[]{:S(2)}) %all-to-all-start) | async-done | bytes 852000 | tf_op jit(solution)/shard_map/all_to_all | solution.py:295
  33.4 1.0 project.1
  34.4 14.8 %all-to-all-start.1 = ((bf16[32,24,128]{2,1,0:T(8,128)(2,1)}), bf16[32,24,128]{2,1,0:T(8,128)(2,1)S(1)}, u32[]{:S(2)}, u32[]{:S(2)}) async-start(bf16[32,24,128]{2,1,0:T(8,128)(2,1)} %project.1), calls=%async_computation.1 | async-start | bytes 393216 | tf_op jit(solution)/shard_map/all_to_all | solution.py:309
  49.3 0.1 dynamic_slice.3
  49.3 0.1 add_convert_fusion.1
  49.4 0.6 copy-done.3
  50.0 0.0 copy-done.4
  50.0 0.1 fusion
  50.1 0.0 collective-permute-done.wa
  50.2 4.0 %collective-permute-start.2 = (bf16[16,208,128]{2,1,0:T(8,128)(2,1)S(1)}, bf16[16,208,128]{2,1,0:T(8,128)(2,1)S(1)}, u32[]{:S(2)}, u32[]{:S(2)}) collective-permute-start(bf16[16,208,128]{2,1,0:T(8,128)(2,1)S(1)} %all-to-all-done.x_ref.mine), channel_id=1, source_target_pairs={{0,1},{1,0},{2,3},{3,2},{4,5},{5,4},{6,7},{7,6},{8,9},{9,8},{10,11... | collective-permute-start | bytes 2555912 | tf_op jit(solution)/shard_map/ppermute | solution.py:312
  54.2 0.8 keyval.1.kv_part
  55.0 5.8 %all-to-all-done.1.parts = bf16[32,24,128]{2,1,0:T(8,128)(2,1)S(1)} async-done(((bf16[32,24,128]{2,1,0:T(8,128)(2,1)}), bf16[32,24,128]{2,1,0:T(8,128)(2,1)S(1)}, u32[]{:S(2)}, u32[]{:S(2)}) %all-to-all-start.1) | async-done | bytes 196640 | tf_op jit(solution)/shard_map/all_to_all | solution.py:309
  60.8 0.7 query.1
  61.6 15.2 %all_to_all.30.q_ref = bf16[32,16,128]{2,1,0:T(8,128)(2,1)S(1)} all-to-all(bf16[32,16,128]{2,1,0:T(8,128)(2,1)S(1)} %get-tuple-element.25), channel_id=1, replica_groups=mesh['blk'=32,'rows'=16] {'blk'}, dimensions={0} | all-to-all | bytes 262144 | tf_op jit(solution)/shard_map/all_to_all | solution.py:333
  76.8 0.0 collective-permute-done.2.other
  76.8 3.1 %attend.1 = bf16[32,32,128]{2,1,0:T(8,128)(2,1)S(1)} custom-call(s32[2]{0:T(128)S(1)} %pad_add_fusion.who, bf16[16,208,128]{2,1,0:T(8,128)(2,1)S(1)} %all-to-all-done.x_ref.mine, bf16[16,208,128]{2,1,0:T(8,128)(2,1)S(1)} %collective-permute-done.2.other, bf16[32,16,128]{2,1,0:T(8,128)(2,1)S(1)} %all_to_all.30.q_ref, bf16[32,16,128]{2,1,0:T(8,128)(2,1)S(1)} %keyval.1.kv_part), custom_call_target="tpu_custom_call" | custom-call | tf_op jit(solution)/shard_map/attend/pallas_call | solution.py:334
  79.9 20.0 %all_to_all.31.parts = bf16[32,32,128]{2,1,0:T(8,128)(2,1)S(1)} all-to-all(bf16[32,32,128]{2,1,0:T(8,128)(2,1)S(1)} %attend.1), channel_id=1, replica_groups=mesh['blk'=32,'rows'=16] {'blk'}, dimensions={0} | all-to-all | bytes 524288 | tf_op jit(solution)/shard_map/all_to_all | solution.py:342
  99.9 0.5 combine.1
  100.4 0.0 copy-start.2
  100.4 14.3 %all_to_all.32.att = bf16[32,16,128]{2,1,0:T(8,128)(2,1)S(1)} all-to-all(bf16[32,16,128]{2,1,0:T(8,128)(2,1)S(1)} %combine.1), channel_id=1, replica_groups=mesh['blk'=32,'rows'=16] {'blk'}, dimensions={0} | all-to-all | bytes 262144 | tf_op jit(solution)/shard_map/all_to_all | solution.py:351
  114.7 0.2 output.1
  115.0 12.6 %all_to_all.33 = bf16[16,8,256]{2,1,0:T(8,128)(2,1)S(1)} all-to-all(bf16[16,8,256]{2,1,0:T(8,128)(2,1)S(1)} %bitcast.5), channel_id=1, replica_groups=mesh['blk'=32,'rows'=16] {'rows'}, dimensions={0} | all-to-all | bytes 131072 | tf_op jit(solution)/shard_map/all_to_all | solution.py:360
  127.5 0.6 add_convert_fusion
  (12 shorter events, 0.0 us)
Async XLA Ops:
  2.7 9.7 %copy-start.5 = (bf16[256,128]{1,0:T(8,128)(2,1)S(1)}, bf16[256,128]{1,0:T(8,128)(2,1)}, u32[]{:S(2)}) copy-start(bf16[256,128]{1,0:T(8,128)(2,1)} %param.16) | copy-start | bytes 196612
  2.7 30.7 %copy-start.1 = (bf16[256,512]{1,0:T(8,128)(2,1)S(1)}, bf16[256,512]{1,0:T(8,128)(2,1)}, u32[]{:S(2)}) copy-start(bf16[256,512]{1,0:T(8,128)(2,1)} %wq.1) | copy-start | bytes 786436
  2.7 30.7 %all-to-all-start = ((bf16[16,208,128]{2,1,0:T(8,128)(2,1)}), bf16[16,208,128]{2,1,0:T(8,128)(2,1)S(1)}, u32[]{:S(2)}, u32[]{:S(2)}) async-start(bf16[16,208,128]{2,1,0:T(8,128)(2,1)} %pack.1), calls=%async_computation | async-start | bytes 1703936 | tf_op jit(solution)/shard_map/all_to_all | solution.py:295
  12.4 37.7 %collective-permute-start.1 = (bf16[256,128]{1,0:T(8,128)(2,1)S(1)}, bf16[256,128]{1,0:T(8,128)(2,1)S(1)}, u32[]{:S(2)}, u32[]{:S(2)}) collective-permute-start(bf16[256,128]{1,0:T(8,128)(2,1)S(1)} %copy-done.5), channel_id=1, source_target_pairs={{0,1},{1,3},{2,5},{3,7},{4,9},{5,11},{6,13},{7,15},{8,0},{9,2},{10... | collective-permute-start | bytes 196616 | tf_op jit(solution)/shard_map/ppermute | solution.py:279
  15.7 34.4 %collective-permute-start = (bf16[256,128]{1,0:T(8,128)(2,1)S(1)}, bf16[256,128]{1,0:T(8,128)(2,1)S(1)}, u32[]{:S(2)}, u32[]{:S(2)}) collective-permute-start(bf16[256,128]{1,0:T(8,128)(2,1)S(1)} %copy-done.5), channel_id=1, source_target_pairs={{0,0},{1,2},{2,4},{3,6},{4,8},{5,10},{6,12},{7,14},{8,1},{9,3},{10... | collective-permute-start | bytes 196616 | tf_op jit(solution)/shard_map/ppermute | solution.py:278
  16.4 0.7 copy-start.6
  34.4 14.8 %copy-start.7 = (s32[128]{0:T(128)S(1)}, s32[128]{0:T(128)}, u32[]{:S(2)}) copy-start(s32[128]{0:T(128)} %param.22) | copy-start | bytes 1540
  34.4 26.4 %all-to-all-start.1 = ((bf16[32,24,128]{2,1,0:T(8,128)(2,1)}), bf16[32,24,128]{2,1,0:T(8,128)(2,1)S(1)}, u32[]{:S(2)}, u32[]{:S(2)}) async-start(bf16[32,24,128]{2,1,0:T(8,128)(2,1)} %project.1), calls=%async_computation.1 | async-start | bytes 393216 | tf_op jit(solution)/shard_map/all_to_all | solution.py:309
  49.3 0.7 copy-start.3
  49.3 0.7 copy-start.4
  50.2 26.6 %collective-permute-start.2 = (bf16[16,208,128]{2,1,0:T(8,128)(2,1)S(1)}, bf16[16,208,128]{2,1,0:T(8,128)(2,1)S(1)}, u32[]{:S(2)}, u32[]{:S(2)}) collective-permute-start(bf16[16,208,128]{2,1,0:T(8,128)(2,1)S(1)} %all-to-all-done.x_ref.mine), channel_id=1, source_target_pairs={{0,1},{1,0},{2,3},{3,2},{4,5},{5,4},{6,7},{7,6},{8,9},{9,8},{10,11... | collective-permute-start | bytes 2555912 | tf_op jit(solution)/shard_map/ppermute | solution.py:312
  99.9 14.9 %copy-start = (bf16[512,256]{1,0:T(8,128)(2,1)S(1)}, bf16[512,256]{1,0:T(8,128)(2,1)}, u32[]{:S(2)}) copy-start(bf16[512,256]{1,0:T(8,128)(2,1)} %w.1) | copy-start | bytes 786436
  100.4 14.4 %copy-start.2 = (bf16[8,256]{1,0:T(8,128)(2,1)S(1)}, bf16[8,256]{1,0:T(8,128)(2,1)}, u32[]{:S(2)}) copy-start(bf16[8,256]{1,0:T(8,128)(2,1)} %hidden.3) | copy-start | bytes 12292

commit v7 on v6

--- a/solution.py
+++ b/solution.py
@@ -24,22 +24,20 @@
     return lax.broadcasted_iota(jnp.int32, shape, dim)
 
 
-def pack_body(lens, hidden, keys_hbm, values_hbm, own_k_hbm, own_v_hbm, out, keys, values, own_k, own_v, packed, sems):
+def pack_body(lens, hidden_hbm, keys_hbm, values_hbm, own_k_hbm, own_v_hbm, out, keys, values, own_k, own_v, packed, rows_x, sems):
     inward = [
         pltpu.make_async_copy(src, dst, sems.at[i])
         for i, (src, dst) in enumerate(
-            ((own_k_hbm, own_k), (keys_hbm, keys), (values_hbm, values), (own_v_hbm, own_v))
+            ((own_k_hbm, own_k), (keys_hbm, keys), (values_hbm, values), (own_v_hbm, own_v), (hidden_hbm, rows_x))
         )
     ]
     for copy in inward:
         copy.start()
     outward = [
-        pltpu.make_async_copy(packed.at[:, first:last, :], out.at[:, first:last, :], sems.at[4 + i])
+        pltpu.make_async_copy(packed.at[:, first:last, :], out.at[:, first:last, :], sems.at[5 + i])
         for i, (first, last) in enumerate(((OK0, OV0), (K0, V0), (V0, OK0), (OV0, END)))
     ]
     b = lax.axis_index("blk")
-    x = hidden[...].astype(F32)
-    x_tile = jnp.concatenate([x[:, :HD], x[:, HD:]], axis=0).astype(BF)
     sub = iota((32, HD), 0)
     slot = 8 * b + sub % 8
     dead = []
@@ -50,6 +48,10 @@
         dead.append(slot >= live)
     for step in range(4):
         inward[step].wait()
+        if step == 3:
+            inward[4].wait()
+            x = rows_x[...].astype(F32)
+            x_tile = jnp.concatenate([x[:, :HD], x[:, HD:]], axis=0).astype(BF)
         for p in range(2):
             for h in range(8):
                 col = slice(h * HD, (h + 1) * HD)
@@ -159,48 +161,61 @@
     scale = HD ** (-0.5) * LOG2E
     sources = (mine, other)
     halves = (lax.rem(r, 2), 1 - lax.rem(r, 2))
-    keys = [s[:, K0:V0, :].reshape(1024, HD) for s in sources]
-    values = [s[:, V0:OK0, :].reshape(1024, HD) for s in sources]
-    row_q = iota((128, HD), 0)
+    rows = 256
+    row_q, lane = iota((128, HD), 0), iota((128, HD), 1)
     row_q = 4 * (row_q // 16) + row_q % 4
-    lane = iota((128, HD), 1)
-    lane_s = iota((128, HD), 1)
-    for t in range(4):
-        q = q_ref[8 * t : 8 * t + 8].reshape(128, HD)
+    lane_s = iota((rows, HD), 1)
+    for t in range(512 // rows):
+        part = slice(rows // 16 * t, rows // 16 * (t + 1))
+        q = q_ref[part].reshape(rows, HD)
         scores, vals = [], []
-        for k, v in zip(keys, values):
+        for s in sources:
+            k = s[:, K0:V0, :].reshape(1024, HD)
             scores.append(lax.dot_general(q, k, NT, preferred_element_type=F32))
-            vals.append(v)
+            vals.append(s[:, V0:OK0, :].reshape(1024, HD))
+        own_scores, own_vals = [], []
         for s, half in zip(sources, halves):
-            own_k = s[4 * t : 4 * t + 4, OK0:OV0, :].reshape(128, HD)
-            own_v = s[4 * t : 4 * t + 4, OV0:X0, :].reshape(128, HD)
             row_k = 8 * (lane // 32) + 4 * half + (lane % 32) // 8
-            sc = lax.dot_general(q, own_k, NT, preferred_element_type=F32)
-            good = (row_k == row_q) & (sc == sc)
-            scores.append(jnp.where(good, sc, -jnp.inf))
-            vals.append(own_v)
+            blocks, block_vals = [], []
+            for u in range(rows // 128):
+                first = 4 * (t * (rows // 128) + u)
+                k = s[first : first + 4, OK0:OV0, :].reshape(128, HD)
+                block_vals.append(s[first : first + 4, OV0:X0, :].reshape(128, HD))
+                sc = lax.dot_general(q[128 * u : 128 * u + 128], k, NT, preferred_element_type=F32)
+                blocks.append(jnp.where((row_k == row_q) & (sc == sc), sc, -jnp.inf))
+            own_scores.append(jnp.concatenate(blocks, axis=0))
+            own_vals.append(block_vals)
         peak = jnp.max(scores[0], axis=1, keepdims=True)
-        for sc in scores[1:]:
+        for sc in scores[1:] + own_scores:
             peak = jnp.maximum(peak, jnp.max(sc, axis=1, keepdims=True))
         peak = peak * scale
         high = peak.astype(BF).astype(F32)
         low = (peak - high).astype(BF).astype(F32)
         shift = high + low
-        mass = jnp.zeros((128, 1), F32)
-        acc = jnp.zeros((128, HD), F32)
+        mass = jnp.zeros((rows, 1), F32)
+        acc = jnp.zeros((rows, HD), F32)
         for sc, v in zip(scores, vals):
             w = jnp.exp2(sc * scale - shift)
             mass = mass + jnp.sum(w, axis=1, keepdims=True)
             acc = acc + jnp.dot(w.astype(BF), v, preferred_element_type=F32)
+        for sc, block_vals in zip(own_scores, own_vals):
+            w = jnp.exp2(sc * scale - shift)
+            mass = mass + jnp.sum(w, axis=1, keepdims=True)
+            w = w.astype(BF)
+            acc = acc + jnp.concatenate(
+                [
+                    jnp.dot(w[128 * u : 128 * u + 128], v, preferred_element_type=F32)
+                    for u, v in enumerate(block_vals)
+                ],
+                axis=0,
+            )
         mass_high = mass.astype(BF).astype(F32)
         stats = jnp.where(
-            lane_s == 0, high,
-            jnp.where(lane_s == 1, low, jnp.where(lane_s == 2, mass_high, jnp.where(lane_s == 3, mass - mass_high, 0.0))),
+            lane_s == 0, high, jnp.where(lane_s == 1, low, jnp.where(lane_s == 2, mass_high, mass - mass_high))
         )
-        out[8 * t : 8 * t + 8, 0:16, :] = acc.astype(BF).reshape(8, 16, HD)
-        rest = kv_part[8 * t : 8 * t + 8].reshape(128, HD).astype(F32)
-        stats = jnp.where(lane_s < 32, stats, rest)
-        out[8 * t : 8 * t + 8, 16:32, :] = stats.astype(BF).reshape(8, 16, HD)
+        stats = jnp.where(lane_s < 32, stats, kv_part[part].reshape(rows, HD).astype(F32))
+        out[part, 0:16, :] = acc.astype(BF).reshape(rows // 16, 16, HD)
+        out[part, 16:32, :] = stats.astype(BF).reshape(rows // 16, 16, HD)
 
 
 def to_every_head(total, start):
@@ -280,7 +295,7 @@
     packed = pl.pallas_call(
         pack_body,
         out_shape=sds((16, END, HD), BF),
-        in_specs=[SM, VM] + [pl.BlockSpec(memory_space=pltpu.HBM)] * 4,
+        in_specs=[SM] + [pl.BlockSpec(memory_space=pltpu.HBM)] * 5,
         out_specs=pl.BlockSpec(memory_space=pltpu.HBM),
         scratch_shapes=[
             pltpu.VMEM((128, 1024), BF),
@@ -288,7 +303,8 @@
             pltpu.VMEM((64, 1024), BF),
             pltpu.VMEM((64, 1024), BF),
             pltpu.VMEM((16, END, HD), BF),
-            pltpu.SemaphoreType.DMA((8,)),
+            pltpu.VMEM((8, 256), BF),
+            pltpu.SemaphoreType.DMA((9,)),
         ],
         name="pack",
     )(lengths, hidden_in, prefix_keys, prefix_values, own_keys.reshape(64, 1024), own_values.reshape(64, 1024))
@@ -305,11 +321,11 @@
         compiler_params=params(),
         name="project",
     )(mine, gain, w_query)
-    positions, parts = lax.optimization_barrier((positions, parts))
+    positions, parts, mine = lax.optimization_barrier((positions, parts, mine))
     parts = lax.all_to_all(parts, "blk", 0, 0, tiled=True)
     cosine, sine = rotary_tables(jnp.concatenate([lax.dynamic_slice_in_dim(positions, 4 * b, 4, 0)] * 4))
-    mine, cosine, first_w, second_w = lax.optimization_barrier((mine, cosine, first_w, second_w))
-    other = lax.ppermute(mine, "rows", [(i, i ^ 1) for i in range(16)])
+    half, first_w, second_w = lax.optimization_barrier((mine[:, :X0, :], first_w, second_w))
+    other = lax.ppermute(half, "rows", [(i, i ^ 1) for i in range(16)])
     kv_part = pl.pallas_call(
         keyval_body,
         grid=(1,),
@@ -327,7 +343,7 @@
         in_specs=[SM, VM, VM, VM],
         out_specs=(VM, VM, VM),
         compiler_params=params(),
-        cost_estimate=pl.CostEstimate(flops=2 * 10**10, bytes_accessed=1 << 20, transcendentals=0),
+        cost_estimate=pl.CostEstimate(flops=4*10**9, bytes_accessed=1 << 20, transcendentals=0),
         name="query",
     )(who, parts, cosine, sine)
     query = lax.all_to_all(query, "blk", 0, 0, tiled=True)

time: 129 us -> 126 us (0.977)
  blocking collectives: 62.1 us -> 59.9 us
    all_to_all x1, blocking collectives: 20 us -> 17.8 us  [on_device(): partial = lax.all_to_all(partial, 'blk', 0, 0, tiled=True)]
where the time goes in v7:
time: 126 us
  blocking collectives  59.9 us (48%)
  starting transfers between devices  32.4 us (26%)
  waiting for transfers between devices  22 us (17%)
  Pallas kernels  8.76 us (7%)
  local copies, waits for them, and re-layouts  1.43 us (1%)
    all_to_all x1, blocking collectives, on_device(): partial = lax.all_to_all(partial, 'blk', 0, 0, tiled=True)  17.8 us
    all_to_all x1, waiting for transfers between devices, on_device(): mine = lax.all_to_all(packed, 'rows', 0, 0, tiled=True)  16.3 us
    all_to_all x1, blocking collectives, on_device(): query = lax.all_to_all(query, 'blk', 0, 0, tiled=True)  15.2 us
    all_to_all x1, starting transfers between devices, on_device(): parts = lax.all_to_all(parts, 'blk', 0, 0, tiled=True)  14.7 us
    all_to_all x1, blocking collectives, on_device(): attended = lax.all_to_all(attended, 'blk', 0, 0, tiled=True)  14.3 us
    all_to_all x1, blocking collectives, on_device(): mixed = lax.all_to_all(mixed.reshape(16, 8, 256), 'rows', 0, 0, tiled=True)  12.6 us
    all_to_all x1, starting transfers between devices, on_device(): mine = lax.all_to_all(packed, 'rows', 0, 0, tiled=True)  9.71 us
    all_to_all x1, waiting for transfers between devices, on_device(): parts = lax.all_to_all(parts, 'blk', 0, 0, tiled=True)  5.69 us
  transfers between devices with their start and end apart: 5, of which 2 were waited for; matrix products, arithmetic and copies ran while one was open for 0% of the time, Pallas kernels for 2%

profile of v7, /device:TPU:1, one launch (start us, length us, event | category | flops | bytes accessed | tf_op | source)
XLA Modules:
  0.0 125.5 jit_solution(4517215389058266590)
XLA Ops:
  0.0 2.7 %pack.1 = bf16[16,208,128]{2,1,0:T(8,128)(2,1)} custom-call(s32[8]{0:T(128)} %lens.1, bf16[8,256]{1,0:T(8,128)(2,1)} %hidden.1, bf16[128,1024]{1,0:T(8,128)(2,1)} %keys_hbm.1, bf16[128,1024]{1,0:T(8,128)(2,1)} %values_hbm.1, bf16[64,1024]{1,0:T(8,128)(2,1)} %bitcast.6, bf16[64,1024]{1,0:T(8,128)(2,1)} %bitcast.7), custom_call_target="tpu_custom_call" | custom-call | tf_op jit(solution)/shard_map/pack/pallas_call | solution.py:295
  2.7 0.0 copy-start.5
  2.7 0.0 copy-start.1
  2.7 9.7 %all-to-all-start = ((bf16[16,208,128]{2,1,0:T(8,128)(2,1)}), bf16[16,208,128]{2,1,0:T(8,128)(2,1)S(1)}, u32[]{:S(2)}, u32[]{:S(2)}) async-start(bf16[16,208,128]{2,1,0:T(8,128)(2,1)} %pack.1), calls=%async_computation | async-start | bytes 1703936 | tf_op jit(solution)/shard_map/all_to_all | solution.py:311
  12.4 3.3 %collective-permute-start.1 = (bf16[256,128]{1,0:T(8,128)(2,1)S(1)}, bf16[256,128]{1,0:T(8,128)(2,1)S(1)}, u32[]{:S(2)}, u32[]{:S(2)}) collective-permute-start(bf16[256,128]{1,0:T(8,128)(2,1)S(1)} %copy-done.5), channel_id=1, source_target_pairs={{0,1},{1,3},{2,5},{3,7},{4,9},{5,11},{6,13},{7,15},{8,0},{9,2},{10... | collective-permute-start | bytes 196616 | tf_op jit(solution)/shard_map/ppermute | solution.py:294
  15.7 0.7 collective-permute-start
  16.4 0.0 copy-start.6
  16.4 0.6 copy-done.6
  17.0 0.1 pad_add_fusion.who
  17.1 16.3 %all-to-all-done.x_ref.mine = bf16[16,208,128]{2,1,0:T(8,128)(2,1)S(1)} async-done(((bf16[16,208,128]{2,1,0:T(8,128)(2,1)}), bf16[16,208,128]{2,1,0:T(8,128)(2,1)S(1)}, u32[]{:S(2)}, u32[]{:S(2)}) %all-to-all-start) | async-done | bytes 852000 | tf_op jit(solution)/shard_map/all_to_all | solution.py:311
  33.4 1.0 project.1
  34.4 14.7 %all-to-all-start.1 = ((bf16[32,24,128]{2,1,0:T(8,128)(2,1)}), bf16[32,24,128]{2,1,0:T(8,128)(2,1)S(1)}, u32[]{:S(2)}, u32[]{:S(2)}) async-start(bf16[32,24,128]{2,1,0:T(8,128)(2,1)} %project.1), calls=%async_computation.1 | async-start | bytes 393216 | tf_op jit(solution)/shard_map/all_to_all | solution.py:325
  49.1 0.0 copy-start.7
  49.1 0.1 slice.3
  49.2 4.0 %collective-permute-start.2 = (bf16[16,192,128]{2,1,0:T(8,128)(2,1)S(1)}, bf16[16,192,128]{2,1,0:T(8,128)(2,1)S(1)}, u32[]{:S(2)}, u32[]{:S(2)}) collective-permute-start(bf16[16,192,128]{2,1,0:T(8,128)(2,1)S(1)} %slice.3), channel_id=1, source_target_pairs={{0,1},{1,0},{2,3},{3,2},{4,5},{5,4},{6,7},{7,6},{8,9},{9,8},{10,11... | collective-permute-start | bytes 2359304 | tf_op jit(solution)/shard_map/ppermute | solution.py:328
  53.3 0.1 dynamic_slice.3
  53.3 0.1 add_convert_fusion.1
  53.4 0.6 copy-done.3
  54.0 0.0 copy-done.4
  54.0 0.1 fusion
  54.1 0.8 keyval.1.kv_part
  55.0 5.7 %all-to-all-done.1.parts = bf16[32,24,128]{2,1,0:T(8,128)(2,1)S(1)} async-done(((bf16[32,24,128]{2,1,0:T(8,128)(2,1)}), bf16[32,24,128]{2,1,0:T(8,128)(2,1)S(1)}, u32[]{:S(2)}, u32[]{:S(2)}) %all-to-all-start.1) | async-done | bytes 196640 | tf_op jit(solution)/shard_map/all_to_all | solution.py:325
  60.6 0.7 query.1
  61.4 15.2 %all_to_all.30.q_ref = bf16[32,16,128]{2,1,0:T(8,128)(2,1)S(1)} all-to-all(bf16[32,16,128]{2,1,0:T(8,128)(2,1)S(1)} %get-tuple-element.25), channel_id=1, replica_groups=mesh['blk'=32,'rows'=16] {'blk'}, dimensions={0} | all-to-all | bytes 262144 | tf_op jit(solution)/shard_map/all_to_all | solution.py:349
  76.6 2.8 %attend.1 = bf16[32,32,128]{2,1,0:T(8,128)(2,1)S(1)} custom-call(s32[2]{0:T(128)S(1)} %pad_add_fusion.who, bf16[16,208,128]{2,1,0:T(8,128)(2,1)S(1)} %all-to-all-done.x_ref.mine, bf16[16,192,128]{2,1,0:T(8,128)(2,1)S(1)} %collective-permute-done.2.other, bf16[32,16,128]{2,1,0:T(8,128)(2,1)S(1)} %all_to_all.30.q_ref, bf16[32,16,128]{2,1,0:T(8,128)(2,1)S(1)} %keyval.1.kv_part), custom_call_target="tpu_custom_call" | custom-call | tf_op jit(solution)/shard_map/attend/pallas_call | solution.py:350
  79.5 17.8 %all_to_all.31.parts = bf16[32,32,128]{2,1,0:T(8,128)(2,1)S(1)} all-to-all(bf16[32,32,128]{2,1,0:T(8,128)(2,1)S(1)} %attend.1), channel_id=1, replica_groups=mesh['blk'=32,'rows'=16] {'blk'}, dimensions={0} | all-to-all | bytes 524288 | tf_op jit(solution)/shard_map/all_to_all | solution.py:358
  97.2 0.5 combine.1
  97.7 0.0 copy-start.2
  97.8 14.3 %all_to_all.32.att = bf16[32,16,128]{2,1,0:T(8,128)(2,1)S(1)} all-to-all(bf16[32,16,128]{2,1,0:T(8,128)(2,1)S(1)} %combine.1), channel_id=1, replica_groups=mesh['blk'=32,'rows'=16] {'blk'}, dimensions={0} | all-to-all | bytes 262144 | tf_op jit(solution)/shard_map/all_to_all | solution.py:367
  112.1 0.2 output.1
  112.3 12.6 %all_to_all.33 = bf16[16,8,256]{2,1,0:T(8,128)(2,1)S(1)} all-to-all(bf16[16,8,256]{2,1,0:T(8,128)(2,1)S(1)} %bitcast.5), channel_id=1, replica_groups=mesh['blk'=32,'rows'=16] {'rows'}, dimensions={0} | all-to-all | bytes 131072 | tf_op jit(solution)/shard_map/all_to_all | solution.py:376
  124.9 0.6 add_convert_fusion
  (13 shorter events, 0.0 us)
Async XLA Ops:
  2.7 9.7 %copy-start.5 = (bf16[256,128]{1,0:T(8,128)(2,1)S(1)}, bf16[256,128]{1,0:T(8,128)(2,1)}, u32[]{:S(2)}) copy-start(bf16[256,128]{1,0:T(8,128)(2,1)} %param.16) | copy-start | bytes 196612
  2.7 30.7 %copy-start.1 = (bf16[256,512]{1,0:T(8,128)(2,1)S(1)}, bf16[256,512]{1,0:T(8,128)(2,1)}, u32[]{:S(2)}) copy-start(bf16[256,512]{1,0:T(8,128)(2,1)} %wq.1) | copy-start | bytes 786436
  2.7 30.7 %all-to-all-start = ((bf16[16,208,128]{2,1,0:T(8,128)(2,1)}), bf16[16,208,128]{2,1,0:T(8,128)(2,1)S(1)}, u32[]{:S(2)}, u32[]{:S(2)}) async-start(bf16[16,208,128]{2,1,0:T(8,128)(2,1)} %pack.1), calls=%async_computation | async-start | bytes 1703936 | tf_op jit(solution)/shard_map/all_to_all | solution.py:311
  12.4 36.8 %collective-permute-start.1 = (bf16[256,128]{1,0:T(8,128)(2,1)S(1)}, bf16[256,128]{1,0:T(8,128)(2,1)S(1)}, u32[]{:S(2)}, u32[]{:S(2)}) collective-permute-start(bf16[256,128]{1,0:T(8,128)(2,1)S(1)} %copy-done.5), channel_id=1, source_target_pairs={{0,1},{1,3},{2,5},{3,7},{4,9},{5,11},{6,13},{7,15},{8,0},{9,2},{10... | collective-permute-start | bytes 196616 | tf_op jit(solution)/shard_map/ppermute | solution.py:294
  15.7 33.5 %collective-permute-start = (bf16[256,128]{1,0:T(8,128)(2,1)S(1)}, bf16[256,128]{1,0:T(8,128)(2,1)S(1)}, u32[]{:S(2)}, u32[]{:S(2)}) collective-permute-start(bf16[256,128]{1,0:T(8,128)(2,1)S(1)} %copy-done.5), channel_id=1, source_target_pairs={{0,0},{1,2},{2,4},{3,6},{4,8},{5,10},{6,12},{7,14},{8,1},{9,3},{10... | collective-permute-start | bytes 196616 | tf_op jit(solution)/shard_map/ppermute | solution.py:293
  16.4 0.7 copy-start.6
  34.4 26.3 %all-to-all-start.1 = ((bf16[32,24,128]{2,1,0:T(8,128)(2,1)}), bf16[32,24,128]{2,1,0:T(8,128)(2,1)S(1)}, u32[]{:S(2)}, u32[]{:S(2)}) async-start(bf16[32,24,128]{2,1,0:T(8,128)(2,1)} %project.1), calls=%async_computation.1 | async-start | bytes 393216 | tf_op jit(solution)/shard_map/all_to_all | solution.py:325
  49.1 4.2 %copy-start.7 = (s32[128]{0:T(128)S(1)}, s32[128]{0:T(128)}, u32[]{:S(2)}) copy-start(s32[128]{0:T(128)} %param.22) | copy-start | bytes 1540
  49.2 27.4 %collective-permute-start.2 = (bf16[16,192,128]{2,1,0:T(8,128)(2,1)S(1)}, bf16[16,192,128]{2,1,0:T(8,128)(2,1)S(1)}, u32[]{:S(2)}, u32[]{:S(2)}) collective-permute-start(bf16[16,192,128]{2,1,0:T(8,128)(2,1)S(1)} %slice.3), channel_id=1, source_target_pairs={{0,1},{1,0},{2,3},{3,2},{4,5},{5,4},{6,7},{7,6},{8,9},{9,8},{10,11... | collective-permute-start | bytes 2359304 | tf_op jit(solution)/shard_map/ppermute | solution.py:328
  53.3 0.7 copy-start.3
  53.3 0.7 copy-start.4
  97.2 14.9 %copy-start = (bf16[512,256]{1,0:T(8,128)(2,1)S(1)}, bf16[512,256]{1,0:T(8,128)(2,1)}, u32[]{:S(2)}) copy-start(bf16[512,256]{1,0:T(8,128)(2,1)} %w.1) | copy-start | bytes 786436
  97.7 14.4 %copy-start.2 = (bf16[8,256]{1,0:T(8,128)(2,1)S(1)}, bf16[8,256]{1,0:T(8,128)(2,1)}, u32[]{:S(2)}) copy-start(bf16[8,256]{1,0:T(8,128)(2,1)} %hidden.1) | copy-start | bytes 12292

commit v8 on v7

--- a/solution.py
+++ b/solution.py
@@ -118,24 +118,13 @@
             out[2 * j + p, :, :] = chunks[j]
 
 
-def keyval_body(who, x_ref, gain, wa, wb, out):
+def keyval_body(who, x_ref, gain, wa, wb, keep, give):
     xg = (gathered_rows(x_ref) * gain[...].astype(F32)).astype(BF)
-    even = lax.rem(who[1], 2) == 0
     first = jnp.dot(xg, wa[...], preferred_element_type=F32)
     second = jnp.dot(xg, wb[...], preferred_element_type=F32)
-    key = jnp.where(even, first, second)
-    value = jnp.where(even, second, first)
-    lane = iota((128, HD), 1)
-    blocks = []
-    for j in range(4):
-        moved_k = pltpu.roll(key, (32 - 32 * j) % HD, 1)
-        moved_v = pltpu.roll(value, (64 - 32 * j) % HD, 1)
-        block = jnp.where(lane < 64, moved_k, moved_v)
-        blocks.append(jnp.where((lane >= 32) & (lane < 96), block, 0.0))
-    for p in range(2):
-        chunks = jnp.concatenate(by_rows_of_four(blocks, p), axis=1).astype(BF)
-        for j in range(16):
-            out[2 * j + p, :, :] = chunks[j]
+    same = lax.rem(who[0], 2) == lax.rem(who[1], 2)
+    keep[...] = jnp.where(same, first, second)
+    give[...] = jnp.where(same, second, first).astype(BF)
 
 
 def rotate(u, cosine, sine):
@@ -156,7 +145,7 @@
         q_out[i, :, :] = query
 
 
-def attend_body(who, mine, other, q_ref, kv_part, out):
+def attend_body(who, mine, other, q_ref, keep, given, out):
     r = who[1]
     scale = HD ** (-0.5) * LOG2E
     sources = (mine, other)
@@ -165,6 +154,9 @@
     row_q, lane = iota((128, HD), 0), iota((128, HD), 1)
     row_q = 4 * (row_q // 16) + row_q % 4
     lane_s = iota((rows, HD), 1)
+    sub_s = iota((8, HD), 0)
+    kv = (keep[...] + given[...].astype(F32)).reshape(16, 8, HD)
+    kv_swapped = half_swap(kv)
     for t in range(512 // rows):
         part = slice(rows // 16 * t, rows // 16 * (t + 1))
         q = q_ref[part].reshape(rows, HD)
@@ -213,39 +205,41 @@
         stats = jnp.where(
             lane_s == 0, high, jnp.where(lane_s == 1, low, jnp.where(lane_s == 2, mass_high, mass - mass_high))
         )
-        stats = jnp.where(lane_s < 32, stats, kv_part[part].reshape(rows, HD).astype(F32))
-        out[part, 0:16, :] = acc.astype(BF).reshape(rows // 16, 16, HD)
-        out[part, 16:32, :] = stats.astype(BF).reshape(rows // 16, 16, HD)
-
-
-def to_every_head(total, start):
-    lane, sub = iota((16, HD), 1), iota((16, HD), 0)
-    whole = jnp.zeros((16, HD), F32)
-    for j in range(4):
-        block = jnp.where(sub // 4 == j, total, 0.0)
-        block = block + pltpu.roll(block, 8, 0)
-        block = block + pltpu.roll(block, 4, 0)
-        block = pltpu.roll(block, (32 * j - start) % HD, 1)
-        whole = jnp.where(lane // 32 == j, block, whole)
-    return whole
-
-
-def combine_body(parts, q_own, scale, cosine, sine, out):
-    stats = parts[:, 16:32, :].astype(F32)
-    total = jnp.sum(stats, axis=0)
-    new_k = (to_every_head(total, 32) * scale[...]).astype(BF).astype(F32)
+        stats = jnp.where(lane_s < 4, stats, 0.0)
+        for u in range(rows // 128):
+            turned = pltpu.roll(stats[128 * u : 128 * u + 128, :].T[0:8, :], 4, 0)
+            for i in range(8):
+                chunk = rows // 16 * t + 8 * u + i
+                part_kv = kv[chunk // 2] if chunk % 2 == 0 else kv_swapped[chunk // 2]
+                rest = jnp.where(sub_s < 4, part_kv, turned)
+                whole = jnp.concatenate([acc[128 * u + 16 * i : 128 * u + 16 * i + 16, :], rest], axis=0)
+                out[chunk, :, :] = whole.astype(BF)
+
+
+def twice(tile):
+    tile = jnp.where(iota((8, HD), 0) < 4, tile, pltpu.roll(tile, 4, 0))
+    return jnp.concatenate([tile, tile], axis=0)
+
+
+def combine_body(who, parts, q_own, scale, cosine, sine, out):
+    rest = parts[:, 16:24, :].astype(F32).reshape(16, 2, 8, HD)
+    new_k = (twice(jnp.sum(rest[:, 0], axis=0)) * scale[...]).astype(BF).astype(F32)
     new_k = rotate(new_k, cosine[...], sine[...]).astype(BF).astype(F32)
-    new_v = (to_every_head(total, 64) * scale[...]).astype(BF).astype(F32)
+    new_v = (twice(jnp.sum(rest[:, 1], axis=0)) * scale[...]).astype(BF).astype(F32)
     new = jnp.sum(q_own[...].astype(F32) * new_k, axis=1, keepdims=True) * (HD ** (-0.5) * LOG2E)
-    acc = parts[:, 0:16, :].astype(F32)
-    peak = stats[:, :, 0:1] + stats[:, :, 1:2]
-    mass = stats[:, :, 2:3] + stats[:, :, 3:4]
+    mine = iota((16, HD), 1) == 16 * lax.rem(who[0], 8) + iota((16, HD), 0)
+    new = jnp.sum(jnp.where(mine, new, 0.0), axis=0, keepdims=True)
+    rest = rest.reshape(32, 8, HD)
+    peak = rest[:, 4:5, :] + rest[:, 5:6, :]
+    mass = rest[:, 6:7, :] + rest[:, 7:8, :]
     top = jnp.maximum(jnp.max(peak, axis=0), new)
     shrink = jnp.exp2(peak - top[None])
     new_w = jnp.exp2(new - top)
     whole = jnp.sum(mass * shrink, axis=0) + new_w
-    summed = jnp.sum(acc * shrink, axis=0) + new_w * new_v
-    attended = (summed / whole).astype(BF)
+    share = jnp.sum(jnp.where(mine[None], shrink / whole[None], 0.0), axis=2, keepdims=True)
+    new_share = jnp.sum(jnp.where(mine, new_w / whole, 0.0), axis=1, keepdims=True)
+    summed = jnp.sum(parts[:, 0:16, :].astype(F32) * share, axis=0) + new_share * new_v
+    attended = summed.astype(BF)
     for i in range(out.shape[0]):
         out[i, :, :] = attended
 
@@ -326,44 +320,45 @@
     cosine, sine = rotary_tables(jnp.concatenate([lax.dynamic_slice_in_dim(positions, 4 * b, 4, 0)] * 4))
     half, first_w, second_w = lax.optimization_barrier((mine[:, :X0, :], first_w, second_w))
     other = lax.ppermute(half, "rows", [(i, i ^ 1) for i in range(16)])
-    kv_part = pl.pallas_call(
+    keep, give = pl.pallas_call(
         keyval_body,
         grid=(1,),
-        out_shape=sds((32, 16, HD), BF),
+        out_shape=(sds((128, HD), F32), sds((128, HD), BF)),
         in_specs=[SM, x_spec, gain_spec] + [pl.BlockSpec((256, HD), lambda i: (0, 0))] * 2,
-        out_specs=pl.BlockSpec((32, 16, HD), lambda i: (0, 0, 0)),
+        out_specs=[pl.BlockSpec((128, HD), lambda i: (0, 0))] * 2,
         compiler_params=params(),
         cost_estimate=pl.CostEstimate(flops=10**9, bytes_accessed=1 << 18, transcendentals=0),
         name="keyval",
     )(who, mine, gain, first_w, second_w)
-    cosine, kv_part = lax.optimization_barrier((cosine, kv_part))
+    given = lax.ppermute(give, "blk", [(i, i ^ 1) for i in range(32)])
+    cosine, given = lax.optimization_barrier((cosine, given))
     query, q_own, row_scale = pl.pallas_call(
         query_body,
         out_shape=(sds((32, 16, HD), BF), sds((16, HD), BF), sds((16, HD), F32)),
         in_specs=[SM, VM, VM, VM],
         out_specs=(VM, VM, VM),
         compiler_params=params(),
-        cost_estimate=pl.CostEstimate(flops=4*10**9, bytes_accessed=1 << 20, transcendentals=0),
+        cost_estimate=pl.CostEstimate(flops=3*10**9, bytes_accessed=1 << 20, transcendentals=0),
         name="query",
     )(who, parts, cosine, sine)
     query = lax.all_to_all(query, "blk", 0, 0, tiled=True)
     partial = pl.pallas_call(
         attend_body,
-        out_shape=sds((32, 32, HD), BF),
-        in_specs=[SM] + [VM] * 4,
+        out_shape=sds((32, 24, HD), BF),
+        in_specs=[SM] + [VM] * 5,
         out_specs=VM,
         compiler_params=params(),
         name="attend",
-    )(who, mine, other, query, kv_part)
+    )(who, mine, other, query, keep, given)
     partial = lax.all_to_all(partial, "blk", 0, 0, tiled=True)
     attended = pl.pallas_call(
         combine_body,
         out_shape=sds((32, 16, HD), BF),
-        in_specs=[VM] * 5,
+        in_specs=[SM] + [VM] * 5,
         out_specs=VM,
         compiler_params=params(),
         name="combine",
-    )(partial, q_own, row_scale, cosine, sine)
+    )(who, partial, q_own, row_scale, cosine, sine)
     attended = lax.all_to_all(attended, "blk", 0, 0, tiled=True)
     mixed, kept = pl.pallas_call(
         output_body,

time: 126 us -> 126 us (level)
  starting transfers between devices: 32.4 us -> 34.8 us
  waiting for transfers between devices: 22 us -> 20.2 us
    all_to_all x1, waiting for transfers between devices: 5.69 us -> 3.2 us  [on_device(): parts = lax.all_to_all(parts, 'blk', 0, 0, tiled=True)]
    all_to_all x1, blocking collectives: 17.8 us -> 15.3 us  [on_device(): partial = lax.all_to_all(partial, 'blk', 0, 0, tiled=True)]
    ppermute x0 -> x1, starting transfers between devices: none -> 2.42 us  [on_device(): given = lax.ppermute(give, 'blk', [(i, i ^ 1) for i in range(32)])]
    all_to_all x1, blocking collectives: 15.2 us -> 17.5 us  [on_device(): query = lax.all_to_all(query, 'blk', 0, 0, tiled=True)]
  transfers between devices with their start and end apart: 5 -> 6, of which waited for: 2 -> 3; matrix products, arithmetic and copies ran while one was open for 0% -> 0% of each run, Pallas kernels for 2% -> 2%
where the time goes in v8:
time: 126 us
  blocking collectives  59.4 us (47%)
  starting transfers between devices  34.8 us (28%)
  waiting for transfers between devices  20.2 us (16%)
  Pallas kernels  9.23 us (7%)
    all_to_all x1, blocking collectives, on_device(): query = lax.all_to_all(query, 'blk', 0, 0, tiled=True)  17.5 us
    all_to_all x1, waiting for transfers between devices, on_device(): mine = lax.all_to_all(packed, 'rows', 0, 0, tiled=True)  16.3 us
    all_to_all x1, blocking collectives, on_device(): partial = lax.all_to_all(partial, 'blk', 0, 0, tiled=True)  15.3 us
    all_to_all x1, starting transfers between devices, on_device(): parts = lax.all_to_all(parts, 'blk', 0, 0, tiled=True)  14.7 us
    all_to_all x1, blocking collectives, on_device(): attended = lax.all_to_all(attended, 'blk', 0, 0, tiled=True)  14 us
    all_to_all x1, blocking collectives, on_device(): mixed = lax.all_to_all(mixed.reshape(16, 8, 256), 'rows', 0, 0, tiled=True)  12.6 us
    all_to_all x1, starting transfers between devices, on_device(): mine = lax.all_to_all(packed, 'rows', 0, 0, tiled=True)  9.71 us
    ppermute x1, starting transfers between devices, on_device(): other = lax.ppermute(half, 'rows', [(i, i ^ 1) for i in range(16)])  4.05 us
  transfers between devices with their start and end apart: 6, of which 3 were waited for; matrix products, arithmetic and copies ran while one was open for 0% of the time, Pallas kernels for 2%

profile of v8, /device:TPU:1, one launch (start us, length us, event | category | flops | bytes accessed | tf_op | source)
XLA Modules:
  0.0 125.6 jit_solution(11168169738281165297)
XLA Ops:
  0.0 2.7 %pack.1 = bf16[16,208,128]{2,1,0:T(8,128)(2,1)} custom-call(s32[8]{0:T(128)} %lens.1, bf16[8,256]{1,0:T(8,128)(2,1)} %hidden.1, bf16[128,1024]{1,0:T(8,128)(2,1)} %keys_hbm.1, bf16[128,1024]{1,0:T(8,128)(2,1)} %values_hbm.1, bf16[64,1024]{1,0:T(8,128)(2,1)} %bitcast.6, bf16[64,1024]{1,0:T(8,128)(2,1)} %bitcast.7), custom_call_target="tpu_custom_call" | custom-call | tf_op jit(solution)/shard_map/pack/pallas_call | solution.py:289
  2.7 0.0 copy-start.5
  2.7 9.7 %all-to-all-start = ((bf16[16,208,128]{2,1,0:T(8,128)(2,1)}), bf16[16,208,128]{2,1,0:T(8,128)(2,1)S(1)}, u32[]{:S(2)}, u32[]{:S(2)}) async-start(bf16[16,208,128]{2,1,0:T(8,128)(2,1)} %pack.1), calls=%async_computation | async-start | bytes 1703936 | tf_op jit(solution)/shard_map/all_to_all | solution.py:305
  12.5 3.3 %collective-permute-start.1 = (bf16[256,128]{1,0:T(8,128)(2,1)S(1)}, bf16[256,128]{1,0:T(8,128)(2,1)S(1)}, u32[]{:S(2)}, u32[]{:S(2)}) collective-permute-start(bf16[256,128]{1,0:T(8,128)(2,1)S(1)} %copy-done.5), channel_id=1, source_target_pairs={{0,1},{1,3},{2,5},{3,7},{4,9},{5,11},{6,13},{7,15},{8,0},{9,2},{10... | collective-permute-start | bytes 196616 | tf_op jit(solution)/shard_map/ppermute | solution.py:288
  15.7 0.7 collective-permute-start
  16.4 0.0 copy-start.6
  16.4 0.6 copy-done.6
  17.1 0.1 pad_add_fusion.who
  17.2 16.3 %all-to-all-done.x_ref.mine = bf16[16,208,128]{2,1,0:T(8,128)(2,1)S(1)} async-done(((bf16[16,208,128]{2,1,0:T(8,128)(2,1)}), bf16[16,208,128]{2,1,0:T(8,128)(2,1)S(1)}, u32[]{:S(2)}, u32[]{:S(2)}) %all-to-all-start) | async-done | bytes 852000 | tf_op jit(solution)/shard_map/all_to_all | solution.py:305
  33.4 1.0 project.1
  34.4 14.7 %all-to-all-start.1 = ((bf16[32,24,128]{2,1,0:T(8,128)(2,1)}), bf16[32,24,128]{2,1,0:T(8,128)(2,1)S(1)}, u32[]{:S(2)}, u32[]{:S(2)}) async-start(bf16[32,24,128]{2,1,0:T(8,128)(2,1)} %project.1), calls=%async_computation.1 | async-start | bytes 393216 | tf_op jit(solution)/shard_map/all_to_all | solution.py:319
  49.1 0.0 copy-start.7
  49.1 0.1 slice.3
  49.2 4.0 %collective-permute-start.2 = (bf16[16,192,128]{2,1,0:T(8,128)(2,1)S(1)}, bf16[16,192,128]{2,1,0:T(8,128)(2,1)S(1)}, u32[]{:S(2)}, u32[]{:S(2)}) collective-permute-start(bf16[16,192,128]{2,1,0:T(8,128)(2,1)S(1)} %slice.3), channel_id=1, source_target_pairs={{0,1},{1,0},{2,3},{3,2},{4,5},{5,4},{6,7},{7,6},{8,9},{9,8},{10,11... | collective-permute-start | bytes 2359304 | tf_op jit(solution)/shard_map/ppermute | solution.py:322
  53.3 0.1 dynamic_slice.3
  53.4 0.1 add_convert_fusion.1
  53.4 0.7 keyval.1
  54.2 0.0 copy-start.3
  54.2 0.0 copy-start.4
  54.2 2.4 %collective-permute-start.3 = (bf16[128,128]{1,0:T(8,128)(2,1)S(1)}, bf16[128,128]{1,0:T(8,128)(2,1)S(1)}, u32[]{:S(2)}, u32[]{:S(2)}) collective-permute-start(bf16[128,128]{1,0:T(8,128)(2,1)S(1)} %get-tuple-element.26), channel_id=1, source_target_pairs={{0,16},{16,0},{32,48},{48,32},{64,80},{80,64},{96,112},{112,96},{1... | collective-permute-start | bytes 98312 | tf_op jit(solution)/shard_map/ppermute | solution.py:333
  56.6 0.1 fusion
  56.8 0.7 collective-permute-done.3.given
  57.5 3.2 %all-to-all-done.1.parts = bf16[32,24,128]{2,1,0:T(8,128)(2,1)S(1)} async-done(((bf16[32,24,128]{2,1,0:T(8,128)(2,1)}), bf16[32,24,128]{2,1,0:T(8,128)(2,1)S(1)}, u32[]{:S(2)}, u32[]{:S(2)}) %all-to-all-start.1) | async-done | bytes 196640 | tf_op jit(solution)/shard_map/all_to_all | solution.py:319
  60.7 0.7 query.1
  61.4 17.5 %all_to_all.30.q_ref = bf16[32,16,128]{2,1,0:T(8,128)(2,1)S(1)} all-to-all(bf16[32,16,128]{2,1,0:T(8,128)(2,1)S(1)} %get-tuple-element.28), channel_id=1, replica_groups=mesh['blk'=32,'rows'=16] {'blk'}, dimensions={0} | all-to-all | bytes 262144 | tf_op jit(solution)/shard_map/all_to_all | solution.py:344
  78.9 2.9 %attend.1 = bf16[32,24,128]{2,1,0:T(8,128)(2,1)S(1)} custom-call(s32[2]{0:T(128)S(1)} %pad_add_fusion.who, bf16[16,208,128]{2,1,0:T(8,128)(2,1)S(1)} %all-to-all-done.x_ref.mine, bf16[16,192,128]{2,1,0:T(8,128)(2,1)S(1)} %collective-permute-done.2.other, bf16[32,16,128]{2,1,0:T(8,128)(2,1)S(1)} %all_to_all.30.q_ref, f32[128,128]{1,0:T(8,128)S(1)} %get-tuple-element.29.keep, ...), custom_call_target="tpu_custom_call" | custom-call | tf_op jit(solution)/shard_map/attend/pallas_call | solution.py:345
  81.9 15.3 %all_to_all.31.parts = bf16[32,24,128]{2,1,0:T(8,128)(2,1)S(1)} all-to-all(bf16[32,24,128]{2,1,0:T(8,128)(2,1)S(1)} %attend.1), channel_id=1, replica_groups=mesh['blk'=32,'rows'=16] {'blk'}, dimensions={0} | all-to-all | bytes 393216 | tf_op jit(solution)/shard_map/all_to_all | solution.py:353
  97.1 0.9 combine.1
  98.1 14.0 %all_to_all.32.att = bf16[32,16,128]{2,1,0:T(8,128)(2,1)S(1)} all-to-all(bf16[32,16,128]{2,1,0:T(8,128)(2,1)S(1)} %combine.1), channel_id=1, replica_groups=mesh['blk'=32,'rows'=16] {'blk'}, dimensions={0} | all-to-all | bytes 262144 | tf_op jit(solution)/shard_map/all_to_all | solution.py:362
  112.1 0.2 output.1
  112.3 12.6 %all_to_all.33 = bf16[16,8,256]{2,1,0:T(8,128)(2,1)S(1)} all-to-all(bf16[16,8,256]{2,1,0:T(8,128)(2,1)S(1)} %bitcast.5), channel_id=1, replica_groups=mesh['blk'=32,'rows'=16] {'rows'}, dimensions={0} | all-to-all | bytes 131072 | tf_op jit(solution)/shard_map/all_to_all | solution.py:371
  125.0 0.6 add_convert_fusion
  (15 shorter events, 0.1 us)
Async XLA Ops:
  2.7 9.7 %copy-start.5 = (bf16[256,128]{1,0:T(8,128)(2,1)S(1)}, bf16[256,128]{1,0:T(8,128)(2,1)}, u32[]{:S(2)}) copy-start(bf16[256,128]{1,0:T(8,128)(2,1)} %param.16) | copy-start | bytes 196612
  2.7 30.7 %copy-start.1 = (bf16[256,512]{1,0:T(8,128)(2,1)S(1)}, bf16[256,512]{1,0:T(8,128)(2,1)}, u32[]{:S(2)}) copy-start(bf16[256,512]{1,0:T(8,128)(2,1)} %wq.1) | copy-start | bytes 786436
  2.7 30.7 %all-to-all-start = ((bf16[16,208,128]{2,1,0:T(8,128)(2,1)}), bf16[16,208,128]{2,1,0:T(8,128)(2,1)S(1)}, u32[]{:S(2)}, u32[]{:S(2)}) async-start(bf16[16,208,128]{2,1,0:T(8,128)(2,1)} %pack.1), calls=%async_computation | async-start | bytes 1703936 | tf_op jit(solution)/shard_map/all_to_all | solution.py:305
  12.5 36.7 %collective-permute-start.1 = (bf16[256,128]{1,0:T(8,128)(2,1)S(1)}, bf16[256,128]{1,0:T(8,128)(2,1)S(1)}, u32[]{:S(2)}, u32[]{:S(2)}) collective-permute-start(bf16[256,128]{1,0:T(8,128)(2,1)S(1)} %copy-done.5), channel_id=1, source_target_pairs={{0,1},{1,3},{2,5},{3,7},{4,9},{5,11},{6,13},{7,15},{8,0},{9,2},{10... | collective-permute-start | bytes 196616 | tf_op jit(solution)/shard_map/ppermute | solution.py:288
  15.7 33.5 %collective-permute-start = (bf16[256,128]{1,0:T(8,128)(2,1)S(1)}, bf16[256,128]{1,0:T(8,128)(2,1)S(1)}, u32[]{:S(2)}, u32[]{:S(2)}) collective-permute-start(bf16[256,128]{1,0:T(8,128)(2,1)S(1)} %copy-done.5), channel_id=1, source_target_pairs={{0,0},{1,2},{2,4},{3,6},{4,8},{5,10},{6,12},{7,14},{8,1},{9,3},{10... | collective-permute-start | bytes 196616 | tf_op jit(solution)/shard_map/ppermute | solution.py:287
  16.4 0.7 copy-start.6
  34.4 26.3 %all-to-all-start.1 = ((bf16[32,24,128]{2,1,0:T(8,128)(2,1)}), bf16[32,24,128]{2,1,0:T(8,128)(2,1)S(1)}, u32[]{:S(2)}, u32[]{:S(2)}) async-start(bf16[32,24,128]{2,1,0:T(8,128)(2,1)} %project.1), calls=%async_computation.1 | async-start | bytes 393216 | tf_op jit(solution)/shard_map/all_to_all | solution.py:319
  49.1 4.2 %copy-start.7 = (s32[128]{0:T(128)S(1)}, s32[128]{0:T(128)}, u32[]{:S(2)}) copy-start(s32[128]{0:T(128)} %param.22) | copy-start | bytes 1540
  49.2 29.7 %collective-permute-start.2 = (bf16[16,192,128]{2,1,0:T(8,128)(2,1)S(1)}, bf16[16,192,128]{2,1,0:T(8,128)(2,1)S(1)}, u32[]{:S(2)}, u32[]{:S(2)}) collective-permute-start(bf16[16,192,128]{2,1,0:T(8,128)(2,1)S(1)} %slice.3), channel_id=1, source_target_pairs={{0,1},{1,0},{2,3},{3,2},{4,5},{5,4},{6,7},{7,6},{8,9},{9,8},{10,11... | collective-permute-start | bytes 2359304 | tf_op jit(solution)/shard_map/ppermute | solution.py:322
  54.2 2.5 %copy-start.3 = (f32[128]{0:T(128)S(1)}, f32[128]{0:T(128)}, u32[]{:S(2)}) copy-start(f32[128]{0:T(128)} %constant.22.clone) | copy-start | bytes 1540
  54.2 2.5 %copy-start.4 = (f32[128]{0:T(128)S(1)}, f32[128]{0:T(128)}, u32[]{:S(2)}) copy-start(f32[128]{0:T(128)} %constant.21.clone) | copy-start | bytes 1540
  54.2 3.3 %collective-permute-start.3 = (bf16[128,128]{1,0:T(8,128)(2,1)S(1)}, bf16[128,128]{1,0:T(8,128)(2,1)S(1)}, u32[]{:S(2)}, u32[]{:S(2)}) collective-permute-start(bf16[128,128]{1,0:T(8,128)(2,1)S(1)} %get-tuple-element.26), channel_id=1, source_target_pairs={{0,16},{16,0},{32,48},{48,32},{64,80},{80,64},{96,112},{112,96},{1... | collective-permute-start | bytes 98312 | tf_op jit(solution)/shard_map/ppermute | solution.py:333
  97.1 14.9 %copy-start = (bf16[512,256]{1,0:T(8,128)(2,1)S(1)}, bf16[512,256]{1,0:T(8,128)(2,1)}, u32[]{:S(2)}) copy-start(bf16[512,256]{1,0:T(8,128)(2,1)} %w.1) | copy-start | bytes 786436
  98.1 14.0 %copy-start.2 = (bf16[8,256]{1,0:T(8,128)(2,1)S(1)}, bf16[8,256]{1,0:T(8,128)(2,1)}, u32[]{:S(2)}) copy-start(bf16[8,256]{1,0:T(8,128)(2,1)} %hidden.1) | copy-start | bytes 12292

commit v9 on v8

--- a/solution.py
+++ b/solution.py
@@ -331,7 +331,6 @@
         name="keyval",
     )(who, mine, gain, first_w, second_w)
     given = lax.ppermute(give, "blk", [(i, i ^ 1) for i in range(32)])
-    cosine, given = lax.optimization_barrier((cosine, given))
     query, q_own, row_scale = pl.pallas_call(
         query_body,
         out_shape=(sds((32, 16, HD), BF), sds((16, HD), BF), sds((16, HD), F32)),

time: 126 us -> 125 us (level)
  blocking collectives: 59.4 us -> 42.8 us
  waiting for transfers between devices: 20.2 us -> 30.6 us
  starting transfers between devices: 34.8 us -> 39 us
    all_to_all x1 -> x0, blocking collectives: 17.5 us -> none  [on_device(): query = lax.all_to_all(query, 'blk', 0, 0, tiled=True)]
    all_to_all x0 -> x1, waiting for transfers between devices: none -> 6.82 us  [on_device(): query = lax.all_to_all(query, 'blk', 0, 0, tiled=True)]
    all_to_all x0 -> x1, starting transfers between devices: none -> 4.45 us  [on_device(): query = lax.all_to_all(query, 'blk', 0, 0, tiled=True)]
    all_to_all x1, waiting for transfers between devices: 3.2 us -> 6.44 us  [on_device(): parts = lax.all_to_all(parts, 'blk', 0, 0, tiled=True)]
  transfers between devices with their start and end apart: 6 -> 7, of which waited for: 3 -> 4; matrix products, arithmetic and copies ran while one was open for 0% -> 0% of each run, Pallas kernels for 2% -> 2%
where the time goes in v9:
time: 125 us
  blocking collectives  42.8 us (34%)
  starting transfers between devices  39 us (31%)
  waiting for transfers between devices  30.6 us (24%)
  Pallas kernels  9.93 us (8%)
  local copies, waits for them, and re-layouts  1.42 us (1%)
    all_to_all x1, waiting for transfers between devices, on_device(): mine = lax.all_to_all(packed, 'rows', 0, 0, tiled=True)  16.4 us
    all_to_all x1, blocking collectives, on_device(): partial = lax.all_to_all(partial, 'blk', 0, 0, tiled=True)  16 us
    all_to_all x1, starting transfers between devices, on_device(): parts = lax.all_to_all(parts, 'blk', 0, 0, tiled=True)  14.7 us
    all_to_all x1, blocking collectives, on_device(): attended = lax.all_to_all(attended, 'blk', 0, 0, tiled=True)  14 us
    all_to_all x1, blocking collectives, on_device(): mixed = lax.all_to_all(mixed.reshape(16, 8, 256), 'rows', 0, 0, tiled=True)  12.7 us
    all_to_all x1, starting transfers between devices, on_device(): mine = lax.all_to_all(packed, 'rows', 0, 0, tiled=True)  9.71 us
    all_to_all x1, waiting for transfers between devices, on_device(): query = lax.all_to_all(query, 'blk', 0, 0, tiled=True)  6.82 us
    all_to_all x1, waiting for transfers between devices, on_device(): parts = lax.all_to_all(parts, 'blk', 0, 0, tiled=True)  6.44 us
  transfers between devices with their start and end apart: 7, of which 4 were waited for; matrix products, arithmetic and copies ran while one was open for 0% of the time, Pallas kernels for 2%

profile of v9, /device:TPU:1, one launch (start us, length us, event | category | flops | bytes accessed | tf_op | source)
XLA Modules:
  0.0 124.8 jit_solution(7360586645665751721)
XLA Ops:
  0.0 2.8 %pack.1 = bf16[16,208,128]{2,1,0:T(8,128)(2,1)} custom-call(s32[8]{0:T(128)} %lens.1, bf16[8,256]{1,0:T(8,128)(2,1)} %hidden.1, bf16[128,1024]{1,0:T(8,128)(2,1)} %keys_hbm.1, bf16[128,1024]{1,0:T(8,128)(2,1)} %values_hbm.1, bf16[64,1024]{1,0:T(8,128)(2,1)} %bitcast.6, bf16[64,1024]{1,0:T(8,128)(2,1)} %bitcast.7), custom_call_target="tpu_custom_call" | custom-call | tf_op jit(solution)/shard_map/pack/pallas_call | solution.py:289
  2.8 0.0 copy-start.5
  2.8 9.7 %all-to-all-start = ((bf16[16,208,128]{2,1,0:T(8,128)(2,1)}), bf16[16,208,128]{2,1,0:T(8,128)(2,1)S(1)}, u32[]{:S(2)}, u32[]{:S(2)}) async-start(bf16[16,208,128]{2,1,0:T(8,128)(2,1)} %pack.1), calls=%async_computation | async-start | bytes 1703936 | tf_op jit(solution)/shard_map/all_to_all | solution.py:305
  12.5 3.3 %collective-permute-start.1 = (bf16[256,128]{1,0:T(8,128)(2,1)S(1)}, bf16[256,128]{1,0:T(8,128)(2,1)S(1)}, u32[]{:S(2)}, u32[]{:S(2)}) collective-permute-start(bf16[256,128]{1,0:T(8,128)(2,1)S(1)} %copy-done.5), channel_id=1, source_target_pairs={{0,1},{1,3},{2,5},{3,7},{4,9},{5,11},{6,13},{7,15},{8,0},{9,2},{10... | collective-permute-start | bytes 196616 | tf_op jit(solution)/shard_map/ppermute | solution.py:288
  15.8 0.7 collective-permute-start
  16.5 0.0 copy-start.6
  16.5 0.6 copy-done.6
  17.1 16.4 %all-to-all-done.x_ref.mine = bf16[16,208,128]{2,1,0:T(8,128)(2,1)S(1)} async-done(((bf16[16,208,128]{2,1,0:T(8,128)(2,1)}), bf16[16,208,128]{2,1,0:T(8,128)(2,1)S(1)}, u32[]{:S(2)}, u32[]{:S(2)}) %all-to-all-start) | async-done | bytes 852000 | tf_op jit(solution)/shard_map/all_to_all | solution.py:305
  33.5 1.0 project.1
  34.5 14.7 %all-to-all-start.1 = ((bf16[32,24,128]{2,1,0:T(8,128)(2,1)}), bf16[32,24,128]{2,1,0:T(8,128)(2,1)S(1)}, u32[]{:S(2)}, u32[]{:S(2)}) async-start(bf16[32,24,128]{2,1,0:T(8,128)(2,1)} %project.1), calls=%async_computation.1 | async-start | bytes 393216 | tf_op jit(solution)/shard_map/all_to_all | solution.py:319
  49.2 0.1 pad_add_fusion.who
  49.2 0.1 slice.3
  49.3 4.0 %collective-permute-start.2 = (bf16[16,192,128]{2,1,0:T(8,128)(2,1)S(1)}, bf16[16,192,128]{2,1,0:T(8,128)(2,1)S(1)}, u32[]{:S(2)}, u32[]{:S(2)}) collective-permute-start(bf16[16,192,128]{2,1,0:T(8,128)(2,1)S(1)} %slice.3), channel_id=1, source_target_pairs={{0,1},{1,0},{2,3},{3,2},{4,5},{5,4},{6,7},{7,6},{8,9},{9,8},{10,11... | collective-permute-start | bytes 2359304 | tf_op jit(solution)/shard_map/ppermute | solution.py:322
  53.4 0.1 dynamic_slice.3
  53.5 0.1 add_convert_fusion.1
  53.6 0.6 copy-done.3
  54.1 0.0 copy-done.4
  54.2 0.1 fusion
  54.3 6.4 %all-to-all-done.1.parts = bf16[32,24,128]{2,1,0:T(8,128)(2,1)S(1)} async-done(((bf16[32,24,128]{2,1,0:T(8,128)(2,1)}), bf16[32,24,128]{2,1,0:T(8,128)(2,1)S(1)}, u32[]{:S(2)}, u32[]{:S(2)}) %all-to-all-start.1) | async-done | bytes 196640 | tf_op jit(solution)/shard_map/all_to_all | solution.py:319
  60.7 1.4 %query.1 = (bf16[32,16,128]{2,1,0:T(8,128)(2,1)}, bf16[16,128]{1,0:T(8,128)(2,1)S(1)}, f32[16,128]{1,0:T(8,128)S(1)}) custom-call(s32[2]{0:T(128)S(1)} %pad_add_fusion.who, bf16[32,24,128]{2,1,0:T(8,128)(2,1)S(1)} %all-to-all-done.1.parts, f32[16,128]{1,0:T(8,128)S(1)} %get-tuple-element.32.cosine, f32[16,128]{1,0:T(8,128)S(1)} %get-tuple-element.31.sine), custom_call_target="tpu_custom_call" | custom-call | flops 3000000000 | bytes 1048576 | tf_op jit(solution)/shard_map/query/pallas_call | solution.py:334
  62.1 4.4 %all-to-all-start.2 = ((bf16[32,16,128]{2,1,0:T(8,128)(2,1)}), bf16[32,16,128]{2,1,0:T(8,128)(2,1)S(1)}, u32[]{:S(2)}, u32[]{:S(2)}) async-start(bf16[32,16,128]{2,1,0:T(8,128)(2,1)} %get-tuple-element.22), calls=%async_computation.2 | async-start | bytes 262144 | tf_op jit(solution)/shard_map/all_to_all | solution.py:343
  66.6 0.7 keyval.1
  67.3 2.1 %collective-permute-start.3 = (bf16[128,128]{1,0:T(8,128)(2,1)S(1)}, bf16[128,128]{1,0:T(8,128)(2,1)S(1)}, u32[]{:S(2)}, u32[]{:S(2)}) collective-permute-start(bf16[128,128]{1,0:T(8,128)(2,1)S(1)} %get-tuple-element.26), channel_id=1, source_target_pairs={{0,16},{16,0},{32,48},{48,32},{64,80},{80,64},{96,112},{112,96},{1... | collective-permute-start | bytes 98312 | tf_op jit(solution)/shard_map/ppermute | solution.py:333
  69.5 0.9 collective-permute-done.3.given
  70.4 6.8 %all-to-all-done.2.q_ref = bf16[32,16,128]{2,1,0:T(8,128)(2,1)S(1)} async-done(((bf16[32,16,128]{2,1,0:T(8,128)(2,1)}), bf16[32,16,128]{2,1,0:T(8,128)(2,1)S(1)}, u32[]{:S(2)}, u32[]{:S(2)}) %all-to-all-start.2) | async-done | bytes 131104 | tf_op jit(solution)/shard_map/all_to_all | solution.py:343
  77.2 2.9 %attend.1 = bf16[32,24,128]{2,1,0:T(8,128)(2,1)S(1)} custom-call(s32[2]{0:T(128)S(1)} %pad_add_fusion.who, bf16[16,208,128]{2,1,0:T(8,128)(2,1)S(1)} %all-to-all-done.x_ref.mine, bf16[16,192,128]{2,1,0:T(8,128)(2,1)S(1)} %collective-permute-done.2.other, bf16[32,16,128]{2,1,0:T(8,128)(2,1)S(1)} %all-to-all-done.2.q_ref, ...), custom_call_target="tpu_custom_call" | custom-call | tf_op jit(solution)/shard_map/attend/pallas_call | solution.py:344
  80.2 16.0 %all_to_all.30.parts = bf16[32,24,128]{2,1,0:T(8,128)(2,1)S(1)} all-to-all(bf16[32,24,128]{2,1,0:T(8,128)(2,1)S(1)} %attend.1), channel_id=1, replica_groups=mesh['blk'=32,'rows'=16] {'blk'}, dimensions={0} | all-to-all | bytes 393216 | tf_op jit(solution)/shard_map/all_to_all | solution.py:352
  96.2 0.9 combine.1
  97.2 14.0 %all_to_all.31.att = bf16[32,16,128]{2,1,0:T(8,128)(2,1)S(1)} all-to-all(bf16[32,16,128]{2,1,0:T(8,128)(2,1)S(1)} %combine.1), channel_id=1, replica_groups=mesh['blk'=32,'rows'=16] {'blk'}, dimensions={0} | all-to-all | bytes 262144 | tf_op jit(solution)/shard_map/all_to_all | solution.py:361
  111.2 0.2 output.1
  111.4 12.7 %all_to_all.32 = bf16[16,8,256]{2,1,0:T(8,128)(2,1)S(1)} all-to-all(bf16[16,8,256]{2,1,0:T(8,128)(2,1)S(1)} %bitcast.5), channel_id=1, replica_groups=mesh['blk'=32,'rows'=16] {'rows'}, dimensions={0} | all-to-all | bytes 131072 | tf_op jit(solution)/shard_map/all_to_all | solution.py:370
  124.2 0.6 add_convert_fusion
  (16 shorter events, 0.1 us)
Async XLA Ops:
  2.8 9.7 %copy-start.5 = (bf16[256,128]{1,0:T(8,128)(2,1)S(1)}, bf16[256,128]{1,0:T(8,128)(2,1)}, u32[]{:S(2)}) copy-start(bf16[256,128]{1,0:T(8,128)(2,1)} %param.16) | copy-start | bytes 196612
  2.8 30.7 %copy-start.1 = (bf16[256,512]{1,0:T(8,128)(2,1)S(1)}, bf16[256,512]{1,0:T(8,128)(2,1)}, u32[]{:S(2)}) copy-start(bf16[256,512]{1,0:T(8,128)(2,1)} %wq.1) | copy-start | bytes 786436
  2.8 30.7 %all-to-all-start = ((bf16[16,208,128]{2,1,0:T(8,128)(2,1)}), bf16[16,208,128]{2,1,0:T(8,128)(2,1)S(1)}, u32[]{:S(2)}, u32[]{:S(2)}) async-start(bf16[16,208,128]{2,1,0:T(8,128)(2,1)} %pack.1), calls=%async_computation | async-start | bytes 1703936 | tf_op jit(solution)/shard_map/all_to_all | solution.py:305
  12.5 36.8 %collective-permute-start.1 = (bf16[256,128]{1,0:T(8,128)(2,1)S(1)}, bf16[256,128]{1,0:T(8,128)(2,1)S(1)}, u32[]{:S(2)}, u32[]{:S(2)}) collective-permute-start(bf16[256,128]{1,0:T(8,128)(2,1)S(1)} %copy-done.5), channel_id=1, source_target_pairs={{0,1},{1,3},{2,5},{3,7},{4,9},{5,11},{6,13},{7,15},{8,0},{9,2},{10... | collective-permute-start | bytes 196616 | tf_op jit(solution)/shard_map/ppermute | solution.py:288
  15.8 33.5 %collective-permute-start = (bf16[256,128]{1,0:T(8,128)(2,1)S(1)}, bf16[256,128]{1,0:T(8,128)(2,1)S(1)}, u32[]{:S(2)}, u32[]{:S(2)}) collective-permute-start(bf16[256,128]{1,0:T(8,128)(2,1)S(1)} %copy-done.5), channel_id=1, source_target_pairs={{0,0},{1,2},{2,4},{3,6},{4,8},{5,10},{6,12},{7,14},{8,1},{9,3},{10... | collective-permute-start | bytes 196616 | tf_op jit(solution)/shard_map/ppermute | solution.py:287
  16.5 0.7 copy-start.6
  34.5 26.3 %all-to-all-start.1 = ((bf16[32,24,128]{2,1,0:T(8,128)(2,1)}), bf16[32,24,128]{2,1,0:T(8,128)(2,1)S(1)}, u32[]{:S(2)}, u32[]{:S(2)}) async-start(bf16[32,24,128]{2,1,0:T(8,128)(2,1)} %project.1), calls=%async_computation.1 | async-start | bytes 393216 | tf_op jit(solution)/shard_map/all_to_all | solution.py:319
  49.2 4.2 %copy-start.7 = (s32[128]{0:T(128)S(1)}, s32[128]{0:T(128)}, u32[]{:S(2)}) copy-start(s32[128]{0:T(128)} %param.22) | copy-start | bytes 1540
  49.3 27.9 %collective-permute-start.2 = (bf16[16,192,128]{2,1,0:T(8,128)(2,1)S(1)}, bf16[16,192,128]{2,1,0:T(8,128)(2,1)S(1)}, u32[]{:S(2)}, u32[]{:S(2)}) collective-permute-start(bf16[16,192,128]{2,1,0:T(8,128)(2,1)S(1)} %slice.3), channel_id=1, source_target_pairs={{0,1},{1,0},{2,3},{3,2},{4,5},{5,4},{6,7},{7,6},{8,9},{9,8},{10,11... | collective-permute-start | bytes 2359304 | tf_op jit(solution)/shard_map/ppermute | solution.py:322
  53.5 0.7 copy-start.3
  53.5 0.7 copy-start.4
  62.1 15.1 %all-to-all-start.2 = ((bf16[32,16,128]{2,1,0:T(8,128)(2,1)}), bf16[32,16,128]{2,1,0:T(8,128)(2,1)S(1)}, u32[]{:S(2)}, u32[]{:S(2)}) async-start(bf16[32,16,128]{2,1,0:T(8,128)(2,1)} %get-tuple-element.22), calls=%async_computation.2 | async-start | bytes 262144 | tf_op jit(solution)/shard_map/all_to_all | solution.py:343
  67.3 3.1 %collective-permute-start.3 = (bf16[128,128]{1,0:T(8,128)(2,1)S(1)}, bf16[128,128]{1,0:T(8,128)(2,1)S(1)}, u32[]{:S(2)}, u32[]{:S(2)}) collective-permute-start(bf16[128,128]{1,0:T(8,128)(2,1)S(1)} %get-tuple-element.26), channel_id=1, source_target_pairs={{0,16},{16,0},{32,48},{48,32},{64,80},{80,64},{96,112},{112,96},{1... | collective-permute-start | bytes 98312 | tf_op jit(solution)/shard_map/ppermute | solution.py:333
  96.2 15.0 %copy-start = (bf16[512,256]{1,0:T(8,128)(2,1)S(1)}, bf16[512,256]{1,0:T(8,128)(2,1)}, u32[]{:S(2)}) copy-start(bf16[512,256]{1,0:T(8,128)(2,1)} %w.1) | copy-start | bytes 786436
  97.2 14.1 %copy-start.2 = (bf16[8,256]{1,0:T(8,128)(2,1)S(1)}, bf16[8,256]{1,0:T(8,128)(2,1)}, u32[]{:S(2)}) copy-start(bf16[8,256]{1,0:T(8,128)(2,1)} %hidden.1) | copy-start | bytes 12292

commit v10 on v9

--- a/solution.py
+++ b/solution.py
@@ -24,20 +24,22 @@
     return lax.broadcasted_iota(jnp.int32, shape, dim)
 
 
-def pack_body(lens, hidden_hbm, keys_hbm, values_hbm, own_k_hbm, own_v_hbm, out, keys, values, own_k, own_v, packed, rows_x, sems):
+def pack_body(lens, hidden, keys_hbm, values_hbm, own_k_hbm, own_v_hbm, out, keys, values, own_k, own_v, packed, sems):
     inward = [
         pltpu.make_async_copy(src, dst, sems.at[i])
         for i, (src, dst) in enumerate(
-            ((own_k_hbm, own_k), (keys_hbm, keys), (values_hbm, values), (own_v_hbm, own_v), (hidden_hbm, rows_x))
+            ((own_k_hbm, own_k), (keys_hbm, keys), (values_hbm, values), (own_v_hbm, own_v))
         )
     ]
     for copy in inward:
         copy.start()
     outward = [
-        pltpu.make_async_copy(packed.at[:, first:last, :], out.at[:, first:last, :], sems.at[5 + i])
+        pltpu.make_async_copy(packed.at[:, first:last, :], out.at[:, first:last, :], sems.at[4 + i])
         for i, (first, last) in enumerate(((OK0, OV0), (K0, V0), (V0, OK0), (OV0, END)))
     ]
     b = lax.axis_index("blk")
+    x = hidden[...].astype(F32)
+    x_tile = jnp.concatenate([x[:, :HD], x[:, HD:]], axis=0).astype(BF)
     sub = iota((32, HD), 0)
     slot = 8 * b + sub % 8
     dead = []
@@ -48,10 +50,6 @@
         dead.append(slot >= live)
     for step in range(4):
         inward[step].wait()
-        if step == 3:
-            inward[4].wait()
-            x = rows_x[...].astype(F32)
-            x_tile = jnp.concatenate([x[:, :HD], x[:, HD:]], axis=0).astype(BF)
         for p in range(2):
             for h in range(8):
                 col = slice(h * HD, (h + 1) * HD)
@@ -112,10 +110,8 @@
     xg = (x * gain[...].astype(F32)).astype(BF)
     q = jnp.dot(xg, wq[...], preferred_element_type=F32)
     heads = [q[:, HD * h : HD * h + HD] for h in range(4)]
-    for p in range(2):
-        chunks = jnp.concatenate(by_rows_of_four(heads, p) + [squares], axis=1).astype(BF)
-        for j in range(16):
-            out[2 * j + p, :, :] = chunks[j]
+    tiles = by_rows_of_four(heads, 0) + [squares] + by_rows_of_four(heads, 1) + [squares]
+    out[...] = jnp.concatenate(tiles, axis=1).reshape(768, HD).astype(BF)
 
 
 def keyval_body(who, x_ref, gain, wa, wb, keep, give):
@@ -132,7 +128,7 @@
 
 
 def query_body(who, parts, cosine, sine, q_out, q_own, scale_out):
-    total = jnp.sum(parts[...].astype(F32), axis=0)
+    total = jnp.sum(parts[...].astype(F32).reshape(32, 24, HD), axis=0)
     square = total[16:17, :] + total[17:18, :]
     inv = lax.rsqrt(square / 8192.0 + 1e-05)
     lane, sub = iota((16, HD), 1), iota((16, HD), 0)
@@ -208,12 +204,16 @@
         stats = jnp.where(lane_s < 4, stats, 0.0)
         for u in range(rows // 128):
             turned = pltpu.roll(stats[128 * u : 128 * u + 128, :].T[0:8, :], 4, 0)
-            for i in range(8):
-                chunk = rows // 16 * t + 8 * u + i
-                part_kv = kv[chunk // 2] if chunk % 2 == 0 else kv_swapped[chunk // 2]
-                rest = jnp.where(sub_s < 4, part_kv, turned)
-                whole = jnp.concatenate([acc[128 * u + 16 * i : 128 * u + 16 * i + 16, :], rest], axis=0)
-                out[chunk, :, :] = whole.astype(BF)
+            for i in range(4):
+                pair = rows // 32 * t + 4 * u + i
+                first = 128 * u + 32 * i
+                tiles = [
+                    acc[first : first + 16, :],
+                    jnp.where(sub_s < 4, kv[pair], turned),
+                    acc[first + 16 : first + 32, :],
+                    jnp.where(sub_s < 4, kv_swapped[pair], turned),
+                ]
+                out[48 * pair : 48 * pair + 48, :] = jnp.concatenate(tiles, axis=0).astype(BF)
 
 
 def twice(tile):
@@ -222,24 +222,36 @@
 
 
 def combine_body(who, parts, q_own, scale, cosine, sine, out):
-    rest = parts[:, 16:24, :].astype(F32).reshape(16, 2, 8, HD)
+    parts = parts[...].astype(F32).reshape(32, 24, HD)
+    rest = parts[:, 16:24, :].reshape(16, 2, 8, HD)
     new_k = (twice(jnp.sum(rest[:, 0], axis=0)) * scale[...]).astype(BF).astype(F32)
     new_k = rotate(new_k, cosine[...], sine[...]).astype(BF).astype(F32)
     new_v = (twice(jnp.sum(rest[:, 1], axis=0)) * scale[...]).astype(BF).astype(F32)
     new = jnp.sum(q_own[...].astype(F32) * new_k, axis=1, keepdims=True) * (HD ** (-0.5) * LOG2E)
-    mine = iota((16, HD), 1) == 16 * lax.rem(who[0], 8) + iota((16, HD), 0)
+    start = 16 * lax.rem(who[0], 8)
+    mine = iota((16, HD), 1) == start + iota((16, HD), 0)
     new = jnp.sum(jnp.where(mine, new, 0.0), axis=0, keepdims=True)
-    rest = rest.reshape(32, 8, HD)
-    peak = rest[:, 4:5, :] + rest[:, 5:6, :]
-    mass = rest[:, 6:7, :] + rest[:, 7:8, :]
-    top = jnp.maximum(jnp.max(peak, axis=0), new)
-    shrink = jnp.exp2(peak - top[None])
+    stats = jnp.concatenate([parts[:, 16 + k, :] for k in range(4, 8)], axis=0).reshape(4, 32, HD)
+    peak = stats[0] + stats[1]
+    mass = stats[2] + stats[3]
+    top = jnp.maximum(jnp.max(peak, axis=0, keepdims=True), new)
+    shrink = jnp.exp2(peak - top)
     new_w = jnp.exp2(new - top)
-    whole = jnp.sum(mass * shrink, axis=0) + new_w
-    share = jnp.sum(jnp.where(mine[None], shrink / whole[None], 0.0), axis=2, keepdims=True)
+    whole = jnp.sum(mass * shrink, axis=0, keepdims=True) + new_w
     new_share = jnp.sum(jnp.where(mine, new_w / whole, 0.0), axis=1, keepdims=True)
-    summed = jnp.sum(parts[:, 0:16, :].astype(F32) * share, axis=0) + new_share * new_v
-    attended = summed.astype(BF)
+    share = pltpu.roll(shrink / whole, lax.rem(HD - start, HD), 1)
+    share = jnp.where(iota((32, HD), 1) < 16, share, 0.0)
+    for shift in (16, 32, 64):
+        share = share + pltpu.roll(share, shift, 1)
+    share = jnp.concatenate([share] * 4, axis=1)
+    share = jnp.where(iota((32, 512), 1) // 16 == iota((32, 512), 0), share, 0.0)
+    share = jnp.sum(share, axis=0, keepdims=True)
+    share = jnp.where(iota((16, 512), 1) % 16 == iota((16, 512), 0), share, 0.0)
+    high = share.astype(BF)
+    low = (share - high.astype(F32)).astype(BF)
+    acc = parts[:, 0:16, :].reshape(512, HD).astype(BF)
+    summed = jnp.dot(high, acc, preferred_element_type=F32) + jnp.dot(low, acc, preferred_element_type=F32)
+    attended = (summed + new_share * new_v).astype(BF)
     for i in range(out.shape[0]):
         out[i, :, :] = attended
 
@@ -289,7 +301,7 @@
     packed = pl.pallas_call(
         pack_body,
         out_shape=sds((16, END, HD), BF),
-        in_specs=[SM] + [pl.BlockSpec(memory_space=pltpu.HBM)] * 5,
+        in_specs=[SM, VM] + [pl.BlockSpec(memory_space=pltpu.HBM)] * 4,
         out_specs=pl.BlockSpec(memory_space=pltpu.HBM),
         scratch_shapes=[
             pltpu.VMEM((128, 1024), BF),
@@ -297,8 +309,7 @@
             pltpu.VMEM((64, 1024), BF),
             pltpu.VMEM((64, 1024), BF),
             pltpu.VMEM((16, END, HD), BF),
-            pltpu.VMEM((8, 256), BF),
-            pltpu.SemaphoreType.DMA((9,)),
+            pltpu.SemaphoreType.DMA((8,)),
         ],
         name="pack",
     )(lengths, hidden_in, prefix_keys, prefix_values, own_keys.reshape(64, 1024), own_values.reshape(64, 1024))
@@ -309,9 +320,9 @@
     parts = pl.pallas_call(
         project_body,
         grid=(1,),
-        out_shape=sds((32, 24, HD), BF),
+        out_shape=sds((768, HD), BF),
         in_specs=[x_spec, gain_spec, pl.BlockSpec((256, 512), lambda i: (0, 0))],
-        out_specs=pl.BlockSpec((32, 24, HD), lambda i: (0, 0, 0)),
+        out_specs=pl.BlockSpec((768, HD), lambda i: (0, 0)),
         compiler_params=params(),
         name="project",
     )(mine, gain, w_query)
@@ -343,7 +354,7 @@
     query = lax.all_to_all(query, "blk", 0, 0, tiled=True)
     partial = pl.pallas_call(
         attend_body,
-        out_shape=sds((32, 24, HD), BF),
+        out_shape=sds((768, HD), BF),
         in_specs=[SM] + [VM] * 5,
         out_specs=VM,
         compiler_params=params(),

time: 125 us -> 126 us (level)
  no operation moved by 1% of the time
where the time goes in v10:
time: 126 us; the launch traced here: 125 us
  blocking collectives  42.8 us (34%)
  starting transfers between devices  39 us (31%)
  waiting for transfers between devices  30.6 us (24%)
  Pallas kernels  10.2 us (8%)
  local copies, waits for them, and re-layouts  1.42 us (1%)
    all_to_all x1, waiting for transfers between devices, on_device(): mine = lax.all_to_all(packed, 'rows', 0, 0, tiled=True)  16.4 us
    all_to_all x1, blocking collectives, on_device(): partial = lax.all_to_all(partial, 'blk', 0, 0, tiled=True)  16 us
    all_to_all x1, starting transfers between devices, on_device(): parts = lax.all_to_all(parts, 'blk', 0, 0, tiled=True)  14.7 us
    all_to_all x1, blocking collectives, on_device(): attended = lax.all_to_all(attended, 'blk', 0, 0, tiled=True)  14 us
    all_to_all x1, blocking collectives, on_device(): mixed = lax.all_to_all(mixed.reshape(16, 8, 256), 'rows', 0, 0, tiled=True)  12.7 us
    all_to_all x1, starting transfers between devices, on_device(): mine = lax.all_to_all(packed, 'rows', 0, 0, tiled=True)  9.71 us
    all_to_all x1, waiting for transfers between devices, on_device(): query = lax.all_to_all(query, 'blk', 0, 0, tiled=True)  6.82 us
    all_to_all x1, waiting for transfers between devices, on_device(): parts = lax.all_to_all(parts, 'blk', 0, 0, tiled=True)  6.44 us
  transfers between devices with their start and end apart: 7, of which 4 were waited for; matrix products, arithmetic and copies ran while one was open for 0% of the time, Pallas kernels for 2%

profile of v10, /device:TPU:1, one launch (start us, length us, event | category | flops | bytes accessed | tf_op | source)
XLA Modules:
  0.0 125.1 jit_solution(255211874730511472)
XLA Ops:
  0.0 2.8 %pack.1 = bf16[16,208,128]{2,1,0:T(8,128)(2,1)} custom-call(s32[8]{0:T(128)} %lens.1, bf16[8,256]{1,0:T(8,128)(2,1)} %hidden.3, bf16[128,1024]{1,0:T(8,128)(2,1)} %keys_hbm.1, bf16[128,1024]{1,0:T(8,128)(2,1)} %values_hbm.1, bf16[64,1024]{1,0:T(8,128)(2,1)} %bitcast.13, bf16[64,1024]{1,0:T(8,128)(2,1)} %bitcast.14), custom_call_target="tpu_custom_call" | custom-call | tf_op jit(solution)/shard_map/pack/pallas_call | solution.py:301
  2.8 0.0 copy-start.5
  2.8 0.0 copy-start.1
  2.8 9.7 %all-to-all-start = ((bf16[16,208,128]{2,1,0:T(8,128)(2,1)}), bf16[16,208,128]{2,1,0:T(8,128)(2,1)S(1)}, u32[]{:S(2)}, u32[]{:S(2)}) async-start(bf16[16,208,128]{2,1,0:T(8,128)(2,1)} %pack.1), calls=%async_computation | async-start | bytes 1703936 | tf_op jit(solution)/shard_map/all_to_all | solution.py:316
  12.5 3.3 %collective-permute-start.1 = (bf16[256,128]{1,0:T(8,128)(2,1)S(1)}, bf16[256,128]{1,0:T(8,128)(2,1)S(1)}, u32[]{:S(2)}, u32[]{:S(2)}) collective-permute-start(bf16[256,128]{1,0:T(8,128)(2,1)S(1)} %copy-done.5), channel_id=1, source_target_pairs={{0,1},{1,3},{2,5},{3,7},{4,9},{5,11},{6,13},{7,15},{8,0},{9,2},{10... | collective-permute-start | bytes 196616 | tf_op jit(solution)/shard_map/ppermute | solution.py:300
  15.8 0.7 collective-permute-start
  16.5 0.6 copy-done.6
  17.2 16.4 %all-to-all-done.x_ref.mine = bf16[16,208,128]{2,1,0:T(8,128)(2,1)S(1)} async-done(((bf16[16,208,128]{2,1,0:T(8,128)(2,1)}), bf16[16,208,128]{2,1,0:T(8,128)(2,1)S(1)}, u32[]{:S(2)}, u32[]{:S(2)}) %all-to-all-start) | async-done | bytes 852000 | tf_op jit(solution)/shard_map/all_to_all | solution.py:316
  33.5 1.0 project.1
  34.5 14.7 %all-to-all-start.1 = ((bf16[32,24,128]{2,1,0:T(8,128)(2,1)}), bf16[32,24,128]{2,1,0:T(8,128)(2,1)S(1)}, u32[]{:S(2)}, u32[]{:S(2)}) async-start(bf16[32,24,128]{2,1,0:T(8,128)(2,1)} %bitcast.4), calls=%async_computation.1 | async-start | bytes 393216 | tf_op jit(solution)/shard_map/all_to_all | solution.py:330
  49.2 0.1 pad_add_fusion.who
  49.3 0.1 slice.3
  49.4 4.0 %collective-permute-start.2 = (bf16[16,192,128]{2,1,0:T(8,128)(2,1)S(1)}, bf16[16,192,128]{2,1,0:T(8,128)(2,1)S(1)}, u32[]{:S(2)}, u32[]{:S(2)}) collective-permute-start(bf16[16,192,128]{2,1,0:T(8,128)(2,1)S(1)} %slice.3), channel_id=1, source_target_pairs={{0,1},{1,0},{2,3},{3,2},{4,5},{5,4},{6,7},{7,6},{8,9},{9,8},{10,11... | collective-permute-start | bytes 2359304 | tf_op jit(solution)/shard_map/ppermute | solution.py:333
  53.4 0.1 dynamic_slice.3
  53.5 0.1 add_convert_fusion.1
  53.6 0.6 copy-done.3
  54.2 0.0 copy-done.4
  54.2 0.1 fusion
  54.3 6.4 %all-to-all-done.1 = bf16[32,24,128]{2,1,0:T(8,128)(2,1)S(1)} async-done(((bf16[32,24,128]{2,1,0:T(8,128)(2,1)}), bf16[32,24,128]{2,1,0:T(8,128)(2,1)S(1)}, u32[]{:S(2)}, u32[]{:S(2)}) %all-to-all-start.1) | async-done | bytes 196640 | tf_op jit(solution)/shard_map/all_to_all | solution.py:330
  60.8 1.4 %query.1 = (bf16[32,16,128]{2,1,0:T(8,128)(2,1)}, bf16[16,128]{1,0:T(8,128)(2,1)S(1)}, f32[16,128]{1,0:T(8,128)S(1)}) custom-call(s32[2]{0:T(128)S(1)} %pad_add_fusion.who, bf16[768,128]{1,0:T(8,128)(2,1)S(1)} %bitcast.11, f32[16,128]{1,0:T(8,128)S(1)} %get-tuple-element.32.cosine, f32[16,128]{1,0:T(8,128)S(1)} %get-tuple-element.31.sine), custom_call_target="tpu_custom_call" | custom-call | flops 3000000000 | bytes 1048576 | tf_op jit(solution)/shard_map/query/pallas_call | solution.py:345
  62.2 4.4 %all-to-all-start.2 = ((bf16[32,16,128]{2,1,0:T(8,128)(2,1)}), bf16[32,16,128]{2,1,0:T(8,128)(2,1)S(1)}, u32[]{:S(2)}, u32[]{:S(2)}) async-start(bf16[32,16,128]{2,1,0:T(8,128)(2,1)} %get-tuple-element.22), calls=%async_computation.2 | async-start | bytes 262144 | tf_op jit(solution)/shard_map/all_to_all | solution.py:354
  66.6 0.7 keyval.1
  67.3 2.1 %collective-permute-start.3 = (bf16[128,128]{1,0:T(8,128)(2,1)S(1)}, bf16[128,128]{1,0:T(8,128)(2,1)S(1)}, u32[]{:S(2)}, u32[]{:S(2)}) collective-permute-start(bf16[128,128]{1,0:T(8,128)(2,1)S(1)} %get-tuple-element.26), channel_id=1, source_target_pairs={{0,16},{16,0},{32,48},{48,32},{64,80},{80,64},{96,112},{112,96},{1... | collective-permute-start | bytes 98312 | tf_op jit(solution)/shard_map/ppermute | solution.py:344
  69.5 0.9 collective-permute-done.3.given
  70.4 6.8 %all-to-all-done.2.q_ref = bf16[32,16,128]{2,1,0:T(8,128)(2,1)S(1)} async-done(((bf16[32,16,128]{2,1,0:T(8,128)(2,1)}), bf16[32,16,128]{2,1,0:T(8,128)(2,1)S(1)}, u32[]{:S(2)}, u32[]{:S(2)}) %all-to-all-start.2) | async-done | bytes 131104 | tf_op jit(solution)/shard_map/all_to_all | solution.py:354
  77.3 2.9 %attend.1 = bf16[768,128]{1,0:T(8,128)(2,1)S(1)} custom-call(s32[2]{0:T(128)S(1)} %pad_add_fusion.who, bf16[16,208,128]{2,1,0:T(8,128)(2,1)S(1)} %all-to-all-done.x_ref.mine, bf16[16,192,128]{2,1,0:T(8,128)(2,1)S(1)} %collective-permute-done.2.other, bf16[32,16,128]{2,1,0:T(8,128)(2,1)S(1)} %all-to-all-done.2.q_ref, f32[128,128]{1,0:T(8,128)S(1)} %get-tuple-element.25.keep, ...), custom_call_target="tpu_custom_call" | custom-call | tf_op jit(solution)/shard_map/attend/pallas_call | solution.py:355
  80.2 16.0 %all_to_all.42 = bf16[32,24,128]{2,1,0:T(8,128)(2,1)S(1)} all-to-all(bf16[32,24,128]{2,1,0:T(8,128)(2,1)S(1)} %bitcast.9), channel_id=1, replica_groups=mesh['blk'=32,'rows'=16] {'blk'}, dimensions={0} | all-to-all | bytes 393216 | tf_op jit(solution)/shard_map/all_to_all | solution.py:363
  96.2 1.2 combine.1
  97.4 14.0 %all_to_all.43.att = bf16[32,16,128]{2,1,0:T(8,128)(2,1)S(1)} all-to-all(bf16[32,16,128]{2,1,0:T(8,128)(2,1)S(1)} %combine.1), channel_id=1, replica_groups=mesh['blk'=32,'rows'=16] {'blk'}, dimensions={0} | all-to-all | bytes 262144 | tf_op jit(solution)/shard_map/all_to_all | solution.py:372
  111.5 0.2 output.1
  111.7 12.7 %all_to_all.44 = bf16[16,8,256]{2,1,0:T(8,128)(2,1)S(1)} all-to-all(bf16[16,8,256]{2,1,0:T(8,128)(2,1)S(1)} %bitcast.12), channel_id=1, replica_groups=mesh['blk'=32,'rows'=16] {'rows'}, dimensions={0} | all-to-all | bytes 131072 | tf_op jit(solution)/shard_map/all_to_all | solution.py:381
  124.5 0.6 add_convert_fusion
  (16 shorter events, 0.1 us)
Async XLA Ops:
  2.8 9.7 %copy-start.5 = (bf16[256,128]{1,0:T(8,128)(2,1)S(1)}, bf16[256,128]{1,0:T(8,128)(2,1)}, u32[]{:S(2)}) copy-start(bf16[256,128]{1,0:T(8,128)(2,1)} %param.16) | copy-start | bytes 196612
  2.8 30.7 %copy-start.1 = (bf16[256,512]{1,0:T(8,128)(2,1)S(1)}, bf16[256,512]{1,0:T(8,128)(2,1)}, u32[]{:S(2)}) copy-start(bf16[256,512]{1,0:T(8,128)(2,1)} %wq.1) | copy-start | bytes 786436
  2.8 30.7 %all-to-all-start = ((bf16[16,208,128]{2,1,0:T(8,128)(2,1)}), bf16[16,208,128]{2,1,0:T(8,128)(2,1)S(1)}, u32[]{:S(2)}, u32[]{:S(2)}) async-start(bf16[16,208,128]{2,1,0:T(8,128)(2,1)} %pack.1), calls=%async_computation | async-start | bytes 1703936 | tf_op jit(solution)/shard_map/all_to_all | solution.py:316
  12.5 36.8 %collective-permute-start.1 = (bf16[256,128]{1,0:T(8,128)(2,1)S(1)}, bf16[256,128]{1,0:T(8,128)(2,1)S(1)}, u32[]{:S(2)}, u32[]{:S(2)}) collective-permute-start(bf16[256,128]{1,0:T(8,128)(2,1)S(1)} %copy-done.5), channel_id=1, source_target_pairs={{0,1},{1,3},{2,5},{3,7},{4,9},{5,11},{6,13},{7,15},{8,0},{9,2},{10... | collective-permute-start | bytes 196616 | tf_op jit(solution)/shard_map/ppermute | solution.py:300
  15.8 33.6 %collective-permute-start = (bf16[256,128]{1,0:T(8,128)(2,1)S(1)}, bf16[256,128]{1,0:T(8,128)(2,1)S(1)}, u32[]{:S(2)}, u32[]{:S(2)}) collective-permute-start(bf16[256,128]{1,0:T(8,128)(2,1)S(1)} %copy-done.5), channel_id=1, source_target_pairs={{0,0},{1,2},{2,4},{3,6},{4,8},{5,10},{6,12},{7,14},{8,1},{9,3},{10... | collective-permute-start | bytes 196616 | tf_op jit(solution)/shard_map/ppermute | solution.py:299
  16.5 0.7 copy-start.6
  34.5 26.3 %all-to-all-start.1 = ((bf16[32,24,128]{2,1,0:T(8,128)(2,1)}), bf16[32,24,128]{2,1,0:T(8,128)(2,1)S(1)}, u32[]{:S(2)}, u32[]{:S(2)}) async-start(bf16[32,24,128]{2,1,0:T(8,128)(2,1)} %bitcast.4), calls=%async_computation.1 | async-start | bytes 393216 | tf_op jit(solution)/shard_map/all_to_all | solution.py:330
  49.3 4.2 %copy-start.7 = (s32[128]{0:T(128)S(1)}, s32[128]{0:T(128)}, u32[]{:S(2)}) copy-start(s32[128]{0:T(128)} %param.22) | copy-start | bytes 1540
  49.4 27.9 %collective-permute-start.2 = (bf16[16,192,128]{2,1,0:T(8,128)(2,1)S(1)}, bf16[16,192,128]{2,1,0:T(8,128)(2,1)S(1)}, u32[]{:S(2)}, u32[]{:S(2)}) collective-permute-start(bf16[16,192,128]{2,1,0:T(8,128)(2,1)S(1)} %slice.3), channel_id=1, source_target_pairs={{0,1},{1,0},{2,3},{3,2},{4,5},{5,4},{6,7},{7,6},{8,9},{9,8},{10,11... | collective-permute-start | bytes 2359304 | tf_op jit(solution)/shard_map/ppermute | solution.py:333
  53.5 0.7 copy-start.3
  53.5 0.7 copy-start.4
  62.2 15.1 %all-to-all-start.2 = ((bf16[32,16,128]{2,1,0:T(8,128)(2,1)}), bf16[32,16,128]{2,1,0:T(8,128)(2,1)S(1)}, u32[]{:S(2)}, u32[]{:S(2)}) async-start(bf16[32,16,128]{2,1,0:T(8,128)(2,1)} %get-tuple-element.22), calls=%async_computation.2 | async-start | bytes 262144 | tf_op jit(solution)/shard_map/all_to_all | solution.py:354
  67.3 3.1 %collective-permute-start.3 = (bf16[128,128]{1,0:T(8,128)(2,1)S(1)}, bf16[128,128]{1,0:T(8,128)(2,1)S(1)}, u32[]{:S(2)}, u32[]{:S(2)}) collective-permute-start(bf16[128,128]{1,0:T(8,128)(2,1)S(1)} %get-tuple-element.26), channel_id=1, source_target_pairs={{0,16},{16,0},{32,48},{48,32},{64,80},{80,64},{96,112},{112,96},{1... | collective-permute-start | bytes 98312 | tf_op jit(solution)/shard_map/ppermute | solution.py:344
  96.2 15.3 %copy-start = (bf16[512,256]{1,0:T(8,128)(2,1)S(1)}, bf16[512,256]{1,0:T(8,128)(2,1)}, u32[]{:S(2)}) copy-start(bf16[512,256]{1,0:T(8,128)(2,1)} %w.1) | copy-start | bytes 786436
  97.4 14.1 %copy-start.2 = (bf16[8,256]{1,0:T(8,128)(2,1)S(1)}, bf16[8,256]{1,0:T(8,128)(2,1)}, u32[]{:S(2)}) copy-start(bf16[8,256]{1,0:T(8,128)(2,1)} %hidden.3) | copy-start | bytes 12292

commit v11 on v10

--- a/solution.py
+++ b/solution.py
@@ -228,30 +228,20 @@
     new_k = rotate(new_k, cosine[...], sine[...]).astype(BF).astype(F32)
     new_v = (twice(jnp.sum(rest[:, 1], axis=0)) * scale[...]).astype(BF).astype(F32)
     new = jnp.sum(q_own[...].astype(F32) * new_k, axis=1, keepdims=True) * (HD ** (-0.5) * LOG2E)
-    start = 16 * lax.rem(who[0], 8)
-    mine = iota((16, HD), 1) == start + iota((16, HD), 0)
-    new = jnp.sum(jnp.where(mine, new, 0.0), axis=0, keepdims=True)
-    stats = jnp.concatenate([parts[:, 16 + k, :] for k in range(4, 8)], axis=0).reshape(4, 32, HD)
-    peak = stats[0] + stats[1]
-    mass = stats[2] + stats[3]
-    top = jnp.maximum(jnp.max(peak, axis=0, keepdims=True), new)
-    shrink = jnp.exp2(peak - top)
-    new_w = jnp.exp2(new - top)
-    whole = jnp.sum(mass * shrink, axis=0, keepdims=True) + new_w
-    new_share = jnp.sum(jnp.where(mine, new_w / whole, 0.0), axis=1, keepdims=True)
-    share = pltpu.roll(shrink / whole, lax.rem(HD - start, HD), 1)
-    share = jnp.where(iota((32, HD), 1) < 16, share, 0.0)
-    for shift in (16, 32, 64):
-        share = share + pltpu.roll(share, shift, 1)
-    share = jnp.concatenate([share] * 4, axis=1)
-    share = jnp.where(iota((32, 512), 1) // 16 == iota((32, 512), 0), share, 0.0)
-    share = jnp.sum(share, axis=0, keepdims=True)
-    share = jnp.where(iota((16, 512), 1) % 16 == iota((16, 512), 0), share, 0.0)
-    high = share.astype(BF)
-    low = (share - high.astype(F32)).astype(BF)
-    acc = parts[:, 0:16, :].reshape(512, HD).astype(BF)
-    summed = jnp.dot(high, acc, preferred_element_type=F32) + jnp.dot(low, acc, preferred_element_type=F32)
-    attended = (summed + new_share * new_v).astype(BF)
+    mine = iota((16, HD), 1) == 16 * lax.rem(who[0], 8) + iota((16, HD), 0)
+    rest = parts[:, 16:24, :]
+    peak = rest[:, 4:5, :] + rest[:, 5:6, :]
+    mass = rest[:, 6:7, :] + rest[:, 7:8, :]
+    top = jnp.max(peak, axis=0)
+    shrink = jnp.exp2(peak - top[None])
+    whole = jnp.sum(mass * shrink, axis=0)
+    share = jnp.sum(jnp.where(mine[None], shrink, 0.0), axis=2, keepdims=True)
+    summed = jnp.sum(parts[:, 0:16, :] * share, axis=0)
+    top = jnp.sum(jnp.where(mine, top, 0.0), axis=1, keepdims=True)
+    whole = jnp.sum(jnp.where(mine, whole, 0.0), axis=1, keepdims=True)
+    over = jnp.maximum(top, new)
+    old_w, new_w = jnp.exp2(top - over), jnp.exp2(new - over)
+    attended = ((summed * old_w + new_w * new_v) / (whole * old_w + new_w)).astype(BF)
     for i in range(out.shape[0]):
         out[i, :, :] = attended
 

time: 126 us -> 125 us (level)
  no operation moved by 1% of the time
where the time goes in v11:
time: 125 us
  blocking collectives  42.8 us (34%)
  starting transfers between devices  39 us (31%)
  waiting for transfers between devices  30.6 us (24%)
  Pallas kernels  9.76 us (8%)
  local copies, waits for them, and re-layouts  1.42 us (1%)
    all_to_all x1, waiting for transfers between devices, on_device(): mine = lax.all_to_all(packed, 'rows', 0, 0, tiled=True)  16.4 us
    all_to_all x1, blocking collectives, on_device(): partial = lax.all_to_all(partial, 'blk', 0, 0, tiled=True)  16 us
    all_to_all x1, starting transfers between devices, on_device(): parts = lax.all_to_all(parts, 'blk', 0, 0, tiled=True)  14.7 us
    all_to_all x1, blocking collectives, on_device(): attended = lax.all_to_all(attended, 'blk', 0, 0, tiled=True)  14 us
    all_to_all x1, blocking collectives, on_device(): mixed = lax.all_to_all(mixed.reshape(16, 8, 256), 'rows', 0, 0, tiled=True)  12.7 us
    all_to_all x1, starting transfers between devices, on_device(): mine = lax.all_to_all(packed, 'rows', 0, 0, tiled=True)  9.71 us
    all_to_all x1, waiting for transfers between devices, on_device(): query = lax.all_to_all(query, 'blk', 0, 0, tiled=True)  6.82 us
    all_to_all x1, waiting for transfers between devices, on_device(): parts = lax.all_to_all(parts, 'blk', 0, 0, tiled=True)  6.44 us
  transfers between devices with their start and end apart: 7, of which 4 were waited for; matrix products, arithmetic and copies ran while one was open for 0% of the time, Pallas kernels for 2%

profile of v11, /device:TPU:1, one launch (start us, length us, event | category | flops | bytes accessed | tf_op | source)
XLA Modules:
  0.0 124.6 jit_solution(10047699453303086041)
XLA Ops:
  0.0 2.8 %pack.1 = bf16[16,208,128]{2,1,0:T(8,128)(2,1)} custom-call(s32[8]{0:T(128)} %lens.1, bf16[8,256]{1,0:T(8,128)(2,1)} %hidden.3, bf16[128,1024]{1,0:T(8,128)(2,1)} %keys_hbm.1, bf16[128,1024]{1,0:T(8,128)(2,1)} %values_hbm.1, bf16[64,1024]{1,0:T(8,128)(2,1)} %bitcast.13, bf16[64,1024]{1,0:T(8,128)(2,1)} %bitcast.14), custom_call_target="tpu_custom_call" | custom-call | tf_op jit(solution)/shard_map/pack/pallas_call | solution.py:291
  2.8 0.0 copy-start.5
  2.8 0.0 copy-start.1
  2.8 9.7 %all-to-all-start = ((bf16[16,208,128]{2,1,0:T(8,128)(2,1)}), bf16[16,208,128]{2,1,0:T(8,128)(2,1)S(1)}, u32[]{:S(2)}, u32[]{:S(2)}) async-start(bf16[16,208,128]{2,1,0:T(8,128)(2,1)} %pack.1), calls=%async_computation | async-start | bytes 1703936 | tf_op jit(solution)/shard_map/all_to_all | solution.py:306
  12.5 3.3 %collective-permute-start.1 = (bf16[256,128]{1,0:T(8,128)(2,1)S(1)}, bf16[256,128]{1,0:T(8,128)(2,1)S(1)}, u32[]{:S(2)}, u32[]{:S(2)}) collective-permute-start(bf16[256,128]{1,0:T(8,128)(2,1)S(1)} %copy-done.5), channel_id=1, source_target_pairs={{0,1},{1,3},{2,5},{3,7},{4,9},{5,11},{6,13},{7,15},{8,0},{9,2},{10... | collective-permute-start | bytes 196616 | tf_op jit(solution)/shard_map/ppermute | solution.py:290
  15.8 0.7 collective-permute-start
  16.5 0.6 copy-done.6
  17.2 16.4 %all-to-all-done.x_ref.mine = bf16[16,208,128]{2,1,0:T(8,128)(2,1)S(1)} async-done(((bf16[16,208,128]{2,1,0:T(8,128)(2,1)}), bf16[16,208,128]{2,1,0:T(8,128)(2,1)S(1)}, u32[]{:S(2)}, u32[]{:S(2)}) %all-to-all-start) | async-done | bytes 852000 | tf_op jit(solution)/shard_map/all_to_all | solution.py:306
  33.5 1.0 project.1
  34.5 14.7 %all-to-all-start.1 = ((bf16[32,24,128]{2,1,0:T(8,128)(2,1)}), bf16[32,24,128]{2,1,0:T(8,128)(2,1)S(1)}, u32[]{:S(2)}, u32[]{:S(2)}) async-start(bf16[32,24,128]{2,1,0:T(8,128)(2,1)} %bitcast.4), calls=%async_computation.1 | async-start | bytes 393216 | tf_op jit(solution)/shard_map/all_to_all | solution.py:320
  49.2 0.1 pad_add_fusion.who
  49.3 0.1 slice.3
  49.4 4.0 %collective-permute-start.2 = (bf16[16,192,128]{2,1,0:T(8,128)(2,1)S(1)}, bf16[16,192,128]{2,1,0:T(8,128)(2,1)S(1)}, u32[]{:S(2)}, u32[]{:S(2)}) collective-permute-start(bf16[16,192,128]{2,1,0:T(8,128)(2,1)S(1)} %slice.3), channel_id=1, source_target_pairs={{0,1},{1,0},{2,3},{3,2},{4,5},{5,4},{6,7},{7,6},{8,9},{9,8},{10,11... | collective-permute-start | bytes 2359304 | tf_op jit(solution)/shard_map/ppermute | solution.py:323
  53.4 0.1 dynamic_slice.3
  53.5 0.1 add_convert_fusion.1
  53.6 0.6 copy-done.3
  54.2 0.0 copy-done.4
  54.2 0.1 fusion
  54.3 6.4 %all-to-all-done.1 = bf16[32,24,128]{2,1,0:T(8,128)(2,1)S(1)} async-done(((bf16[32,24,128]{2,1,0:T(8,128)(2,1)}), bf16[32,24,128]{2,1,0:T(8,128)(2,1)S(1)}, u32[]{:S(2)}, u32[]{:S(2)}) %all-to-all-start.1) | async-done | bytes 196640 | tf_op jit(solution)/shard_map/all_to_all | solution.py:320
  60.8 1.4 %query.1 = (bf16[32,16,128]{2,1,0:T(8,128)(2,1)}, bf16[16,128]{1,0:T(8,128)(2,1)S(1)}, f32[16,128]{1,0:T(8,128)S(1)}) custom-call(s32[2]{0:T(128)S(1)} %pad_add_fusion.who, bf16[768,128]{1,0:T(8,128)(2,1)S(1)} %bitcast.11, f32[16,128]{1,0:T(8,128)S(1)} %get-tuple-element.32.cosine, f32[16,128]{1,0:T(8,128)S(1)} %get-tuple-element.31.sine), custom_call_target="tpu_custom_call" | custom-call | flops 3000000000 | bytes 1048576 | tf_op jit(solution)/shard_map/query/pallas_call | solution.py:335
  62.2 4.4 %all-to-all-start.2 = ((bf16[32,16,128]{2,1,0:T(8,128)(2,1)}), bf16[32,16,128]{2,1,0:T(8,128)(2,1)S(1)}, u32[]{:S(2)}, u32[]{:S(2)}) async-start(bf16[32,16,128]{2,1,0:T(8,128)(2,1)} %get-tuple-element.22), calls=%async_computation.2 | async-start | bytes 262144 | tf_op jit(solution)/shard_map/all_to_all | solution.py:344
  66.6 0.7 keyval.1
  67.3 2.1 %collective-permute-start.3 = (bf16[128,128]{1,0:T(8,128)(2,1)S(1)}, bf16[128,128]{1,0:T(8,128)(2,1)S(1)}, u32[]{:S(2)}, u32[]{:S(2)}) collective-permute-start(bf16[128,128]{1,0:T(8,128)(2,1)S(1)} %get-tuple-element.26), channel_id=1, source_target_pairs={{0,16},{16,0},{32,48},{48,32},{64,80},{80,64},{96,112},{112,96},{1... | collective-permute-start | bytes 98312 | tf_op jit(solution)/shard_map/ppermute | solution.py:334
  69.5 0.9 collective-permute-done.3.given
  70.4 6.8 %all-to-all-done.2.q_ref = bf16[32,16,128]{2,1,0:T(8,128)(2,1)S(1)} async-done(((bf16[32,16,128]{2,1,0:T(8,128)(2,1)}), bf16[32,16,128]{2,1,0:T(8,128)(2,1)S(1)}, u32[]{:S(2)}, u32[]{:S(2)}) %all-to-all-start.2) | async-done | bytes 131104 | tf_op jit(solution)/shard_map/all_to_all | solution.py:344
  77.3 2.9 %attend.1 = bf16[768,128]{1,0:T(8,128)(2,1)S(1)} custom-call(s32[2]{0:T(128)S(1)} %pad_add_fusion.who, bf16[16,208,128]{2,1,0:T(8,128)(2,1)S(1)} %all-to-all-done.x_ref.mine, bf16[16,192,128]{2,1,0:T(8,128)(2,1)S(1)} %collective-permute-done.2.other, bf16[32,16,128]{2,1,0:T(8,128)(2,1)S(1)} %all-to-all-done.2.q_ref, f32[128,128]{1,0:T(8,128)S(1)} %get-tuple-element.25.keep, ...), custom_call_target="tpu_custom_call" | custom-call | tf_op jit(solution)/shard_map/attend/pallas_call | solution.py:345
  80.2 16.0 %all_to_all.42 = bf16[32,24,128]{2,1,0:T(8,128)(2,1)S(1)} all-to-all(bf16[32,24,128]{2,1,0:T(8,128)(2,1)S(1)} %bitcast.9), channel_id=1, replica_groups=mesh['blk'=32,'rows'=16] {'blk'}, dimensions={0} | all-to-all | bytes 393216 | tf_op jit(solution)/shard_map/all_to_all | solution.py:353
  96.2 0.8 combine.1
  97.0 14.0 %all_to_all.43.att = bf16[32,16,128]{2,1,0:T(8,128)(2,1)S(1)} all-to-all(bf16[32,16,128]{2,1,0:T(8,128)(2,1)S(1)} %combine.1), channel_id=1, replica_groups=mesh['blk'=32,'rows'=16] {'blk'}, dimensions={0} | all-to-all | bytes 262144 | tf_op jit(solution)/shard_map/all_to_all | solution.py:362
  111.1 0.2 output.1
  111.3 12.7 %all_to_all.44 = bf16[16,8,256]{2,1,0:T(8,128)(2,1)S(1)} all-to-all(bf16[16,8,256]{2,1,0:T(8,128)(2,1)S(1)} %bitcast.12), channel_id=1, replica_groups=mesh['blk'=32,'rows'=16] {'rows'}, dimensions={0} | all-to-all | bytes 131072 | tf_op jit(solution)/shard_map/all_to_all | solution.py:371
  124.0 0.6 add_convert_fusion
  (16 shorter events, 0.1 us)
Async XLA Ops:
  2.8 9.7 %copy-start.5 = (bf16[256,128]{1,0:T(8,128)(2,1)S(1)}, bf16[256,128]{1,0:T(8,128)(2,1)}, u32[]{:S(2)}) copy-start(bf16[256,128]{1,0:T(8,128)(2,1)} %param.16) | copy-start | bytes 196612
  2.8 30.7 %copy-start.1 = (bf16[256,512]{1,0:T(8,128)(2,1)S(1)}, bf16[256,512]{1,0:T(8,128)(2,1)}, u32[]{:S(2)}) copy-start(bf16[256,512]{1,0:T(8,128)(2,1)} %wq.1) | copy-start | bytes 786436
  2.8 30.7 %all-to-all-start = ((bf16[16,208,128]{2,1,0:T(8,128)(2,1)}), bf16[16,208,128]{2,1,0:T(8,128)(2,1)S(1)}, u32[]{:S(2)}, u32[]{:S(2)}) async-start(bf16[16,208,128]{2,1,0:T(8,128)(2,1)} %pack.1), calls=%async_computation | async-start | bytes 1703936 | tf_op jit(solution)/shard_map/all_to_all | solution.py:306
  12.5 36.8 %collective-permute-start.1 = (bf16[256,128]{1,0:T(8,128)(2,1)S(1)}, bf16[256,128]{1,0:T(8,128)(2,1)S(1)}, u32[]{:S(2)}, u32[]{:S(2)}) collective-permute-start(bf16[256,128]{1,0:T(8,128)(2,1)S(1)} %copy-done.5), channel_id=1, source_target_pairs={{0,1},{1,3},{2,5},{3,7},{4,9},{5,11},{6,13},{7,15},{8,0},{9,2},{10... | collective-permute-start | bytes 196616 | tf_op jit(solution)/shard_map/ppermute | solution.py:290
  15.8 33.6 %collective-permute-start = (bf16[256,128]{1,0:T(8,128)(2,1)S(1)}, bf16[256,128]{1,0:T(8,128)(2,1)S(1)}, u32[]{:S(2)}, u32[]{:S(2)}) collective-permute-start(bf16[256,128]{1,0:T(8,128)(2,1)S(1)} %copy-done.5), channel_id=1, source_target_pairs={{0,0},{1,2},{2,4},{3,6},{4,8},{5,10},{6,12},{7,14},{8,1},{9,3},{10... | collective-permute-start | bytes 196616 | tf_op jit(solution)/shard_map/ppermute | solution.py:289
  16.5 0.7 copy-start.6
  34.5 26.3 %all-to-all-start.1 = ((bf16[32,24,128]{2,1,0:T(8,128)(2,1)}), bf16[32,24,128]{2,1,0:T(8,128)(2,1)S(1)}, u32[]{:S(2)}, u32[]{:S(2)}) async-start(bf16[32,24,128]{2,1,0:T(8,128)(2,1)} %bitcast.4), calls=%async_computation.1 | async-start | bytes 393216 | tf_op jit(solution)/shard_map/all_to_all | solution.py:320
  49.3 4.2 %copy-start.7 = (s32[128]{0:T(128)S(1)}, s32[128]{0:T(128)}, u32[]{:S(2)}) copy-start(s32[128]{0:T(128)} %param.22) | copy-start | bytes 1540
  49.4 27.9 %collective-permute-start.2 = (bf16[16,192,128]{2,1,0:T(8,128)(2,1)S(1)}, bf16[16,192,128]{2,1,0:T(8,128)(2,1)S(1)}, u32[]{:S(2)}, u32[]{:S(2)}) collective-permute-start(bf16[16,192,128]{2,1,0:T(8,128)(2,1)S(1)} %slice.3), channel_id=1, source_target_pairs={{0,1},{1,0},{2,3},{3,2},{4,5},{5,4},{6,7},{7,6},{8,9},{9,8},{10,11... | collective-permute-start | bytes 2359304 | tf_op jit(solution)/shard_map/ppermute | solution.py:323
  53.5 0.7 copy-start.3
  53.5 0.7 copy-start.4
  62.2 15.1 %all-to-all-start.2 = ((bf16[32,16,128]{2,1,0:T(8,128)(2,1)}), bf16[32,16,128]{2,1,0:T(8,128)(2,1)S(1)}, u32[]{:S(2)}, u32[]{:S(2)}) async-start(bf16[32,16,128]{2,1,0:T(8,128)(2,1)} %get-tuple-element.22), calls=%async_computation.2 | async-start | bytes 262144 | tf_op jit(solution)/shard_map/all_to_all | solution.py:344
  67.3 3.1 %collective-permute-start.3 = (bf16[128,128]{1,0:T(8,128)(2,1)S(1)}, bf16[128,128]{1,0:T(8,128)(2,1)S(1)}, u32[]{:S(2)}, u32[]{:S(2)}) collective-permute-start(bf16[128,128]{1,0:T(8,128)(2,1)S(1)} %get-tuple-element.26), channel_id=1, source_target_pairs={{0,16},{16,0},{32,48},{48,32},{64,80},{80,64},{96,112},{112,96},{1... | collective-permute-start | bytes 98312 | tf_op jit(solution)/shard_map/ppermute | solution.py:334
  96.2 14.8 %copy-start = (bf16[512,256]{1,0:T(8,128)(2,1)S(1)}, bf16[512,256]{1,0:T(8,128)(2,1)}, u32[]{:S(2)}) copy-start(bf16[512,256]{1,0:T(8,128)(2,1)} %w.1) | copy-start | bytes 786436
  97.0 14.1 %copy-start.2 = (bf16[8,256]{1,0:T(8,128)(2,1)S(1)}, bf16[8,256]{1,0:T(8,128)(2,1)}, u32[]{:S(2)}) copy-start(bf16[8,256]{1,0:T(8,128)(2,1)} %hidden.3) | copy-start | bytes 12292

commit v12 on v11

--- a/solution.py
+++ b/solution.py
@@ -304,7 +304,8 @@
         name="pack",
     )(lengths, hidden_in, prefix_keys, prefix_values, own_keys.reshape(64, 1024), own_values.reshape(64, 1024))
     mine = lax.all_to_all(packed, "rows", 0, 0, tiled=True)
-    gain = norm_gain.reshape(1, 256)
+    cosine, sine = rotary_tables(jnp.concatenate([lax.dynamic_slice_in_dim(positions, 4 * b, 4, 0)] * 4))
+    gain, cosine, sine = lax.optimization_barrier((norm_gain.reshape(1, 256), cosine, sine))
     x_spec = pl.BlockSpec((16, END - X0, HD), lambda i: (0, X0 // 16, 0))
     gain_spec = pl.BlockSpec((1, 256), lambda i: (0, 0))
     parts = pl.pallas_call(
@@ -316,9 +317,8 @@
         compiler_params=params(),
         name="project",
     )(mine, gain, w_query)
-    positions, parts, mine = lax.optimization_barrier((positions, parts, mine))
+    parts, mine = lax.optimization_barrier((parts, mine))
     parts = lax.all_to_all(parts, "blk", 0, 0, tiled=True)
-    cosine, sine = rotary_tables(jnp.concatenate([lax.dynamic_slice_in_dim(positions, 4 * b, 4, 0)] * 4))
     half, first_w, second_w = lax.optimization_barrier((mine[:, :X0, :], first_w, second_w))
     other = lax.ppermute(half, "rows", [(i, i ^ 1) for i in range(16)])
     keep, give = pl.pallas_call(
@@ -338,9 +338,10 @@
         in_specs=[SM, VM, VM, VM],
         out_specs=(VM, VM, VM),
         compiler_params=params(),
-        cost_estimate=pl.CostEstimate(flops=3*10**9, bytes_accessed=1 << 20, transcendentals=0),
+        cost_estimate=pl.CostEstimate(flops=2*10**9, bytes_accessed=1 << 20, transcendentals=0),
         name="query",
     )(who, parts, cosine, sine)
+    query, given = lax.optimization_barrier((query, given))
     query = lax.all_to_all(query, "blk", 0, 0, tiled=True)
     partial = pl.pallas_call(
         attend_body,

time: 125 us -> 125 us (level)
  blocking collectives: 42.8 us -> 58.5 us
  waiting for transfers between devices: 30.6 us -> 19.1 us
  starting transfers between devices: 39 us -> 34.8 us
    all_to_all x0 -> x1, blocking collectives: none -> 16.6 us  [on_device(): query = lax.all_to_all(query, 'blk', 0, 0, tiled=True)]
    all_to_all x1 -> x0, waiting for transfers between devices: 6.82 us -> none  [on_device(): query = lax.all_to_all(query, 'blk', 0, 0, tiled=True)]
    all_to_all x1 -> x0, starting transfers between devices: 4.45 us -> none  [on_device(): query = lax.all_to_all(query, 'blk', 0, 0, tiled=True)]
    all_to_all x1, waiting for transfers between devices: 6.44 us -> 4.16 us  [on_device(): parts = lax.all_to_all(parts, 'blk', 0, 0, tiled=True)]
    all_to_all x1, waiting for transfers between devices: 16.4 us -> 15 us  [on_device(): mine = lax.all_to_all(packed, 'rows', 0, 0, tiled=True)]
  transfers between devices with their start and end apart: 7 -> 6, of which waited for: 4 -> 2; matrix products, arithmetic and copies ran while one was open for 0% -> 0% of each run, Pallas kernels for 2% -> 2%
where the time goes in v12:
time: 125 us; the launch traced here: 124 us
  blocking collectives  58.5 us (47%)
  starting transfers between devices  34.8 us (28%)
  waiting for transfers between devices  19.1 us (15%)
  Pallas kernels  9.06 us (7%)
  local copies, waits for them, and re-layouts  1.95 us (2%)
    all_to_all x1, blocking collectives, on_device(): query = lax.all_to_all(query, 'blk', 0, 0, tiled=True)  16.6 us
    all_to_all x1, blocking collectives, on_device(): partial = lax.all_to_all(partial, 'blk', 0, 0, tiled=True)  15.3 us
    all_to_all x1, waiting for transfers between devices, on_device(): mine = lax.all_to_all(packed, 'rows', 0, 0, tiled=True)  15 us
    all_to_all x1, starting transfers between devices, on_device(): parts = lax.all_to_all(parts, 'blk', 0, 0, tiled=True)  14.7 us
    all_to_all x1, blocking collectives, on_device(): attended = lax.all_to_all(attended, 'blk', 0, 0, tiled=True)  14 us
    all_to_all x1, blocking collectives, on_device(): mixed = lax.all_to_all(mixed.reshape(16, 8, 256), 'rows', 0, 0, tiled=True)  12.6 us
    all_to_all x1, starting transfers between devices, on_device(): mine = lax.all_to_all(packed, 'rows', 0, 0, tiled=True)  9.71 us
    all_to_all x1, waiting for transfers between devices, on_device(): parts = lax.all_to_all(parts, 'blk', 0, 0, tiled=True)  4.16 us
  transfers between devices with their start and end apart: 6, of which 2 were waited for; matrix products, arithmetic and copies ran while one was open for 0% of the time, Pallas kernels for 2%

profile of v12, /device:TPU:1, one launch (start us, length us, event | category | flops | bytes accessed | tf_op | source)
XLA Modules:
  0.0 124.5 jit_solution(12103658028552840953)
XLA Ops:
  0.0 2.7 %pack.1 = bf16[16,208,128]{2,1,0:T(8,128)(2,1)} custom-call(s32[8]{0:T(128)} %lens.1, bf16[8,256]{1,0:T(8,128)(2,1)} %hidden.3, bf16[128,1024]{1,0:T(8,128)(2,1)} %keys_hbm.1, bf16[128,1024]{1,0:T(8,128)(2,1)} %values_hbm.1, bf16[64,1024]{1,0:T(8,128)(2,1)} %bitcast.13, bf16[64,1024]{1,0:T(8,128)(2,1)} %bitcast.14), custom_call_target="tpu_custom_call" | custom-call | tf_op jit(solution)/shard_map/pack/pallas_call | solution.py:291
  2.7 0.0 copy-start.5
  2.7 0.0 copy-start.1
  2.8 9.7 %all-to-all-start = ((bf16[16,208,128]{2,1,0:T(8,128)(2,1)}), bf16[16,208,128]{2,1,0:T(8,128)(2,1)S(1)}, u32[]{:S(2)}, u32[]{:S(2)}) async-start(bf16[16,208,128]{2,1,0:T(8,128)(2,1)} %pack.1), calls=%async_computation | async-start | bytes 1703936 | tf_op jit(solution)/shard_map/all_to_all | solution.py:306
  12.5 3.3 %collective-permute-start.1 = (bf16[256,128]{1,0:T(8,128)(2,1)S(1)}, bf16[256,128]{1,0:T(8,128)(2,1)S(1)}, u32[]{:S(2)}, u32[]{:S(2)}) collective-permute-start(bf16[256,128]{1,0:T(8,128)(2,1)S(1)} %copy-done.5), channel_id=1, source_target_pairs={{0,1},{1,3},{2,5},{3,7},{4,9},{5,11},{6,13},{7,15},{8,0},{9,2},{10... | collective-permute-start | bytes 196616 | tf_op jit(solution)/shard_map/ppermute | solution.py:290
  15.8 0.7 collective-permute-start
  16.4 0.0 copy-start.6
  16.4 0.6 copy-done.6
  17.1 0.1 dynamic_slice.3
  17.2 0.1 add_convert_fusion.1
  17.3 0.6 copy-done.3
  17.8 0.0 copy-done.4
  17.8 0.1 fusion
  18.0 0.5 copy-done.7
  18.5 15.0 %all-to-all-done.x_ref.mine = bf16[16,208,128]{2,1,0:T(8,128)(2,1)S(1)} async-done(((bf16[16,208,128]{2,1,0:T(8,128)(2,1)}), bf16[16,208,128]{2,1,0:T(8,128)(2,1)S(1)}, u32[]{:S(2)}, u32[]{:S(2)}) %all-to-all-start) | async-done | bytes 852000 | tf_op jit(solution)/shard_map/all_to_all | solution.py:306
  33.5 1.0 project.1
  34.4 14.7 %all-to-all-start.1 = ((bf16[32,24,128]{2,1,0:T(8,128)(2,1)}), bf16[32,24,128]{2,1,0:T(8,128)(2,1)S(1)}, u32[]{:S(2)}, u32[]{:S(2)}) async-start(bf16[32,24,128]{2,1,0:T(8,128)(2,1)} %bitcast.4), calls=%async_computation.1 | async-start | bytes 393216 | tf_op jit(solution)/shard_map/all_to_all | solution.py:321
  49.1 0.1 slice.3
  49.2 4.0 %collective-permute-start.2 = (bf16[16,192,128]{2,1,0:T(8,128)(2,1)S(1)}, bf16[16,192,128]{2,1,0:T(8,128)(2,1)S(1)}, u32[]{:S(2)}, u32[]{:S(2)}) collective-permute-start(bf16[16,192,128]{2,1,0:T(8,128)(2,1)S(1)} %slice.3), channel_id=1, source_target_pairs={{0,1},{1,0},{2,3},{3,2},{4,5},{5,4},{6,7},{7,6},{8,9},{9,8},{10,11... | collective-permute-start | bytes 2359304 | tf_op jit(solution)/shard_map/ppermute | solution.py:323
  53.3 0.1 pad_add_fusion.who
  53.4 0.7 keyval.1
  54.1 2.4 %collective-permute-start.3 = (bf16[128,128]{1,0:T(8,128)(2,1)S(1)}, bf16[128,128]{1,0:T(8,128)(2,1)S(1)}, u32[]{:S(2)}, u32[]{:S(2)}) collective-permute-start(bf16[128,128]{1,0:T(8,128)(2,1)S(1)} %get-tuple-element.31), channel_id=1, source_target_pairs={{0,16},{16,0},{32,48},{48,32},{64,80},{80,64},{96,112},{112,96},{1... | collective-permute-start | bytes 98312 | tf_op jit(solution)/shard_map/ppermute | solution.py:334
  56.5 4.2 %all-to-all-done.1 = bf16[32,24,128]{2,1,0:T(8,128)(2,1)S(1)} async-done(((bf16[32,24,128]{2,1,0:T(8,128)(2,1)}), bf16[32,24,128]{2,1,0:T(8,128)(2,1)S(1)}, u32[]{:S(2)}, u32[]{:S(2)}) %all-to-all-start.1) | async-done | bytes 196640 | tf_op jit(solution)/shard_map/all_to_all | solution.py:321
  60.7 0.7 query.1
  61.5 16.6 %all_to_all.42.q_ref = bf16[32,16,128]{2,1,0:T(8,128)(2,1)S(1)} all-to-all(bf16[32,16,128]{2,1,0:T(8,128)(2,1)S(1)} %get-tuple-element.32), channel_id=1, replica_groups=mesh['blk'=32,'rows'=16] {'blk'}, dimensions={0} | all-to-all | bytes 262144 | tf_op jit(solution)/shard_map/all_to_all | solution.py:345
  78.0 2.9 %attend.1 = bf16[768,128]{1,0:T(8,128)(2,1)S(1)} custom-call(s32[2]{0:T(128)S(1)} %pad_add_fusion.who, bf16[16,208,128]{2,1,0:T(8,128)(2,1)S(1)} %all-to-all-done.x_ref.mine, bf16[16,192,128]{2,1,0:T(8,128)(2,1)S(1)} %collective-permute-done.2.other, bf16[32,16,128]{2,1,0:T(8,128)(2,1)S(1)} %all_to_all.42.q_ref, f32[128,128]{1,0:T(8,128)S(1)} %get-tuple-element.33.keep, ...), custom_call_target="tpu_custom_call" | custom-call | tf_op jit(solution)/shard_map/attend/pallas_call | solution.py:346
  81.0 15.3 %all_to_all.43 = bf16[32,24,128]{2,1,0:T(8,128)(2,1)S(1)} all-to-all(bf16[32,24,128]{2,1,0:T(8,128)(2,1)S(1)} %bitcast.9), channel_id=1, replica_groups=mesh['blk'=32,'rows'=16] {'blk'}, dimensions={0} | all-to-all | bytes 393216 | tf_op jit(solution)/shard_map/all_to_all | solution.py:354
  96.3 0.8 combine.1
  97.0 14.0 %all_to_all.44.att = bf16[32,16,128]{2,1,0:T(8,128)(2,1)S(1)} all-to-all(bf16[32,16,128]{2,1,0:T(8,128)(2,1)S(1)} %combine.1), channel_id=1, replica_groups=mesh['blk'=32,'rows'=16] {'blk'}, dimensions={0} | all-to-all | bytes 262144 | tf_op jit(solution)/shard_map/all_to_all | solution.py:363
  111.0 0.2 output.1
  111.3 12.6 %all_to_all.45 = bf16[16,8,256]{2,1,0:T(8,128)(2,1)S(1)} all-to-all(bf16[16,8,256]{2,1,0:T(8,128)(2,1)S(1)} %bitcast.12), channel_id=1, replica_groups=mesh['blk'=32,'rows'=16] {'rows'}, dimensions={0} | all-to-all | bytes 131072 | tf_op jit(solution)/shard_map/all_to_all | solution.py:372
  123.9 0.6 add_convert_fusion
  (15 shorter events, 0.1 us)
Async XLA Ops:
  2.7 9.7 %copy-start.5 = (bf16[256,128]{1,0:T(8,128)(2,1)S(1)}, bf16[256,128]{1,0:T(8,128)(2,1)}, u32[]{:S(2)}) copy-start(bf16[256,128]{1,0:T(8,128)(2,1)} %param.16) | copy-start | bytes 196612
  2.7 30.7 %copy-start.1 = (bf16[256,512]{1,0:T(8,128)(2,1)S(1)}, bf16[256,512]{1,0:T(8,128)(2,1)}, u32[]{:S(2)}) copy-start(bf16[256,512]{1,0:T(8,128)(2,1)} %wq.1) | copy-start | bytes 786436
  2.8 30.7 %all-to-all-start = ((bf16[16,208,128]{2,1,0:T(8,128)(2,1)}), bf16[16,208,128]{2,1,0:T(8,128)(2,1)S(1)}, u32[]{:S(2)}, u32[]{:S(2)}) async-start(bf16[16,208,128]{2,1,0:T(8,128)(2,1)} %pack.1), calls=%async_computation | async-start | bytes 1703936 | tf_op jit(solution)/shard_map/all_to_all | solution.py:306
  12.5 36.7 %collective-permute-start.1 = (bf16[256,128]{1,0:T(8,128)(2,1)S(1)}, bf16[256,128]{1,0:T(8,128)(2,1)S(1)}, u32[]{:S(2)}, u32[]{:S(2)}) collective-permute-start(bf16[256,128]{1,0:T(8,128)(2,1)S(1)} %copy-done.5), channel_id=1, source_target_pairs={{0,1},{1,3},{2,5},{3,7},{4,9},{5,11},{6,13},{7,15},{8,0},{9,2},{10... | collective-permute-start | bytes 196616 | tf_op jit(solution)/shard_map/ppermute | solution.py:290
  15.8 33.5 %collective-permute-start = (bf16[256,128]{1,0:T(8,128)(2,1)S(1)}, bf16[256,128]{1,0:T(8,128)(2,1)S(1)}, u32[]{:S(2)}, u32[]{:S(2)}) collective-permute-start(bf16[256,128]{1,0:T(8,128)(2,1)S(1)} %copy-done.5), channel_id=1, source_target_pairs={{0,0},{1,2},{2,4},{3,6},{4,8},{5,10},{6,12},{7,14},{8,1},{9,3},{10... | collective-permute-start | bytes 196616 | tf_op jit(solution)/shard_map/ppermute | solution.py:289
  16.4 0.7 copy-start.6
  17.2 0.7 copy-start.3
  17.2 0.7 copy-start.4
  17.8 0.7 copy-start.7
  34.4 26.3 %all-to-all-start.1 = ((bf16[32,24,128]{2,1,0:T(8,128)(2,1)}), bf16[32,24,128]{2,1,0:T(8,128)(2,1)S(1)}, u32[]{:S(2)}, u32[]{:S(2)}) async-start(bf16[32,24,128]{2,1,0:T(8,128)(2,1)} %bitcast.4), calls=%async_computation.1 | async-start | bytes 393216 | tf_op jit(solution)/shard_map/all_to_all | solution.py:321
  49.2 28.8 %collective-permute-start.2 = (bf16[16,192,128]{2,1,0:T(8,128)(2,1)S(1)}, bf16[16,192,128]{2,1,0:T(8,128)(2,1)S(1)}, u32[]{:S(2)}, u32[]{:S(2)}) collective-permute-start(bf16[16,192,128]{2,1,0:T(8,128)(2,1)S(1)} %slice.3), channel_id=1, source_target_pairs={{0,1},{1,0},{2,3},{3,2},{4,5},{5,4},{6,7},{7,6},{8,9},{9,8},{10,11... | collective-permute-start | bytes 2359304 | tf_op jit(solution)/shard_map/ppermute | solution.py:323
  54.1 7.4 %collective-permute-start.3 = (bf16[128,128]{1,0:T(8,128)(2,1)S(1)}, bf16[128,128]{1,0:T(8,128)(2,1)S(1)}, u32[]{:S(2)}, u32[]{:S(2)}) collective-permute-start(bf16[128,128]{1,0:T(8,128)(2,1)S(1)} %get-tuple-element.31), channel_id=1, source_target_pairs={{0,16},{16,0},{32,48},{48,32},{64,80},{80,64},{96,112},{112,96},{1... | collective-permute-start | bytes 98312 | tf_op jit(solution)/shard_map/ppermute | solution.py:334
  96.3 14.8 %copy-start = (bf16[512,256]{1,0:T(8,128)(2,1)S(1)}, bf16[512,256]{1,0:T(8,128)(2,1)}, u32[]{:S(2)}) copy-start(bf16[512,256]{1,0:T(8,128)(2,1)} %w.1) | copy-start | bytes 786436
  97.0 14.0 %copy-start.2 = (bf16[8,256]{1,0:T(8,128)(2,1)S(1)}, bf16[8,256]{1,0:T(8,128)(2,1)}, u32[]{:S(2)}) copy-start(bf16[8,256]{1,0:T(8,128)(2,1)} %hidden.3) | copy-start | bytes 12292

commit v13 on v12

--- a/solution.py
+++ b/solution.py
@@ -341,7 +341,6 @@
         cost_estimate=pl.CostEstimate(flops=2*10**9, bytes_accessed=1 << 20, transcendentals=0),
         name="query",
     )(who, parts, cosine, sine)
-    query, given = lax.optimization_barrier((query, given))
     query = lax.all_to_all(query, "blk", 0, 0, tiled=True)
     partial = pl.pallas_call(
         attend_body,

time: 125 us -> 125 us (level)
  blocking collectives: 58.5 us -> 42.7 us
  waiting for transfers between devices: 19.1 us -> 30.1 us
  starting transfers between devices: 34.8 us -> 39 us
    all_to_all x1 -> x0, blocking collectives: 16.6 us -> none  [on_device(): query = lax.all_to_all(query, 'blk', 0, 0, tiled=True)]
    all_to_all x0 -> x1, waiting for transfers between devices: none -> 6.82 us  [on_device(): query = lax.all_to_all(query, 'blk', 0, 0, tiled=True)]
    all_to_all x0 -> x1, starting transfers between devices: none -> 4.45 us  [on_device(): query = lax.all_to_all(query, 'blk', 0, 0, tiled=True)]
    all_to_all x1, waiting for transfers between devices: 4.16 us -> 7.32 us  [on_device(): parts = lax.all_to_all(parts, 'blk', 0, 0, tiled=True)]
  transfers between devices with their start and end apart: 6 -> 7, of which waited for: 2 -> 4; matrix products, arithmetic and copies ran while one was open for 0% -> 0% of each run, Pallas kernels for 2% -> 2%
where the time goes in v13:
time: 125 us
  blocking collectives  42.7 us (34%)
  starting transfers between devices  39 us (31%)
  waiting for transfers between devices  30.1 us (24%)
  Pallas kernels  9.77 us (8%)
  local copies, waits for them, and re-layouts  1.95 us (2%)
    all_to_all x1, blocking collectives, on_device(): partial = lax.all_to_all(partial, 'blk', 0, 0, tiled=True)  16 us
    all_to_all x1, waiting for transfers between devices, on_device(): mine = lax.all_to_all(packed, 'rows', 0, 0, tiled=True)  15 us
    all_to_all x1, starting transfers between devices, on_device(): parts = lax.all_to_all(parts, 'blk', 0, 0, tiled=True)  14.7 us
    all_to_all x1, blocking collectives, on_device(): attended = lax.all_to_all(attended, 'blk', 0, 0, tiled=True)  14 us
    all_to_all x1, blocking collectives, on_device(): mixed = lax.all_to_all(mixed.reshape(16, 8, 256), 'rows', 0, 0, tiled=True)  12.7 us
    all_to_all x1, starting transfers between devices, on_device(): mine = lax.all_to_all(packed, 'rows', 0, 0, tiled=True)  9.71 us
    all_to_all x1, waiting for transfers between devices, on_device(): parts = lax.all_to_all(parts, 'blk', 0, 0, tiled=True)  7.32 us
    all_to_all x1, waiting for transfers between devices, on_device(): query = lax.all_to_all(query, 'blk', 0, 0, tiled=True)  6.82 us
  transfers between devices with their start and end apart: 7, of which 4 were waited for; matrix products, arithmetic and copies ran while one was open for 0% of the time, Pallas kernels for 2%

profile of v13, /device:TPU:1, one launch (start us, length us, event | category | flops | bytes accessed | tf_op | source)
XLA Modules:
  0.0 124.5 jit_solution(17826149496726585698)
XLA Ops:
  0.0 2.8 %pack.1 = bf16[16,208,128]{2,1,0:T(8,128)(2,1)} custom-call(s32[8]{0:T(128)} %lens.1, bf16[8,256]{1,0:T(8,128)(2,1)} %hidden.3, bf16[128,1024]{1,0:T(8,128)(2,1)} %keys_hbm.1, bf16[128,1024]{1,0:T(8,128)(2,1)} %values_hbm.1, bf16[64,1024]{1,0:T(8,128)(2,1)} %bitcast.13, bf16[64,1024]{1,0:T(8,128)(2,1)} %bitcast.14), custom_call_target="tpu_custom_call" | custom-call | tf_op jit(solution)/shard_map/pack/pallas_call | solution.py:291
  2.8 0.0 copy-start.5
  2.8 9.7 %all-to-all-start = ((bf16[16,208,128]{2,1,0:T(8,128)(2,1)}), bf16[16,208,128]{2,1,0:T(8,128)(2,1)S(1)}, u32[]{:S(2)}, u32[]{:S(2)}) async-start(bf16[16,208,128]{2,1,0:T(8,128)(2,1)} %pack.1), calls=%async_computation | async-start | bytes 1703936 | tf_op jit(solution)/shard_map/all_to_all | solution.py:306
  12.5 3.3 %collective-permute-start.1 = (bf16[256,128]{1,0:T(8,128)(2,1)S(1)}, bf16[256,128]{1,0:T(8,128)(2,1)S(1)}, u32[]{:S(2)}, u32[]{:S(2)}) collective-permute-start(bf16[256,128]{1,0:T(8,128)(2,1)S(1)} %copy-done.5), channel_id=1, source_target_pairs={{0,1},{1,3},{2,5},{3,7},{4,9},{5,11},{6,13},{7,15},{8,0},{9,2},{10... | collective-permute-start | bytes 196616 | tf_op jit(solution)/shard_map/ppermute | solution.py:290
  15.8 0.7 collective-permute-start
  16.5 0.6 copy-done.6
  17.1 0.1 dynamic_slice.3
  17.2 0.1 add_convert_fusion.1
  17.3 0.6 copy-done.3
  17.9 0.0 copy-done.4
  17.9 0.1 fusion
  18.0 0.5 copy-done.7
  18.6 15.0 %all-to-all-done.x_ref.mine = bf16[16,208,128]{2,1,0:T(8,128)(2,1)S(1)} async-done(((bf16[16,208,128]{2,1,0:T(8,128)(2,1)}), bf16[16,208,128]{2,1,0:T(8,128)(2,1)S(1)}, u32[]{:S(2)}, u32[]{:S(2)}) %all-to-all-start) | async-done | bytes 852000 | tf_op jit(solution)/shard_map/all_to_all | solution.py:306
  33.5 1.0 project.1
  34.5 14.7 %all-to-all-start.1 = ((bf16[32,24,128]{2,1,0:T(8,128)(2,1)}), bf16[32,24,128]{2,1,0:T(8,128)(2,1)S(1)}, u32[]{:S(2)}, u32[]{:S(2)}) async-start(bf16[32,24,128]{2,1,0:T(8,128)(2,1)} %bitcast.4), calls=%async_computation.1 | async-start | bytes 393216 | tf_op jit(solution)/shard_map/all_to_all | solution.py:321
  49.2 0.1 slice.3
  49.3 4.0 %collective-permute-start.2 = (bf16[16,192,128]{2,1,0:T(8,128)(2,1)S(1)}, bf16[16,192,128]{2,1,0:T(8,128)(2,1)S(1)}, u32[]{:S(2)}, u32[]{:S(2)}) collective-permute-start(bf16[16,192,128]{2,1,0:T(8,128)(2,1)S(1)} %slice.3), channel_id=1, source_target_pairs={{0,1},{1,0},{2,3},{3,2},{4,5},{5,4},{6,7},{7,6},{8,9},{9,8},{10,11... | collective-permute-start | bytes 2359304 | tf_op jit(solution)/shard_map/ppermute | solution.py:323
  53.3 0.1 pad_add_fusion.who
  53.4 7.3 %all-to-all-done.1 = bf16[32,24,128]{2,1,0:T(8,128)(2,1)S(1)} async-done(((bf16[32,24,128]{2,1,0:T(8,128)(2,1)}), bf16[32,24,128]{2,1,0:T(8,128)(2,1)S(1)}, u32[]{:S(2)}, u32[]{:S(2)}) %all-to-all-start.1) | async-done | bytes 196640 | tf_op jit(solution)/shard_map/all_to_all | solution.py:321
  60.7 1.4 %query.1 = (bf16[32,16,128]{2,1,0:T(8,128)(2,1)}, bf16[16,128]{1,0:T(8,128)(2,1)S(1)}, f32[16,128]{1,0:T(8,128)S(1)}) custom-call(s32[2]{0:T(128)S(1)} %pad_add_fusion.who, bf16[768,128]{1,0:T(8,128)(2,1)S(1)} %bitcast.11, f32[16,128]{1,0:T(8,128)S(1)} %get-tuple-element.24.cosine, f32[16,128]{1,0:T(8,128)S(1)} %get-tuple-element.25.sine), custom_call_target="tpu_custom_call" | custom-call | flops 2000000000 | bytes 1048576 | tf_op jit(solution)/shard_map/query/pallas_call | solution.py:335
  62.1 4.4 %all-to-all-start.2 = ((bf16[32,16,128]{2,1,0:T(8,128)(2,1)}), bf16[32,16,128]{2,1,0:T(8,128)(2,1)S(1)}, u32[]{:S(2)}, u32[]{:S(2)}) async-start(bf16[32,16,128]{2,1,0:T(8,128)(2,1)} %get-tuple-element.26), calls=%async_computation.2 | async-start | bytes 262144 | tf_op jit(solution)/shard_map/all_to_all | solution.py:344
  66.6 0.7 keyval.1
  67.3 2.1 %collective-permute-start.3 = (bf16[128,128]{1,0:T(8,128)(2,1)S(1)}, bf16[128,128]{1,0:T(8,128)(2,1)S(1)}, u32[]{:S(2)}, u32[]{:S(2)}) collective-permute-start(bf16[128,128]{1,0:T(8,128)(2,1)S(1)} %get-tuple-element.30), channel_id=1, source_target_pairs={{0,16},{16,0},{32,48},{48,32},{64,80},{80,64},{96,112},{112,96},{1... | collective-permute-start | bytes 98312 | tf_op jit(solution)/shard_map/ppermute | solution.py:334
  69.5 0.9 collective-permute-done.3.given
  70.4 6.8 %all-to-all-done.2.q_ref = bf16[32,16,128]{2,1,0:T(8,128)(2,1)S(1)} async-done(((bf16[32,16,128]{2,1,0:T(8,128)(2,1)}), bf16[32,16,128]{2,1,0:T(8,128)(2,1)S(1)}, u32[]{:S(2)}, u32[]{:S(2)}) %all-to-all-start.2) | async-done | bytes 131104 | tf_op jit(solution)/shard_map/all_to_all | solution.py:344
  77.3 2.9 %attend.1 = bf16[768,128]{1,0:T(8,128)(2,1)S(1)} custom-call(s32[2]{0:T(128)S(1)} %pad_add_fusion.who, bf16[16,208,128]{2,1,0:T(8,128)(2,1)S(1)} %all-to-all-done.x_ref.mine, bf16[16,192,128]{2,1,0:T(8,128)(2,1)S(1)} %collective-permute-done.2.other, bf16[32,16,128]{2,1,0:T(8,128)(2,1)S(1)} %all-to-all-done.2.q_ref, f32[128,128]{1,0:T(8,128)S(1)} %get-tuple-element.29.keep, ...), custom_call_target="tpu_custom_call" | custom-call | tf_op jit(solution)/shard_map/attend/pallas_call | solution.py:345
  80.2 16.0 %all_to_all.42 = bf16[32,24,128]{2,1,0:T(8,128)(2,1)S(1)} all-to-all(bf16[32,24,128]{2,1,0:T(8,128)(2,1)S(1)} %bitcast.9), channel_id=1, replica_groups=mesh['blk'=32,'rows'=16] {'blk'}, dimensions={0} | all-to-all | bytes 393216 | tf_op jit(solution)/shard_map/all_to_all | solution.py:353
  96.1 0.8 combine.1
  96.9 14.0 %all_to_all.43.att = bf16[32,16,128]{2,1,0:T(8,128)(2,1)S(1)} all-to-all(bf16[32,16,128]{2,1,0:T(8,128)(2,1)S(1)} %combine.1), channel_id=1, replica_groups=mesh['blk'=32,'rows'=16] {'blk'}, dimensions={0} | all-to-all | bytes 262144 | tf_op jit(solution)/shard_map/all_to_all | solution.py:362
  111.0 0.2 output.1
  111.2 12.7 %all_to_all.44 = bf16[16,8,256]{2,1,0:T(8,128)(2,1)S(1)} all-to-all(bf16[16,8,256]{2,1,0:T(8,128)(2,1)S(1)} %bitcast.12), channel_id=1, replica_groups=mesh['blk'=32,'rows'=16] {'rows'}, dimensions={0} | all-to-all | bytes 131072 | tf_op jit(solution)/shard_map/all_to_all | solution.py:371
  123.9 0.6 add_convert_fusion
  (16 shorter events, 0.1 us)
Async XLA Ops:
  2.8 9.7 %copy-start.5 = (bf16[256,128]{1,0:T(8,128)(2,1)S(1)}, bf16[256,128]{1,0:T(8,128)(2,1)}, u32[]{:S(2)}) copy-start(bf16[256,128]{1,0:T(8,128)(2,1)} %param.16) | copy-start | bytes 196612
  2.8 30.7 %copy-start.1 = (bf16[256,512]{1,0:T(8,128)(2,1)S(1)}, bf16[256,512]{1,0:T(8,128)(2,1)}, u32[]{:S(2)}) copy-start(bf16[256,512]{1,0:T(8,128)(2,1)} %wq.1) | copy-start | bytes 786436
  2.8 30.7 %all-to-all-start = ((bf16[16,208,128]{2,1,0:T(8,128)(2,1)}), bf16[16,208,128]{2,1,0:T(8,128)(2,1)S(1)}, u32[]{:S(2)}, u32[]{:S(2)}) async-start(bf16[16,208,128]{2,1,0:T(8,128)(2,1)} %pack.1), calls=%async_computation | async-start | bytes 1703936 | tf_op jit(solution)/shard_map/all_to_all | solution.py:306
  12.5 36.7 %collective-permute-start.1 = (bf16[256,128]{1,0:T(8,128)(2,1)S(1)}, bf16[256,128]{1,0:T(8,128)(2,1)S(1)}, u32[]{:S(2)}, u32[]{:S(2)}) collective-permute-start(bf16[256,128]{1,0:T(8,128)(2,1)S(1)} %copy-done.5), channel_id=1, source_target_pairs={{0,1},{1,3},{2,5},{3,7},{4,9},{5,11},{6,13},{7,15},{8,0},{9,2},{10... | collective-permute-start | bytes 196616 | tf_op jit(solution)/shard_map/ppermute | solution.py:290
  15.8 33.5 %collective-permute-start = (bf16[256,128]{1,0:T(8,128)(2,1)S(1)}, bf16[256,128]{1,0:T(8,128)(2,1)S(1)}, u32[]{:S(2)}, u32[]{:S(2)}) collective-permute-start(bf16[256,128]{1,0:T(8,128)(2,1)S(1)} %copy-done.5), channel_id=1, source_target_pairs={{0,0},{1,2},{2,4},{3,6},{4,8},{5,10},{6,12},{7,14},{8,1},{9,3},{10... | collective-permute-start | bytes 196616 | tf_op jit(solution)/shard_map/ppermute | solution.py:289
  16.5 0.7 copy-start.6
  17.2 0.7 copy-start.3
  17.2 0.7 copy-start.4
  17.9 0.7 copy-start.7
  34.5 26.3 %all-to-all-start.1 = ((bf16[32,24,128]{2,1,0:T(8,128)(2,1)}), bf16[32,24,128]{2,1,0:T(8,128)(2,1)S(1)}, u32[]{:S(2)}, u32[]{:S(2)}) async-start(bf16[32,24,128]{2,1,0:T(8,128)(2,1)} %bitcast.4), calls=%async_computation.1 | async-start | bytes 393216 | tf_op jit(solution)/shard_map/all_to_all | solution.py:321
  49.3 28.0 %collective-permute-start.2 = (bf16[16,192,128]{2,1,0:T(8,128)(2,1)S(1)}, bf16[16,192,128]{2,1,0:T(8,128)(2,1)S(1)}, u32[]{:S(2)}, u32[]{:S(2)}) collective-permute-start(bf16[16,192,128]{2,1,0:T(8,128)(2,1)S(1)} %slice.3), channel_id=1, source_target_pairs={{0,1},{1,0},{2,3},{3,2},{4,5},{5,4},{6,7},{7,6},{8,9},{9,8},{10,11... | collective-permute-start | bytes 2359304 | tf_op jit(solution)/shard_map/ppermute | solution.py:323
  62.1 15.1 %all-to-all-start.2 = ((bf16[32,16,128]{2,1,0:T(8,128)(2,1)}), bf16[32,16,128]{2,1,0:T(8,128)(2,1)S(1)}, u32[]{:S(2)}, u32[]{:S(2)}) async-start(bf16[32,16,128]{2,1,0:T(8,128)(2,1)} %get-tuple-element.26), calls=%async_computation.2 | async-start | bytes 262144 | tf_op jit(solution)/shard_map/all_to_all | solution.py:344
  67.3 3.1 %collective-permute-start.3 = (bf16[128,128]{1,0:T(8,128)(2,1)S(1)}, bf16[128,128]{1,0:T(8,128)(2,1)S(1)}, u32[]{:S(2)}, u32[]{:S(2)}) collective-permute-start(bf16[128,128]{1,0:T(8,128)(2,1)S(1)} %get-tuple-element.30), channel_id=1, source_target_pairs={{0,16},{16,0},{32,48},{48,32},{64,80},{80,64},{96,112},{112,96},{1... | collective-permute-start | bytes 98312 | tf_op jit(solution)/shard_map/ppermute | solution.py:334
  96.1 14.8 %copy-start = (bf16[512,256]{1,0:T(8,128)(2,1)S(1)}, bf16[512,256]{1,0:T(8,128)(2,1)}, u32[]{:S(2)}) copy-start(bf16[512,256]{1,0:T(8,128)(2,1)} %w.1) | copy-start | bytes 786436
  96.9 14.1 %copy-start.2 = (bf16[8,256]{1,0:T(8,128)(2,1)S(1)}, bf16[8,256]{1,0:T(8,128)(2,1)}, u32[]{:S(2)}) copy-start(bf16[8,256]{1,0:T(8,128)(2,1)} %hidden.3) | copy-start | bytes 12292

commit v14 on v13

--- a/solution.py
+++ b/solution.py
@@ -24,22 +24,19 @@
     return lax.broadcasted_iota(jnp.int32, shape, dim)
 
 
-def pack_body(lens, hidden, keys_hbm, values_hbm, own_k_hbm, own_v_hbm, out, keys, values, own_k, own_v, packed, sems):
-    inward = [
-        pltpu.make_async_copy(src, dst, sems.at[i])
-        for i, (src, dst) in enumerate(
-            ((own_k_hbm, own_k), (keys_hbm, keys), (values_hbm, values), (own_v_hbm, own_v))
-        )
+def pack_body(lens, hidden, keys, values, own_k, own_v, out, packed, sems):
+    outward = [
+        pltpu.make_async_copy(packed.at[:, first:last, :], out.at[:, first:last, :], sems.at[i])
+        for i, (first, last) in enumerate(((K0, V0), (V0, OK0), (OK0, OV0), (OV0, END)))
     ]
-    for copy in inward:
-        copy.start()
-    outward = [
-        pltpu.make_async_copy(packed.at[:, first:last, :], out.at[:, first:last, :], sems.at[4 + i])
-        for i, (first, last) in enumerate(((OK0, OV0), (K0, V0), (V0, OK0), (OV0, END)))
-    ]
+    places = [(2 * h + p, p, slice(h * HD, (h + 1) * HD)) for p in range(2) for h in range(8)]
+    for d, p, col in places:
+        packed[d, K0:V0, :] = keys[64 * p : 64 * p + 64, col]
+    outward[0].start()
+    for d, p, col in places:
+        packed[d, V0:OK0, :] = values[64 * p : 64 * p + 64, col]
+    outward[1].start()
     b = lax.axis_index("blk")
-    x = hidden[...].astype(F32)
-    x_tile = jnp.concatenate([x[:, :HD], x[:, HD:]], axis=0).astype(BF)
     sub = iota((32, HD), 0)
     slot = 8 * b + sub % 8
     dead = []
@@ -48,23 +45,16 @@
         for k in range(4):
             live = jnp.where(sub // 8 == k, lens[4 * p + k], live)
         dead.append(slot >= live)
-    for step in range(4):
-        inward[step].wait()
-        for p in range(2):
-            for h in range(8):
-                col = slice(h * HD, (h + 1) * HD)
-                d = 2 * h + p
-                if step == 0:
-                    own = own_k[32 * p : 32 * p + 32, col].astype(F32)
-                    packed[d, OK0:OV0, :] = jnp.where(dead[p], jnp.nan, own).astype(BF)
-                elif step == 1:
-                    packed[d, K0:V0, :] = keys[64 * p : 64 * p + 64, col]
-                elif step == 2:
-                    packed[d, V0:OK0, :] = values[64 * p : 64 * p + 64, col]
-                else:
-                    packed[d, OV0:X0, :] = own_v[32 * p : 32 * p + 32, col]
-                    packed[d, X0:END, :] = x_tile
-        outward[step].start()
+    for d, p, col in places:
+        own = own_k[32 * p : 32 * p + 32, col].astype(F32)
+        packed[d, OK0:OV0, :] = jnp.where(dead[p], jnp.nan, own).astype(BF)
+    outward[2].start()
+    x = hidden[...].astype(F32)
+    x_tile = jnp.concatenate([x[:, :HD], x[:, HD:]], axis=0).astype(BF)
+    for d, p, col in places:
+        packed[d, OV0:X0, :] = own_v[32 * p : 32 * p + 32, col]
+        packed[d, X0:END, :] = x_tile
+    outward[3].start()
     for copy in outward:
         copy.wait()
 
@@ -291,15 +281,11 @@
     packed = pl.pallas_call(
         pack_body,
         out_shape=sds((16, END, HD), BF),
-        in_specs=[SM, VM] + [pl.BlockSpec(memory_space=pltpu.HBM)] * 4,
+        in_specs=[SM] + [VM] * 5,
         out_specs=pl.BlockSpec(memory_space=pltpu.HBM),
         scratch_shapes=[
-            pltpu.VMEM((128, 1024), BF),
-            pltpu.VMEM((128, 1024), BF),
-            pltpu.VMEM((64, 1024), BF),
-            pltpu.VMEM((64, 1024), BF),
             pltpu.VMEM((16, END, HD), BF),
-            pltpu.SemaphoreType.DMA((8,)),
+            pltpu.SemaphoreType.DMA((4,)),
         ],
         name="pack",
     )(lengths, hidden_in, prefix_keys, prefix_values, own_keys.reshape(64, 1024), own_values.reshape(64, 1024))

time: 125 us -> 125 us (level)
  no operation moved by 1% of the time
where the time goes in v14:
time: 125 us; the launch traced here: 124 us
  blocking collectives  42.7 us (34%)
  starting transfers between devices  39 us (31%)
  waiting for transfers between devices  30.1 us (24%)
  Pallas kernels  9.17 us (7%)
  local copies, waits for them, and re-layouts  1.95 us (2%)
    all_to_all x1, blocking collectives, on_device(): partial = lax.all_to_all(partial, 'blk', 0, 0, tiled=True)  16 us
    all_to_all x1, waiting for transfers between devices, on_device(): mine = lax.all_to_all(packed, 'rows', 0, 0, tiled=True)  15 us
    all_to_all x1, starting transfers between devices, on_device(): parts = lax.all_to_all(parts, 'blk', 0, 0, tiled=True)  14.7 us
    all_to_all x1, blocking collectives, on_device(): attended = lax.all_to_all(attended, 'blk', 0, 0, tiled=True)  14 us
    all_to_all x1, blocking collectives, on_device(): mixed = lax.all_to_all(mixed.reshape(16, 8, 256), 'rows', 0, 0, tiled=True)  12.7 us
    all_to_all x1, starting transfers between devices, on_device(): mine = lax.all_to_all(packed, 'rows', 0, 0, tiled=True)  9.71 us
    all_to_all x1, waiting for transfers between devices, on_device(): parts = lax.all_to_all(parts, 'blk', 0, 0, tiled=True)  7.32 us
    all_to_all x1, waiting for transfers between devices, on_device(): query = lax.all_to_all(query, 'blk', 0, 0, tiled=True)  6.82 us
  transfers between devices with their start and end apart: 7, of which 4 were waited for; matrix products, arithmetic and copies ran while one was open for 0% of the time, Pallas kernels for 2%

profile of v14, /device:TPU:1, one launch (start us, length us, event | category | flops | bytes accessed | tf_op | source)
XLA Modules:
  0.0 123.9 jit_solution(17905093819601568516)
XLA Ops:
  0.0 2.2 %pack.1 = bf16[16,208,128]{2,1,0:T(8,128)(2,1)} custom-call(s32[8]{0:T(128)} %lens.1, bf16[8,256]{1,0:T(8,128)(2,1)} %hidden.3, bf16[128,1024]{1,0:T(8,128)(2,1)} %keys.1, bf16[128,1024]{1,0:T(8,128)(2,1)} %values.1, bf16[64,1024]{1,0:T(8,128)(2,1)} %bitcast.13, bf16[64,1024]{1,0:T(8,128)(2,1)} %bitcast.14), custom_call_target="tpu_custom_call" | custom-call | tf_op jit(solution)/shard_map/pack/pallas_call | solution.py:281
  2.2 0.0 copy-start.5
  2.2 9.7 %all-to-all-start = ((bf16[16,208,128]{2,1,0:T(8,128)(2,1)}), bf16[16,208,128]{2,1,0:T(8,128)(2,1)S(1)}, u32[]{:S(2)}, u32[]{:S(2)}) async-start(bf16[16,208,128]{2,1,0:T(8,128)(2,1)} %pack.1), calls=%async_computation | async-start | bytes 1703936 | tf_op jit(solution)/shard_map/all_to_all | solution.py:292
  11.9 3.3 %collective-permute-start.1 = (bf16[256,128]{1,0:T(8,128)(2,1)S(1)}, bf16[256,128]{1,0:T(8,128)(2,1)S(1)}, u32[]{:S(2)}, u32[]{:S(2)}) collective-permute-start(bf16[256,128]{1,0:T(8,128)(2,1)S(1)} %copy-done.5), channel_id=1, source_target_pairs={{0,1},{1,3},{2,5},{3,7},{4,9},{5,11},{6,13},{7,15},{8,0},{9,2},{10... | collective-permute-start | bytes 196616 | tf_op jit(solution)/shard_map/ppermute | solution.py:280
  15.2 0.7 collective-permute-start
  15.9 0.6 copy-done.6
  16.5 0.1 dynamic_slice.3
  16.6 0.1 add_convert_fusion.1
  16.7 0.6 copy-done.3
  17.3 0.0 copy-done.4
  17.3 0.1 fusion
  17.4 0.5 copy-done.7
  18.0 15.0 %all-to-all-done.x_ref.mine = bf16[16,208,128]{2,1,0:T(8,128)(2,1)S(1)} async-done(((bf16[16,208,128]{2,1,0:T(8,128)(2,1)}), bf16[16,208,128]{2,1,0:T(8,128)(2,1)S(1)}, u32[]{:S(2)}, u32[]{:S(2)}) %all-to-all-start) | async-done | bytes 852000 | tf_op jit(solution)/shard_map/all_to_all | solution.py:292
  32.9 1.0 project.1
  33.9 14.7 %all-to-all-start.1 = ((bf16[32,24,128]{2,1,0:T(8,128)(2,1)}), bf16[32,24,128]{2,1,0:T(8,128)(2,1)S(1)}, u32[]{:S(2)}, u32[]{:S(2)}) async-start(bf16[32,24,128]{2,1,0:T(8,128)(2,1)} %bitcast.4), calls=%async_computation.1 | async-start | bytes 393216 | tf_op jit(solution)/shard_map/all_to_all | solution.py:307
  48.6 0.1 slice.3
  48.7 4.0 %collective-permute-start.2 = (bf16[16,192,128]{2,1,0:T(8,128)(2,1)S(1)}, bf16[16,192,128]{2,1,0:T(8,128)(2,1)S(1)}, u32[]{:S(2)}, u32[]{:S(2)}) collective-permute-start(bf16[16,192,128]{2,1,0:T(8,128)(2,1)S(1)} %slice.3), channel_id=1, source_target_pairs={{0,1},{1,0},{2,3},{3,2},{4,5},{5,4},{6,7},{7,6},{8,9},{9,8},{10,11... | collective-permute-start | bytes 2359304 | tf_op jit(solution)/shard_map/ppermute | solution.py:309
  52.7 0.1 pad_add_fusion.who
  52.8 7.3 %all-to-all-done.1 = bf16[32,24,128]{2,1,0:T(8,128)(2,1)S(1)} async-done(((bf16[32,24,128]{2,1,0:T(8,128)(2,1)}), bf16[32,24,128]{2,1,0:T(8,128)(2,1)S(1)}, u32[]{:S(2)}, u32[]{:S(2)}) %all-to-all-start.1) | async-done | bytes 196640 | tf_op jit(solution)/shard_map/all_to_all | solution.py:307
  60.1 1.4 %query.1 = (bf16[32,16,128]{2,1,0:T(8,128)(2,1)}, bf16[16,128]{1,0:T(8,128)(2,1)S(1)}, f32[16,128]{1,0:T(8,128)S(1)}) custom-call(s32[2]{0:T(128)S(1)} %pad_add_fusion.who, bf16[768,128]{1,0:T(8,128)(2,1)S(1)} %bitcast.11, f32[16,128]{1,0:T(8,128)S(1)} %get-tuple-element.24.cosine, f32[16,128]{1,0:T(8,128)S(1)} %get-tuple-element.25.sine), custom_call_target="tpu_custom_call" | custom-call | flops 2000000000 | bytes 1048576 | tf_op jit(solution)/shard_map/query/pallas_call | solution.py:321
  61.5 4.4 %all-to-all-start.2 = ((bf16[32,16,128]{2,1,0:T(8,128)(2,1)}), bf16[32,16,128]{2,1,0:T(8,128)(2,1)S(1)}, u32[]{:S(2)}, u32[]{:S(2)}) async-start(bf16[32,16,128]{2,1,0:T(8,128)(2,1)} %get-tuple-element.26), calls=%async_computation.2 | async-start | bytes 262144 | tf_op jit(solution)/shard_map/all_to_all | solution.py:330
  66.0 0.7 keyval.1
  66.7 2.1 %collective-permute-start.3 = (bf16[128,128]{1,0:T(8,128)(2,1)S(1)}, bf16[128,128]{1,0:T(8,128)(2,1)S(1)}, u32[]{:S(2)}, u32[]{:S(2)}) collective-permute-start(bf16[128,128]{1,0:T(8,128)(2,1)S(1)} %get-tuple-element.30), channel_id=1, source_target_pairs={{0,16},{16,0},{32,48},{48,32},{64,80},{80,64},{96,112},{112,96},{1... | collective-permute-start | bytes 98312 | tf_op jit(solution)/shard_map/ppermute | solution.py:320
  68.9 0.9 collective-permute-done.3.given
  69.8 6.8 %all-to-all-done.2.q_ref = bf16[32,16,128]{2,1,0:T(8,128)(2,1)S(1)} async-done(((bf16[32,16,128]{2,1,0:T(8,128)(2,1)}), bf16[32,16,128]{2,1,0:T(8,128)(2,1)S(1)}, u32[]{:S(2)}, u32[]{:S(2)}) %all-to-all-start.2) | async-done | bytes 131104 | tf_op jit(solution)/shard_map/all_to_all | solution.py:330
  76.7 2.9 %attend.1 = bf16[768,128]{1,0:T(8,128)(2,1)S(1)} custom-call(s32[2]{0:T(128)S(1)} %pad_add_fusion.who, bf16[16,208,128]{2,1,0:T(8,128)(2,1)S(1)} %all-to-all-done.x_ref.mine, bf16[16,192,128]{2,1,0:T(8,128)(2,1)S(1)} %collective-permute-done.2.other, bf16[32,16,128]{2,1,0:T(8,128)(2,1)S(1)} %all-to-all-done.2.q_ref, f32[128,128]{1,0:T(8,128)S(1)} %get-tuple-element.29.keep, ...), custom_call_target="tpu_custom_call" | custom-call | tf_op jit(solution)/shard_map/attend/pallas_call | solution.py:331
  79.6 16.0 %all_to_all.42 = bf16[32,24,128]{2,1,0:T(8,128)(2,1)S(1)} all-to-all(bf16[32,24,128]{2,1,0:T(8,128)(2,1)S(1)} %bitcast.9), channel_id=1, replica_groups=mesh['blk'=32,'rows'=16] {'blk'}, dimensions={0} | all-to-all | bytes 393216 | tf_op jit(solution)/shard_map/all_to_all | solution.py:339
  95.5 0.8 combine.1
  96.3 14.0 %all_to_all.43.att = bf16[32,16,128]{2,1,0:T(8,128)(2,1)S(1)} all-to-all(bf16[32,16,128]{2,1,0:T(8,128)(2,1)S(1)} %combine.1), channel_id=1, replica_groups=mesh['blk'=32,'rows'=16] {'blk'}, dimensions={0} | all-to-all | bytes 262144 | tf_op jit(solution)/shard_map/all_to_all | solution.py:348
  110.4 0.2 output.1
  110.6 12.7 %all_to_all.44 = bf16[16,8,256]{2,1,0:T(8,128)(2,1)S(1)} all-to-all(bf16[16,8,256]{2,1,0:T(8,128)(2,1)S(1)} %bitcast.12), channel_id=1, replica_groups=mesh['blk'=32,'rows'=16] {'rows'}, dimensions={0} | all-to-all | bytes 131072 | tf_op jit(solution)/shard_map/all_to_all | solution.py:357
  123.3 0.6 add_convert_fusion
  (16 shorter events, 0.1 us)
Async XLA Ops:
  2.2 9.7 %copy-start.5 = (bf16[256,128]{1,0:T(8,128)(2,1)S(1)}, bf16[256,128]{1,0:T(8,128)(2,1)}, u32[]{:S(2)}) copy-start(bf16[256,128]{1,0:T(8,128)(2,1)} %param.16) | copy-start | bytes 196612
  2.2 30.7 %copy-start.1 = (bf16[256,512]{1,0:T(8,128)(2,1)S(1)}, bf16[256,512]{1,0:T(8,128)(2,1)}, u32[]{:S(2)}) copy-start(bf16[256,512]{1,0:T(8,128)(2,1)} %wq.1) | copy-start | bytes 786436
  2.2 30.7 %all-to-all-start = ((bf16[16,208,128]{2,1,0:T(8,128)(2,1)}), bf16[16,208,128]{2,1,0:T(8,128)(2,1)S(1)}, u32[]{:S(2)}, u32[]{:S(2)}) async-start(bf16[16,208,128]{2,1,0:T(8,128)(2,1)} %pack.1), calls=%async_computation | async-start | bytes 1703936 | tf_op jit(solution)/shard_map/all_to_all | solution.py:292
  11.9 36.7 %collective-permute-start.1 = (bf16[256,128]{1,0:T(8,128)(2,1)S(1)}, bf16[256,128]{1,0:T(8,128)(2,1)S(1)}, u32[]{:S(2)}, u32[]{:S(2)}) collective-permute-start(bf16[256,128]{1,0:T(8,128)(2,1)S(1)} %copy-done.5), channel_id=1, source_target_pairs={{0,1},{1,3},{2,5},{3,7},{4,9},{5,11},{6,13},{7,15},{8,0},{9,2},{10... | collective-permute-start | bytes 196616 | tf_op jit(solution)/shard_map/ppermute | solution.py:280
  15.2 33.5 %collective-permute-start = (bf16[256,128]{1,0:T(8,128)(2,1)S(1)}, bf16[256,128]{1,0:T(8,128)(2,1)S(1)}, u32[]{:S(2)}, u32[]{:S(2)}) collective-permute-start(bf16[256,128]{1,0:T(8,128)(2,1)S(1)} %copy-done.5), channel_id=1, source_target_pairs={{0,0},{1,2},{2,4},{3,6},{4,8},{5,10},{6,12},{7,14},{8,1},{9,3},{10... | collective-permute-start | bytes 196616 | tf_op jit(solution)/shard_map/ppermute | solution.py:279
  15.9 0.7 copy-start.6
  16.6 0.7 copy-start.3
  16.6 0.7 copy-start.4
  17.3 0.7 copy-start.7
  33.9 26.3 %all-to-all-start.1 = ((bf16[32,24,128]{2,1,0:T(8,128)(2,1)}), bf16[32,24,128]{2,1,0:T(8,128)(2,1)S(1)}, u32[]{:S(2)}, u32[]{:S(2)}) async-start(bf16[32,24,128]{2,1,0:T(8,128)(2,1)} %bitcast.4), calls=%async_computation.1 | async-start | bytes 393216 | tf_op jit(solution)/shard_map/all_to_all | solution.py:307
  48.7 28.0 %collective-permute-start.2 = (bf16[16,192,128]{2,1,0:T(8,128)(2,1)S(1)}, bf16[16,192,128]{2,1,0:T(8,128)(2,1)S(1)}, u32[]{:S(2)}, u32[]{:S(2)}) collective-permute-start(bf16[16,192,128]{2,1,0:T(8,128)(2,1)S(1)} %slice.3), channel_id=1, source_target_pairs={{0,1},{1,0},{2,3},{3,2},{4,5},{5,4},{6,7},{7,6},{8,9},{9,8},{10,11... | collective-permute-start | bytes 2359304 | tf_op jit(solution)/shard_map/ppermute | solution.py:309
  61.5 15.1 %all-to-all-start.2 = ((bf16[32,16,128]{2,1,0:T(8,128)(2,1)}), bf16[32,16,128]{2,1,0:T(8,128)(2,1)S(1)}, u32[]{:S(2)}, u32[]{:S(2)}) async-start(bf16[32,16,128]{2,1,0:T(8,128)(2,1)} %get-tuple-element.26), calls=%async_computation.2 | async-start | bytes 262144 | tf_op jit(solution)/shard_map/all_to_all | solution.py:330
  66.7 3.1 %collective-permute-start.3 = (bf16[128,128]{1,0:T(8,128)(2,1)S(1)}, bf16[128,128]{1,0:T(8,128)(2,1)S(1)}, u32[]{:S(2)}, u32[]{:S(2)}) collective-permute-start(bf16[128,128]{1,0:T(8,128)(2,1)S(1)} %get-tuple-element.30), channel_id=1, source_target_pairs={{0,16},{16,0},{32,48},{48,32},{64,80},{80,64},{96,112},{112,96},{1... | collective-permute-start | bytes 98312 | tf_op jit(solution)/shard_map/ppermute | solution.py:320
  95.5 14.8 %copy-start = (bf16[512,256]{1,0:T(8,128)(2,1)S(1)}, bf16[512,256]{1,0:T(8,128)(2,1)}, u32[]{:S(2)}) copy-start(bf16[512,256]{1,0:T(8,128)(2,1)} %w.1) | copy-start | bytes 786436
  96.3 14.1 %copy-start.2 = (bf16[8,256]{1,0:T(8,128)(2,1)S(1)}, bf16[8,256]{1,0:T(8,128)(2,1)}, u32[]{:S(2)}) copy-start(bf16[8,256]{1,0:T(8,128)(2,1)} %hidden.3) | copy-start | bytes 12292

commit v15 on v14

--- a/solution.py
+++ b/solution.py
@@ -136,7 +136,8 @@
     scale = HD ** (-0.5) * LOG2E
     sources = (mine, other)
     halves = (lax.rem(r, 2), 1 - lax.rem(r, 2))
-    rows = 256
+    rows = 128
+    ones = jnp.ones((1024, HD), BF)
     row_q, lane = iota((128, HD), 0), iota((128, HD), 1)
     row_q = 4 * (row_q // 16) + row_q % 4
     lane_s = iota((rows, HD), 1)
@@ -150,7 +151,7 @@
         for s in sources:
             k = s[:, K0:V0, :].reshape(1024, HD)
             scores.append(lax.dot_general(q, k, NT, preferred_element_type=F32))
-            vals.append(s[:, V0:OK0, :].reshape(1024, HD))
+            vals.append(jnp.concatenate([s[:, V0:OK0, :].reshape(1024, HD), ones], axis=1))
         own_scores, own_vals = [], []
         for s, half in zip(sources, halves):
             row_k = 8 * (lane // 32) + 4 * half + (lane % 32) // 8
@@ -158,7 +159,8 @@
             for u in range(rows // 128):
                 first = 4 * (t * (rows // 128) + u)
                 k = s[first : first + 4, OK0:OV0, :].reshape(128, HD)
-                block_vals.append(s[first : first + 4, OV0:X0, :].reshape(128, HD))
+                v = s[first : first + 4, OV0:X0, :].reshape(128, HD)
+                block_vals.append(jnp.concatenate([v, ones[0:128, :]], axis=1))
                 sc = lax.dot_general(q[128 * u : 128 * u + 128], k, NT, preferred_element_type=F32)
                 blocks.append(jnp.where((row_k == row_q) & (sc == sc), sc, -jnp.inf))
             own_scores.append(jnp.concatenate(blocks, axis=0))
@@ -170,15 +172,12 @@
         high = peak.astype(BF).astype(F32)
         low = (peak - high).astype(BF).astype(F32)
         shift = high + low
-        mass = jnp.zeros((rows, 1), F32)
-        acc = jnp.zeros((rows, HD), F32)
+        acc = jnp.zeros((rows, 2 * HD), F32)
         for sc, v in zip(scores, vals):
             w = jnp.exp2(sc * scale - shift)
-            mass = mass + jnp.sum(w, axis=1, keepdims=True)
             acc = acc + jnp.dot(w.astype(BF), v, preferred_element_type=F32)
         for sc, block_vals in zip(own_scores, own_vals):
             w = jnp.exp2(sc * scale - shift)
-            mass = mass + jnp.sum(w, axis=1, keepdims=True)
             w = w.astype(BF)
             acc = acc + jnp.concatenate(
                 [
@@ -187,6 +186,7 @@
                 ],
                 axis=0,
             )
+        mass, acc = acc[:, HD:], acc[:, :HD]
         mass_high = mass.astype(BF).astype(F32)
         stats = jnp.where(
             lane_s == 0, high, jnp.where(lane_s == 1, low, jnp.where(lane_s == 2, mass_high, mass - mass_high))

time: 125 us -> 124 us (level)
  no operation moved by 1% of the time
where the time goes in v15:
time: 124 us
  blocking collectives  42.7 us (34%)
  starting transfers between devices  39 us (31%)
  waiting for transfers between devices  30.1 us (24%)
  Pallas kernels  8.98 us (7%)
  local copies, waits for them, and re-layouts  1.95 us (2%)
    all_to_all x1, blocking collectives, on_device(): partial = lax.all_to_all(partial, 'blk', 0, 0, tiled=True)  15.9 us
    all_to_all x1, waiting for transfers between devices, on_device(): mine = lax.all_to_all(packed, 'rows', 0, 0, tiled=True)  15 us
    all_to_all x1, starting transfers between devices, on_device(): parts = lax.all_to_all(parts, 'blk', 0, 0, tiled=True)  14.7 us
    all_to_all x1, blocking collectives, on_device(): attended = lax.all_to_all(attended, 'blk', 0, 0, tiled=True)  14 us
    all_to_all x1, blocking collectives, on_device(): mixed = lax.all_to_all(mixed.reshape(16, 8, 256), 'rows', 0, 0, tiled=True)  12.7 us
    all_to_all x1, starting transfers between devices, on_device(): mine = lax.all_to_all(packed, 'rows', 0, 0, tiled=True)  9.71 us
    all_to_all x1, waiting for transfers between devices, on_device(): parts = lax.all_to_all(parts, 'blk', 0, 0, tiled=True)  7.32 us
    all_to_all x1, waiting for transfers between devices, on_device(): query = lax.all_to_all(query, 'blk', 0, 0, tiled=True)  6.82 us
  transfers between devices with their start and end apart: 7, of which 4 were waited for; matrix products, arithmetic and copies ran while one was open for 0% of the time, Pallas kernels for 2%

profile of v15, /device:TPU:1, one launch (start us, length us, event | category | flops | bytes accessed | tf_op | source)
XLA Modules:
  0.0 123.7 jit_solution(13499809338337860686)
XLA Ops:
  0.0 2.2 %pack.1 = bf16[16,208,128]{2,1,0:T(8,128)(2,1)} custom-call(s32[8]{0:T(128)} %lens.1, bf16[8,256]{1,0:T(8,128)(2,1)} %hidden.3, bf16[128,1024]{1,0:T(8,128)(2,1)} %keys.1, bf16[128,1024]{1,0:T(8,128)(2,1)} %values.1, bf16[64,1024]{1,0:T(8,128)(2,1)} %bitcast.13, bf16[64,1024]{1,0:T(8,128)(2,1)} %bitcast.14), custom_call_target="tpu_custom_call" | custom-call | tf_op jit(solution)/shard_map/pack/pallas_call | solution.py:281
  2.2 0.0 copy-start.1
  2.2 9.7 %all-to-all-start = ((bf16[16,208,128]{2,1,0:T(8,128)(2,1)}), bf16[16,208,128]{2,1,0:T(8,128)(2,1)S(1)}, u32[]{:S(2)}, u32[]{:S(2)}) async-start(bf16[16,208,128]{2,1,0:T(8,128)(2,1)} %pack.1), calls=%async_computation | async-start | bytes 1703936 | tf_op jit(solution)/shard_map/all_to_all | solution.py:292
  11.9 3.3 %collective-permute-start.1 = (bf16[256,128]{1,0:T(8,128)(2,1)S(1)}, bf16[256,128]{1,0:T(8,128)(2,1)S(1)}, u32[]{:S(2)}, u32[]{:S(2)}) collective-permute-start(bf16[256,128]{1,0:T(8,128)(2,1)S(1)} %copy-done.5), channel_id=1, source_target_pairs={{0,1},{1,3},{2,5},{3,7},{4,9},{5,11},{6,13},{7,15},{8,0},{9,2},{10... | collective-permute-start | bytes 196616 | tf_op jit(solution)/shard_map/ppermute | solution.py:280
  15.2 0.7 collective-permute-start
  15.9 0.6 copy-done.6
  16.5 0.1 dynamic_slice.3
  16.6 0.1 add_convert_fusion.1
  16.7 0.6 copy-done.3
  17.3 0.0 copy-done.4
  17.3 0.1 fusion
  17.4 0.5 copy-done.7
  18.0 15.0 %all-to-all-done.x_ref.mine = bf16[16,208,128]{2,1,0:T(8,128)(2,1)S(1)} async-done(((bf16[16,208,128]{2,1,0:T(8,128)(2,1)}), bf16[16,208,128]{2,1,0:T(8,128)(2,1)S(1)}, u32[]{:S(2)}, u32[]{:S(2)}) %all-to-all-start) | async-done | bytes 852000 | tf_op jit(solution)/shard_map/all_to_all | solution.py:292
  32.9 1.0 project.1
  33.9 14.7 %all-to-all-start.1 = ((bf16[32,24,128]{2,1,0:T(8,128)(2,1)}), bf16[32,24,128]{2,1,0:T(8,128)(2,1)S(1)}, u32[]{:S(2)}, u32[]{:S(2)}) async-start(bf16[32,24,128]{2,1,0:T(8,128)(2,1)} %bitcast.4), calls=%async_computation.1 | async-start | bytes 393216 | tf_op jit(solution)/shard_map/all_to_all | solution.py:307
  48.6 0.1 slice.3
  48.7 4.0 %collective-permute-start.2 = (bf16[16,192,128]{2,1,0:T(8,128)(2,1)S(1)}, bf16[16,192,128]{2,1,0:T(8,128)(2,1)S(1)}, u32[]{:S(2)}, u32[]{:S(2)}) collective-permute-start(bf16[16,192,128]{2,1,0:T(8,128)(2,1)S(1)} %slice.3), channel_id=1, source_target_pairs={{0,1},{1,0},{2,3},{3,2},{4,5},{5,4},{6,7},{7,6},{8,9},{9,8},{10,11... | collective-permute-start | bytes 2359304 | tf_op jit(solution)/shard_map/ppermute | solution.py:309
  52.7 0.1 pad_add_fusion.who
  52.8 7.3 %all-to-all-done.1 = bf16[32,24,128]{2,1,0:T(8,128)(2,1)S(1)} async-done(((bf16[32,24,128]{2,1,0:T(8,128)(2,1)}), bf16[32,24,128]{2,1,0:T(8,128)(2,1)S(1)}, u32[]{:S(2)}, u32[]{:S(2)}) %all-to-all-start.1) | async-done | bytes 196640 | tf_op jit(solution)/shard_map/all_to_all | solution.py:307
  60.1 1.4 %query.1 = (bf16[32,16,128]{2,1,0:T(8,128)(2,1)}, bf16[16,128]{1,0:T(8,128)(2,1)S(1)}, f32[16,128]{1,0:T(8,128)S(1)}) custom-call(s32[2]{0:T(128)S(1)} %pad_add_fusion.who, bf16[768,128]{1,0:T(8,128)(2,1)S(1)} %bitcast.11, f32[16,128]{1,0:T(8,128)S(1)} %get-tuple-element.24.cosine, f32[16,128]{1,0:T(8,128)S(1)} %get-tuple-element.25.sine), custom_call_target="tpu_custom_call" | custom-call | flops 2000000000 | bytes 1048576 | tf_op jit(solution)/shard_map/query/pallas_call | solution.py:321
  61.5 4.4 %all-to-all-start.2 = ((bf16[32,16,128]{2,1,0:T(8,128)(2,1)}), bf16[32,16,128]{2,1,0:T(8,128)(2,1)S(1)}, u32[]{:S(2)}, u32[]{:S(2)}) async-start(bf16[32,16,128]{2,1,0:T(8,128)(2,1)} %get-tuple-element.26), calls=%async_computation.2 | async-start | bytes 262144 | tf_op jit(solution)/shard_map/all_to_all | solution.py:330
  66.0 0.7 keyval.1
  66.7 2.1 %collective-permute-start.3 = (bf16[128,128]{1,0:T(8,128)(2,1)S(1)}, bf16[128,128]{1,0:T(8,128)(2,1)S(1)}, u32[]{:S(2)}, u32[]{:S(2)}) collective-permute-start(bf16[128,128]{1,0:T(8,128)(2,1)S(1)} %get-tuple-element.30), channel_id=1, source_target_pairs={{0,16},{16,0},{32,48},{48,32},{64,80},{80,64},{96,112},{112,96},{1... | collective-permute-start | bytes 98312 | tf_op jit(solution)/shard_map/ppermute | solution.py:320
  68.9 0.9 collective-permute-done.3.given
  69.8 6.8 %all-to-all-done.2.q_ref = bf16[32,16,128]{2,1,0:T(8,128)(2,1)S(1)} async-done(((bf16[32,16,128]{2,1,0:T(8,128)(2,1)}), bf16[32,16,128]{2,1,0:T(8,128)(2,1)S(1)}, u32[]{:S(2)}, u32[]{:S(2)}) %all-to-all-start.2) | async-done | bytes 131104 | tf_op jit(solution)/shard_map/all_to_all | solution.py:330
  76.7 2.7 %attend.1 = bf16[768,128]{1,0:T(8,128)(2,1)S(1)} custom-call(s32[2]{0:T(128)S(1)} %pad_add_fusion.who, bf16[16,208,128]{2,1,0:T(8,128)(2,1)S(1)} %all-to-all-done.x_ref.mine, bf16[16,192,128]{2,1,0:T(8,128)(2,1)S(1)} %collective-permute-done.2.other, bf16[32,16,128]{2,1,0:T(8,128)(2,1)S(1)} %all-to-all-done.2.q_ref, f32[128,128]{1,0:T(8,128)S(1)} %get-tuple-element.29.keep, ...), custom_call_target="tpu_custom_call" | custom-call | tf_op jit(solution)/shard_map/attend/pallas_call | solution.py:331
  79.4 15.9 %all_to_all.42 = bf16[32,24,128]{2,1,0:T(8,128)(2,1)S(1)} all-to-all(bf16[32,24,128]{2,1,0:T(8,128)(2,1)S(1)} %bitcast.9), channel_id=1, replica_groups=mesh['blk'=32,'rows'=16] {'blk'}, dimensions={0} | all-to-all | bytes 393216 | tf_op jit(solution)/shard_map/all_to_all | solution.py:339
  95.3 0.8 combine.1
  96.1 14.0 %all_to_all.43.att = bf16[32,16,128]{2,1,0:T(8,128)(2,1)S(1)} all-to-all(bf16[32,16,128]{2,1,0:T(8,128)(2,1)S(1)} %combine.1), channel_id=1, replica_groups=mesh['blk'=32,'rows'=16] {'blk'}, dimensions={0} | all-to-all | bytes 262144 | tf_op jit(solution)/shard_map/all_to_all | solution.py:348
  110.2 0.2 output.1
  110.4 12.7 %all_to_all.44 = bf16[16,8,256]{2,1,0:T(8,128)(2,1)S(1)} all-to-all(bf16[16,8,256]{2,1,0:T(8,128)(2,1)S(1)} %bitcast.12), channel_id=1, replica_groups=mesh['blk'=32,'rows'=16] {'rows'}, dimensions={0} | all-to-all | bytes 131072 | tf_op jit(solution)/shard_map/all_to_all | solution.py:357
  123.1 0.6 add_convert_fusion
  (16 shorter events, 0.1 us)
Async XLA Ops:
  2.2 9.7 %copy-start.5 = (bf16[256,128]{1,0:T(8,128)(2,1)S(1)}, bf16[256,128]{1,0:T(8,128)(2,1)}, u32[]{:S(2)}) copy-start(bf16[256,128]{1,0:T(8,128)(2,1)} %param.16) | copy-start | bytes 196612
  2.2 30.7 %copy-start.1 = (bf16[256,512]{1,0:T(8,128)(2,1)S(1)}, bf16[256,512]{1,0:T(8,128)(2,1)}, u32[]{:S(2)}) copy-start(bf16[256,512]{1,0:T(8,128)(2,1)} %wq.1) | copy-start | bytes 786436
  2.2 30.7 %all-to-all-start = ((bf16[16,208,128]{2,1,0:T(8,128)(2,1)}), bf16[16,208,128]{2,1,0:T(8,128)(2,1)S(1)}, u32[]{:S(2)}, u32[]{:S(2)}) async-start(bf16[16,208,128]{2,1,0:T(8,128)(2,1)} %pack.1), calls=%async_computation | async-start | bytes 1703936 | tf_op jit(solution)/shard_map/all_to_all | solution.py:292
  11.9 36.7 %collective-permute-start.1 = (bf16[256,128]{1,0:T(8,128)(2,1)S(1)}, bf16[256,128]{1,0:T(8,128)(2,1)S(1)}, u32[]{:S(2)}, u32[]{:S(2)}) collective-permute-start(bf16[256,128]{1,0:T(8,128)(2,1)S(1)} %copy-done.5), channel_id=1, source_target_pairs={{0,1},{1,3},{2,5},{3,7},{4,9},{5,11},{6,13},{7,15},{8,0},{9,2},{10... | collective-permute-start | bytes 196616 | tf_op jit(solution)/shard_map/ppermute | solution.py:280
  15.2 33.5 %collective-permute-start = (bf16[256,128]{1,0:T(8,128)(2,1)S(1)}, bf16[256,128]{1,0:T(8,128)(2,1)S(1)}, u32[]{:S(2)}, u32[]{:S(2)}) collective-permute-start(bf16[256,128]{1,0:T(8,128)(2,1)S(1)} %copy-done.5), channel_id=1, source_target_pairs={{0,0},{1,2},{2,4},{3,6},{4,8},{5,10},{6,12},{7,14},{8,1},{9,3},{10... | collective-permute-start | bytes 196616 | tf_op jit(solution)/shard_map/ppermute | solution.py:279
  15.9 0.7 copy-start.6
  16.6 0.7 copy-start.3
  16.6 0.7 copy-start.4
  17.3 0.7 copy-start.7
  33.9 26.3 %all-to-all-start.1 = ((bf16[32,24,128]{2,1,0:T(8,128)(2,1)}), bf16[32,24,128]{2,1,0:T(8,128)(2,1)S(1)}, u32[]{:S(2)}, u32[]{:S(2)}) async-start(bf16[32,24,128]{2,1,0:T(8,128)(2,1)} %bitcast.4), calls=%async_computation.1 | async-start | bytes 393216 | tf_op jit(solution)/shard_map/all_to_all | solution.py:307
  48.7 28.0 %collective-permute-start.2 = (bf16[16,192,128]{2,1,0:T(8,128)(2,1)S(1)}, bf16[16,192,128]{2,1,0:T(8,128)(2,1)S(1)}, u32[]{:S(2)}, u32[]{:S(2)}) collective-permute-start(bf16[16,192,128]{2,1,0:T(8,128)(2,1)S(1)} %slice.3), channel_id=1, source_target_pairs={{0,1},{1,0},{2,3},{3,2},{4,5},{5,4},{6,7},{7,6},{8,9},{9,8},{10,11... | collective-permute-start | bytes 2359304 | tf_op jit(solution)/shard_map/ppermute | solution.py:309
  61.5 15.1 %all-to-all-start.2 = ((bf16[32,16,128]{2,1,0:T(8,128)(2,1)}), bf16[32,16,128]{2,1,0:T(8,128)(2,1)S(1)}, u32[]{:S(2)}, u32[]{:S(2)}) async-start(bf16[32,16,128]{2,1,0:T(8,128)(2,1)} %get-tuple-element.26), calls=%async_computation.2 | async-start | bytes 262144 | tf_op jit(solution)/shard_map/all_to_all | solution.py:330
  66.7 3.1 %collective-permute-start.3 = (bf16[128,128]{1,0:T(8,128)(2,1)S(1)}, bf16[128,128]{1,0:T(8,128)(2,1)S(1)}, u32[]{:S(2)}, u32[]{:S(2)}) collective-permute-start(bf16[128,128]{1,0:T(8,128)(2,1)S(1)} %get-tuple-element.30), channel_id=1, source_target_pairs={{0,16},{16,0},{32,48},{48,32},{64,80},{80,64},{96,112},{112,96},{1... | collective-permute-start | bytes 98312 | tf_op jit(solution)/shard_map/ppermute | solution.py:320
  95.3 14.8 %copy-start = (bf16[512,256]{1,0:T(8,128)(2,1)S(1)}, bf16[512,256]{1,0:T(8,128)(2,1)}, u32[]{:S(2)}) copy-start(bf16[512,256]{1,0:T(8,128)(2,1)} %w.1) | copy-start | bytes 786436
  96.1 14.1 %copy-start.2 = (bf16[8,256]{1,0:T(8,128)(2,1)S(1)}, bf16[8,256]{1,0:T(8,128)(2,1)}, u32[]{:S(2)}) copy-start(bf16[8,256]{1,0:T(8,128)(2,1)} %hidden.3) | copy-start | bytes 12292

commit v16 on v15

--- a/solution.py
+++ b/solution.py
@@ -327,6 +327,7 @@
         cost_estimate=pl.CostEstimate(flops=2*10**9, bytes_accessed=1 << 20, transcendentals=0),
         name="query",
     )(who, parts, cosine, sine)
+    query, given = lax.optimization_barrier((query, given))
     query = lax.all_to_all(query, "blk", 0, 0, tiled=True)
     partial = pl.pallas_call(
         attend_body,

time: 124 us -> 124 us (level)
  blocking collectives: 42.7 us -> 58.5 us
  waiting for transfers between devices: 30.1 us -> 19.1 us
  starting transfers between devices: 39 us -> 34.8 us
    all_to_all x0 -> x1, blocking collectives: none -> 16.6 us  [on_device(): query = lax.all_to_all(query, 'blk', 0, 0, tiled=True)]
    all_to_all x1 -> x0, waiting for transfers between devices: 6.82 us -> none  [on_device(): query = lax.all_to_all(query, 'blk', 0, 0, tiled=True)]
    all_to_all x1 -> x0, starting transfers between devices: 4.45 us -> none  [on_device(): query = lax.all_to_all(query, 'blk', 0, 0, tiled=True)]
    all_to_all x1, waiting for transfers between devices: 7.32 us -> 4.17 us  [on_device(): parts = lax.all_to_all(parts, 'blk', 0, 0, tiled=True)]
  transfers between devices with their start and end apart: 7 -> 6, of which waited for: 4 -> 2; matrix products, arithmetic and copies ran while one was open for 0% -> 0% of each run, Pallas kernels for 2% -> 2%
where the time goes in v16:
time: 124 us
  blocking collectives  58.5 us (47%)
  starting transfers between devices  34.8 us (28%)
  waiting for transfers between devices  19.1 us (15%)
  Pallas kernels  8.27 us (7%)
  local copies, waits for them, and re-layouts  1.95 us (2%)
    all_to_all x1, blocking collectives, on_device(): query = lax.all_to_all(query, 'blk', 0, 0, tiled=True)  16.6 us
    all_to_all x1, blocking collectives, on_device(): partial = lax.all_to_all(partial, 'blk', 0, 0, tiled=True)  15.3 us
    all_to_all x1, waiting for transfers between devices, on_device(): mine = lax.all_to_all(packed, 'rows', 0, 0, tiled=True)  15 us
    all_to_all x1, starting transfers between devices, on_device(): parts = lax.all_to_all(parts, 'blk', 0, 0, tiled=True)  14.7 us
    all_to_all x1, blocking collectives, on_device(): attended = lax.all_to_all(attended, 'blk', 0, 0, tiled=True)  14 us
    all_to_all x1, blocking collectives, on_device(): mixed = lax.all_to_all(mixed.reshape(16, 8, 256), 'rows', 0, 0, tiled=True)  12.6 us
    all_to_all x1, starting transfers between devices, on_device(): mine = lax.all_to_all(packed, 'rows', 0, 0, tiled=True)  9.71 us
    all_to_all x1, waiting for transfers between devices, on_device(): parts = lax.all_to_all(parts, 'blk', 0, 0, tiled=True)  4.17 us
  transfers between devices with their start and end apart: 6, of which 2 were waited for; matrix products, arithmetic and copies ran while one was open for 0% of the time, Pallas kernels for 2%

profile of v16, /device:TPU:1, one launch (start us, length us, event | category | flops | bytes accessed | tf_op | source)
XLA Modules:
  0.0 123.7 jit_solution(17269231882858004624)
XLA Ops:
  0.0 2.1 %pack.1 = bf16[16,208,128]{2,1,0:T(8,128)(2,1)} custom-call(s32[8]{0:T(128)} %lens.1, bf16[8,256]{1,0:T(8,128)(2,1)} %hidden.3, bf16[128,1024]{1,0:T(8,128)(2,1)} %keys.1, bf16[128,1024]{1,0:T(8,128)(2,1)} %values.1, bf16[64,1024]{1,0:T(8,128)(2,1)} %bitcast.13, bf16[64,1024]{1,0:T(8,128)(2,1)} %bitcast.14), custom_call_target="tpu_custom_call" | custom-call | tf_op jit(solution)/shard_map/pack/pallas_call | solution.py:281
  2.1 0.0 copy-start.5
  2.2 0.0 copy-start.1
  2.2 9.7 %all-to-all-start = ((bf16[16,208,128]{2,1,0:T(8,128)(2,1)}), bf16[16,208,128]{2,1,0:T(8,128)(2,1)S(1)}, u32[]{:S(2)}, u32[]{:S(2)}) async-start(bf16[16,208,128]{2,1,0:T(8,128)(2,1)} %pack.1), calls=%async_computation | async-start | bytes 1703936 | tf_op jit(solution)/shard_map/all_to_all | solution.py:292
  11.9 3.3 %collective-permute-start.1 = (bf16[256,128]{1,0:T(8,128)(2,1)S(1)}, bf16[256,128]{1,0:T(8,128)(2,1)S(1)}, u32[]{:S(2)}, u32[]{:S(2)}) collective-permute-start(bf16[256,128]{1,0:T(8,128)(2,1)S(1)} %copy-done.5), channel_id=1, source_target_pairs={{0,1},{1,3},{2,5},{3,7},{4,9},{5,11},{6,13},{7,15},{8,0},{9,2},{10... | collective-permute-start | bytes 196616 | tf_op jit(solution)/shard_map/ppermute | solution.py:280
  15.2 0.7 collective-permute-start
  15.9 0.6 copy-done.6
  16.5 0.1 dynamic_slice.3
  16.6 0.1 add_convert_fusion.1
  16.7 0.6 copy-done.3
  17.2 0.0 copy-done.4
  17.3 0.1 fusion
  17.4 0.5 copy-done.7
  17.9 15.0 %all-to-all-done.x_ref.mine = bf16[16,208,128]{2,1,0:T(8,128)(2,1)S(1)} async-done(((bf16[16,208,128]{2,1,0:T(8,128)(2,1)}), bf16[16,208,128]{2,1,0:T(8,128)(2,1)S(1)}, u32[]{:S(2)}, u32[]{:S(2)}) %all-to-all-start) | async-done | bytes 852000 | tf_op jit(solution)/shard_map/all_to_all | solution.py:292
  32.9 1.0 project.1
  33.8 14.7 %all-to-all-start.1 = ((bf16[32,24,128]{2,1,0:T(8,128)(2,1)}), bf16[32,24,128]{2,1,0:T(8,128)(2,1)S(1)}, u32[]{:S(2)}, u32[]{:S(2)}) async-start(bf16[32,24,128]{2,1,0:T(8,128)(2,1)} %bitcast.4), calls=%async_computation.1 | async-start | bytes 393216 | tf_op jit(solution)/shard_map/all_to_all | solution.py:307
  48.5 0.1 slice.3
  48.7 4.0 %collective-permute-start.2 = (bf16[16,192,128]{2,1,0:T(8,128)(2,1)S(1)}, bf16[16,192,128]{2,1,0:T(8,128)(2,1)S(1)}, u32[]{:S(2)}, u32[]{:S(2)}) collective-permute-start(bf16[16,192,128]{2,1,0:T(8,128)(2,1)S(1)} %slice.3), channel_id=1, source_target_pairs={{0,1},{1,0},{2,3},{3,2},{4,5},{5,4},{6,7},{7,6},{8,9},{9,8},{10,11... | collective-permute-start | bytes 2359304 | tf_op jit(solution)/shard_map/ppermute | solution.py:309
  52.7 0.1 pad_add_fusion.who
  52.8 0.7 keyval.1
  53.5 2.4 %collective-permute-start.3 = (bf16[128,128]{1,0:T(8,128)(2,1)S(1)}, bf16[128,128]{1,0:T(8,128)(2,1)S(1)}, u32[]{:S(2)}, u32[]{:S(2)}) collective-permute-start(bf16[128,128]{1,0:T(8,128)(2,1)S(1)} %get-tuple-element.31), channel_id=1, source_target_pairs={{0,16},{16,0},{32,48},{48,32},{64,80},{80,64},{96,112},{112,96},{1... | collective-permute-start | bytes 98312 | tf_op jit(solution)/shard_map/ppermute | solution.py:320
  55.9 4.2 %all-to-all-done.1 = bf16[32,24,128]{2,1,0:T(8,128)(2,1)S(1)} async-done(((bf16[32,24,128]{2,1,0:T(8,128)(2,1)}), bf16[32,24,128]{2,1,0:T(8,128)(2,1)S(1)}, u32[]{:S(2)}, u32[]{:S(2)}) %all-to-all-start.1) | async-done | bytes 196640 | tf_op jit(solution)/shard_map/all_to_all | solution.py:307
  60.1 0.7 query.1
  60.9 16.6 %all_to_all.42.q_ref = bf16[32,16,128]{2,1,0:T(8,128)(2,1)S(1)} all-to-all(bf16[32,16,128]{2,1,0:T(8,128)(2,1)S(1)} %get-tuple-element.32), channel_id=1, replica_groups=mesh['blk'=32,'rows'=16] {'blk'}, dimensions={0} | all-to-all | bytes 262144 | tf_op jit(solution)/shard_map/all_to_all | solution.py:331
  77.5 2.7 %attend.1 = bf16[768,128]{1,0:T(8,128)(2,1)S(1)} custom-call(s32[2]{0:T(128)S(1)} %pad_add_fusion.who, bf16[16,208,128]{2,1,0:T(8,128)(2,1)S(1)} %all-to-all-done.x_ref.mine, bf16[16,192,128]{2,1,0:T(8,128)(2,1)S(1)} %collective-permute-done.2.other, bf16[32,16,128]{2,1,0:T(8,128)(2,1)S(1)} %all_to_all.42.q_ref, f32[128,128]{1,0:T(8,128)S(1)} %get-tuple-element.33.keep, ...), custom_call_target="tpu_custom_call" | custom-call | tf_op jit(solution)/shard_map/attend/pallas_call | solution.py:332
  80.2 15.3 %all_to_all.43 = bf16[32,24,128]{2,1,0:T(8,128)(2,1)S(1)} all-to-all(bf16[32,24,128]{2,1,0:T(8,128)(2,1)S(1)} %bitcast.9), channel_id=1, replica_groups=mesh['blk'=32,'rows'=16] {'blk'}, dimensions={0} | all-to-all | bytes 393216 | tf_op jit(solution)/shard_map/all_to_all | solution.py:340
  95.5 0.8 combine.1
  96.2 0.0 copy-start.2
  96.2 14.0 %all_to_all.44.att = bf16[32,16,128]{2,1,0:T(8,128)(2,1)S(1)} all-to-all(bf16[32,16,128]{2,1,0:T(8,128)(2,1)S(1)} %combine.1), channel_id=1, replica_groups=mesh['blk'=32,'rows'=16] {'blk'}, dimensions={0} | all-to-all | bytes 262144 | tf_op jit(solution)/shard_map/all_to_all | solution.py:349
  110.2 0.2 output.1
  110.5 12.6 %all_to_all.45 = bf16[16,8,256]{2,1,0:T(8,128)(2,1)S(1)} all-to-all(bf16[16,8,256]{2,1,0:T(8,128)(2,1)S(1)} %bitcast.12), channel_id=1, replica_groups=mesh['blk'=32,'rows'=16] {'rows'}, dimensions={0} | all-to-all | bytes 131072 | tf_op jit(solution)/shard_map/all_to_all | solution.py:358
  123.1 0.6 add_convert_fusion
  (15 shorter events, 0.1 us)
Async XLA Ops:
  2.1 9.7 %copy-start.5 = (bf16[256,128]{1,0:T(8,128)(2,1)S(1)}, bf16[256,128]{1,0:T(8,128)(2,1)}, u32[]{:S(2)}) copy-start(bf16[256,128]{1,0:T(8,128)(2,1)} %param.16) | copy-start | bytes 196612
  2.2 30.7 %copy-start.1 = (bf16[256,512]{1,0:T(8,128)(2,1)S(1)}, bf16[256,512]{1,0:T(8,128)(2,1)}, u32[]{:S(2)}) copy-start(bf16[256,512]{1,0:T(8,128)(2,1)} %wq.1) | copy-start | bytes 786436
  2.2 30.7 %all-to-all-start = ((bf16[16,208,128]{2,1,0:T(8,128)(2,1)}), bf16[16,208,128]{2,1,0:T(8,128)(2,1)S(1)}, u32[]{:S(2)}, u32[]{:S(2)}) async-start(bf16[16,208,128]{2,1,0:T(8,128)(2,1)} %pack.1), calls=%async_computation | async-start | bytes 1703936 | tf_op jit(solution)/shard_map/all_to_all | solution.py:292
  11.9 36.7 %collective-permute-start.1 = (bf16[256,128]{1,0:T(8,128)(2,1)S(1)}, bf16[256,128]{1,0:T(8,128)(2,1)S(1)}, u32[]{:S(2)}, u32[]{:S(2)}) collective-permute-start(bf16[256,128]{1,0:T(8,128)(2,1)S(1)} %copy-done.5), channel_id=1, source_target_pairs={{0,1},{1,3},{2,5},{3,7},{4,9},{5,11},{6,13},{7,15},{8,0},{9,2},{10... | collective-permute-start | bytes 196616 | tf_op jit(solution)/shard_map/ppermute | solution.py:280
  15.2 33.5 %collective-permute-start = (bf16[256,128]{1,0:T(8,128)(2,1)S(1)}, bf16[256,128]{1,0:T(8,128)(2,1)S(1)}, u32[]{:S(2)}, u32[]{:S(2)}) collective-permute-start(bf16[256,128]{1,0:T(8,128)(2,1)S(1)} %copy-done.5), channel_id=1, source_target_pairs={{0,0},{1,2},{2,4},{3,6},{4,8},{5,10},{6,12},{7,14},{8,1},{9,3},{10... | collective-permute-start | bytes 196616 | tf_op jit(solution)/shard_map/ppermute | solution.py:279
  15.8 0.7 copy-start.6
  16.6 0.7 copy-start.3
  16.6 0.7 copy-start.4
  17.3 0.7 copy-start.7
  33.8 26.3 %all-to-all-start.1 = ((bf16[32,24,128]{2,1,0:T(8,128)(2,1)}), bf16[32,24,128]{2,1,0:T(8,128)(2,1)S(1)}, u32[]{:S(2)}, u32[]{:S(2)}) async-start(bf16[32,24,128]{2,1,0:T(8,128)(2,1)} %bitcast.4), calls=%async_computation.1 | async-start | bytes 393216 | tf_op jit(solution)/shard_map/all_to_all | solution.py:307
  48.7 28.8 %collective-permute-start.2 = (bf16[16,192,128]{2,1,0:T(8,128)(2,1)S(1)}, bf16[16,192,128]{2,1,0:T(8,128)(2,1)S(1)}, u32[]{:S(2)}, u32[]{:S(2)}) collective-permute-start(bf16[16,192,128]{2,1,0:T(8,128)(2,1)S(1)} %slice.3), channel_id=1, source_target_pairs={{0,1},{1,0},{2,3},{3,2},{4,5},{5,4},{6,7},{7,6},{8,9},{9,8},{10,11... | collective-permute-start | bytes 2359304 | tf_op jit(solution)/shard_map/ppermute | solution.py:309
  53.5 7.3 %collective-permute-start.3 = (bf16[128,128]{1,0:T(8,128)(2,1)S(1)}, bf16[128,128]{1,0:T(8,128)(2,1)S(1)}, u32[]{:S(2)}, u32[]{:S(2)}) collective-permute-start(bf16[128,128]{1,0:T(8,128)(2,1)S(1)} %get-tuple-element.31), channel_id=1, source_target_pairs={{0,16},{16,0},{32,48},{48,32},{64,80},{80,64},{96,112},{112,96},{1... | collective-permute-start | bytes 98312 | tf_op jit(solution)/shard_map/ppermute | solution.py:320
  95.5 14.8 %copy-start = (bf16[512,256]{1,0:T(8,128)(2,1)S(1)}, bf16[512,256]{1,0:T(8,128)(2,1)}, u32[]{:S(2)}) copy-start(bf16[512,256]{1,0:T(8,128)(2,1)} %w.1) | copy-start | bytes 786436
  96.2 14.0 %copy-start.2 = (bf16[8,256]{1,0:T(8,128)(2,1)S(1)}, bf16[8,256]{1,0:T(8,128)(2,1)}, u32[]{:S(2)}) copy-start(bf16[8,256]{1,0:T(8,128)(2,1)} %hidden.3) | copy-start | bytes 12292

commit v17 on v15

--- a/solution.py
+++ b/solution.py
@@ -68,7 +68,7 @@
 
 
 def gathered_rows(x_ref):
-    xr = x_ref[...].astype(F32)
+    xr = x_ref[:, X0:END, :].astype(F32)
     return jnp.concatenate(
         [xr[:, :8, :].reshape(128, HD), xr[:, 8:, :].reshape(128, HD)], axis=1
     )
@@ -292,14 +292,11 @@
     mine = lax.all_to_all(packed, "rows", 0, 0, tiled=True)
     cosine, sine = rotary_tables(jnp.concatenate([lax.dynamic_slice_in_dim(positions, 4 * b, 4, 0)] * 4))
     gain, cosine, sine = lax.optimization_barrier((norm_gain.reshape(1, 256), cosine, sine))
-    x_spec = pl.BlockSpec((16, END - X0, HD), lambda i: (0, X0 // 16, 0))
-    gain_spec = pl.BlockSpec((1, 256), lambda i: (0, 0))
     parts = pl.pallas_call(
         project_body,
-        grid=(1,),
         out_shape=sds((768, HD), BF),
-        in_specs=[x_spec, gain_spec, pl.BlockSpec((256, 512), lambda i: (0, 0))],
-        out_specs=pl.BlockSpec((768, HD), lambda i: (0, 0)),
+        in_specs=[VM] * 3,
+        out_specs=VM,
         compiler_params=params(),
         name="project",
     )(mine, gain, w_query)
@@ -309,10 +306,9 @@
     other = lax.ppermute(half, "rows", [(i, i ^ 1) for i in range(16)])
     keep, give = pl.pallas_call(
         keyval_body,
-        grid=(1,),
         out_shape=(sds((128, HD), F32), sds((128, HD), BF)),
-        in_specs=[SM, x_spec, gain_spec] + [pl.BlockSpec((256, HD), lambda i: (0, 0))] * 2,
-        out_specs=[pl.BlockSpec((128, HD), lambda i: (0, 0))] * 2,
+        in_specs=[SM] + [VM] * 4,
+        out_specs=(VM, VM),
         compiler_params=params(),
         cost_estimate=pl.CostEstimate(flops=10**9, bytes_accessed=1 << 18, transcendentals=0),
         name="keyval",

time: 124 us -> 124 us (level)
  no operation moved by 1% of the time
where the time goes in v17:
time: 124 us
  blocking collectives  42.7 us (34%)
  starting transfers between devices  39 us (31%)
  waiting for transfers between devices  30.1 us (24%)
  Pallas kernels  8.98 us (7%)
  local copies, waits for them, and re-layouts  1.95 us (2%)
    all_to_all x1, blocking collectives, on_device(): partial = lax.all_to_all(partial, 'blk', 0, 0, tiled=True)  15.9 us
    all_to_all x1, waiting for transfers between devices, on_device(): mine = lax.all_to_all(packed, 'rows', 0, 0, tiled=True)  15 us
    all_to_all x1, starting transfers between devices, on_device(): parts = lax.all_to_all(parts, 'blk', 0, 0, tiled=True)  14.7 us
    all_to_all x1, blocking collectives, on_device(): attended = lax.all_to_all(attended, 'blk', 0, 0, tiled=True)  14 us
    all_to_all x1, blocking collectives, on_device(): mixed = lax.all_to_all(mixed.reshape(16, 8, 256), 'rows', 0, 0, tiled=True)  12.7 us
    all_to_all x1, starting transfers between devices, on_device(): mine = lax.all_to_all(packed, 'rows', 0, 0, tiled=True)  9.71 us
    all_to_all x1, waiting for transfers between devices, on_device(): parts = lax.all_to_all(parts, 'blk', 0, 0, tiled=True)  7.32 us
    all_to_all x1, waiting for transfers between devices, on_device(): query = lax.all_to_all(query, 'blk', 0, 0, tiled=True)  6.82 us
  transfers between devices with their start and end apart: 7, of which 4 were waited for; matrix products, arithmetic and copies ran while one was open for 0% of the time, Pallas kernels for 2%

profile of v17, /device:TPU:1, one launch (start us, length us, event | category | flops | bytes accessed | tf_op | source)
XLA Modules:
  0.0 123.7 jit_solution(16064762990001490607)
XLA Ops:
  0.0 2.2 %pack.1 = bf16[16,208,128]{2,1,0:T(8,128)(2,1)} custom-call(s32[8]{0:T(128)} %lens.1, bf16[8,256]{1,0:T(8,128)(2,1)} %hidden.3, bf16[128,1024]{1,0:T(8,128)(2,1)} %keys.1, bf16[128,1024]{1,0:T(8,128)(2,1)} %values.1, bf16[64,1024]{1,0:T(8,128)(2,1)} %bitcast.13, bf16[64,1024]{1,0:T(8,128)(2,1)} %bitcast.14), custom_call_target="tpu_custom_call" | custom-call | tf_op jit(solution)/shard_map/pack/pallas_call | solution.py:281
  2.2 0.0 copy-start.1
  2.2 9.7 %all-to-all-start = ((bf16[16,208,128]{2,1,0:T(8,128)(2,1)}), bf16[16,208,128]{2,1,0:T(8,128)(2,1)S(1)}, u32[]{:S(2)}, u32[]{:S(2)}) async-start(bf16[16,208,128]{2,1,0:T(8,128)(2,1)} %pack.1), calls=%async_computation | async-start | bytes 1703936 | tf_op jit(solution)/shard_map/all_to_all | solution.py:292
  11.9 3.3 %collective-permute-start.1 = (bf16[256,128]{1,0:T(8,128)(2,1)S(1)}, bf16[256,128]{1,0:T(8,128)(2,1)S(1)}, u32[]{:S(2)}, u32[]{:S(2)}) collective-permute-start(bf16[256,128]{1,0:T(8,128)(2,1)S(1)} %copy-done.5), channel_id=1, source_target_pairs={{0,1},{1,3},{2,5},{3,7},{4,9},{5,11},{6,13},{7,15},{8,0},{9,2},{10... | collective-permute-start | bytes 196616 | tf_op jit(solution)/shard_map/ppermute | solution.py:280
  15.2 0.7 collective-permute-start
  15.9 0.6 copy-done.6
  16.5 0.1 dynamic_slice.3
  16.6 0.1 add_convert_fusion.1
  16.7 0.6 copy-done.3
  17.3 0.0 copy-done.4
  17.3 0.1 fusion
  17.4 0.5 copy-done.7
  18.0 15.0 %all-to-all-done.x_ref.mine = bf16[16,208,128]{2,1,0:T(8,128)(2,1)S(1)} async-done(((bf16[16,208,128]{2,1,0:T(8,128)(2,1)}), bf16[16,208,128]{2,1,0:T(8,128)(2,1)S(1)}, u32[]{:S(2)}, u32[]{:S(2)}) %all-to-all-start) | async-done | bytes 852000 | tf_op jit(solution)/shard_map/all_to_all | solution.py:292
  32.9 1.0 project.1
  33.9 14.7 %all-to-all-start.1 = ((bf16[32,24,128]{2,1,0:T(8,128)(2,1)}), bf16[32,24,128]{2,1,0:T(8,128)(2,1)S(1)}, u32[]{:S(2)}, u32[]{:S(2)}) async-start(bf16[32,24,128]{2,1,0:T(8,128)(2,1)} %bitcast.4), calls=%async_computation.1 | async-start | bytes 393216 | tf_op jit(solution)/shard_map/all_to_all | solution.py:304
  48.6 0.1 slice.3
  48.7 4.0 %collective-permute-start.2 = (bf16[16,192,128]{2,1,0:T(8,128)(2,1)S(1)}, bf16[16,192,128]{2,1,0:T(8,128)(2,1)S(1)}, u32[]{:S(2)}, u32[]{:S(2)}) collective-permute-start(bf16[16,192,128]{2,1,0:T(8,128)(2,1)S(1)} %slice.3), channel_id=1, source_target_pairs={{0,1},{1,0},{2,3},{3,2},{4,5},{5,4},{6,7},{7,6},{8,9},{9,8},{10,11... | collective-permute-start | bytes 2359304 | tf_op jit(solution)/shard_map/ppermute | solution.py:306
  52.7 0.1 pad_add_fusion.who
  52.8 7.3 %all-to-all-done.1 = bf16[32,24,128]{2,1,0:T(8,128)(2,1)S(1)} async-done(((bf16[32,24,128]{2,1,0:T(8,128)(2,1)}), bf16[32,24,128]{2,1,0:T(8,128)(2,1)S(1)}, u32[]{:S(2)}, u32[]{:S(2)}) %all-to-all-start.1) | async-done | bytes 196640 | tf_op jit(solution)/shard_map/all_to_all | solution.py:304
  60.1 1.4 %query.1 = (bf16[32,16,128]{2,1,0:T(8,128)(2,1)}, bf16[16,128]{1,0:T(8,128)(2,1)S(1)}, f32[16,128]{1,0:T(8,128)S(1)}) custom-call(s32[2]{0:T(128)S(1)} %pad_add_fusion.who, bf16[768,128]{1,0:T(8,128)(2,1)S(1)} %bitcast.11, f32[16,128]{1,0:T(8,128)S(1)} %get-tuple-element.24.cosine, f32[16,128]{1,0:T(8,128)S(1)} %get-tuple-element.25.sine), custom_call_target="tpu_custom_call" | custom-call | flops 2000000000 | bytes 1048576 | tf_op jit(solution)/shard_map/query/pallas_call | solution.py:317
  61.5 4.4 %all-to-all-start.2 = ((bf16[32,16,128]{2,1,0:T(8,128)(2,1)}), bf16[32,16,128]{2,1,0:T(8,128)(2,1)S(1)}, u32[]{:S(2)}, u32[]{:S(2)}) async-start(bf16[32,16,128]{2,1,0:T(8,128)(2,1)} %get-tuple-element.26), calls=%async_computation.2 | async-start | bytes 262144 | tf_op jit(solution)/shard_map/all_to_all | solution.py:326
  66.0 0.7 keyval.1
  66.7 2.1 %collective-permute-start.3 = (bf16[128,128]{1,0:T(8,128)(2,1)S(1)}, bf16[128,128]{1,0:T(8,128)(2,1)S(1)}, u32[]{:S(2)}, u32[]{:S(2)}) collective-permute-start(bf16[128,128]{1,0:T(8,128)(2,1)S(1)} %get-tuple-element.30), channel_id=1, source_target_pairs={{0,16},{16,0},{32,48},{48,32},{64,80},{80,64},{96,112},{112,96},{1... | collective-permute-start | bytes 98312 | tf_op jit(solution)/shard_map/ppermute | solution.py:316
  68.9 0.9 collective-permute-done.3.given
  69.8 6.8 %all-to-all-done.2.q_ref = bf16[32,16,128]{2,1,0:T(8,128)(2,1)S(1)} async-done(((bf16[32,16,128]{2,1,0:T(8,128)(2,1)}), bf16[32,16,128]{2,1,0:T(8,128)(2,1)S(1)}, u32[]{:S(2)}, u32[]{:S(2)}) %all-to-all-start.2) | async-done | bytes 131104 | tf_op jit(solution)/shard_map/all_to_all | solution.py:326
  76.6 2.7 %attend.1 = bf16[768,128]{1,0:T(8,128)(2,1)S(1)} custom-call(s32[2]{0:T(128)S(1)} %pad_add_fusion.who, bf16[16,208,128]{2,1,0:T(8,128)(2,1)S(1)} %all-to-all-done.x_ref.mine, bf16[16,192,128]{2,1,0:T(8,128)(2,1)S(1)} %collective-permute-done.2.other, bf16[32,16,128]{2,1,0:T(8,128)(2,1)S(1)} %all-to-all-done.2.q_ref, f32[128,128]{1,0:T(8,128)S(1)} %get-tuple-element.29.keep, ...), custom_call_target="tpu_custom_call" | custom-call | tf_op jit(solution)/shard_map/attend/pallas_call | solution.py:327
  79.4 15.9 %all_to_all.42 = bf16[32,24,128]{2,1,0:T(8,128)(2,1)S(1)} all-to-all(bf16[32,24,128]{2,1,0:T(8,128)(2,1)S(1)} %bitcast.9), channel_id=1, replica_groups=mesh['blk'=32,'rows'=16] {'blk'}, dimensions={0} | all-to-all | bytes 393216 | tf_op jit(solution)/shard_map/all_to_all | solution.py:335
  95.3 0.8 combine.1
  96.1 14.0 %all_to_all.43.att = bf16[32,16,128]{2,1,0:T(8,128)(2,1)S(1)} all-to-all(bf16[32,16,128]{2,1,0:T(8,128)(2,1)S(1)} %combine.1), channel_id=1, replica_groups=mesh['blk'=32,'rows'=16] {'blk'}, dimensions={0} | all-to-all | bytes 262144 | tf_op jit(solution)/shard_map/all_to_all | solution.py:344
  110.2 0.2 output.1
  110.4 12.7 %all_to_all.44 = bf16[16,8,256]{2,1,0:T(8,128)(2,1)S(1)} all-to-all(bf16[16,8,256]{2,1,0:T(8,128)(2,1)S(1)} %bitcast.12), channel_id=1, replica_groups=mesh['blk'=32,'rows'=16] {'rows'}, dimensions={0} | all-to-all | bytes 131072 | tf_op jit(solution)/shard_map/all_to_all | solution.py:353
  123.1 0.6 add_convert_fusion
  (16 shorter events, 0.1 us)
Async XLA Ops:
  2.2 9.7 %copy-start.5 = (bf16[256,128]{1,0:T(8,128)(2,1)S(1)}, bf16[256,128]{1,0:T(8,128)(2,1)}, u32[]{:S(2)}) copy-start(bf16[256,128]{1,0:T(8,128)(2,1)} %param.16) | copy-start | bytes 196612
  2.2 30.7 %copy-start.1 = (bf16[256,512]{1,0:T(8,128)(2,1)S(1)}, bf16[256,512]{1,0:T(8,128)(2,1)}, u32[]{:S(2)}) copy-start(bf16[256,512]{1,0:T(8,128)(2,1)} %wq.1) | copy-start | bytes 786436
  2.2 30.7 %all-to-all-start = ((bf16[16,208,128]{2,1,0:T(8,128)(2,1)}), bf16[16,208,128]{2,1,0:T(8,128)(2,1)S(1)}, u32[]{:S(2)}, u32[]{:S(2)}) async-start(bf16[16,208,128]{2,1,0:T(8,128)(2,1)} %pack.1), calls=%async_computation | async-start | bytes 1703936 | tf_op jit(solution)/shard_map/all_to_all | solution.py:292
  11.9 36.7 %collective-permute-start.1 = (bf16[256,128]{1,0:T(8,128)(2,1)S(1)}, bf16[256,128]{1,0:T(8,128)(2,1)S(1)}, u32[]{:S(2)}, u32[]{:S(2)}) collective-permute-start(bf16[256,128]{1,0:T(8,128)(2,1)S(1)} %copy-done.5), channel_id=1, source_target_pairs={{0,1},{1,3},{2,5},{3,7},{4,9},{5,11},{6,13},{7,15},{8,0},{9,2},{10... | collective-permute-start | bytes 196616 | tf_op jit(solution)/shard_map/ppermute | solution.py:280
  15.2 33.5 %collective-permute-start = (bf16[256,128]{1,0:T(8,128)(2,1)S(1)}, bf16[256,128]{1,0:T(8,128)(2,1)S(1)}, u32[]{:S(2)}, u32[]{:S(2)}) collective-permute-start(bf16[256,128]{1,0:T(8,128)(2,1)S(1)} %copy-done.5), channel_id=1, source_target_pairs={{0,0},{1,2},{2,4},{3,6},{4,8},{5,10},{6,12},{7,14},{8,1},{9,3},{10... | collective-permute-start | bytes 196616 | tf_op jit(solution)/shard_map/ppermute | solution.py:279
  15.9 0.7 copy-start.6
  16.6 0.7 copy-start.3
  16.6 0.7 copy-start.4
  17.3 0.7 copy-start.7
  33.9 26.3 %all-to-all-start.1 = ((bf16[32,24,128]{2,1,0:T(8,128)(2,1)}), bf16[32,24,128]{2,1,0:T(8,128)(2,1)S(1)}, u32[]{:S(2)}, u32[]{:S(2)}) async-start(bf16[32,24,128]{2,1,0:T(8,128)(2,1)} %bitcast.4), calls=%async_computation.1 | async-start | bytes 393216 | tf_op jit(solution)/shard_map/all_to_all | solution.py:304
  48.7 28.0 %collective-permute-start.2 = (bf16[16,192,128]{2,1,0:T(8,128)(2,1)S(1)}, bf16[16,192,128]{2,1,0:T(8,128)(2,1)S(1)}, u32[]{:S(2)}, u32[]{:S(2)}) collective-permute-start(bf16[16,192,128]{2,1,0:T(8,128)(2,1)S(1)} %slice.3), channel_id=1, source_target_pairs={{0,1},{1,0},{2,3},{3,2},{4,5},{5,4},{6,7},{7,6},{8,9},{9,8},{10,11... | collective-permute-start | bytes 2359304 | tf_op jit(solution)/shard_map/ppermute | solution.py:306
  61.5 15.1 %all-to-all-start.2 = ((bf16[32,16,128]{2,1,0:T(8,128)(2,1)}), bf16[32,16,128]{2,1,0:T(8,128)(2,1)S(1)}, u32[]{:S(2)}, u32[]{:S(2)}) async-start(bf16[32,16,128]{2,1,0:T(8,128)(2,1)} %get-tuple-element.26), calls=%async_computation.2 | async-start | bytes 262144 | tf_op jit(solution)/shard_map/all_to_all | solution.py:326
  66.7 3.1 %collective-permute-start.3 = (bf16[128,128]{1,0:T(8,128)(2,1)S(1)}, bf16[128,128]{1,0:T(8,128)(2,1)S(1)}, u32[]{:S(2)}, u32[]{:S(2)}) collective-permute-start(bf16[128,128]{1,0:T(8,128)(2,1)S(1)} %get-tuple-element.30), channel_id=1, source_target_pairs={{0,16},{16,0},{32,48},{48,32},{64,80},{80,64},{96,112},{112,96},{1... | collective-permute-start | bytes 98312 | tf_op jit(solution)/shard_map/ppermute | solution.py:316
  95.3 14.8 %copy-start = (bf16[512,256]{1,0:T(8,128)(2,1)S(1)}, bf16[512,256]{1,0:T(8,128)(2,1)}, u32[]{:S(2)}) copy-start(bf16[512,256]{1,0:T(8,128)(2,1)} %w.1) | copy-start | bytes 786436
  96.1 14.1 %copy-start.2 = (bf16[8,256]{1,0:T(8,128)(2,1)S(1)}, bf16[8,256]{1,0:T(8,128)(2,1)}, u32[]{:S(2)}) copy-start(bf16[8,256]{1,0:T(8,128)(2,1)} %hidden.3) | copy-start | bytes 12292
